TPU v7x, 256 devices: a whole 4x4x8 slice. The times are simulated.
256 devices in a mesh: ctx: 64 (over x, z_lo, y), dp: 4 (over z_hi, core).
Axes of the slice: x: 4, y: 4, z: 8 (z_hi: 2, z_lo: 4; z = z_hi * 4 + z_lo), core: 2. Of those that a mesh axis runs over, the one named last changes fastest.
Arguments:
- tokens: bfloat16 [4, 8192, 1536], P('dp', 'ctx'), may hold values from -6 to 6
- w_in: bfloat16 [1536, 2880], replicated, may hold values from -0.15625 to 0.15625
- conv_taps: float32 [7, 2880], replicated, may hold values from -2.4 to 2.4
- residues: float32 [960, 16], P('ctx'), may hold values from -1.5 to 1.5
- rates: float32 [960, 16], P('ctx'), may hold values from 3.6621094e-05 to 0.08
- cotangent: bfloat16 [4, 8192, 960], P('dp', 'ctx'), may hold values from -6 to 6
Outputs:
- output: bfloat16 [4, 8192, 960], P('dp', 'ctx')
- grad_tokens: bfloat16 [4, 8192, 1536], P('dp', 'ctx')
- grad_weight: bfloat16 [1536, 2880], P('ctx', 'dp')
- grad_taps: float32 [7, 2880], replicated
- grad_residues: float32 [960, 16], P('ctx')
All inputs are finite; a program needn't handle non-finite values.
Results may differ from a plain program's by a relative error of at most 0.02.
Values may be sent and summed in bfloat16 or wider, within the bound.
No kernel may reach another device: no remote copies, remote signals or barrier semaphores. Data moves between devices by JAX's collectives and lax.ppermute only.
A program may use at most 192 MiB of HBM per device.

v0:
```python
import math

import jax
import jax.numpy as jnp
from jax import lax
from jax.sharding import PartitionSpec as P

BLK = 128


precise = lax.Precision.HIGH


def shifted(block, axis, distance):
    devices = range(lax.axis_size(axis))
    route = [(i - distance, i) for i in devices if i - distance in devices]
    return lax.ppermute(block, axis, route)


def powers(rates, offsets):
    return jnp.exp(-rates[:, :, None] * offsets[None, None, :])


def mixed_dot(form, data, factor):
    upper = factor.astype(jnp.bfloat16)
    lower = (factor - upper.astype(jnp.float32)).astype(jnp.bfloat16)
    first = jnp.einsum(form, data, upper, preferred_element_type=jnp.float32)
    return first + jnp.einsum(form, data, lower, preferred_element_type=jnp.float32)


def lag_matrix(reff, rates, blk):
    pos = jnp.arange(blk).astype(jnp.float32)
    lagged = jnp.einsum("ck,ckn->cn", reff, powers(rates, pos), precision=precise)
    index = jnp.arange(blk)[:, None] - jnp.arange(blk)[None, :]
    return jnp.where(index[None] >= 0, lagged[:, jnp.maximum(index, 0)], 0.0)


def block_links(rates, count, blk):
    order = jnp.arange(count)
    gap = order[:, None] - order[None, :] - 1
    depth = (blk * jnp.maximum(gap, 0)).astype(jnp.float32)
    return jnp.where(
        gap[None, None] >= 0, jnp.exp(-rates[:, :, None, None] * depth[None, None]), 0.0
    )


def forward_local(u3, reff, rates, incoming):
    count, blk = (u3.shape[1], u3.shape[2])
    pos = jnp.arange(blk).astype(jnp.float32)
    inner = mixed_dot("cbj,cij->cbi", u3, lag_matrix(reff, rates, blk))
    ends = mixed_dot("cbj,ckj->ckb", u3, powers(rates, blk - 1.0 - pos))
    entry = powers(rates, (blk * jnp.arange(count)).astype(jnp.float32))
    starts = jnp.einsum("ckbd,ckd->ckb", block_links(rates, count, blk), ends, precision=precise)
    starts = starts + entry * incoming[:, :, None]
    outer = jnp.einsum(
        "ckb,cki->cbi", reff[:, :, None] * starts, powers(rates, pos + 1.0), precision=precise
    )
    return (inner + outer, starts)


def backward_local(g3, u3, reff, rates, starts, later):
    count, blk = (g3.shape[1], g3.shape[2])
    pos = jnp.arange(blk).astype(jnp.float32)
    inner = mixed_dot("cbi,cij->cbj", g3, lag_matrix(reff, rates, blk))
    heads = mixed_dot("cbi,cki->ckb", g3, powers(rates, pos))
    exits = powers(rates, (blk * (count - 1 - jnp.arange(count))).astype(jnp.float32))
    tails = jnp.einsum("ckdb,ckd->ckb", block_links(rates, count, blk), heads, precision=precise)
    tails = tails + exits * later[:, :, None]
    outer = jnp.einsum(
        "ckb,ckj->cbj", reff[:, :, None] * tails, powers(rates, blk - pos), precision=precise
    )
    cross = jnp.sum(starts * heads, axis=2) * jnp.exp(-rates)
    pair = jnp.einsum("cbi,cbj->cij", g3, u3, preferred_element_type=jnp.float32)
    index = jnp.arange(blk)[:, None] - jnp.arange(blk)[None, :]
    pair = jnp.where(index[None] >= 0, pair, 0.0)
    near = jnp.einsum(
        "cij,ckj->cki", pair, jnp.exp(rates[:, :, None] * pos[None, None, :]), precision=precise
    )
    near = jnp.sum(near * powers(rates, pos), axis=2)
    return (inner + outer, cross + near)


def grouped(func, arrays):
    chans = arrays[0].shape[0]
    blk = arrays[0].shape[-1]
    groups = max(1, chans * blk * blk // (1 << 22))
    while chans % groups:
        groups = groups + 1
    split = tuple((a.reshape((groups, chans // groups) + a.shape[1:]) for a in arrays))
    results = lax.map(lambda items: func(*items), split)
    return tuple((r.reshape((chans,) + r.shape[2:]) for r in results))


def local(tokens, w_in, conv_taps, residues, rates, cotangent):
    rim = conv_taps.shape[0] - 1
    feats = tokens[0]
    rows = feats.shape[0]
    width = cotangent.shape[2]
    modes = rates.shape[1]
    total = lax.axis_size("ctx") * rows
    scale = 1.0 / math.sqrt(lax.axis_size("dp") * total)
    z = jnp.dot(feats, w_in, preferred_element_type=jnp.float32).astype(jnp.bfloat16)
    before = shifted(z[rows - rim :], "ctx", 1)
    padded = jnp.concatenate([before, z], axis=0)
    mixed = jnp.zeros((rows, z.shape[1]), jnp.float32)
    for j in range(rim + 1):
        mixed = mixed + conv_taps[j] * padded[rim - j : rim - j + rows].astype(jnp.float32)
    query = mixed[:, :width]
    keyed = mixed[:, width : 2 * width]
    valued = mixed[:, 2 * width :]
    product = (keyed * valued).astype(jnp.bfloat16)
    amp_mine = jnp.sqrt(-jnp.expm1(-2.0 * rates))
    reff = residues * amp_mine
    blk = min(BLK, total)
    spread = lax.all_to_all(product.T, "ctx", split_axis=0, concat_axis=1, tiled=True)
    u3 = spread.reshape(spread.shape[0], total // blk, blk)
    empty = jnp.zeros((spread.shape[0], modes), jnp.float32)
    conv3, starts = grouped(forward_local, (u3, reff, rates, empty))
    back = lax.all_to_all(
        conv3.reshape(spread.shape[0], total).astype(jnp.bfloat16),
        "ctx",
        split_axis=1,
        concat_axis=0,
        tiled=True,
    )
    long_out = back.T
    output = (query * long_out.astype(jnp.float32)).astype(jnp.bfloat16)
    upstream = cotangent[0].astype(jnp.float32)
    dquery = upstream * long_out.astype(jnp.float32)
    dlong = (upstream * query).astype(jnp.bfloat16)
    gspread = lax.all_to_all(dlong.T, "ctx", split_axis=0, concat_axis=1, tiled=True)
    g3 = gspread.reshape(gspread.shape[0], total // blk, blk)
    du3, draw = grouped(backward_local, (g3, u3, reff, rates, starts, empty))
    dback = lax.all_to_all(
        du3.reshape(gspread.shape[0], total).astype(jnp.bfloat16),
        "ctx",
        split_axis=1,
        concat_axis=0,
        tiled=True,
    )
    dproduct = dback.T
    filt = draw
    filt = lax.psum(filt, "dp")
    grad_residues = amp_mine * filt * scale
    dprod32 = dproduct.astype(jnp.float32)
    dmixed = jnp.concatenate([dquery, dprod32 * valued, dprod32 * keyed], axis=1).astype(
        jnp.bfloat16
    )
    dm32 = dmixed.astype(jnp.float32)
    tap_rows = []
    for j in range(rim + 1):
        tap_rows.append(
            jnp.sum(dm32 * padded[rim - j : rim - j + rows].astype(jnp.float32), axis=0)
        )
    grad_taps = lax.psum(jnp.stack(tap_rows, axis=0), ("ctx", "dp")) * scale
    after = shifted(dmixed[:rim], "ctx", -1)
    dpad = jnp.concatenate([dmixed, after], axis=0)
    dz = jnp.zeros((rows, dmixed.shape[1]), jnp.float32)
    for j in range(rim + 1):
        dz = dz + conv_taps[j] * dpad[j : j + rows].astype(jnp.float32)
    dz = dz.astype(jnp.bfloat16)
    grad_feats = lax.dot_general(
        dz, w_in, (((1,), (1,)), ((), ())), preferred_element_type=jnp.float32
    ).astype(jnp.bfloat16)
    full_term = lax.dot_general(
        feats, dz, (((0,), (0,)), ((), ())), preferred_element_type=jnp.float32
    )
    feat_count = full_term.shape[0]
    chan_count = full_term.shape[1]
    ctx_count = lax.axis_size("ctx")
    pieces = full_term.reshape(ctx_count, feat_count // ctx_count, chan_count)
    arrived = lax.all_to_all(
        pieces.astype(jnp.bfloat16), "ctx", split_axis=0, concat_axis=0, tiled=True
    ).astype(pieces.dtype)
    row_part = jnp.sum(arrived, axis=0)
    weight_sum = lax.psum_scatter(
        row_part.astype(jnp.bfloat16), "dp", scatter_dimension=1, tiled=True
    ).astype(jnp.float32)
    grad_weight = (weight_sum * scale).astype(jnp.bfloat16)
    return (output[None], grad_feats[None], grad_weight, grad_taps, grad_residues)


def solution(mesh):
    in_specs = (
        P("dp", "ctx", None),
        P(),
        P(),
        P("ctx", None),
        P("ctx", None),
        P("dp", "ctx", None),
    )
    out_specs = (P("dp", "ctx", None), P("dp", "ctx", None), P("ctx", "dp"), P(), P("ctx", None))
    return jax.shard_map(local, mesh=mesh, in_specs=in_specs, out_specs=out_specs, check_vma=False)
```

profile of v0, /device:TPU:32, one launch (start us, length us, event | category | flops | bytes accessed | tf_op | source)
XLA Modules:
  0.0 649.5 jit_solution(15393544391522919796)
XLA Ops:
  8.0 1.0 copy-done
  9.0 6.0 convolution_convert_fusion.1
  15.6 3.5 collective-permute-start
  19.7 3.9 collective-permute-done
  24.1 5.5 fusion.17
  29.7 1.2 copy-done.1
  31.0 0.8 all_to_all.42
  31.7 9.5 %all-to-all-start.2 = ((bf16[64,15,128]{2,1,0:T(8,128)(2,1)}), bf16[64,15,128]{2,1,0:T(8,128)(2,1)S(1)}, u32[]{:S(2)}, u32[]{:S(2)}) async-start(bf16[64,15,128]{2,1,0:T(8,128)(2,1)} %all_to_all.42), calls=%async_computation.2 | async-start | bytes 524288 | tf_op jit(solution)/shard_map/all_to_all | solution.py:131
  41.4 54.4 %gather_fusion = f32[16384,15]{1,0:T(8,128)} fusion(f32[15,128]{0,1:T(8,128)S(1)} %bitcast.94, s32[16384]{0:T(1024)S(1)} %bitcast_clamp_fusion), kind=kCustom, calls=%fused_computation | custom fusion | bytes 2031616 | tf_op jit(solution)/shard_map/while/body/eval_jaxpr/gather | solution.py:35
  95.8 5.3 copy.25
  101.9 4.0 fusion.1
  106.4 0.7 fusion.33
  107.3 21.0 %all_to_all.51 = bf16[15,64,128]{2,0,1:T(8,128)(2,1)S(1)} all-to-all(bf16[15,64,128]{2,0,1:T(8,128)(2,1)S(1)} %copy.28), channel_id=1, replica_groups=mesh['ctx'=64,'dp'=4] {'ctx'}, dimensions={1} | all-to-all | bytes 491520 | tf_op jit(solution)/shard_map/all_to_all | solution.py:134
  128.3 0.8 convert_bitcast_fusion
  129.2 1.9 reshape.143
  131.0 2.2 fusion.43
  133.3 0.8 all_to_all.18
  134.0 5.9 all-to-all-start
  141.6 8.9 %all-to-all-done = bf16[64,15,128]{2,1,0:T(8,128)(2,1)S(1)} async-done(((bf16[64,15,128]{2,1,0:T(8,128)(2,1)}), bf16[64,15,128]{2,1,0:T(8,128)(2,1)S(1)}, u32[]{:S(2)}, u32[]{:S(2)}) %all-to-all-start) | async-done | bytes 245792 | tf_op jit(solution)/shard_map/all_to_all | solution.py:115
  150.5 1.0 fusion.61
  151.4 1.0 convolution_add_fusion.5
  152.4 7.0 %fusion.2 = f32[15,16,1,64]{3,2,1,0:T(1,128)S(1)} fusion(f32[15,16,64,1]{2,3,1,0:T(1,128)S(1)} %bitcast.104, f32[64,64]{1,0:T(8,128)} %copy-done.23, f32[15,16]{1,0:T(8,128)S(1)} %get-tuple-element.71, pred[64,64]{1,0:T(8,128)(4,1)} %copy-done.24), kind=kOutput, calls=%fused_computation.5 | convolution fusion | flops 7864320 | bytes 144320 | tf_op jit(solution)/shard_map/while/body/eval_jaxpr/ckbd,ckd->ckb/dot_general | solution.py:53
  160.6 0.7 fusion.32
  161.5 16.2 %all_to_all.52 = bf16[15,64,128]{2,0,1:T(8,128)(2,1)S(1)} all-to-all(bf16[15,64,128]{2,0,1:T(8,128)(2,1)S(1)} %copy.26), channel_id=1, replica_groups=mesh['ctx'=64,'dp'=4] {'ctx'}, dimensions={1} | all-to-all | bytes 491520 | tf_op jit(solution)/shard_map/all_to_all | solution.py:119
  177.8 0.8 convert_bitcast_fusion.1
  178.6 1.9 reshape.142
  180.5 2.0 fusion.41
  182.5 0.9 pad_maximum_fusion.2
  183.4 1.4 copy.29
  184.8 4.1 collective-permute-start.1
  189.0 1.8 collective-permute-done.1
  190.8 1.2 copy.30
  192.0 1.5 pad_maximum_fusion
  193.5 1.1 copy-done.4
  194.6 11.3 %fusion = bf16[1536,2880]{0,1:T(8,128)(2,1)} fusion(bf16[1,128,1536]{2,1,0:T(8,128)(2,1)S(1)} %copy-done, bf16[134,2880]{0,1:T(8,128)(2,1)S(1)} %pad_maximum_fusion, f32[2880]{0:T(1024)S(1)} %copy-done.20, f32[2880]{0:T(1024)S(1)} %copy-done.22, f32[2880]{0:T(1024)S(1)} %copy-done.12, f32[2880]{0:T(1024)S(1)} %copy-done.14, f32[2880]{0:T(1024)S(1)} %copy-done.16, ...), kind=kOutput, calls=%fused_computation.2 | convolution fusion | flops 1146470400 | bytes 14487552 | tf_op jit(solution)/shard_map/dot_general | solution.py:165
  206.0 12.5 %copy.31 = bf16[1536,2880]{1,0:T(8,128)(2,1)} copy(bf16[1536,2880]{0,1:T(8,128)(2,1)} %fusion) | data formatting | bytes 17694720 | tf_op jit(solution)/shard_map/convert_element_type | solution.py:173
  218.4 10.6 %all-to-all-start.4 = ((bf16[64,24,2880]{2,1,0:T(8,128)(2,1)}), bf16[64,24,2880]{2,1,0:T(8,128)(2,1)}, u32[]{:S(2)}, u32[]{:S(2)}) async-start(bf16[64,24,2880]{2,1,0:T(8,128)(2,1)} %bitcast.95), calls=%async_computation.4 | async-start | bytes 18087936 | tf_op jit(solution)/shard_map/all_to_all | solution.py:172
  229.7 1.0 fusion.34
  230.7 102.7 %psum.15 = f32[15,16]{1,0:T(8,128)S(1)} all-reduce(f32[15,16]{1,0:T(8,128)S(1)} %multiply_add_fusion.2), channel_id=1, replica_groups=mesh['ctx'=64,'dp'=4] {'dp'}, use_global_device_ids=true, to_apply=%region_12.13 | all-reduce | flops 240 | bytes 1920 | tf_op jit(solution)/shard_map/psum | solution.py:143
  334.1 5.0 fusion.30
  339.3 0.8 stack.31
  340.3 14.8 %fusion.11 = bf16[1,128,1536]{2,1,0:T(8,128)(2,1)} fusion(bf16[1536,2880]{0,1:T(8,128)(2,1)} %param.7, bf16[134,2880]{0,1:T(8,128)(2,1)} %copy-done.4, f32[2880]{0:T(1024)S(1)} %copy-done.20, f32[2880]{0:T(1024)S(1)} %copy-done.22, f32[2880]{0:T(1024)S(1)} %copy-done.12, f32[2880]{0:T(1024)S(1)} %copy-done.14, f32[2880]{0:T(1024)S(1)} %copy-done.16, ...), kind=kOutput, calls=%fused_computation.24 | convolution fusion | flops 1142243328 | bytes 14482176 | tf_op jit(solution)/shard_map/dot_general | solution.py:162
  355.1 71.7 %all-to-all-done.4 = bf16[64,24,2880]{2,1,0:T(8,128)(2,1)} async-done(((bf16[64,24,2880]{2,1,0:T(8,128)(2,1)}), bf16[64,24,2880]{2,1,0:T(8,128)(2,1)}, u32[]{:S(2)}, u32[]{:S(2)}) %all-to-all-start.4) | async-done | bytes 8847392 | tf_op jit(solution)/shard_map/all_to_all | solution.py:172
  426.8 4.9 reduce_sum.95
  431.8 1.2 copy.38
  432.9 205.6 %all-reduce.2.cloned.1.call-done = f32[7,2880]{1,0:T(8,128)} async-done(((f32[7,2880]{1,0:T(8,128)}), f32[7,2880]{1,0:T(8,128)}) %all-reduce.2.cloned.1.call-update) | async-done | bytes 80656 | tf_op jit(solution)/shard_map/psum | solution.py:155
  638.6 1.5 broadcast_multiply_fusion
  640.1 1.0 copy.39
  (99 shorter events, 8.4 us)
Async XLA Ops:
  8.0 1.0 copy-start
  15.0 4.1 copy-start.9
  15.0 4.1 copy-start.25
  15.0 4.4 copy-start.10
  15.6 8.1 %collective-permute-start = (bf16[6,2880]{1,0:T(8,128)(2,1)S(1)}, bf16[6,2880]{1,0:T(8,128)(2,1)S(1)}, u32[]{:S(2)}, u32[]{:S(2)}) collective-permute-start(bf16[6,2880]{1,0:T(8,128)(2,1)S(1)} %copy.22), channel_id=1, source_target_pairs={{0,4},{4,8},{8,12},{12,16},{16,20},{20,24},{24,28},{28,32},{32,36}... | collective-permute-start | bytes 103688 | tf_op jit(solution)/shard_map/ppermute | solution.py:17
  19.7 9.9 %copy-start.11 = (f32[2880]{0:T(1024)}, f32[2880]{0:T(1024)S(1)}, u32[]{:S(2)}) copy-start(f32[2880]{0:T(1024)S(1)} %get-tuple-element.47) | copy-start | bytes 34564
  19.7 9.9 %copy-start.13 = (f32[2880]{0:T(1024)}, f32[2880]{0:T(1024)S(1)}, u32[]{:S(2)}) copy-start(f32[2880]{0:T(1024)S(1)} %get-tuple-element.56) | copy-start | bytes 34564
  19.7 9.9 %copy-start.15 = (f32[2880]{0:T(1024)}, f32[2880]{0:T(1024)S(1)}, u32[]{:S(2)}) copy-start(f32[2880]{0:T(1024)S(1)} %get-tuple-element.57) | copy-start | bytes 34564
  19.7 9.9 %copy-start.17 = (f32[2880]{0:T(1024)}, f32[2880]{0:T(1024)S(1)}, u32[]{:S(2)}) copy-start(f32[2880]{0:T(1024)S(1)} %get-tuple-element.58) | copy-start | bytes 34564
  19.7 9.9 %copy-start.19 = (f32[2880]{0:T(1024)}, f32[2880]{0:T(1024)S(1)}, u32[]{:S(2)}) copy-start(f32[2880]{0:T(1024)S(1)} %get-tuple-element.59) | copy-start | bytes 34564
  19.7 9.9 %copy-start.21 = (f32[2880]{0:T(1024)}, f32[2880]{0:T(1024)S(1)}, u32[]{:S(2)}) copy-start(f32[2880]{0:T(1024)S(1)} %get-tuple-element.60) | copy-start | bytes 34564
  24.1 6.8 %copy-start.5 = (bf16[1,128,960]{1,2,0:T(8,128)(2,1)S(1)}, bf16[1,128,960]{1,2,0:T(8,128)(2,1)}, u32[]{:S(2)}) copy-start(bf16[1,128,960]{1,2,0:T(8,128)(2,1)} %param.11) | copy-start | bytes 737284
  29.7 1.2 copy-start.1
  31.7 69.5 %all-to-all-start.2 = ((bf16[64,15,128]{2,1,0:T(8,128)(2,1)}), bf16[64,15,128]{2,1,0:T(8,128)(2,1)S(1)}, u32[]{:S(2)}, u32[]{:S(2)}) async-start(bf16[64,15,128]{2,1,0:T(8,128)(2,1)} %all_to_all.42), calls=%async_computation.2 | async-start | bytes 524288 | tf_op jit(solution)/shard_map/all_to_all | solution.py:131
  101.2 4.7 copy-start.24
  101.3 4.6 copy-start.23
  134.0 16.4 %all-to-all-start = ((bf16[64,15,128]{2,1,0:T(8,128)(2,1)}), bf16[64,15,128]{2,1,0:T(8,128)(2,1)S(1)}, u32[]{:S(2)}, u32[]{:S(2)}) async-start(bf16[64,15,128]{2,1,0:T(8,128)(2,1)} %all_to_all.18), calls=%async_computation | async-start | bytes 524288 | tf_op jit(solution)/shard_map/all_to_all | solution.py:115
  159.5 0.9 copy-start.7
  159.9 0.6 copy-start.26
  159.9 0.7 copy-start.28
  161.4 19.2 %copy-start.6 = (bf16[1,128,960]{1,2,0:T(8,128)(2,1)S(1)}, bf16[1,128,960]{1,2,0:T(8,128)(2,1)}, u32[]{:S(2)}) copy-start(bf16[1,128,960]{1,2,0:T(8,128)(2,1)} %param.11) | copy-start | bytes 737284
  178.6 3.9 copy-start.2
  178.6 3.9 copy-start.3
  184.8 6.0 collective-permute-start.1
  192.0 2.6 copy-start.12
  192.0 2.6 copy-start.14
  192.0 2.6 copy-start.16
  192.0 2.6 copy-start.18
  192.0 2.6 copy-start.20
  192.0 2.6 copy-start.22
  193.5 1.1 copy-start.4
  218.4 10.7 %copy-start.8 = (f32[15,16,1,64]{3,2,1,0:T(1,128)S(1)}, f32[15,16,1,64]{3,2,1,0:T(1,128)}, u32[]{:S(2)}) copy-start(f32[15,16,1,64]{3,2,1,0:T(1,128)} %copy-done.7) | copy-start | bytes 184324
  218.4 10.7 %copy-start.27 = (f32[64]{0:T(128)S(1)}, f32[64]{0:T(128)}, u32[]{:S(2)}) copy-start(f32[64]{0:T(128)} %multiply_convert_fusion.4) | copy-start | bytes 772
  218.4 208.4 %all-to-all-start.4 = ((bf16[64,24,2880]{2,1,0:T(8,128)(2,1)}), bf16[64,24,2880]{2,1,0:T(8,128)(2,1)}, u32[]{:S(2)}, u32[]{:S(2)}) async-start(bf16[64,24,2880]{2,1,0:T(8,128)(2,1)} %bitcast.95), calls=%async_computation.4 | async-start | bytes 18087936 | tf_op jit(solution)/shard_map/all_to_all | solution.py:172
  229.1 409.5 %all-reduce.2.cloned.1.call-start = ((), (), s32[]{:S(2)}) async-start(), calls=%async_computation.6 | async-start | bytes 188416 | tf_op jit(solution)/shard_map/psum | solution.py:155
  340.0 300.1 %reduce-scatter.4.cloned.1.call-start = ((), (), s32[]{:S(2)}) async-start(), calls=%async_computation.7 | async-start | bytes 921600
Sparse Core Ops, SparseCore 0:
  340.2 298.3 all-reduce.1
Sparse Core Ops, SparseCore 1:
  433.0 38.9 reduce-scatter.3
where the time goes:
time: 662 us; the launch traced here: 649 us
  waiting for transfers between devices  292 us (44%)
  blocking collectives  140 us (21%)
  local copies, waits for them, and re-layouts  88.6 us (13%)
  matrix products  50.2 us (8%)
  starting transfers between devices  34 us (5%)
  other arithmetic  28.5 us (4%)
  between operations  16.3 us (2%)
    psum x1, waiting for transfers between devices, local(): grad_taps = lax.psum(jnp.stack(tap_rows, axis=0), ('ctx', 'dp')) * scale  206 us
    psum x1, blocking collectives, local(): filt = lax.psum(filt, 'dp')  103 us
    all_to_all x1, waiting for transfers between devices, local(): lax.all_to_all(pieces.astype(jnp.bfloat16), 'ctx', split_axis=0, concat_a...  71.7 us
    gather x2, local copies, waits for them, and re-layouts, lag_matrix(): return jnp.where(index[None] >= 0, lagged[:, jnp.maximum(index, 0)], 0.0)  59.7 us
    all_to_all x1, blocking collectives, local(): lax.all_to_all(du3.reshape(gspread.shape[0], total).astype(jnp.bfloat16),...  21 us
    all_to_all x1, blocking collectives, local(): lax.all_to_all(conv3.reshape(spread.shape[0], total).astype(jnp.bfloat16)...  16.2 us
    dot_general x1, matrix products, local(): lax.dot_general(dz, w_in, (((1,), (1,)), ((), ())), preferred_element_typ...  14.8 us
  transfers between devices with their start and end apart: 7, of which 5 were waited for; matrix products, arithmetic and copies ran while one was open for 14% of the time, Pallas kernels for 0%

commit v1 on v0

v1 whole, which is shorter than its diff:
```python
import functools
import math

import jax
import jax.numpy as jnp
from jax import lax
from jax.experimental import pallas as pl
from jax.experimental.pallas import tpu as pltpu
from jax.sharding import Mesh, PartitionSpec as P

F32 = jnp.float32
BF16 = jnp.bfloat16
HALO = 16
EXT = 136
SEG = 17
PADC = 1024
MODES = 16


def rounded(a):
    return a.astype(BF16).astype(F32)


def kernel_a(tp, tk, tn, w, taps, rates, cot, cotn, zf, mix, es, ends, acc, cots, us, dls):
    step = pl.program_id(0)
    rows = jnp.concatenate([tp[...], tk[...], tn[...]], axis=0)
    part = jnp.dot(rows, w[...], preferred_element_type=F32)

    @pl.when(step == 0)
    def _():
        acc[...] = part

    @pl.when(step > 0)
    def _():
        acc[...] += part

    @pl.when(step == pl.num_programs(0) - 1)
    def _():
        width = cot.shape[1]
        own = cot.shape[0]
        for g in range(3):
            zf[:, g * PADC : g * PADC + width] = rounded(acc[:, g * width : (g + 1) * width])
            zf[:, g * PADC + width : (g + 1) * PADC] = jnp.zeros((zf.shape[0], PADC - width), F32)
        cots[...] = jnp.zeros(cots.shape, F32)
        cots[0:own, 0:width] = cot[...].astype(F32)
        cots[own : own + HALO, 0:width] = cotn[...].astype(F32)
        sub = lax.broadcasted_iota(jnp.int32, (8, 128), 0)
        subf = sub.astype(F32)
        fdepth = jnp.where(sub == 7, 0.0, (EXT - 8 - SEG) - SEG * subf)
        bdepth = jnp.where(sub == 0, 0.0, SEG * subf - 8.0)

        def tile(ct, carry):
            lane = pl.multiple_of(ct * 128, 128)
            lanes = pl.ds(lane, 128)
            mixed = []
            for g in range(3):
                cols = pl.ds(pl.multiple_of(g * PADC + lane, 128), 128)
                total = taps[0:1, cols] * zf[pl.ds(HALO, EXT), cols]
                for j in range(1, 7):
                    total = total + taps[j : j + 1, cols] * zf[pl.ds(HALO - j, EXT), cols]
                mix[g, :, lanes] = total
                mixed.append(total)
            us[...] = rounded(mixed[1] * mixed[2])
            dls[...] = rounded(cots[0:EXT, lanes] * mixed[0])
            rate = rates[:, lanes]
            decay = jnp.exp(-rate)
            for half in range(2):
                ks = range(half * 8, half * 8 + 8)
                al = [jnp.broadcast_to(decay[k : k + 1, :], (8, 128)) for k in ks]
                rl = [jnp.broadcast_to(rate[k : k + 1, :], (8, 128)) for k in ks]
                st = [jnp.zeros((8, 128), F32)] * 8
                snap = st
                for t in range(SEG):
                    uv = us[pl.ds(t, 8, stride=SEG), :]
                    st = [a * s + uv for a, s in zip(al, st)]
                    if t == 8:
                        snap = st
                for i, k in enumerate(ks):
                    es[0, k, :, lanes] = st[i]
                    full = jnp.where(sub == 7, snap[i], st[i]) * jnp.exp(-rl[i] * fdepth)
                    ends[k : k + 1, lanes] = jnp.sum(full, axis=0, keepdims=True)
                st = [jnp.zeros((8, 128), F32)] * 8
                for t in range(SEG - 1, -1, -1):
                    dv = dls[pl.ds(t, 8, stride=SEG), :]
                    st = [a * s + dv for a, s in zip(al, st)]
                    if t == 8:
                        snap = st
                for i, k in enumerate(ks):
                    es[1, k, :, lanes] = st[i]
                    full = jnp.where(sub == 0, snap[i], st[i]) * jnp.exp(-rl[i] * bdepth)
                    ends[MODES + k : MODES + k + 1, lanes] = jnp.sum(full, axis=0, keepdims=True)
            return carry

        lax.fori_loop(0, PADC // 128, tile, 0)


def kernel_b(
    zf, mix, es, inc, taps, rates, reff, cot, cotn,
    out, dz, dzb, sums, cots, us, dls, longs, dps, dms, outs, dzs, packed,
):
    width = cot.shape[1]
    own = cot.shape[0]
    cots[...] = jnp.zeros(cots.shape, F32)
    cots[0:own, 0:width] = cot[...].astype(F32)
    cots[own : own + HALO, 0:width] = cotn[...].astype(F32)
    sub = lax.broadcasted_iota(jnp.int32, (8, 128), 0)

    def tile(ct, carry):
        lane = pl.multiple_of(ct * 128, 128)
        lanes = pl.ds(lane, 128)
        us[...] = rounded(mix[1, :, lanes] * mix[2, :, lanes])
        dls[...] = rounded(cots[0:EXT, lanes] * mix[0, :, lanes])
        rate = rates[:, lanes]
        decay = jnp.exp(-rate)
        gain = reff[:, lanes]
        for half in range(2):
            ks = range(half * 8, half * 8 + 8)
            al = [jnp.broadcast_to(decay[k : k + 1, :], (8, 128)) for k in ks]
            gl = [jnp.broadcast_to(gain[k : k + 1, :], (8, 128)) for k in ks]
            rl = [jnp.broadcast_to(rate[k : k + 1, :], (8, 128)) for k in ks]
            fwd = []
            bwd = []
            for i, k in enumerate(ks):
                jump = [jnp.exp(-float(SEG * m) * rl[i]) for m in (1, 2, 4)]
                x = jnp.where(sub == 0, inc[k : k + 1, lanes], pltpu.roll(es[0, k, :, lanes], 1, 0))
                for m, d in zip((1, 2, 4), jump):
                    x = x + jnp.where(sub >= m, pltpu.roll(x, m, 0) * d, 0.0)
                fwd.append(x)
                x = jnp.where(
                    sub == 7, inc[MODES + k : MODES + k + 1, lanes], pltpu.roll(es[1, k, :, lanes], 7, 0)
                )
                for m, d in zip((1, 2, 4), jump):
                    x = x + jnp.where(sub < 8 - m, pltpu.roll(x, 8 - m, 0) * d, 0.0)
                bwd.append(x)
            gr = [jnp.zeros((8, 128), F32)] * 8
            st = fwd
            for t in range(SEG):
                uv = us[pl.ds(t, 8, stride=SEG), :]
                dv = dls[pl.ds(t, 8, stride=SEG), :]
                if t >= 9:
                    dv = jnp.where(sub < 7, dv, 0.0)
                st = [a * s + uv for a, s in zip(al, st)]
                gr = [q + dv * s for q, s in zip(gr, st)]
                total = sum(g * s for g, s in zip(gl, st))
                if half:
                    total = total + longs[pl.ds(t, 8, stride=SEG), :]
                longs[pl.ds(t, 8, stride=SEG), :] = total
            for i, k in enumerate(ks):
                sums[24 + k : 25 + k, lanes] = jnp.sum(gr[i], axis=0, keepdims=True)
            st = bwd
            for t in range(SEG - 1, -1, -1):
                dv = dls[pl.ds(t, 8, stride=SEG), :]
                st = [a * s + dv for a, s in zip(al, st)]
                total = sum(g * s for g, s in zip(gl, st))
                if half:
                    total = total + dps[pl.ds(t, 8, stride=SEG), :]
                dps[pl.ds(t, 8, stride=SEG), :] = total
        long_out = rounded(longs[...])
        dprod = rounded(dps[...])
        outs[:, lanes] = mix[0, 0:own, lanes] * long_out[0:own]
        dms[0] = rounded(cots[0:EXT, lanes] * long_out)
        dms[1] = rounded(dprod * mix[2, :, lanes])
        dms[2] = rounded(dprod * mix[1, :, lanes])
        for g in range(3):
            cols = pl.ds(pl.multiple_of(g * PADC + lane, 128), 128)
            mine = dms[g, 0:own, :]
            total = taps[0:1, cols] * mine
            sums[8 * g : 8 * g + 1, lanes] = jnp.sum(
                mine * zf[pl.ds(HALO, own), cols], axis=0, keepdims=True
            )
            for j in range(1, 7):
                total = total + taps[j : j + 1, cols] * dms[g, pl.ds(j, own), :]
                sums[8 * g + j : 8 * g + j + 1, lanes] = jnp.sum(
                    mine * zf[pl.ds(HALO - j, own), cols], axis=0, keepdims=True
                )
            sums[8 * g + 7 : 8 * g + 8, lanes] = jnp.zeros((1, 128), F32)
            dzs[:, cols] = total
        return carry

    lax.fori_loop(0, PADC // 128, tile, 0)
    out[...] = outs[:, 0:width].astype(BF16)
    for g in range(3):
        packed[:, g * width : (g + 1) * width] = dzs[:, g * PADC : g * PADC + width]
    dz[...] = packed[...].astype(BF16)
    piece = dzb.shape[2] // 2
    for b in range(8):
        for h in range(2):
            off = h * 8 * piece + (b % 2) * 4 * piece + (b // 2) * piece
            dzb[b, :, h * piece : (h + 1) * piece] = packed[:, off : off + piece].astype(BF16)


def ring(a, ax, d, n=4):
    return lax.ppermute(a, ax, [(i, (i + d) % n) for i in range(n)])


def gathered(a, ax, d):
    return ring(a, ax, d)


def local(tokens, w_in, conv_taps, residues, rates, cotangent):
    feats = tokens[0]
    cot = cotangent[0]
    own, width = cot.shape
    chans = 3 * width
    xi, zi, yi = lax.axis_index("x"), lax.axis_index("zl"), lax.axis_index("y")
    ctx = ("x", "zl", "y")
    count = 64
    scale = 1.0 / math.sqrt(4 * count * own)
    tprev = lax.ppermute(feats[own - HALO :], ctx, [(i, i + 1) for i in range(count - 1)])
    firsts = jnp.concatenate([feats[:HALO], cot[:HALO]], axis=1)
    nexts = lax.ppermute(firsts, ctx, [(i, i - 1) for i in range(1, count)])
    tnext = nexts[:, : feats.shape[1]]
    cnext = nexts[:, feats.shape[1] :]
    amp_mine = jnp.sqrt(-jnp.expm1(-2.0 * rates))
    held = jnp.concatenate([rates, residues * amp_mine], axis=1)[None]
    for ax in ("y", "zl", "x"):
        held = jnp.concatenate([held] + [ring(held, ax, d) for d in (1, 2, 3)], axis=0)
    slots = jnp.arange(count)
    sx, sz, sy = slots // 16, (slots // 4) % 4, slots % 4
    source = ((xi - sx) % 4) * 16 + ((zi - sz) % 4) * 4 + (yi - sy) % 4
    held = held[source]
    params = jnp.transpose(held, (2, 0, 1)).reshape(2 * MODES, width)
    params = jnp.pad(params, ((0, 0), (0, PADC - width)))
    rate, gain = params[:MODES], params[MODES:]
    taps = jnp.pad(conv_taps.reshape(7, 3, width), ((0, 1), (0, 0), (0, PADC - width)))
    taps = taps.reshape(8, 3 * PADC)

    depth = feats.shape[1]
    kblk = 256
    vmem = pltpu.CompilerParams(vmem_limit_bytes=48 * 1024 * 1024)

    def whole(shape):
        return pl.BlockSpec(shape, lambda k: (0,) * len(shape))

    ext_rows = own + 2 * HALO
    zf, mix, es, ends = pl.pallas_call(
        kernel_a,
        grid=(depth // kblk,),
        in_specs=[
            pl.BlockSpec((HALO, kblk), lambda k: (0, k)),
            pl.BlockSpec((own, kblk), lambda k: (0, k)),
            pl.BlockSpec((HALO, kblk), lambda k: (0, k)),
            pl.BlockSpec((kblk, chans), lambda k: (k, 0)),
            whole((8, 3 * PADC)),
            whole((MODES, PADC)),
            whole((own, width)),
            whole((HALO, width)),
        ],
        out_specs=[
            whole((ext_rows, 3 * PADC)),
            whole((3, EXT, PADC)),
            whole((2, MODES, 8, PADC)),
            whole((2 * MODES, PADC)),
        ],
        out_shape=[
            jax.ShapeDtypeStruct((ext_rows, 3 * PADC), F32),
            jax.ShapeDtypeStruct((3, EXT, PADC), F32),
            jax.ShapeDtypeStruct((2, MODES, 8, PADC), F32),
            jax.ShapeDtypeStruct((2 * MODES, PADC), F32),
        ],
        scratch_shapes=[
            pltpu.VMEM((ext_rows, chans), F32),
            pltpu.VMEM((own + HALO, PADC), F32),
            pltpu.VMEM((EXT, 128), F32),
            pltpu.VMEM((EXT, 128), F32),
        ],
        compiler_params=vmem,
        cost_estimate=pl.CostEstimate(flops=1500000000, bytes_accessed=14000000, transcendentals=0),
    )(tprev, feats, tnext, w_in, taps, rate, cot, cnext)

    rate2 = jnp.concatenate([rate, rate], axis=0)
    ahead = (jnp.arange(2 * MODES) < MODES)[:, None]
    total = ends
    incoming = None
    reach = []
    for ax, me, span in (("y", yi, own), ("zl", zi, 4 * own), ("x", xi, 16 * own)):
        prefix = jnp.zeros_like(total)
        whole_sum = jnp.zeros_like(total)
        for d in range(4):
            other = total if d == 0 else ring(total, ax, d)
            m = (me - d) % 4
            gap = jnp.where(ahead, me - 1 - m, m - me - 1)
            far = jnp.where(ahead, 3 - m, m)
            if d > 0:
                weight = jnp.exp(-rate2 * (span * jnp.maximum(gap, 0)).astype(F32))
                prefix = prefix + jnp.where(gap >= 0, weight * other, 0.0)
            whole_sum = whole_sum + jnp.exp(-rate2 * (span * far).astype(F32)) * other
        reach.append((prefix, jnp.exp(-rate2 * (span * jnp.where(ahead, me, 3 - me)).astype(F32))))
        total = whole_sum
    incoming = reach[0][0] + reach[0][1] * (reach[1][0] + reach[1][1] * reach[2][0])

    piece = chans // 16
    out, dz, dzb, sums = pl.pallas_call(
        kernel_b,
        out_shape=[
            jax.ShapeDtypeStruct((own, width), BF16),
            jax.ShapeDtypeStruct((own, chans), BF16),
            jax.ShapeDtypeStruct((8, own, 2 * piece), BF16),
            jax.ShapeDtypeStruct((40, PADC), F32),
        ],
        scratch_shapes=[
            pltpu.VMEM((own + HALO, PADC), F32),
            pltpu.VMEM((EXT, 128), F32),
            pltpu.VMEM((EXT, 128), F32),
            pltpu.VMEM((EXT, 128), F32),
            pltpu.VMEM((EXT, 128), F32),
            pltpu.VMEM((3, EXT, 128), F32),
            pltpu.VMEM((own, PADC), F32),
            pltpu.VMEM((own, 3 * PADC), F32),
            pltpu.VMEM((own, chans), F32),
        ],
        compiler_params=vmem,
        cost_estimate=pl.CostEstimate(flops=200000000, bytes_accessed=10000000, transcendentals=0),
    )(zf, mix, es, incoming, taps, rate, gain, cot, cnext)

    fblk = depth // count
    shuffled = feats.reshape(own, 4, 4, 4, fblk).transpose(0, 3, 1, 2, 4).reshape(own, depth)
    ours = jnp.stack([shuffled] + [ring(shuffled, "x", d) for d in (1, 2, 3)], axis=0)
    theirs = lax.ppermute(ours, "core", [(0, 1), (1, 0)])
    tok_all = jnp.stack([ours, theirs], axis=0).reshape(8 * own, depth)

    def summed(a, ax):
        return a + ring(a, ax, 1) + ring(a, ax, 2) + ring(a, ax, 3)

    for ax in ("y", "zl", "x", ("zh", "core")):
        sums = summed(sums, ax)
    grad_taps = sums[:24].reshape(3, 8, PADC)[:, :7, :width].transpose(1, 0, 2).reshape(7, chans)
    grad_taps = grad_taps * scale
    index = (xi * 4 + zi) * 4 + yi
    held_chans = width // count
    mine = lax.dynamic_slice_in_dim(sums[24:, :width], index * held_chans, held_chans, axis=1)
    grad_residues = amp_mine * mine.T * scale

    arrived = lax.all_to_all(dzb, ("x", "core"), split_axis=0, concat_axis=0, tiled=True)
    ci = lax.axis_index("core")
    order = jnp.arange(8)
    want = ((xi - order % 4) % 4) * 2 + jnp.where(order < 4, ci, 1 - ci)
    arrived = arrived[want].reshape(8 * own, 2 * piece)
    term = lax.dot_general(
        tok_all, arrived, (((0,), (0,)), ((), ())), preferred_element_type=F32
    ).astype(BF16)
    got = lax.all_to_all(term.reshape(4, depth // 4, 2 * piece), "y", 0, 0, tiled=True)
    got = jnp.sum(got.astype(F32), axis=0).astype(BF16)
    got = got.reshape(16, fblk, 2, piece).transpose(0, 2, 1, 3).reshape(32, fblk, piece)
    last = lax.all_to_all(got, ("x", "zl", "zh"), 0, 0, tiled=True)
    last = jnp.sum(last.reshape(4, 8, fblk, piece).astype(F32), axis=1) * scale
    grad_weight = last.transpose(1, 0, 2).reshape(fblk, 4 * piece).astype(BF16)

    grad_feats = lax.dot_general(
        dz, w_in, (((1,), (1,)), ((), ())), preferred_element_type=F32
    ).astype(BF16)
    return (out[None], grad_feats[None], grad_weight, grad_taps, grad_residues)


def solution(mesh):
    fine = Mesh(mesh.devices.reshape(4, 4, 4, 2, 2), ("x", "zl", "y", "zh", "core"))
    ctx = ("x", "zl", "y")
    dp = ("zh", "core")
    in_specs = (P(dp, ctx, None), P(), P(), P(ctx, None), P(ctx, None), P(dp, ctx, None))
    out_specs = (P(dp, ctx, None), P(dp, ctx, None), P(ctx, dp), P(), P(ctx, None))
    return jax.shard_map(local, mesh=fine, in_specs=in_specs, out_specs=out_specs, check_vma=False)
```

time: 662 us -> 237 us (0.36); the launches traced: 649 us -> 236 us
  waiting for transfers between devices: 292 us -> 56.9 us
  blocking collectives: 140 us -> 0 us
  starting transfers between devices: 34 us -> 94.7 us
  local copies, waits for them, and re-layouts: 88.6 us -> 34.3 us
  matrix products: 50.2 us -> 8.85 us
  Pallas kernels: 0 us -> 19.7 us
  between operations: 16.3 us -> 1.67 us
  other arithmetic: 28.5 us -> 19.8 us
    psum x1 -> x0, waiting for transfers between devices: 206 us -> none  [local(): grad_taps = lax.psum(jnp.stack(tap_rows, axis=0), ('ctx', 'dp')) * scale]
    psum x1 -> x0, blocking collectives: 103 us -> none  [local(): filt = lax.psum(filt, 'dp')]
    ppermute x2 -> x36, starting transfers between devices: 7.62 us -> 78.2 us  [the longest x33 72.4 us: ring(): return lax.ppermute(a, ax, [(i, (i + d) % n) for i in range(n)])]
    all_to_all x3, waiting for transfers between devices: 80.6 us -> 15.2 us  [the longest x1 10.8 us: local(): last = lax.all_to_all(got, ('x', 'zl', 'zh'), 0, 0, tiled=True)]
    gather x2, local copies, waits for them, and re-layouts: 59.7 us -> 2.22 us  [the longest x1 1.58 us: local(): arrived = arrived[want].reshape(8 * own, 2 * piece)]
    all_to_all x2 -> x0, blocking collectives: 37.2 us -> none  [the longest x1 21 us: local(): lax.all_to_all(du3.reshape(gspread.shape[0], total).astype(jnp.bfloat16),...]
    ppermute x2 -> x36, waiting for transfers between devices: 5.74 us -> 41.7 us  [the longest x33 41.7 us: ring(): return lax.ppermute(a, ax, [(i, (i + d) % n) for i in range(n)])]
    dot_general x17 -> x1, matrix products: 35.4 us -> 3.21 us  [local(): lax.dot_general(tok_all, arrived, (((0,), (0,)), ((), ())), preferred_ele...]
  transfers between devices with their start and end apart: 7 -> 39, of which waited for: 5 -> 18; matrix products, arithmetic and copies ran while one was open for 14% -> 24% of each run, Pallas kernels for 0% -> 8%
where the time goes in v1:
time: 237 us; the launch traced here: 236 us
  starting transfers between devices  94.7 us (40%)
  waiting for transfers between devices  56.9 us (24%)
  local copies, waits for them, and re-layouts  34.3 us (14%)
  other arithmetic  19.8 us (8%)
  Pallas kernels  19.7 us (8%)
  matrix products  8.85 us (4%)
    ppermute x33, starting transfers between devices, ring(): return lax.ppermute(a, ax, [(i, (i + d) % n) for i in range(n)])  72.4 us
    ppermute x33, waiting for transfers between devices, ring(): return lax.ppermute(a, ax, [(i, (i + d) % n) for i in range(n)])  41.7 us
    unnamed x79, local copies, waits for them, and re-layouts  20.4 us
    all_to_all x1, waiting for transfers between devices, local(): last = lax.all_to_all(got, ('x', 'zl', 'zh'), 0, 0, tiled=True)  10.8 us
    pallas_call x1, Pallas kernels, local(): pl.pallas_call(kernel_a, grid=(depth // kblk,), in_specs=[pl.BlockSpec((H...  10.6 us
    pallas_call x1, Pallas kernels, local(): pl.pallas_call(kernel_b, out_shape=[jax.ShapeDtypeStruct((own, width), BF...  9.13 us
    all_to_all x1, starting transfers between devices, local(): last = lax.all_to_all(got, ('x', 'zl', 'zh'), 0, 0, tiled=True)  8.98 us
    another operation x2, other arithmetic, local(): tok_all = jnp.stack([ours, theirs], axis=0).reshape(8 * own, depth)  6.51 us
  transfers between devices with their start and end apart: 39, of which 18 were waited for; matrix products, arithmetic and copies ran while one was open for 24% of the time, Pallas kernels for 8%

profile of v1, /device:TPU:32, one launch (start us, length us, event | category | flops | bytes accessed | tf_op | source)
XLA Modules:
  0.0 235.9 jit_solution(13918403024957578267)
XLA Ops:
  2.3 1.7 collective-permute-start.2
  4.0 2.9 %collective-permute-start.3 = (f32[1,15,32]{1,2,0:T(8,128)S(1)}, f32[1,15,32]{1,2,0:T(8,128)S(1)}, u32[]{:S(2)}, u32[]{:S(2)}) collective-permute-start(f32[1,15,32]{1,2,0:T(8,128)S(1)} %maximum_bitcast_fusion), channel_id=1, source_target_pairs={{0,8},{4,12},{8,0},{12,4},{1,9},{5,13},{9,1},{13,5},{2,10},{6,14},... | collective-permute-start | bytes 5768 | tf_op jit(solution)/shard_map/ppermute | solution.py:193
  11.1 2.7 %collective-permute-start.21 = (bf16[128,1536]{0,1:T(8,128)(2,1)S(1)}, bf16[128,1536]{0,1:T(8,128)(2,1)}, u32[]{:S(2)}, u32[]{:S(2)}) collective-permute-start(bf16[128,1536]{0,1:T(8,128)(2,1)S(1)} %bitcast.78), channel_id=1, source_target_pairs={{0,128},{64,192},{128,0},{192,64},{1,129},{65,193},{129,1},{193,65... | collective-permute-start | bytes 1179656 | tf_op jit(solution)/shard_map/ppermute | solution.py:193
  17.4 1.9 collective-permute-start.1
  19.3 3.9 %collective-permute-start = (bf16[16,1536]{1,0:T(8,128)(2,1)S(1)}, bf16[16,1536]{1,0:T(8,128)(2,1)S(1)}, u32[]{:S(2)}, u32[]{:S(2)}) collective-permute-start(bf16[16,1536]{1,0:T(8,128)(2,1)S(1)} %get-tuple-element.59), channel_id=1, source_target_pairs={{0,4},{4,8},{8,12},{12,16},{16,20},{20,24},{24,28},{28,32},{32,36}... | collective-permute-start | bytes 147464 | tf_op jit(solution)/shard_map/ppermute | solution.py:209
  23.3 2.0 collective-permute-start.5
  25.3 2.3 collective-permute-done.5
  27.6 3.3 %collective-permute-start.6 = (f32[4,15,32]{1,2,0:T(8,128)S(1)}, f32[4,15,32]{1,2,0:T(8,128)S(1)}, u32[]{:S(2)}, u32[]{:S(2)}) collective-permute-start(f32[4,15,32]{1,2,0:T(8,128)S(1)} %pad_maximum_fusion.3), channel_id=1, source_target_pairs={{0,32},{16,48},{32,0},{48,16},{1,33},{17,49},{33,1},{49,17},{2,34}... | collective-permute-start | bytes 23048 | tf_op jit(solution)/shard_map/ppermute | solution.py:193
  30.9 2.3 collective-permute-done.6
  33.2 2.7 %collective-permute-start.7 = (f32[4,15,32]{1,2,0:T(8,128)S(1)}, f32[4,15,32]{1,2,0:T(8,128)S(1)}, u32[]{:S(2)}, u32[]{:S(2)}) collective-permute-start(f32[4,15,32]{1,2,0:T(8,128)S(1)} %pad_maximum_fusion.3), channel_id=1, source_target_pairs={{0,48},{16,0},{32,16},{48,32},{1,49},{17,1},{33,17},{49,33},{2,50}... | collective-permute-start | bytes 23048 | tf_op jit(solution)/shard_map/ppermute | solution.py:193
  36.0 1.9 collective-permute-done.7
  37.9 3.0 %collective-permute-start.8 = (f32[16,15,32]{1,2,0:T(8,128)S(1)}, f32[16,15,32]{1,2,0:T(8,128)S(1)}, u32[]{:S(2)}, u32[]{:S(2)}) collective-permute-start(f32[16,15,32]{1,2,0:T(8,128)S(1)} %get-tuple-element.62), channel_id=1, source_target_pairs={{0,64},{64,128},{128,192},{192,0},{1,65},{65,129},{129,193},{193,1... | collective-permute-start | bytes 92168 | tf_op jit(solution)/shard_map/ppermute | solution.py:193
  41.5 12.4 %copy.180.w = bf16[1536,2880]{1,0:T(8,128)(2,1)} copy(bf16[1536,2880]{0,1:T(8,128)(2,1)} %param.7) | data formatting | bytes 17694720 | tf_op args[1]
  54.5 7.3 %collective-permute-done.9 = f32[16,15,32]{1,2,0:T(8,128)S(1)} collective-permute-done((f32[16,15,32]{1,2,0:T(8,128)S(1)}, f32[16,15,32]{1,2,0:T(8,128)S(1)}, u32[]{:S(2)}, u32[]{:S(2)}) %collective-permute-start.9) | collective-permute-done | bytes 30752 | tf_op jit(solution)/shard_map/ppermute | solution.py:193
  61.8 1.6 collective-permute-start.10
  63.4 5.5 %collective-permute-done.10 = f32[16,15,32]{1,2,0:T(8,128)S(1)} collective-permute-done((f32[16,15,32]{1,2,0:T(8,128)}, f32[16,15,32]{1,2,0:T(8,128)S(1)}, u32[]{:S(2)}, u32[]{:S(2)}) %collective-permute-start.10) | collective-permute-done | bytes 30752 | tf_op jit(solution)/shard_map/ppermute | solution.py:193
  70.4 10.6 %shard_map.101 = (f32[160,3072]{1,0:T(8,128)S(1)}, f32[3,136,1024]{2,1,0:T(8,128)S(1)}, f32[2,16,8,1024]{3,2,1,0:T(8,128)S(1)}, f32[32,1024]{1,0:T(8,128)S(1)}) custom-call(bf16[16,1536]{1,0:T(8,128)(2,1)S(1)} %collective-permute-done.tp, bf16[128,1536]{1,0:T(8,128)(2,1)S(1)} %bitcast.71, bf16[16,1536]{1,0:T(8,128)(2,1)S(1)} %slice.57.tn, ...), custom_call_target="tpu_custom_call" | custom-call | flops 1500000000 | bytes 14000000 | tf_op jit(solution)/shard_map/pallas_call | solution.py:236
  84.0 5.5 %collective-permute-start.12 = (f32[32,1024]{1,0:T(8,128)S(1)}, f32[32,1024]{1,0:T(8,128)S(1)}, u32[]{:S(2)}, u32[]{:S(2)}) collective-permute-start(f32[32,1024]{1,0:T(8,128)S(1)} %get-tuple-element.16), channel_id=1, source_target_pairs={{0,8},{4,12},{8,0},{12,4},{1,9},{5,13},{9,1},{13,5},{2,10},{6,14},... | collective-permute-start | bytes 393224 | tf_op jit(solution)/shard_map/ppermute | solution.py:193
  90.9 3.6 %collective-permute-start.22 = (bf16[128,1536]{0,1:T(8,128)(2,1)S(1)}, bf16[128,1536]{0,1:T(8,128)(2,1)}, u32[]{:S(2)}, u32[]{:S(2)}) collective-permute-start(bf16[128,1536]{0,1:T(8,128)(2,1)S(1)} %bitcast.79), channel_id=1, source_target_pairs={{0,192},{64,0},{128,64},{192,128},{1,193},{65,1},{129,65},{193,129... | collective-permute-start | bytes 1179656 | tf_op jit(solution)/shard_map/ppermute | solution.py:193
  97.0 3.2 %collective-permute-start.15 = (f32[32,1024]{1,0:T(8,128)S(1)}, f32[32,1024]{1,0:T(8,128)S(1)}, u32[]{:S(2)}, u32[]{:S(2)}) collective-permute-start(f32[32,1024]{1,0:T(8,128)S(1)} %fusion.46), channel_id=1, source_target_pairs={{0,32},{16,48},{32,0},{48,16},{1,33},{17,49},{33,1},{49,17},{2,34}... | collective-permute-start | bytes 393224 | tf_op jit(solution)/shard_map/ppermute | solution.py:193
  100.2 3.2 %collective-permute-start.16 = (f32[32,1024]{1,0:T(8,128)S(1)}, f32[32,1024]{1,0:T(8,128)S(1)}, u32[]{:S(2)}, u32[]{:S(2)}) collective-permute-start(f32[32,1024]{1,0:T(8,128)S(1)} %fusion.46), channel_id=1, source_target_pairs={{0,48},{16,0},{32,16},{48,32},{1,49},{17,1},{33,17},{49,33},{2,50}... | collective-permute-start | bytes 393224 | tf_op jit(solution)/shard_map/ppermute | solution.py:193
  104.1 2.0 collective-permute-done.16
  107.1 4.9 %collective-permute-start.18 = (f32[32,1024]{1,0:T(8,128)S(1)}, f32[32,1024]{1,0:T(8,128)S(1)}, u32[]{:S(2)}, u32[]{:S(2)}) collective-permute-start(f32[32,1024]{1,0:T(8,128)S(1)} %fusion.70), channel_id=1, source_target_pairs={{0,128},{64,192},{128,0},{192,64},{1,129},{65,193},{129,1},{193,65... | collective-permute-start | bytes 393224 | tf_op jit(solution)/shard_map/ppermute | solution.py:193
  112.3 3.2 %fusion.121 = (bf16[1,4,128,1536]{2,3,1,0:T(8,128)(2,1)}, bf16[4,128,1536]{1,2,0:T(8,128)(2,1)}) fusion(bf16[1,128,1536]{1,2,0:T(8,128)(2,1)} %bitcast.17, bf16[1,128,1536]{1,2,0:T(8,128)(2,1)} %bitcast.16, bf16[1,128,1536]{1,2,0:T(8,128)(2,1)} %bitcast.15, bf16[1,128,1536]{1,2,0:T(8,128)(2,1)S(1)} %bitcast.80), kind=kLoop, calls=%fused_computation.215 | loop fusion | flops 2359296 | bytes 4718592 | tf_op jit(solution)/shard_map/stack | solution.py:320
  118.5 9.1 %shard_map.102 = (bf16[128,960]{1,0:T(8,128)(2,1)S(1)}, bf16[128,2880]{1,0:T(8,128)(2,1)S(1)}, bf16[8,128,360]{2,1,0:T(8,128)(2,1)S(1)}, f32[40,1024]{1,0:T(8,128)S(1)}) custom-call(f32[160,3072]{1,0:T(8,128)} %copy-done.1, f32[3,136,1024]{2,1,0:T(8,128)S(1)} %get-tuple-element.14.mix, f32[2,16,8,1024]{3,2,1,0:T(8,128)S(1)} %copy-done.3, ...), custom_call_target="tpu_custom_call" | custom-call | flops 200000000 | bytes 10000000 | tf_op jit(solution)/shard_map/pallas_call | solution.py:293
  128.8 2.7 %collective-permute-start.25 = (f32[40,1024]{1,0:T(8,128)S(1)}, f32[40,1024]{1,0:T(8,128)S(1)}, u32[]{:S(2)}, u32[]{:S(2)}) collective-permute-start(f32[40,1024]{1,0:T(8,128)S(1)} %get-tuple-element.20), channel_id=1, source_target_pairs={{0,8},{4,12},{8,0},{12,4},{1,9},{5,13},{9,1},{13,5},{2,10},{6,14},... | collective-permute-start | bytes 491528 | tf_op jit(solution)/shard_map/ppermute | solution.py:193
  132.7 5.7 %collective-permute-done.24 = f32[40,1024]{1,0:T(8,128)S(1)} collective-permute-done((f32[40,1024]{1,0:T(8,128)S(1)}, f32[40,1024]{1,0:T(8,128)S(1)}, u32[]{:S(2)}, u32[]{:S(2)}) %collective-permute-start.24) | collective-permute-done | bytes 163872 | tf_op jit(solution)/shard_map/ppermute | solution.py:193
  139.9 3.7 %collective-permute-start.28 = (f32[40,1024]{1,0:T(8,128)S(1)}, f32[40,1024]{1,0:T(8,128)}, u32[]{:S(2)}, u32[]{:S(2)}) collective-permute-start(f32[40,1024]{1,0:T(8,128)S(1)} %add_add_fusion.3), channel_id=1, source_target_pairs={{0,32},{16,48},{32,0},{48,16},{1,33},{17,49},{33,1},{49,17},{2,34}... | collective-permute-start | bytes 491528 | tf_op jit(solution)/shard_map/ppermute | solution.py:193
  145.2 2.3 copy.185
  147.4 3.5 %all-to-all-start = ((bf16[8,128,360]{1,2,0:T(8,128)(2,1)}), bf16[8,128,360]{1,2,0:T(8,128)(2,1)S(1)}, u32[]{:S(2)}, u32[]{:S(2)}) async-start(bf16[8,128,360]{1,2,0:T(8,128)(2,1)} %copy.185), calls=%async_computation | async-start | bytes 1474560 | tf_op jit(solution)/shard_map/all_to_all | solution.py:334
  151.0 2.2 collective-permute-done.28
  153.3 3.1 %collective-permute-done.29 = f32[40,1024]{1,0:T(8,128)} collective-permute-done((f32[40,1024]{1,0:T(8,128)S(1)}, f32[40,1024]{1,0:T(8,128)}, u32[]{:S(2)}, u32[]{:S(2)}) %collective-permute-start.29) | collective-permute-done | bytes 163872 | tf_op jit(solution)/shard_map/ppermute | solution.py:193
  156.3 1.8 add_add_fusion.2
  158.1 3.4 %collective-permute-start.30 = (f32[40,1024]{1,0:T(8,128)}, f32[40,1024]{1,0:T(8,128)S(1)}, u32[]{:S(2)}, u32[]{:S(2)}) collective-permute-start(f32[40,1024]{1,0:T(8,128)} %add_add_fusion.2), channel_id=1, source_target_pairs={{0,64},{64,128},{128,192},{192,0},{1,65},{65,129},{129,193},{193,1... | collective-permute-start | bytes 491528 | tf_op jit(solution)/shard_map/ppermute | solution.py:193
  161.5 2.7 %collective-permute-start.32 = (f32[40,1024]{1,0:T(8,128)}, f32[40,1024]{1,0:T(8,128)}, u32[]{:S(2)}, u32[]{:S(2)}) collective-permute-start(f32[40,1024]{1,0:T(8,128)} %add_add_fusion.2), channel_id=1, source_target_pairs={{0,192},{64,0},{128,64},{192,128},{1,193},{65,1},{129,65},{193,129... | collective-permute-start | bytes 491528 | tf_op jit(solution)/shard_map/ppermute | solution.py:193
  164.2 3.3 %collective-permute-done.30 = f32[40,1024]{1,0:T(8,128)S(1)} collective-permute-done((f32[40,1024]{1,0:T(8,128)}, f32[40,1024]{1,0:T(8,128)S(1)}, u32[]{:S(2)}, u32[]{:S(2)}) %collective-permute-start.30) | collective-permute-done | bytes 163872 | tf_op jit(solution)/shard_map/ppermute | solution.py:193
  167.5 3.1 %collective-permute-done.31 = f32[40,1024]{1,0:T(8,128)} collective-permute-done((f32[40,1024]{1,0:T(8,128)}, f32[40,1024]{1,0:T(8,128)}, u32[]{:S(2)}, u32[]{:S(2)}) %collective-permute-start.31) | collective-permute-done | bytes 163872 | tf_op jit(solution)/shard_map/ppermute | solution.py:193
  172.0 5.0 %collective-permute-start.34 = (f32[40,1024]{1,0:T(8,128)S(1)}, f32[40,1024]{1,0:T(8,128)}, u32[]{:S(2)}, u32[]{:S(2)}) collective-permute-start(f32[40,1024]{1,0:T(8,128)S(1)} %add_add_fusion.1), channel_id=1, source_target_pairs={{0,2},{1,3},{2,0},{3,1},{4,6},{5,7},{6,4},{7,5},{8,10},{9,11},{10,... | collective-permute-start | bytes 491528 | tf_op jit(solution)/shard_map/ppermute | solution.py:193
  176.9 5.3 %collective-permute-start.35 = (f32[40,1024]{1,0:T(8,128)S(1)}, f32[40,1024]{1,0:T(8,128)}, u32[]{:S(2)}, u32[]{:S(2)}) collective-permute-start(f32[40,1024]{1,0:T(8,128)S(1)} %add_add_fusion.1), channel_id=1, source_target_pairs={{0,3},{1,0},{2,1},{3,2},{4,7},{5,4},{6,5},{7,6},{8,11},{9,8},{10,9... | collective-permute-start | bytes 491528 | tf_op jit(solution)/shard_map/ppermute | solution.py:193
  182.2 1.6 gather_fusion.1
  183.8 3.3 %pad_maximum_fusion = bf16[2,4,128,1536]{2,3,1,0:T(8,128)(2,1)} fusion(bf16[1,4,128,1536]{2,3,1,0:T(8,128)(2,1)} %bitcast.19, bf16[1,4,128,1536]{2,3,1,0:T(8,128)(2,1)S(1)} %copy-done.5), kind=kLoop, calls=%fused_computation.2 | loop fusion | flops 1572864 | bytes 6291456 | tf_op jit(solution)/shard_map/stack | solution.py:320
  187.1 4.7 %copy.184 = bf16[2,4,128,1536]{3,2,1,0:T(8,128)(2,1)} copy(bf16[2,4,128,1536]{2,3,1,0:T(8,128)(2,1)} %pad_maximum_fusion) | data formatting | bytes 6291456 | tf_op jit(solution)/shard_map/stack | solution.py:320
  191.8 3.2 %convolution_convert_fusion = bf16[1536,360]{0,1:T(8,128)(2,1)S(1)} fusion(bf16[1024,1536]{1,0:T(8,128)(2,1)} %bitcast.75, bf16[8,128,360]{1,2,0:T(8,128)(2,1)S(1)} %copy-done.6), kind=kOutput, calls=%fused_computation.3 | convolution fusion | flops 1133015040 | bytes 4988928 | tf_op jit(solution)/shard_map/dot_general | solution.py:339
  196.2 4.0 %all-to-all-start.1 = ((bf16[4,384,360]{1,2,0:T(8,128)(2,1)}), bf16[4,384,360]{1,2,0:T(8,128)(2,1)S(1)}, u32[]{:S(2)}, u32[]{:S(2)}) async-start(bf16[4,384,360]{1,2,0:T(8,128)(2,1)} %bitcast.67), calls=%async_computation.1 | async-start | bytes 2211840 | tf_op jit(solution)/shard_map/all_to_all | solution.py:342
  200.1 5.6 %fusion = bf16[1,128,1536]{2,1,0:T(8,128)(2,1)} fusion(bf16[128,2880]{1,0:T(8,128)(2,1)S(1)} %get-tuple-element.18, bf16[1536,2880]{0,1:T(8,128)(2,1)} %param.7), kind=kOutput, calls=%fused_computation.5 | convolution fusion | flops 1132658688 | bytes 9977856 | tf_op jit(solution)/shard_map/dot_general | solution.py:349
  207.8 4.4 %all-to-all-done.1 = bf16[4,384,360]{1,2,0:T(8,128)(2,1)S(1)} async-done(((bf16[4,384,360]{1,2,0:T(8,128)(2,1)}), bf16[4,384,360]{1,2,0:T(8,128)(2,1)S(1)}, u32[]{:S(2)}, u32[]{:S(2)}) %all-to-all-start.1) | async-done | bytes 1105952 | tf_op jit(solution)/shard_map/all_to_all | solution.py:342
  213.6 9.0 %all-to-all-start.2 = ((bf16[32,24,180]{2,1,0:T(8,128)(2,1)}), bf16[32,24,180]{2,1,0:T(8,128)(2,1)S(1)}, u32[]{:S(2)}, u32[]{:S(2)}) async-start(bf16[32,24,180]{2,1,0:T(8,128)(2,1)} %bitcast.23), calls=%async_computation.2 | async-start | bytes 786432 | tf_op jit(solution)/shard_map/all_to_all | solution.py:345
  224.3 10.8 %all-to-all-done.2 = bf16[32,24,180]{2,1,0:T(8,128)(2,1)S(1)} async-done(((bf16[32,24,180]{2,1,0:T(8,128)(2,1)}), bf16[32,24,180]{2,1,0:T(8,128)(2,1)S(1)}, u32[]{:S(2)}, u32[]{:S(2)}) %all-to-all-start.2) | async-done | bytes 276512 | tf_op jit(solution)/shard_map/all_to_all | solution.py:345
  (176 shorter events, 37.1 us)
Async XLA Ops:
  0.6 13.2 %copy-start = (bf16[1,128,1536]{2,1,0:T(8,128)(2,1)S(1)}, bf16[1,128,1536]{2,1,0:T(8,128)(2,1)}, u32[]{:S(2)}) copy-start(bf16[1,128,1536]{2,1,0:T(8,128)(2,1)} %param.6) | copy-start | bytes 1179652
  0.6 14.6 %copy-start.8 = (bf16[1,128,960]{1,2,0:T(8,128)(2,1)S(1)}, bf16[1,128,960]{1,2,0:T(8,128)(2,1)}, u32[]{:S(2)}) copy-start(bf16[1,128,960]{1,2,0:T(8,128)(2,1)} %param.11) | copy-start | bytes 737284
  0.7 14.7 %copy-start.12 = (f32[7,2880]{1,0:T(8,128)S(1)}, f32[7,2880]{1,0:T(8,128)}, u32[]{:S(2)}) copy-start(f32[7,2880]{1,0:T(8,128)} %param.8) | copy-start | bytes 241924
  1.5 14.1 %copy-start.9 = (f32[15,16]{0,1:T(8,128)}, f32[15,16]{0,1:T(8,128)S(1)}, u32[]{:S(2)}) copy-start(f32[15,16]{0,1:T(8,128)S(1)} %copy.176) | copy-start | bytes 2884
  2.3 15.1 %collective-permute-start.2 = (f32[1,15,32]{1,2,0:T(8,128)S(1)}, f32[1,15,32]{1,2,0:T(8,128)S(1)}, u32[]{:S(2)}, u32[]{:S(2)}) collective-permute-start(f32[1,15,32]{1,2,0:T(8,128)S(1)} %maximum_bitcast_fusion), channel_id=1, source_target_pairs={{0,4},{4,8},{8,12},{12,0},{1,5},{5,9},{9,13},{13,1},{2,6},{6,10},{... | collective-permute-start | bytes 5768 | tf_op jit(solution)/shard_map/ppermute | solution.py:193
  4.0 15.3 %collective-permute-start.3 = (f32[1,15,32]{1,2,0:T(8,128)S(1)}, f32[1,15,32]{1,2,0:T(8,128)S(1)}, u32[]{:S(2)}, u32[]{:S(2)}) collective-permute-start(f32[1,15,32]{1,2,0:T(8,128)S(1)} %maximum_bitcast_fusion), channel_id=1, source_target_pairs={{0,8},{4,12},{8,0},{12,4},{1,9},{5,13},{9,1},{13,5},{2,10},{6,14},... | collective-permute-start | bytes 5768 | tf_op jit(solution)/shard_map/ppermute | solution.py:193
  6.9 16.4 %collective-permute-start.4 = (f32[1,15,32]{1,2,0:T(8,128)S(1)}, f32[1,15,32]{1,2,0:T(8,128)S(1)}, u32[]{:S(2)}, u32[]{:S(2)}) collective-permute-start(f32[1,15,32]{1,2,0:T(8,128)S(1)} %maximum_bitcast_fusion), channel_id=1, source_target_pairs={{0,12},{4,0},{8,4},{12,8},{1,13},{5,1},{9,5},{13,9},{2,14},{6,2},{... | collective-permute-start | bytes 5768 | tf_op jit(solution)/shard_map/ppermute | solution.py:193
  9.5 102.6 %collective-permute-start.20 = (bf16[128,1536]{0,1:T(8,128)(2,1)S(1)}, bf16[128,1536]{0,1:T(8,128)(2,1)}, u32[]{:S(2)}, u32[]{:S(2)}) collective-permute-start(bf16[128,1536]{0,1:T(8,128)(2,1)S(1)} %bitcast.77), channel_id=1, source_target_pairs={{0,64},{64,128},{128,192},{192,0},{1,65},{65,129},{129,193},{193,1... | collective-permute-start | bytes 1179656 | tf_op jit(solution)/shard_map/ppermute | solution.py:193
  11.1 101.0 %collective-permute-start.21 = (bf16[128,1536]{0,1:T(8,128)(2,1)S(1)}, bf16[128,1536]{0,1:T(8,128)(2,1)}, u32[]{:S(2)}, u32[]{:S(2)}) collective-permute-start(bf16[128,1536]{0,1:T(8,128)(2,1)S(1)} %bitcast.78), channel_id=1, source_target_pairs={{0,128},{64,192},{128,0},{192,64},{1,129},{65,193},{129,1},{193,65... | collective-permute-start | bytes 1179656 | tf_op jit(solution)/shard_map/ppermute | solution.py:193
  17.4 53.0 %collective-permute-start.1 = (bf16[16,2496]{1,0:T(8,128)(2,1)S(1)}, bf16[16,2496]{1,0:T(8,128)(2,1)S(1)}, u32[]{:S(2)}, u32[]{:S(2)}) collective-permute-start(bf16[16,2496]{1,0:T(8,128)(2,1)S(1)} %pad_maximum_fusion.2), channel_id=1, source_target_pairs={{4,0},{8,4},{12,8},{16,12},{20,16},{24,20},{28,24},{32,28},{36,32}... | collective-permute-start | bytes 239624 | tf_op jit(solution)/shard_map/ppermute | solution.py:211
  19.3 51.1 %collective-permute-start = (bf16[16,1536]{1,0:T(8,128)(2,1)S(1)}, bf16[16,1536]{1,0:T(8,128)(2,1)S(1)}, u32[]{:S(2)}, u32[]{:S(2)}) collective-permute-start(bf16[16,1536]{1,0:T(8,128)(2,1)S(1)} %get-tuple-element.59), channel_id=1, source_target_pairs={{0,4},{4,8},{8,12},{12,16},{16,20},{20,24},{24,28},{28,32},{32,36}... | collective-permute-start | bytes 147464 | tf_op jit(solution)/shard_map/ppermute | solution.py:209
  23.3 4.3 %collective-permute-start.5 = (f32[4,15,32]{1,2,0:T(8,128)S(1)}, f32[4,15,32]{1,2,0:T(8,128)S(1)}, u32[]{:S(2)}, u32[]{:S(2)}) collective-permute-start(f32[4,15,32]{1,2,0:T(8,128)S(1)} %pad_maximum_fusion.3), channel_id=1, source_target_pairs={{0,16},{16,32},{32,48},{48,0},{1,17},{17,33},{33,49},{49,1},{2,18}... | collective-permute-start | bytes 23048 | tf_op jit(solution)/shard_map/ppermute | solution.py:193
  27.6 5.6 %collective-permute-start.6 = (f32[4,15,32]{1,2,0:T(8,128)S(1)}, f32[4,15,32]{1,2,0:T(8,128)S(1)}, u32[]{:S(2)}, u32[]{:S(2)}) collective-permute-start(f32[4,15,32]{1,2,0:T(8,128)S(1)} %pad_maximum_fusion.3), channel_id=1, source_target_pairs={{0,32},{16,48},{32,0},{48,16},{1,33},{17,49},{33,1},{49,17},{2,34}... | collective-permute-start | bytes 23048 | tf_op jit(solution)/shard_map/ppermute | solution.py:193
  33.2 4.6 %collective-permute-start.7 = (f32[4,15,32]{1,2,0:T(8,128)S(1)}, f32[4,15,32]{1,2,0:T(8,128)S(1)}, u32[]{:S(2)}, u32[]{:S(2)}) collective-permute-start(f32[4,15,32]{1,2,0:T(8,128)S(1)} %pad_maximum_fusion.3), channel_id=1, source_target_pairs={{0,48},{16,0},{32,16},{48,32},{1,49},{17,1},{33,17},{49,33},{2,50}... | collective-permute-start | bytes 23048 | tf_op jit(solution)/shard_map/ppermute | solution.py:193
  37.9 16.1 %copy-start.29 = (f32[16,15,32]{1,2,0:T(8,128)}, f32[16,15,32]{1,2,0:T(8,128)S(1)}, u32[]{:S(2)}) copy-start(f32[16,15,32]{1,2,0:T(8,128)S(1)} %get-tuple-element.62) | copy-start | bytes 92164
  37.9 16.1 %collective-permute-start.8 = (f32[16,15,32]{1,2,0:T(8,128)S(1)}, f32[16,15,32]{1,2,0:T(8,128)S(1)}, u32[]{:S(2)}, u32[]{:S(2)}) collective-permute-start(f32[16,15,32]{1,2,0:T(8,128)S(1)} %get-tuple-element.62), channel_id=1, source_target_pairs={{0,64},{64,128},{128,192},{192,0},{1,65},{65,129},{129,193},{193,1... | collective-permute-start | bytes 92168 | tf_op jit(solution)/shard_map/ppermute | solution.py:193
  53.9 7.9 %collective-permute-start.9 = (f32[16,15,32]{1,2,0:T(8,128)S(1)}, f32[16,15,32]{1,2,0:T(8,128)S(1)}, u32[]{:S(2)}, u32[]{:S(2)}) collective-permute-start(f32[16,15,32]{1,2,0:T(8,128)S(1)} %get-tuple-element.62), channel_id=1, source_target_pairs={{0,128},{64,192},{128,0},{192,64},{1,129},{65,193},{129,1},{193,65... | collective-permute-start | bytes 92168 | tf_op jit(solution)/shard_map/ppermute | solution.py:193
  61.8 7.2 %collective-permute-start.10 = (f32[16,15,32]{1,2,0:T(8,128)}, f32[16,15,32]{1,2,0:T(8,128)S(1)}, u32[]{:S(2)}, u32[]{:S(2)}) collective-permute-start(f32[16,15,32]{1,2,0:T(8,128)} %copy-done.29), channel_id=1, source_target_pairs={{0,192},{64,0},{128,64},{192,128},{1,193},{65,1},{129,65},{193,129... | collective-permute-start | bytes 92168 | tf_op jit(solution)/shard_map/ppermute | solution.py:193
  83.3 7.7 %collective-permute-start.11 = (f32[32,1024]{1,0:T(8,128)S(1)}, f32[32,1024]{1,0:T(8,128)S(1)}, u32[]{:S(2)}, u32[]{:S(2)}) collective-permute-start(f32[32,1024]{1,0:T(8,128)S(1)} %get-tuple-element.16), channel_id=1, source_target_pairs={{0,4},{4,8},{8,12},{12,0},{1,5},{5,9},{9,13},{13,1},{2,6},{6,10},{... | collective-permute-start | bytes 393224 | tf_op jit(solution)/shard_map/ppermute | solution.py:193
  84.0 10.6 %collective-permute-start.12 = (f32[32,1024]{1,0:T(8,128)S(1)}, f32[32,1024]{1,0:T(8,128)S(1)}, u32[]{:S(2)}, u32[]{:S(2)}) collective-permute-start(f32[32,1024]{1,0:T(8,128)S(1)} %get-tuple-element.16), channel_id=1, source_target_pairs={{0,8},{4,12},{8,0},{12,4},{1,9},{5,13},{9,1},{13,5},{2,10},{6,14},... | collective-permute-start | bytes 393224 | tf_op jit(solution)/shard_map/ppermute | solution.py:193
  89.5 5.1 %collective-permute-start.13 = (f32[32,1024]{1,0:T(8,128)S(1)}, f32[32,1024]{1,0:T(8,128)S(1)}, u32[]{:S(2)}, u32[]{:S(2)}) collective-permute-start(f32[32,1024]{1,0:T(8,128)S(1)} %get-tuple-element.16), channel_id=1, source_target_pairs={{0,12},{4,0},{8,4},{12,8},{1,13},{5,1},{9,5},{13,9},{2,14},{6,2},{... | collective-permute-start | bytes 393224 | tf_op jit(solution)/shard_map/ppermute | solution.py:193
  90.9 21.1 %collective-permute-start.22 = (bf16[128,1536]{0,1:T(8,128)(2,1)S(1)}, bf16[128,1536]{0,1:T(8,128)(2,1)}, u32[]{:S(2)}, u32[]{:S(2)}) collective-permute-start(bf16[128,1536]{0,1:T(8,128)(2,1)S(1)} %bitcast.79), channel_id=1, source_target_pairs={{0,192},{64,0},{128,64},{192,128},{1,193},{65,1},{129,65},{193,129... | collective-permute-start | bytes 1179656 | tf_op jit(solution)/shard_map/ppermute | solution.py:193
  94.7 5.5 %collective-permute-start.14 = (f32[32,1024]{1,0:T(8,128)S(1)}, f32[32,1024]{1,0:T(8,128)S(1)}, u32[]{:S(2)}, u32[]{:S(2)}) collective-permute-start(f32[32,1024]{1,0:T(8,128)S(1)} %fusion.46), channel_id=1, source_target_pairs={{0,16},{16,32},{32,48},{48,0},{1,17},{17,33},{33,49},{49,1},{2,18}... | collective-permute-start | bytes 393224 | tf_op jit(solution)/shard_map/ppermute | solution.py:193
  97.0 7.1 %collective-permute-start.15 = (f32[32,1024]{1,0:T(8,128)S(1)}, f32[32,1024]{1,0:T(8,128)S(1)}, u32[]{:S(2)}, u32[]{:S(2)}) collective-permute-start(f32[32,1024]{1,0:T(8,128)S(1)} %fusion.46), channel_id=1, source_target_pairs={{0,32},{16,48},{32,0},{48,16},{1,33},{17,49},{33,1},{49,17},{2,34}... | collective-permute-start | bytes 393224 | tf_op jit(solution)/shard_map/ppermute | solution.py:193
  100.2 6.0 %collective-permute-start.16 = (f32[32,1024]{1,0:T(8,128)S(1)}, f32[32,1024]{1,0:T(8,128)S(1)}, u32[]{:S(2)}, u32[]{:S(2)}) collective-permute-start(f32[32,1024]{1,0:T(8,128)S(1)} %fusion.46), channel_id=1, source_target_pairs={{0,48},{16,0},{32,16},{48,32},{1,49},{17,1},{33,17},{49,33},{2,50}... | collective-permute-start | bytes 393224 | tf_op jit(solution)/shard_map/ppermute | solution.py:193
  106.1 9.3 %copy-start.7 = (f32[32,1024]{1,0:T(8,128)}, f32[32,1024]{1,0:T(8,128)S(1)}, u32[]{:S(2)}) copy-start(f32[32,1024]{1,0:T(8,128)S(1)} %collective-permute-done.16) | copy-start | bytes 393220
  107.0 8.4 %collective-permute-start.17 = (f32[32,1024]{1,0:T(8,128)S(1)}, f32[32,1024]{1,0:T(8,128)S(1)}, u32[]{:S(2)}, u32[]{:S(2)}) collective-permute-start(f32[32,1024]{1,0:T(8,128)S(1)} %fusion.70), channel_id=1, source_target_pairs={{0,64},{64,128},{128,192},{192,0},{1,65},{65,129},{129,193},{193,1... | collective-permute-start | bytes 393224 | tf_op jit(solution)/shard_map/ppermute | solution.py:193
  107.1 9.3 %collective-permute-start.18 = (f32[32,1024]{1,0:T(8,128)S(1)}, f32[32,1024]{1,0:T(8,128)S(1)}, u32[]{:S(2)}, u32[]{:S(2)}) collective-permute-start(f32[32,1024]{1,0:T(8,128)S(1)} %fusion.70), channel_id=1, source_target_pairs={{0,128},{64,192},{128,0},{192,64},{1,129},{65,193},{129,1},{193,65... | collective-permute-start | bytes 393224 | tf_op jit(solution)/shard_map/ppermute | solution.py:193
  112.1 5.0 %collective-permute-start.19 = (f32[32,1024]{1,0:T(8,128)S(1)}, f32[32,1024]{1,0:T(8,128)S(1)}, u32[]{:S(2)}, u32[]{:S(2)}) collective-permute-start(f32[32,1024]{1,0:T(8,128)S(1)} %fusion.70), channel_id=1, source_target_pairs={{0,192},{64,0},{128,64},{192,128},{1,193},{65,1},{129,65},{193,129... | collective-permute-start | bytes 393224 | tf_op jit(solution)/shard_map/ppermute | solution.py:193
  112.1 5.0 %copy-start.13 = (f32[32]{0:T(128)S(1)}, f32[32]{0:T(128)}, u32[]{:S(2)}) copy-start(f32[32]{0:T(128)} %get-tuple-element.88) | copy-start | bytes 388
  115.4 68.4 %collective-permute-start.23 = (bf16[4,128,1536]{1,2,0:T(8,128)(2,1)}, bf16[4,128,1536]{1,2,0:T(8,128)(2,1)}, u32[]{:S(2)}, u32[]{:S(2)}) collective-permute-start(bf16[4,128,1536]{1,2,0:T(8,128)(2,1)} %get-tuple-element.57), channel_id=1, source_target_pairs={{0,1},{1,0},{2,3},{3,2},{4,5},{5,4},{6,7},{7,6},{8,9},{9,8},{10,11... | collective-permute-start | bytes 4718600 | tf_op jit(solution)/shard_map/ppermute | solution.py:319
  128.5 9.8 %collective-permute-start.24 = (f32[40,1024]{1,0:T(8,128)S(1)}, f32[40,1024]{1,0:T(8,128)S(1)}, u32[]{:S(2)}, u32[]{:S(2)}) collective-permute-start(f32[40,1024]{1,0:T(8,128)S(1)} %get-tuple-element.20), channel_id=1, source_target_pairs={{0,4},{4,8},{8,12},{12,0},{1,5},{5,9},{9,13},{13,1},{2,6},{6,10},{... | collective-permute-start | bytes 491528 | tf_op jit(solution)/shard_map/ppermute | solution.py:193
  128.8 9.6 %collective-permute-start.25 = (f32[40,1024]{1,0:T(8,128)S(1)}, f32[40,1024]{1,0:T(8,128)S(1)}, u32[]{:S(2)}, u32[]{:S(2)}) collective-permute-start(f32[40,1024]{1,0:T(8,128)S(1)} %get-tuple-element.20), channel_id=1, source_target_pairs={{0,8},{4,12},{8,0},{12,4},{1,9},{5,13},{9,1},{13,5},{2,10},{6,14},... | collective-permute-start | bytes 491528 | tf_op jit(solution)/shard_map/ppermute | solution.py:193
  131.4 7.5 %collective-permute-start.26 = (f32[40,1024]{1,0:T(8,128)S(1)}, f32[40,1024]{1,0:T(8,128)S(1)}, u32[]{:S(2)}, u32[]{:S(2)}) collective-permute-start(f32[40,1024]{1,0:T(8,128)S(1)} %get-tuple-element.20), channel_id=1, source_target_pairs={{0,12},{4,0},{8,4},{12,8},{1,13},{5,1},{9,5},{13,9},{2,14},{6,2},{... | collective-permute-start | bytes 491528 | tf_op jit(solution)/shard_map/ppermute | solution.py:193
  138.9 12.1 %collective-permute-start.27 = (f32[40,1024]{1,0:T(8,128)S(1)}, f32[40,1024]{1,0:T(8,128)}, u32[]{:S(2)}, u32[]{:S(2)}) collective-permute-start(f32[40,1024]{1,0:T(8,128)S(1)} %add_add_fusion.3), channel_id=1, source_target_pairs={{0,16},{16,32},{32,48},{48,0},{1,17},{17,33},{33,49},{49,1},{2,18}... | collective-permute-start | bytes 491528 | tf_op jit(solution)/shard_map/ppermute | solution.py:193
  139.9 13.4 %collective-permute-start.28 = (f32[40,1024]{1,0:T(8,128)S(1)}, f32[40,1024]{1,0:T(8,128)}, u32[]{:S(2)}, u32[]{:S(2)}) collective-permute-start(f32[40,1024]{1,0:T(8,128)S(1)} %add_add_fusion.3), channel_id=1, source_target_pairs={{0,32},{16,48},{32,0},{48,16},{1,33},{17,49},{33,1},{49,17},{2,34}... | collective-permute-start | bytes 491528 | tf_op jit(solution)/shard_map/ppermute | solution.py:193
  143.6 12.7 %collective-permute-start.29 = (f32[40,1024]{1,0:T(8,128)S(1)}, f32[40,1024]{1,0:T(8,128)}, u32[]{:S(2)}, u32[]{:S(2)}) collective-permute-start(f32[40,1024]{1,0:T(8,128)S(1)} %add_add_fusion.3), channel_id=1, source_target_pairs={{0,48},{16,0},{32,16},{48,32},{1,49},{17,1},{33,17},{49,33},{2,50}... | collective-permute-start | bytes 491528 | tf_op jit(solution)/shard_map/ppermute | solution.py:193
  147.4 34.8 %all-to-all-start = ((bf16[8,128,360]{1,2,0:T(8,128)(2,1)}), bf16[8,128,360]{1,2,0:T(8,128)(2,1)S(1)}, u32[]{:S(2)}, u32[]{:S(2)}) async-start(bf16[8,128,360]{1,2,0:T(8,128)(2,1)} %copy.185), calls=%async_computation | async-start | bytes 1474560 | tf_op jit(solution)/shard_map/all_to_all | solution.py:334
  151.0 32.8 %copy-start.5 = (bf16[1,4,128,1536]{2,3,1,0:T(8,128)(2,1)S(1)}, bf16[1,4,128,1536]{2,3,1,0:T(8,128)(2,1)}, u32[]{:S(2)}) copy-start(bf16[1,4,128,1536]{2,3,1,0:T(8,128)(2,1)} %get-tuple-element.56) | copy-start | bytes 4718596
  158.1 9.4 %collective-permute-start.30 = (f32[40,1024]{1,0:T(8,128)}, f32[40,1024]{1,0:T(8,128)S(1)}, u32[]{:S(2)}, u32[]{:S(2)}) collective-permute-start(f32[40,1024]{1,0:T(8,128)} %add_add_fusion.2), channel_id=1, source_target_pairs={{0,64},{64,128},{128,192},{192,0},{1,65},{65,129},{129,193},{193,1... | collective-permute-start | bytes 491528 | tf_op jit(solution)/shard_map/ppermute | solution.py:193
  161.5 9.2 %collective-permute-start.31 = (f32[40,1024]{1,0:T(8,128)}, f32[40,1024]{1,0:T(8,128)}, u32[]{:S(2)}, u32[]{:S(2)}) collective-permute-start(f32[40,1024]{1,0:T(8,128)} %add_add_fusion.2), channel_id=1, source_target_pairs={{0,128},{64,192},{128,0},{192,64},{1,129},{65,193},{129,1},{193,65... | collective-permute-start | bytes 491528 | tf_op jit(solution)/shard_map/ppermute | solution.py:193
  161.5 9.2 %collective-permute-start.32 = (f32[40,1024]{1,0:T(8,128)}, f32[40,1024]{1,0:T(8,128)}, u32[]{:S(2)}, u32[]{:S(2)}) collective-permute-start(f32[40,1024]{1,0:T(8,128)} %add_add_fusion.2), channel_id=1, source_target_pairs={{0,192},{64,0},{128,64},{192,128},{1,193},{65,1},{129,65},{193,129... | collective-permute-start | bytes 491528 | tf_op jit(solution)/shard_map/ppermute | solution.py:193
  171.9 34.8 %collective-permute-start.33 = (f32[40,1024]{1,0:T(8,128)S(1)}, f32[40,1024]{1,0:T(8,128)}, u32[]{:S(2)}, u32[]{:S(2)}) collective-permute-start(f32[40,1024]{1,0:T(8,128)S(1)} %add_add_fusion.1), channel_id=1, source_target_pairs={{0,1},{1,2},{2,3},{3,0},{4,5},{5,6},{6,7},{7,4},{8,9},{9,10},{10,1... | collective-permute-start | bytes 491528 | tf_op jit(solution)/shard_map/ppermute | solution.py:193
  172.0 34.7 %collective-permute-start.34 = (f32[40,1024]{1,0:T(8,128)S(1)}, f32[40,1024]{1,0:T(8,128)}, u32[]{:S(2)}, u32[]{:S(2)}) collective-permute-start(f32[40,1024]{1,0:T(8,128)S(1)} %add_add_fusion.1), channel_id=1, source_target_pairs={{0,2},{1,3},{2,0},{3,1},{4,6},{5,7},{6,4},{7,5},{8,10},{9,11},{10,... | collective-permute-start | bytes 491528 | tf_op jit(solution)/shard_map/ppermute | solution.py:193
  176.9 29.7 %collective-permute-start.35 = (f32[40,1024]{1,0:T(8,128)S(1)}, f32[40,1024]{1,0:T(8,128)}, u32[]{:S(2)}, u32[]{:S(2)}) collective-permute-start(f32[40,1024]{1,0:T(8,128)S(1)} %add_add_fusion.1), channel_id=1, source_target_pairs={{0,3},{1,0},{2,1},{3,2},{4,7},{5,4},{6,5},{7,6},{8,11},{9,8},{10,9... | collective-permute-start | bytes 491528 | tf_op jit(solution)/shard_map/ppermute | solution.py:193
  196.2 16.0 %all-to-all-start.1 = ((bf16[4,384,360]{1,2,0:T(8,128)(2,1)}), bf16[4,384,360]{1,2,0:T(8,128)(2,1)S(1)}, u32[]{:S(2)}, u32[]{:S(2)}) async-start(bf16[4,384,360]{1,2,0:T(8,128)(2,1)} %bitcast.67), calls=%async_computation.1 | async-start | bytes 2211840 | tf_op jit(solution)/shard_map/all_to_all | solution.py:342
  212.7 10.9 %copy-start.10 = (f32[15,16]{0,1:T(8,128)S(1)}, f32[15,16]{0,1:T(8,128)}, u32[]{:S(2)}) copy-start(f32[15,16]{0,1:T(8,128)} %copy-done.9) | copy-start | bytes 2884
  213.6 21.4 %all-to-all-start.2 = ((bf16[32,24,180]{2,1,0:T(8,128)(2,1)}), bf16[32,24,180]{2,1,0:T(8,128)(2,1)S(1)}, u32[]{:S(2)}, u32[]{:S(2)}) async-start(bf16[32,24,180]{2,1,0:T(8,128)(2,1)} %bitcast.23), calls=%async_computation.2 | async-start | bytes 786432 | tf_op jit(solution)/shard_map/all_to_all | solution.py:345
  (22 other events, 93.0 us)

commit v2 on v1

v2 whole, which is shorter than its diff:
```python
import math

import jax
import jax.numpy as jnp
from jax import lax
from jax.experimental import pallas as pl
from jax.experimental.pallas import tpu as pltpu
from jax.sharding import Mesh, PartitionSpec as P

F32 = jnp.float32
BF16 = jnp.bfloat16
HALO = 16
EXT = 136
SEG = 17
PADC = 1024
MODES = 16
NT = (((1,), (1,)), ((), ()))


def rounded(a):
    return a.astype(BF16).astype(F32)


def project(tp, tk, tn, wt, taps, cott, cotnt, zf, mix, cots, us, dls, acc, turn):
    step = pl.program_id(0)
    rows = jnp.concatenate([tp[...], tk[...], tn[...]], axis=0)
    part = lax.dot_general(rows, wt[...], NT, preferred_element_type=F32)

    @pl.when(step == 0)
    def _():
        acc[...] = part

    @pl.when(step > 0)
    def _():
        acc[...] += part

    @pl.when(step == pl.num_programs(0) - 1)
    def _():
        width, own = cott.shape
        for g in range(3):
            zf[:, g * PADC : g * PADC + width] = rounded(acc[:, g * width : (g + 1) * width])
            zf[:, g * PADC + width : (g + 1) * PADC] = jnp.zeros((zf.shape[0], PADC - width), F32)
        turn[...] = jnp.zeros(turn.shape, F32)
        turn[0:width, 0:own] = cott[...].astype(F32)
        turn[0:width, own : own + HALO] = cotnt[...].astype(F32)

        def tile(ct, carry):
            lane = pl.multiple_of(ct * 128, 128)
            lanes = pl.ds(lane, 128)
            mixed = []
            for g in range(3):
                cols = pl.ds(pl.multiple_of(g * PADC + lane, 128), 128)
                total = taps[0:1, cols] * zf[pl.ds(HALO, EXT), cols]
                for j in range(1, 7):
                    total = total + taps[j : j + 1, cols] * zf[pl.ds(HALO - j, EXT), cols]
                mix[g, :, lanes] = total
                mixed.append(total)
            cot = jnp.concatenate(
                [turn[lanes, 0:128].T, turn[lanes, 128:256].T[0 : EXT - 128]], axis=0
            )
            cots[:, lanes] = cot
            us[:, lanes] = rounded(mixed[1] * mixed[2])
            dls[:, lanes] = rounded(cot * mixed[0])
            return carry

        lax.fori_loop(0, PADC // 128, tile, 0)


def first_params(rates, residues, amp, out, held):
    count = rates.shape[0]
    held[...] = jnp.zeros(held.shape, F32)
    held[0:count, 0:MODES] = rates[...]
    held[0:count, MODES : 2 * MODES] = residues[...] * amp[...]
    out[...] = held[...].T[0 : 2 * MODES, 0:count]


def placed(place, refs, held, goal):
    me = place[0]
    wide = refs[0].shape[1]
    total = None
    for d, ref in enumerate(refs):
        held[...] = jnp.zeros(held.shape, F32)
        held[:, 0:wide] = ref[...]
        part = pltpu.roll(held[...], lax.rem(me + (4 - d), 4) * wide, 1)
        total = part if total is None else total + part
    return total[:, 0:goal]


def join_params(place, r0, r1, r2, r3, out, held):
    out[...] = placed(place, (r0, r1, r2, r3), held, out.shape[1])


def end_states(place, r0, r1, r2, r3, us, dls, rates, gains, es, ends, endb, ut, dt, held):
    joined = placed(place, (r0, r1, r2, r3), held, PADC)
    rates[...] = joined[0:MODES]
    gains[...] = joined[MODES : 2 * MODES]
    sub = lax.broadcasted_iota(jnp.int32, (8, 128), 0)
    subf = sub.astype(F32)
    fdepth = jnp.where(sub == 7, 0.0, (EXT - 8 - SEG) - SEG * subf)
    bdepth = jnp.where(sub == 0, 0.0, SEG * subf - 8.0)

    def tile(ct, carry):
        lanes = pl.ds(pl.multiple_of(ct * 128, 128), 128)
        ut[...] = us[:, lanes]
        dt[...] = dls[:, lanes]
        rate = rates[:, lanes]
        decay = jnp.exp(-rate)
        for half in range(2):
            ks = range(half * 8, half * 8 + 8)
            al = [jnp.broadcast_to(decay[k : k + 1, :], (8, 128)) for k in ks]
            rl = [jnp.broadcast_to(rate[k : k + 1, :], (8, 128)) for k in ks]
            st = [jnp.zeros((8, 128), F32)] * 8
            snap = st
            for t in range(SEG):
                uv = ut[pl.ds(t, 8, stride=SEG), :]
                st = [a * s + uv for a, s in zip(al, st)]
                if t == 8:
                    snap = st
            for i, k in enumerate(ks):
                es[0, k, :, lanes] = st[i]
                full = jnp.where(sub == 7, snap[i], st[i]) * jnp.exp(-rl[i] * fdepth)
                ends[k : k + 1, lanes] = jnp.sum(full, axis=0, keepdims=True)
            st = [jnp.zeros((8, 128), F32)] * 8
            for t in range(SEG - 1, -1, -1):
                dv = dt[pl.ds(t, 8, stride=SEG), :]
                st = [a * s + dv for a, s in zip(al, st)]
                if t == 8:
                    snap = st
            for i, k in enumerate(ks):
                es[1, k, :, lanes] = st[i]
                full = jnp.where(sub == 0, snap[i], st[i]) * jnp.exp(-rl[i] * bdepth)
                ends[MODES + k : MODES + k + 1, lanes] = jnp.sum(full, axis=0, keepdims=True)
        return carry

    lax.fori_loop(0, PADC // 128, tile, 0)
    endb[...] = ends[...].astype(BF16)


def make_level(span):
    def level(place, own, r1, r2, r3, rates, total, totalb, prefix):
        me = place[0]
        rate = rates[...] * float(span)
        before = jnp.zeros((MODES, PADC), F32)
        after = before
        whole_f = before
        whole_b = before
        for d, ref in enumerate((own, r1, r2, r3)):
            m = lax.rem(me + (4 - d), 4)
            f = ref[0:MODES, :].astype(F32)
            b = ref[MODES : 2 * MODES, :].astype(F32)
            whole_f = whole_f + f * jnp.exp(-rate * (3 - m).astype(F32))
            whole_b = whole_b + b * jnp.exp(-rate * m.astype(F32))
            if d > 0:
                gf = me - 1 - m
                gb = m - me - 1
                wf = jnp.exp(-rate * jnp.maximum(gf, 0).astype(F32))
                wb = jnp.exp(-rate * jnp.maximum(gb, 0).astype(F32))
                before = before + jnp.where(gf >= 0, 1.0, 0.0) * (wf * f)
                after = after + jnp.where(gb >= 0, 1.0, 0.0) * (wb * b)
        prefix[0:MODES, :] = before
        prefix[MODES : 2 * MODES, :] = after
        total[0:MODES, :] = whole_f
        total[MODES : 2 * MODES, :] = whole_b
        totalb[0:MODES, :] = whole_f.astype(BF16)
        totalb[MODES : 2 * MODES, :] = whole_b.astype(BF16)

    return level


def finish(
    place, zf, mix, es, py, pz, px, taps, rates, reff, cots, us, dls,
    outt, dz, dzb, sums, inc, ut, dt, longs, dps, dms, outs, dzs, dzt, packed,
):
    width, own = outt.shape
    rate_all = rates[...] * float(own)
    for back in range(2):
        part = pl.ds(back * MODES, MODES)
        near, mid = place[2], place[1]
        if back:
            near, mid = 3 - near, 3 - mid
        far = pz[part, :] + jnp.exp(-rate_all * (4 * mid).astype(F32)) * px[part, :]
        inc[part, :] = py[part, :] + jnp.exp(-rate_all * near.astype(F32)) * far
    sub = lax.broadcasted_iota(jnp.int32, (8, 128), 0)

    def tile(ct, carry):
        lane = pl.multiple_of(ct * 128, 128)
        lanes = pl.ds(lane, 128)
        ut[...] = us[:, lanes]
        dt[...] = dls[:, lanes]
        rate = rates[:, lanes]
        decay = jnp.exp(-rate)
        gain = reff[:, lanes]
        for half in range(2):
            ks = range(half * 8, half * 8 + 8)
            al = [jnp.broadcast_to(decay[k : k + 1, :], (8, 128)) for k in ks]
            gl = [jnp.broadcast_to(gain[k : k + 1, :], (8, 128)) for k in ks]
            rl = [jnp.broadcast_to(rate[k : k + 1, :], (8, 128)) for k in ks]
            fwd = []
            bwd = []
            for i, k in enumerate(ks):
                jump = [jnp.exp(-float(SEG * m) * rl[i]) for m in (1, 2, 4)]
                x = jnp.where(sub == 0, inc[k : k + 1, lanes], pltpu.roll(es[0, k, :, lanes], 1, 0))
                for m, d in zip((1, 2, 4), jump):
                    x = x + jnp.where(sub >= m, pltpu.roll(x, m, 0) * d, 0.0)
                fwd.append(x)
                x = jnp.where(
                    sub == 7, inc[MODES + k : MODES + k + 1, lanes], pltpu.roll(es[1, k, :, lanes], 7, 0)
                )
                for m, d in zip((1, 2, 4), jump):
                    x = x + jnp.where(sub < 8 - m, pltpu.roll(x, 8 - m, 0) * d, 0.0)
                bwd.append(x)
            gr = [jnp.zeros((8, 128), F32)] * 8
            st = fwd
            for t in range(SEG):
                uv = ut[pl.ds(t, 8, stride=SEG), :]
                dv = dt[pl.ds(t, 8, stride=SEG), :]
                if t >= 9:
                    dv = jnp.where(sub < 7, dv, 0.0)
                st = [a * s + uv for a, s in zip(al, st)]
                gr = [q + dv * s for q, s in zip(gr, st)]
                total = sum(g * s for g, s in zip(gl, st))
                if half:
                    total = total + longs[pl.ds(t, 8, stride=SEG), :]
                longs[pl.ds(t, 8, stride=SEG), :] = total
            for i, k in enumerate(ks):
                sums[24 + k : 25 + k, lanes] = jnp.sum(gr[i], axis=0, keepdims=True)
            st = bwd
            for t in range(SEG - 1, -1, -1):
                dv = dt[pl.ds(t, 8, stride=SEG), :]
                st = [a * s + dv for a, s in zip(al, st)]
                total = sum(g * s for g, s in zip(gl, st))
                if half:
                    total = total + dps[pl.ds(t, 8, stride=SEG), :]
                dps[pl.ds(t, 8, stride=SEG), :] = total
        long_out = rounded(longs[...])
        dprod = rounded(dps[...])
        outs[lanes, :] = (mix[0, 0:own, lanes] * long_out[0:own]).T
        dms[0] = rounded(cots[:, lanes] * long_out)
        dms[1] = rounded(dprod * mix[2, :, lanes])
        dms[2] = rounded(dprod * mix[1, :, lanes])
        for g in range(3):
            cols = pl.ds(pl.multiple_of(g * PADC + lane, 128), 128)
            mine = dms[g, 0:own, :]
            total = taps[0:1, cols] * mine
            sums[8 * g : 8 * g + 1, lanes] = jnp.sum(
                mine * zf[pl.ds(HALO, own), cols], axis=0, keepdims=True
            )
            for j in range(1, 7):
                total = total + taps[j : j + 1, cols] * dms[g, pl.ds(j, own), :]
                sums[8 * g + j : 8 * g + j + 1, lanes] = jnp.sum(
                    mine * zf[pl.ds(HALO - j, own), cols], axis=0, keepdims=True
                )
            sums[8 * g + 7 : 8 * g + 8, lanes] = jnp.zeros((1, 128), F32)
            dzs[:, cols] = total
            dzt[cols, :] = total.T
        return carry

    lax.fori_loop(0, PADC // 128, tile, 0)
    outt[...] = outs[0:width, :].astype(BF16)
    for g in range(3):
        dz[:, g * width : (g + 1) * width] = dzs[:, g * PADC : g * PADC + width].astype(BF16)
        packed[g * width : (g + 1) * width, :] = dzt[g * PADC : g * PADC + width, :]
    piece = dzb.shape[1] // 2
    for b in range(8):
        offs = [h * 8 * piece + (b % 2) * 4 * piece + (b // 2) * piece for h in range(2)]
        both = [packed[off : off + piece, :] for off in offs]
        dzb[b] = jnp.concatenate(both, axis=0).astype(BF16)


def weight_term(place, arrived, ours, theirs, term):
    me = place[0]
    core = place[1]
    chunk = term.shape[2]
    slots = (me, lax.bitwise_xor(me, 1), 3 - me, lax.bitwise_xor(3 - me, 1))
    pairs = []
    for ref, c in ((ours, core), (theirs, 1 - core)):
        for p in range(2):
            left = [arrived[slots[2 * p + i] * 2 + c] for i in range(2)]
            pairs.append((jnp.concatenate(left, axis=1), ref, p))
    for j in range(4):
        total = None
        for left, ref, p in pairs:
            right = ref[p, :, j * chunk : (j + 1) * chunk]
            part = jnp.dot(left, right, preferred_element_type=F32)
            total = part if total is None else total + part
        term[j] = total.astype(BF16)


def split_rows(got, blocks, turn):
    chans = got.shape[1]
    fblk = blocks.shape[1]
    piece = blocks.shape[2]
    turn[0:chans, :] = (
        got[0].astype(F32) + got[1].astype(F32) + got[2].astype(F32) + got[3].astype(F32)
    )
    turn[chans:, :] = jnp.zeros((turn.shape[0] - chans, turn.shape[1]), F32)
    flipped = turn[...].T
    for q in range(16):
        for h in range(2):
            part = flipped[q * fblk : (q + 1) * fblk, h * piece : (h + 1) * piece]
            blocks[2 * q + h] = part.astype(BF16)


def ring(a, ax, d):
    return lax.ppermute(a, ax, [(i, (i + d) % 4) for i in range(4)])


def params(mb):
    return pltpu.CompilerParams(vmem_limit_bytes=mb * 1024 * 1024)


def local(tokens, w_in, conv_taps, residues, rates, cotangent):
    feats = tokens[0]
    cot = cotangent[0]
    own, width = cot.shape
    depth = feats.shape[1]
    chans = 3 * width
    count = 64
    piece = chans // 16
    fblk = depth // count
    xi, zi, yi = lax.axis_index("x"), lax.axis_index("zl"), lax.axis_index("y")
    ci = lax.axis_index("core")
    ctx = ("x", "zl", "y")
    scale = 1.0 / math.sqrt(4 * count * own)
    smem = pl.BlockSpec(memory_space=pltpu.SMEM)
    vm = pl.BlockSpec(memory_space=pltpu.VMEM)
    each = width // count
    amp_mine = jnp.sqrt(-jnp.expm1(-2.0 * rates))
    held = pl.pallas_call(
        first_params,
        in_specs=[vm] * 3,
        out_specs=vm,
        out_shape=jax.ShapeDtypeStruct((2 * MODES, each), F32),
        scratch_shapes=[pltpu.VMEM((128, 128), F32)],
        compiler_params=params(4),
        name="first_params",
    )(rates, residues, amp_mine)
    early = None
    for ax, me in (("y", yi), ("zl", zi)):
        blocks = [held] + [ring(held, ax, d) for d in (1, 2, 3)]
        each = 4 * each
        held = pl.pallas_call(
            join_params,
            in_specs=[smem] + [vm] * 4,
            out_specs=vm,
            out_shape=jax.ShapeDtypeStruct((2 * MODES, each), F32),
            scratch_shapes=[pltpu.VMEM((2 * MODES, 256), F32)],
            compiler_params=params(4),
            name="join_params",
        )(me.reshape(1), *blocks)
        if early is None:
            early = held
    blocks = [held] + [ring(held, "x", d) for d in (1, 2, 3)]
    taps = jnp.pad(conv_taps.reshape(7, 3, width), ((0, 1), (0, 0), (0, PADC - width)))
    taps = taps.reshape(8, 3 * PADC)
    tprev = lax.ppermute(feats[own - HALO :], ctx, [(i, i + 1) for i in range(count - 1)])
    firsts = jnp.concatenate([feats[:HALO], cot[:HALO]], axis=1)
    nexts = lax.ppermute(firsts, ctx, [(i, i - 1) for i in range(1, count)])
    tnext = nexts[:, :depth]
    cnext = nexts[:, depth:].T

    kblk = 256

    def whole(shape):
        return pl.BlockSpec(shape, lambda k: (0,) * len(shape))

    ext_rows = own + 2 * HALO
    shapes = [(ext_rows, 3 * PADC), (3, EXT, PADC), (EXT, PADC), (EXT, PADC), (EXT, PADC)]
    zf, mix, cots, us, dls = pl.pallas_call(
        project,
        grid=(depth // kblk,),
        in_specs=[
            pl.BlockSpec((HALO, kblk), lambda k: (0, k)),
            pl.BlockSpec((own, kblk), lambda k: (0, k)),
            pl.BlockSpec((HALO, kblk), lambda k: (0, k)),
            pl.BlockSpec((chans, kblk), lambda k: (0, k)),
            whole((8, 3 * PADC)),
            whole((width, own)),
            whole((width, HALO)),
        ],
        out_specs=[whole(s) for s in shapes],
        out_shape=[jax.ShapeDtypeStruct(s, F32) for s in shapes],
        scratch_shapes=[pltpu.VMEM((ext_rows, chans), F32), pltpu.VMEM((PADC, 256), F32)],
        compiler_params=params(24),
        cost_estimate=pl.CostEstimate(flops=1500000000, bytes_accessed=14000000, transcendentals=0),
        name="project",
    )(tprev, feats, tnext, w_in.T, taps, cot.T, cnext)

    *blocks, us, dls = lax.optimization_barrier((*blocks, us, dls))
    rate, gain, es, ends, endb = pl.pallas_call(
        end_states,
        in_specs=[smem] + [vm] * 6,
        out_specs=[vm] * 5,
        out_shape=[
            jax.ShapeDtypeStruct((MODES, PADC), F32),
            jax.ShapeDtypeStruct((MODES, PADC), F32),
            jax.ShapeDtypeStruct((2, MODES, 8, PADC), F32),
            jax.ShapeDtypeStruct((2 * MODES, PADC), F32),
            jax.ShapeDtypeStruct((2 * MODES, PADC), BF16),
        ],
        scratch_shapes=[
            pltpu.VMEM((EXT, 128), F32),
            pltpu.VMEM((EXT, 128), F32),
            pltpu.VMEM((2 * MODES, PADC), F32),
        ],
        compiler_params=params(12),
        cost_estimate=pl.CostEstimate(flops=20000000, bytes_accessed=3000000, transcendentals=0),
        name="end_states",
    )(xi.reshape(1), *blocks, us, dls)

    mine, _ = lax.optimization_barrier((feats, early))
    pair = lax.ppermute(mine, "y", [(i, i ^ 1) for i in range(4)])
    two = jnp.stack([mine, pair], axis=0)

    prefixes = []
    total, sent = ends, endb
    for ax, me, span in (("y", yi, own), ("zl", zi, 4 * own), ("x", xi, 16 * own)):
        near = [ring(sent, ax, d) for d in (1, 2, 3)]
        total, sent, prefix = pl.pallas_call(
            make_level(span),
            in_specs=[smem] + [vm] * 5,
            out_specs=[vm] * 3,
            out_shape=[
                jax.ShapeDtypeStruct((2 * MODES, PADC), F32),
                jax.ShapeDtypeStruct((2 * MODES, PADC), BF16),
                jax.ShapeDtypeStruct((2 * MODES, PADC), F32),
            ],
            compiler_params=params(8),
            name="level",
        )(me.reshape(1), total, *near, rate)
        prefixes.append(prefix)
        if ax == "y":
            two, _ = lax.optimization_barrier((two, sent))
            other = lax.ppermute(two, "y", [(i, 3 - i) for i in range(4)])
    other, prefixes[2] = lax.optimization_barrier((other, prefixes[2]))
    ours = jnp.concatenate([two, other], axis=0)
    theirs = lax.ppermute(ours, "core", [(0, 1), (1, 0)])

    outt, dz, dzb, sums = pl.pallas_call(
        finish,
        in_specs=[smem] + [vm] * 12,
        out_specs=[vm] * 4,
        out_shape=[
            jax.ShapeDtypeStruct((width, own), BF16),
            jax.ShapeDtypeStruct((own, chans), BF16),
            jax.ShapeDtypeStruct((8, 2 * piece, own), BF16),
            jax.ShapeDtypeStruct((40, PADC), F32),
        ],
        scratch_shapes=[
            pltpu.VMEM((2 * MODES, PADC), F32),
            pltpu.VMEM((EXT, 128), F32),
            pltpu.VMEM((EXT, 128), F32),
            pltpu.VMEM((EXT, 128), F32),
            pltpu.VMEM((EXT, 128), F32),
            pltpu.VMEM((3, EXT, 128), F32),
            pltpu.VMEM((PADC, own), F32),
            pltpu.VMEM((own, 3 * PADC), F32),
            pltpu.VMEM((3 * PADC, own), F32),
            pltpu.VMEM((chans, own), F32),
        ],
        compiler_params=params(24),
        cost_estimate=pl.CostEstimate(flops=200000000, bytes_accessed=10000000, transcendentals=0),
        name="finish",
    )(jnp.stack([xi, zi, yi]), zf, mix, es, *prefixes, taps, rate, gain, cots, us, dls)
    output = outt.T

    arrived = lax.all_to_all(dzb, ("y", "core"), split_axis=0, concat_axis=0, tiled=True)
    term = pl.pallas_call(
        weight_term,
        in_specs=[smem] + [vm] * 3,
        out_specs=vm,
        out_shape=jax.ShapeDtypeStruct((4, 2 * piece, depth // 4), BF16),
        compiler_params=params(24),
        cost_estimate=pl.CostEstimate(flops=1200000000, bytes_accessed=6000000, transcendentals=0),
        name="weight_term",
    )(jnp.stack([yi, ci]), arrived, ours.reshape(2, 2 * own, depth), theirs.reshape(2, 2 * own, depth))
    got = lax.all_to_all(term, "x", 0, 0, tiled=True)
    blocks = pl.pallas_call(
        split_rows,
        in_specs=[vm],
        out_specs=vm,
        out_shape=jax.ShapeDtypeStruct((32, fblk, piece), BF16),
        scratch_shapes=[pltpu.VMEM((384, depth // 4), F32)],
        compiler_params=params(12),
        name="split_rows",
    )(got)
    last = lax.all_to_all(blocks, ("zl", "y", "zh"), 0, 0, tiled=True)
    last = jnp.sum(last.reshape(4, 4, 2, fblk, piece).astype(F32), axis=(0, 2)) * scale
    grad_weight = last.transpose(1, 0, 2).reshape(fblk, 4 * piece).astype(BF16)

    for ax, behind in (("zl", term), ("y", got), ("x", None), (("zh", "core"), None)):
        short = sums.astype(BF16)
        parts = [short] + [ring(short, ax, d) for d in (1, 2, 3)]
        if behind is not None:
            *parts, _ = lax.optimization_barrier((*parts, behind))
        sums = sum(p.astype(F32) for p in parts)
    grad_taps = sums[:24].reshape(3, 8, PADC)[:, :7, :width].transpose(1, 0, 2).reshape(7, chans)
    grad_taps = grad_taps * scale
    index = (xi * 4 + zi) * 4 + yi
    held_chans = width // count
    chosen = lax.dynamic_slice_in_dim(sums[24:, :width], index * held_chans, held_chans, axis=1)
    grad_residues = amp_mine * chosen.T * scale

    dz, _ = lax.optimization_barrier((dz, term))
    grad_feats = lax.dot_general(dz, w_in, NT, preferred_element_type=F32).astype(BF16)
    return (output[None], grad_feats[None], grad_weight, grad_taps, grad_residues)


def solution(mesh):
    fine = Mesh(mesh.devices.reshape(4, 4, 4, 2, 2), ("x", "zl", "y", "zh", "core"))
    ctx = ("x", "zl", "y")
    dp = ("zh", "core")
    in_specs = (P(dp, ctx, None), P(), P(), P(ctx, None), P(ctx, None), P(dp, ctx, None))
    out_specs = (P(dp, ctx, None), P(dp, ctx, None), P(ctx, dp), P(), P(ctx, None))
    return jax.shard_map(local, mesh=fine, in_specs=in_specs, out_specs=out_specs, check_vma=False)
```

time: 237 us -> 173 us (0.73)
  the two profiles are of different devices: /device:TPU:32 before, /device:TPU:1 now
where the time goes in v2:
time: 173 us
  starting transfers between devices  74.7 us (43%)
  waiting for transfers between devices  52.7 us (30%)
  Pallas kernels  25.2 us (15%)
  local copies, waits for them, and re-layouts  12.8 us (7%)
  matrix products  5.65 us (3%)
    ppermute x30, starting transfers between devices, ring(): return lax.ppermute(a, ax, [(i, (i + d) % 4) for i in range(4)])  46.4 us
    ppermute x30, waiting for transfers between devices, ring(): return lax.ppermute(a, ax, [(i, (i + d) % 4) for i in range(4)])  30.5 us
    all_to_all x1, waiting for transfers between devices, local(): lax.all_to_all(dzb, ('y', 'core'), split_axis=0, concat_axis=0, tiled=True)  11.7 us
    all_to_all x1, waiting for transfers between devices, local(): last = lax.all_to_all(blocks, ('zl', 'y', 'zh'), 0, 0, tiled=True)  10.5 us
    ppermute x1, starting transfers between devices, local(): theirs = lax.ppermute(ours, 'core', [(0, 1), (1, 0)])  9.22 us
    unnamed x23, local copies, waits for them, and re-layouts  9.13 us
    pallas_call x1, Pallas kernels, local(): pl.pallas_call(finish, in_specs=[smem] + [vm] * 12, out_specs=[vm] * 4, o...  8.77 us
    pallas_call x1, Pallas kernels, local(): pl.pallas_call(project, grid=(depth // kblk,), in_specs=[pl.BlockSpec((HA...  7.69 us
  transfers between devices with their start and end apart: 38, of which 21 were waited for; matrix products, arithmetic and copies ran while one was open for 6% of the time, Pallas kernels for 12%

profile of v2, /device:TPU:1, one launch (start us, length us, event | category | flops | bytes accessed | tf_op | source)
XLA Modules:
  0.0 172.7 jit_solution(12330527314866682432)
XLA Ops:
  0.7 0.8 copy.38
  3.7 3.6 %collective-permute-start.4 = (f32[32,15]{1,0:T(8,128)S(1)}, f32[32,15]{1,0:T(8,128)S(1)}, u32[]{:S(2)}, u32[]{:S(2)}) collective-permute-start(f32[32,15]{1,0:T(8,128)S(1)} %first_params.1.r0), channel_id=1, source_target_pairs={{0,12},{4,0},{8,4},{12,8},{1,13},{5,1},{9,5},{13,9},{2,14},{6,2},{... | collective-permute-start | bytes 5768 | tf_op jit(solution)/shard_map/ppermute | solution.py:305
  8.3 0.8 slice_bitcast_fusion.1
  9.2 3.5 %collective-permute-start = (bf16[16,1536]{1,0:T(8,128)(2,1)S(1)}, bf16[16,1536]{1,0:T(8,128)(2,1)S(1)}, u32[]{:S(2)}, u32[]{:S(2)}) collective-permute-start(bf16[16,1536]{1,0:T(8,128)(2,1)S(1)} %get-tuple-element.111), channel_id=1, source_target_pairs={{0,4},{4,8},{8,12},{12,16},{16,20},{20,24},{24,28},{28,32},{32,36}... | collective-permute-start | bytes 147464 | tf_op jit(solution)/shard_map/ppermute | solution.py:356
  12.7 1.0 copy.43
  13.9 4.4 %collective-permute-start.7 = (f32[32,60]{1,0:T(8,128)S(1)}, f32[32,60]{1,0:T(8,128)S(1)}, u32[]{:S(2)}, u32[]{:S(2)}) collective-permute-start(f32[32,60]{1,0:T(8,128)S(1)} %join_params.2.r0), channel_id=1, source_target_pairs={{0,48},{16,0},{32,16},{48,32},{1,49},{17,1},{33,17},{49,33},{2,50}... | collective-permute-start | bytes 23048 | tf_op jit(solution)/shard_map/ppermute | solution.py:305
  18.3 1.3 collective-permute-start.1
  19.6 1.0 reshape.42
  20.6 1.4 collective-permute-start.6
  22.1 2.4 %collective-permute-start.5 = (f32[32,60]{1,0:T(8,128)S(1)}, f32[32,60]{1,0:T(8,128)S(1)}, u32[]{:S(2)}, u32[]{:S(2)}) collective-permute-start(f32[32,60]{1,0:T(8,128)S(1)} %join_params.2.r0), channel_id=1, source_target_pairs={{0,16},{16,32},{32,48},{48,0},{1,17},{17,33},{33,49},{49,1},{2,18}... | collective-permute-start | bytes 23048 | tf_op jit(solution)/shard_map/ppermute | solution.py:305
  24.6 3.3 %collective-permute-done.5.r1 = f32[32,60]{1,0:T(8,128)S(1)} collective-permute-done((f32[32,60]{1,0:T(8,128)S(1)}, f32[32,60]{1,0:T(8,128)S(1)}, u32[]{:S(2)}, u32[]{:S(2)}) %collective-permute-start.5) | collective-permute-done | bytes 7712 | tf_op jit(solution)/shard_map/ppermute | solution.py:305
  27.9 2.8 %collective-permute-start.10 = (f32[32,240]{1,0:T(8,128)S(1)}, f32[32,240]{1,0:T(8,128)S(1)}, u32[]{:S(2)}, u32[]{:S(2)}) collective-permute-start(f32[32,240]{1,0:T(8,128)S(1)} %join_params.3.r0), channel_id=1, source_target_pairs={{0,192},{64,0},{128,64},{192,128},{1,193},{65,1},{129,65},{193,129... | collective-permute-start | bytes 92168 | tf_op jit(solution)/shard_map/ppermute | solution.py:305
  31.9 3.5 %copy-done = bf16[1536,2880]{0,1:T(8,128)(2,1)S(1)} copy-done((bf16[1536,2880]{0,1:T(8,128)(2,1)S(1)}, bf16[1536,2880]{0,1:T(8,128)(2,1)}, u32[]{:S(2)}) %copy-start) | copy-done | bytes 8847384
  35.4 7.7 %project.1 = (f32[160,3072]{1,0:T(8,128)S(1)}, f32[3,136,1024]{2,1,0:T(8,128)S(1)}, f32[136,1024]{1,0:T(8,128)S(1)}, f32[136,1024]{1,0:T(8,128)S(1)}, f32[136,1024]{1,0:T(8,128)S(1)}) custom-call(bf16[16,1536]{1,0:T(8,128)(2,1)S(1)} %collective-permute-done.tp, bf16[128,1536]{1,0:T(8,128)(2,1)S(1)} %bitcast.46, bf16[16,1536]{1,0:T(8,128)(2,1)S(1)} %slice.44.tn, ...), custom_call_target="tpu_custom_call" | custom-call | flops 1500000000 | bytes 14000000 | tf_op jit(solution)/shard_map/project/pallas_call | solution.py:369
  43.1 2.0 %end_states.1 = (f32[16,1024]{1,0:T(8,128)S(1)}, f32[16,1024]{1,0:T(8,128)S(1)}, f32[2,16,8,1024]{3,2,1,0:T(8,128)S(1)}, f32[32,1024]{1,0:T(8,128)S(1)}, bf16[32,1024]{1,0:T(8,128)(2,1)S(1)}) custom-call(s32[1]{0:T(128)} %bitcast.place, f32[32,240]{1,0:T(8,128)S(1)} %join_params.3.r0, f32[32,240]{1,0:T(8,128)S(1)} %collective-permute-done.8.r1, ...), custom_call_target="tpu_custom_call" | custom-call | flops 20000000 | bytes 3000000 | tf_op jit(solution)/shard_map/end_states/pallas_call | solution.py:390
  47.3 1.0 collective-permute-done.13.r3
  48.4 2.0 %collective-permute-done.12.r2 = bf16[32,1024]{1,0:T(8,128)(2,1)S(1)} collective-permute-done((bf16[32,1024]{1,0:T(8,128)(2,1)S(1)}, bf16[32,1024]{1,0:T(8,128)(2,1)S(1)}, u32[]{:S(2)}, u32[]{:S(2)}) %collective-permute-start.12) | collective-permute-done | bytes 65568 | tf_op jit(solution)/shard_map/ppermute | solution.py:305
  51.3 1.4 collective-permute-start.18
  52.8 2.1 %collective-permute-start.16 = (bf16[32,1024]{1,0:T(8,128)(2,1)S(1)}, bf16[32,1024]{1,0:T(8,128)(2,1)S(1)}, u32[]{:S(2)}, u32[]{:S(2)}) collective-permute-start(bf16[32,1024]{1,0:T(8,128)(2,1)S(1)} %get-tuple-element.61), channel_id=1, source_target_pairs={{0,48},{16,0},{32,16},{48,32},{1,49},{17,1},{33,17},{49,33},{2,50}... | collective-permute-start | bytes 196616 | tf_op jit(solution)/shard_map/ppermute | solution.py:305
  56.3 2.7 %collective-permute-done.15.r2 = bf16[32,1024]{1,0:T(8,128)(2,1)S(1)} collective-permute-done((bf16[32,1024]{1,0:T(8,128)(2,1)S(1)}, bf16[32,1024]{1,0:T(8,128)(2,1)S(1)}, u32[]{:S(2)}, u32[]{:S(2)}) %collective-permute-start.15) | collective-permute-done | bytes 65568 | tf_op jit(solution)/shard_map/ppermute | solution.py:305
  58.9 0.9 collective-permute-done.14.r1
  60.0 2.1 %collective-permute-start.21 = (bf16[32,1024]{1,0:T(8,128)(2,1)S(1)}, bf16[32,1024]{1,0:T(8,128)(2,1)S(1)}, u32[]{:S(2)}, u32[]{:S(2)}) collective-permute-start(bf16[32,1024]{1,0:T(8,128)(2,1)S(1)} %get-tuple-element.66), channel_id=1, source_target_pairs={{0,192},{64,0},{128,64},{192,128},{1,193},{65,1},{129,65},{193,129... | collective-permute-start | bytes 196616 | tf_op jit(solution)/shard_map/ppermute | solution.py:305
  62.2 1.0 collective-permute-start.20
  63.5 3.3 %collective-permute-done.20.r2 = bf16[32,1024]{1,0:T(8,128)(2,1)S(1)} collective-permute-done((bf16[32,1024]{1,0:T(8,128)(2,1)S(1)}, bf16[32,1024]{1,0:T(8,128)(2,1)S(1)}, u32[]{:S(2)}, u32[]{:S(2)}) %collective-permute-start.20) | collective-permute-done | bytes 65568 | tf_op jit(solution)/shard_map/ppermute | solution.py:305
  66.8 1.0 collective-permute-done.19.r1
  68.8 9.2 %collective-permute-start.22 = (bf16[4,128,1536]{2,1,0:T(8,128)(2,1)S(1)}, bf16[4,128,1536]{2,1,0:T(8,128)(2,1)}, u32[]{:S(2)}, u32[]{:S(2)}) collective-permute-start(bf16[4,128,1536]{2,1,0:T(8,128)(2,1)S(1)} %constant_dynamic-update-slice_fusion), channel_id=1, source_target_pairs={{0,1},{1,0},{2,3},{3,2},{4,5},{5,4},{6,7},{7,6},{8,9},{9,8},{10,11... | collective-permute-start | bytes 4718600 | tf_op jit(solution)/shard_map/ppermute | solution.py:437
  78.0 8.8 %finish.1 = (bf16[960,128]{1,0:T(8,128)(2,1)}, bf16[128,2880]{1,0:T(8,128)(2,1)S(1)}, bf16[8,360,128]{2,1,0:T(8,128)(2,1)S(1)}, f32[40,1024]{1,0:T(8,128)S(1)}) custom-call(s32[3]{0:T(128)S(1)} %pad_add_fusion.place, f32[160,3072]{1,0:T(8,128)S(1)} %get-tuple-element.45.zf, f32[3,136,1024]{2,1,0:T(8,128)S(1)} %get-tuple-element.46.mix, ...), custom_call_target="tpu_custom_call" | custom-call | flops 200000000 | bytes 10000000 | tf_op jit(solution)/shard_map/finish/pallas_call | solution.py:439
  86.8 0.9 copy-done.3
  87.7 3.6 %all-to-all-start = ((bf16[8,360,128]{2,1,0:T(8,128)(2,1)}), bf16[8,360,128]{2,1,0:T(8,128)(2,1)S(1)}, u32[]{:S(2)}, u32[]{:S(2)}) async-start(bf16[8,360,128]{2,1,0:T(8,128)(2,1)} %copy-done.3), calls=%async_computation | async-start | bytes 1474560 | tf_op jit(solution)/shard_map/all_to_all | solution.py:467
  91.3 11.7 %all-to-all-done.arrived = bf16[8,360,128]{2,1,0:T(8,128)(2,1)S(1)} async-done(((bf16[8,360,128]{2,1,0:T(8,128)(2,1)}), bf16[8,360,128]{2,1,0:T(8,128)(2,1)S(1)}, u32[]{:S(2)}, u32[]{:S(2)}) %all-to-all-start) | async-done | bytes 737312 | tf_op jit(solution)/shard_map/all_to_all | solution.py:467
  103.0 4.2 %weight_term.1 = bf16[4,360,384]{2,1,0:T(8,128)(2,1)} custom-call(s32[2]{0:T(128)S(1)} %pad_add_fusion.1.place, bf16[8,360,128]{2,1,0:T(8,128)(2,1)S(1)} %all-to-all-done.arrived, bf16[2,256,1536]{2,1,0:T(8,128)(2,1)S(1)} %bitcast.44, bf16[2,256,1536]{2,1,0:T(8,128)(2,1)} %bitcast.17.theirs), custom_call_target="tpu_custom_call" | custom-call | flops 1200000000 | bytes 6000000 | tf_op jit(solution)/shard_map/weight_term/pallas_call | solution.py:468
  107.2 3.5 %all-to-all-start.1 = ((bf16[4,360,384]{2,1,0:T(8,128)(2,1)}), bf16[4,360,384]{2,1,0:T(8,128)(2,1)S(1)}, u32[]{:S(2)}, u32[]{:S(2)}) async-start(bf16[4,360,384]{2,1,0:T(8,128)(2,1)} %weight_term.1), calls=%async_computation.1 | async-start | bytes 2211840 | tf_op jit(solution)/shard_map/all_to_all | solution.py:477
  111.6 1.3 collective-permute-start.23
  112.9 1.2 collective-permute-done.25
  114.1 2.4 %collective-permute-done.24 = bf16[40,1024]{1,0:T(8,128)(2,1)S(1)} collective-permute-done((bf16[40,1024]{1,0:T(8,128)(2,1)S(1)}, bf16[40,1024]{1,0:T(8,128)(2,1)S(1)}, u32[]{:S(2)}, u32[]{:S(2)}) %collective-permute-start.24) | collective-permute-done | bytes 81952 | tf_op jit(solution)/shard_map/ppermute | solution.py:305
  116.6 1.5 collective-permute-done.23
  118.1 2.5 %collective-permute-start.28 = (bf16[40,1024]{1,0:T(8,128)(2,1)S(1)}, bf16[40,1024]{1,0:T(8,128)(2,1)S(1)}, u32[]{:S(2)}, u32[]{:S(2)}) collective-permute-start(bf16[40,1024]{1,0:T(8,128)(2,1)S(1)} %add_convert_fusion.2), channel_id=1, source_target_pairs={{0,12},{4,0},{8,4},{12,8},{1,13},{5,1},{9,5},{13,9},{2,14},{6,2},{... | collective-permute-start | bytes 245768 | tf_op jit(solution)/shard_map/ppermute | solution.py:305
  121.3 1.6 collective-permute-done.28
  122.8 2.8 %collective-permute-done.27 = bf16[40,1024]{1,0:T(8,128)(2,1)S(1)} collective-permute-done((bf16[40,1024]{1,0:T(8,128)(2,1)S(1)}, bf16[40,1024]{1,0:T(8,128)(2,1)S(1)}, u32[]{:S(2)}, u32[]{:S(2)}) %collective-permute-start.27) | collective-permute-done | bytes 81952 | tf_op jit(solution)/shard_map/ppermute | solution.py:305
  126.3 1.9 %collective-permute-start.31 = (bf16[40,1024]{1,0:T(8,128)(2,1)S(1)}, bf16[40,1024]{1,0:T(8,128)(2,1)S(1)}, u32[]{:S(2)}, u32[]{:S(2)}) collective-permute-start(bf16[40,1024]{1,0:T(8,128)(2,1)S(1)} %add_convert_fusion.1), channel_id=1, source_target_pairs={{0,192},{64,0},{128,64},{192,128},{1,193},{65,1},{129,65},{193,129... | collective-permute-start | bytes 245768 | tf_op jit(solution)/shard_map/ppermute | solution.py:305
  129.9 3.1 %collective-permute-done.30 = bf16[40,1024]{1,0:T(8,128)(2,1)S(1)} collective-permute-done((bf16[40,1024]{1,0:T(8,128)(2,1)S(1)}, bf16[40,1024]{1,0:T(8,128)(2,1)S(1)}, u32[]{:S(2)}, u32[]{:S(2)}) %collective-permute-start.30) | collective-permute-done | bytes 81952 | tf_op jit(solution)/shard_map/ppermute | solution.py:305
  133.9 5.8 %collective-permute-start.34 = (bf16[40,1024]{1,0:T(8,128)(2,1)S(1)}, bf16[40,1024]{1,0:T(8,128)(2,1)S(1)}, u32[]{:S(2)}, u32[]{:S(2)}) collective-permute-start(bf16[40,1024]{1,0:T(8,128)(2,1)S(1)} %add_convert_fusion), channel_id=1, source_target_pairs={{0,3},{1,0},{2,1},{3,2},{4,7},{5,4},{6,5},{7,6},{8,11},{9,8},{10,9... | collective-permute-start | bytes 245768 | tf_op jit(solution)/shard_map/ppermute | solution.py:305
  139.8 5.3 %collective-permute-start.33 = (bf16[40,1024]{1,0:T(8,128)(2,1)S(1)}, bf16[40,1024]{1,0:T(8,128)(2,1)S(1)}, u32[]{:S(2)}, u32[]{:S(2)}) collective-permute-start(bf16[40,1024]{1,0:T(8,128)(2,1)S(1)} %add_convert_fusion), channel_id=1, source_target_pairs={{0,2},{1,3},{2,0},{3,1},{4,6},{5,7},{6,4},{7,5},{8,10},{9,11},{10,... | collective-permute-start | bytes 245768 | tf_op jit(solution)/shard_map/ppermute | solution.py:305
  145.0 2.1 %collective-permute-start.32 = (bf16[40,1024]{1,0:T(8,128)(2,1)S(1)}, bf16[40,1024]{1,0:T(8,128)(2,1)S(1)}, u32[]{:S(2)}, u32[]{:S(2)}) collective-permute-start(bf16[40,1024]{1,0:T(8,128)(2,1)S(1)} %add_convert_fusion), channel_id=1, source_target_pairs={{0,1},{1,2},{2,3},{3,0},{4,5},{5,6},{6,7},{7,4},{8,9},{9,10},{10,1... | collective-permute-start | bytes 245768 | tf_op jit(solution)/shard_map/ppermute | solution.py:305
  147.2 5.6 %fusion = bf16[1,128,1536]{2,1,0:T(8,128)(2,1)} fusion(bf16[128,2880]{1,0:T(8,128)(2,1)S(1)} %get-tuple-element.75, bf16[1536,2880]{0,1:T(8,128)(2,1)} %param.7), kind=kOutput, calls=%fused_computation.1 | convolution fusion | flops 1132658688 | bytes 9977856 | tf_op jit(solution)/shard_map/dot_general | solution.py:505
  152.8 1.0 split_rows.1
  153.9 5.8 %all-to-all-start.2 = ((bf16[32,24,180]{2,1,0:T(8,128)(2,1)}), bf16[32,24,180]{2,1,0:T(8,128)(2,1)S(1)}, u32[]{:S(2)}, u32[]{:S(2)}) async-start(bf16[32,24,180]{2,1,0:T(8,128)(2,1)} %split_rows.1), calls=%async_computation.2 | async-start | bytes 786432 | tf_op jit(solution)/shard_map/all_to_all | solution.py:487
  161.4 10.5 %all-to-all-done.2 = bf16[32,24,180]{2,1,0:T(8,128)(2,1)S(1)} async-done(((bf16[32,24,180]{2,1,0:T(8,128)(2,1)}), bf16[32,24,180]{2,1,0:T(8,128)(2,1)S(1)}, u32[]{:S(2)}, u32[]{:S(2)}) %all-to-all-start.2) | async-done | bytes 276512 | tf_op jit(solution)/shard_map/all_to_all | solution.py:487
  (89 shorter events, 18.0 us)
Async XLA Ops:
  0.6 31.3 %copy-start.1 = (bf16[1,128,1536]{2,1,0:T(8,128)(2,1)S(1)}, bf16[1,128,1536]{2,1,0:T(8,128)(2,1)}, u32[]{:S(2)}) copy-start(bf16[1,128,1536]{2,1,0:T(8,128)(2,1)} %param.6) | copy-start | bytes 1179652
  0.6 31.2 %copy-start.2 = (bf16[1,128,960]{1,2,0:T(8,128)(2,1)S(1)}, bf16[1,128,960]{1,2,0:T(8,128)(2,1)}, u32[]{:S(2)}) copy-start(bf16[1,128,960]{1,2,0:T(8,128)(2,1)} %param.11) | copy-start | bytes 737284
  1.5 0.6 copy-start.6
  2.2 0.7 copy-start.4
  2.9 0.7 copy-start.5
  3.7 10.1 %collective-permute-start.4 = (f32[32,15]{1,0:T(8,128)S(1)}, f32[32,15]{1,0:T(8,128)S(1)}, u32[]{:S(2)}, u32[]{:S(2)}) collective-permute-start(f32[32,15]{1,0:T(8,128)S(1)} %first_params.1.r0), channel_id=1, source_target_pairs={{0,12},{4,0},{8,4},{12,8},{1,13},{5,1},{9,5},{13,9},{2,14},{6,2},{... | collective-permute-start | bytes 5768 | tf_op jit(solution)/shard_map/ppermute | solution.py:305
  7.3 6.4 %collective-permute-start.3 = (f32[32,15]{1,0:T(8,128)S(1)}, f32[32,15]{1,0:T(8,128)S(1)}, u32[]{:S(2)}, u32[]{:S(2)}) collective-permute-start(f32[32,15]{1,0:T(8,128)S(1)} %first_params.1.r0), channel_id=1, source_target_pairs={{0,8},{4,12},{8,0},{12,4},{1,9},{5,13},{9,1},{13,5},{2,10},{6,14},... | collective-permute-start | bytes 5768 | tf_op jit(solution)/shard_map/ppermute | solution.py:305
  7.7 6.1 %collective-permute-start.2 = (f32[32,15]{1,0:T(8,128)S(1)}, f32[32,15]{1,0:T(8,128)S(1)}, u32[]{:S(2)}, u32[]{:S(2)}) collective-permute-start(f32[32,15]{1,0:T(8,128)S(1)} %first_params.1.r0), channel_id=1, source_target_pairs={{0,4},{4,8},{8,12},{12,0},{1,5},{5,9},{9,13},{13,1},{2,6},{6,10},{... | collective-permute-start | bytes 5768 | tf_op jit(solution)/shard_map/ppermute | solution.py:305
  9.2 22.7 %collective-permute-start = (bf16[16,1536]{1,0:T(8,128)(2,1)S(1)}, bf16[16,1536]{1,0:T(8,128)(2,1)S(1)}, u32[]{:S(2)}, u32[]{:S(2)}) collective-permute-start(bf16[16,1536]{1,0:T(8,128)(2,1)S(1)} %get-tuple-element.111), channel_id=1, source_target_pairs={{0,4},{4,8},{8,12},{12,16},{16,20},{20,24},{24,28},{28,32},{32,36}... | collective-permute-start | bytes 147464 | tf_op jit(solution)/shard_map/ppermute | solution.py:356
  13.9 8.2 %collective-permute-start.7 = (f32[32,60]{1,0:T(8,128)S(1)}, f32[32,60]{1,0:T(8,128)S(1)}, u32[]{:S(2)}, u32[]{:S(2)}) collective-permute-start(f32[32,60]{1,0:T(8,128)S(1)} %join_params.2.r0), channel_id=1, source_target_pairs={{0,48},{16,0},{32,16},{48,32},{1,49},{17,1},{33,17},{49,33},{2,50}... | collective-permute-start | bytes 23048 | tf_op jit(solution)/shard_map/ppermute | solution.py:305
  18.3 32.9 %collective-permute-start.17 = (bf16[128,1536]{1,0:T(8,128)(2,1)}, bf16[128,1536]{1,0:T(8,128)(2,1)S(1)}, u32[]{:S(2)}, u32[]{:S(2)}) collective-permute-start(bf16[128,1536]{1,0:T(8,128)(2,1)} %bitcast.45), channel_id=1, source_target_pairs={{0,4},{4,0},{8,12},{12,8},{1,5},{5,1},{9,13},{13,9},{2,6},{6,2},{1... | collective-permute-start | bytes 1179656 | tf_op jit(solution)/shard_map/ppermute | solution.py:412
  18.3 12.7 %collective-permute-start.1 = (bf16[16,2496]{1,0:T(8,128)(2,1)S(1)}, bf16[16,2496]{1,0:T(8,128)(2,1)S(1)}, u32[]{:S(2)}, u32[]{:S(2)}) collective-permute-start(bf16[16,2496]{1,0:T(8,128)(2,1)S(1)} %pad_maximum_fusion.1), channel_id=1, source_target_pairs={{4,0},{8,4},{12,8},{16,12},{20,16},{24,20},{28,24},{32,28},{36,32}... | collective-permute-start | bytes 239624 | tf_op jit(solution)/shard_map/ppermute | solution.py:358
  20.6 3.9 %collective-permute-start.6 = (f32[32,60]{1,0:T(8,128)S(1)}, f32[32,60]{1,0:T(8,128)S(1)}, u32[]{:S(2)}, u32[]{:S(2)}) collective-permute-start(f32[32,60]{1,0:T(8,128)S(1)} %join_params.2.r0), channel_id=1, source_target_pairs={{0,32},{16,48},{32,0},{48,16},{1,33},{17,49},{33,1},{49,17},{2,34}... | collective-permute-start | bytes 23048 | tf_op jit(solution)/shard_map/ppermute | solution.py:305
  22.1 5.8 %collective-permute-start.5 = (f32[32,60]{1,0:T(8,128)S(1)}, f32[32,60]{1,0:T(8,128)S(1)}, u32[]{:S(2)}, u32[]{:S(2)}) collective-permute-start(f32[32,60]{1,0:T(8,128)S(1)} %join_params.2.r0), channel_id=1, source_target_pairs={{0,16},{16,32},{32,48},{48,0},{1,17},{17,33},{33,49},{49,1},{2,18}... | collective-permute-start | bytes 23048 | tf_op jit(solution)/shard_map/ppermute | solution.py:305
  27.9 15.2 %collective-permute-start.10 = (f32[32,240]{1,0:T(8,128)S(1)}, f32[32,240]{1,0:T(8,128)S(1)}, u32[]{:S(2)}, u32[]{:S(2)}) collective-permute-start(f32[32,240]{1,0:T(8,128)S(1)} %join_params.3.r0), channel_id=1, source_target_pairs={{0,192},{64,0},{128,64},{192,128},{1,193},{65,1},{129,65},{193,129... | collective-permute-start | bytes 92168 | tf_op jit(solution)/shard_map/ppermute | solution.py:305
  30.8 12.4 %collective-permute-start.9 = (f32[32,240]{1,0:T(8,128)S(1)}, f32[32,240]{1,0:T(8,128)S(1)}, u32[]{:S(2)}, u32[]{:S(2)}) collective-permute-start(f32[32,240]{1,0:T(8,128)S(1)} %join_params.3.r0), channel_id=1, source_target_pairs={{0,128},{64,192},{128,0},{192,64},{1,129},{65,193},{129,1},{193,65... | collective-permute-start | bytes 92168 | tf_op jit(solution)/shard_map/ppermute | solution.py:305
  31.1 12.1 %collective-permute-start.8 = (f32[32,240]{1,0:T(8,128)S(1)}, f32[32,240]{1,0:T(8,128)S(1)}, u32[]{:S(2)}, u32[]{:S(2)}) collective-permute-start(f32[32,240]{1,0:T(8,128)S(1)} %join_params.3.r0), channel_id=1, source_target_pairs={{0,64},{64,128},{128,192},{192,0},{1,65},{65,129},{129,193},{193,1... | collective-permute-start | bytes 92168 | tf_op jit(solution)/shard_map/ppermute | solution.py:305
  31.9 3.5 %copy-start = (bf16[1536,2880]{0,1:T(8,128)(2,1)S(1)}, bf16[1536,2880]{0,1:T(8,128)(2,1)}, u32[]{:S(2)}) copy-start(bf16[1536,2880]{0,1:T(8,128)(2,1)} %param.7) | copy-start | bytes 26542084
  45.2 3.2 %collective-permute-start.13 = (bf16[32,1024]{1,0:T(8,128)(2,1)S(1)}, bf16[32,1024]{1,0:T(8,128)(2,1)S(1)}, u32[]{:S(2)}, u32[]{:S(2)}) collective-permute-start(bf16[32,1024]{1,0:T(8,128)(2,1)S(1)} %get-tuple-element.57), channel_id=1, source_target_pairs={{0,12},{4,0},{8,4},{12,8},{1,13},{5,1},{9,5},{13,9},{2,14},{6,2},{... | collective-permute-start | bytes 196616 | tf_op jit(solution)/shard_map/ppermute | solution.py:305
  45.7 4.6 %collective-permute-start.12 = (bf16[32,1024]{1,0:T(8,128)(2,1)S(1)}, bf16[32,1024]{1,0:T(8,128)(2,1)S(1)}, u32[]{:S(2)}, u32[]{:S(2)}) collective-permute-start(bf16[32,1024]{1,0:T(8,128)(2,1)S(1)} %get-tuple-element.57), channel_id=1, source_target_pairs={{0,8},{4,12},{8,0},{12,4},{1,9},{5,13},{9,1},{13,5},{2,10},{6,14},... | collective-permute-start | bytes 196616 | tf_op jit(solution)/shard_map/ppermute | solution.py:305
  46.5 4.5 %collective-permute-start.11 = (bf16[32,1024]{1,0:T(8,128)(2,1)S(1)}, bf16[32,1024]{1,0:T(8,128)(2,1)S(1)}, u32[]{:S(2)}, u32[]{:S(2)}) collective-permute-start(bf16[32,1024]{1,0:T(8,128)(2,1)S(1)} %get-tuple-element.57), channel_id=1, source_target_pairs={{0,4},{4,8},{8,12},{12,0},{1,5},{5,9},{9,13},{13,1},{2,6},{6,10},{... | collective-permute-start | bytes 196616 | tf_op jit(solution)/shard_map/ppermute | solution.py:305
  51.3 17.3 %collective-permute-start.18 = (bf16[2,128,1536]{2,1,0:T(8,128)(2,1)S(1)}, bf16[2,128,1536]{2,1,0:T(8,128)(2,1)S(1)}, u32[]{:S(2)}, u32[]{:S(2)}) collective-permute-start(bf16[2,128,1536]{2,1,0:T(8,128)(2,1)S(1)} %pad_maximum_fusion), channel_id=1, source_target_pairs={{0,12},{4,8},{8,4},{12,0},{1,13},{5,9},{9,5},{13,1},{2,14},{6,10},... | collective-permute-start | bytes 2359304 | tf_op jit(solution)/shard_map/ppermute | solution.py:434
  52.8 3.5 %collective-permute-start.16 = (bf16[32,1024]{1,0:T(8,128)(2,1)S(1)}, bf16[32,1024]{1,0:T(8,128)(2,1)S(1)}, u32[]{:S(2)}, u32[]{:S(2)}) collective-permute-start(bf16[32,1024]{1,0:T(8,128)(2,1)S(1)} %get-tuple-element.61), channel_id=1, source_target_pairs={{0,48},{16,0},{32,16},{48,32},{1,49},{17,1},{33,17},{49,33},{2,50}... | collective-permute-start | bytes 196616 | tf_op jit(solution)/shard_map/ppermute | solution.py:305
  54.9 4.0 %collective-permute-start.15 = (bf16[32,1024]{1,0:T(8,128)(2,1)S(1)}, bf16[32,1024]{1,0:T(8,128)(2,1)S(1)}, u32[]{:S(2)}, u32[]{:S(2)}) collective-permute-start(bf16[32,1024]{1,0:T(8,128)(2,1)S(1)} %get-tuple-element.61), channel_id=1, source_target_pairs={{0,32},{16,48},{32,0},{48,16},{1,33},{17,49},{33,1},{49,17},{2,34}... | collective-permute-start | bytes 196616 | tf_op jit(solution)/shard_map/ppermute | solution.py:305
  54.9 4.9 %collective-permute-start.14 = (bf16[32,1024]{1,0:T(8,128)(2,1)S(1)}, bf16[32,1024]{1,0:T(8,128)(2,1)S(1)}, u32[]{:S(2)}, u32[]{:S(2)}) collective-permute-start(bf16[32,1024]{1,0:T(8,128)(2,1)S(1)} %get-tuple-element.61), channel_id=1, source_target_pairs={{0,16},{16,32},{32,48},{48,0},{1,17},{17,33},{33,49},{49,1},{2,18}... | collective-permute-start | bytes 196616 | tf_op jit(solution)/shard_map/ppermute | solution.py:305
  60.0 3.5 %collective-permute-start.21 = (bf16[32,1024]{1,0:T(8,128)(2,1)S(1)}, bf16[32,1024]{1,0:T(8,128)(2,1)S(1)}, u32[]{:S(2)}, u32[]{:S(2)}) collective-permute-start(bf16[32,1024]{1,0:T(8,128)(2,1)S(1)} %get-tuple-element.66), channel_id=1, source_target_pairs={{0,192},{64,0},{128,64},{192,128},{1,193},{65,1},{129,65},{193,129... | collective-permute-start | bytes 196616 | tf_op jit(solution)/shard_map/ppermute | solution.py:305
  62.2 4.6 %collective-permute-start.20 = (bf16[32,1024]{1,0:T(8,128)(2,1)S(1)}, bf16[32,1024]{1,0:T(8,128)(2,1)S(1)}, u32[]{:S(2)}, u32[]{:S(2)}) collective-permute-start(bf16[32,1024]{1,0:T(8,128)(2,1)S(1)} %get-tuple-element.66), channel_id=1, source_target_pairs={{0,128},{64,192},{128,0},{192,64},{1,129},{65,193},{129,1},{193,65... | collective-permute-start | bytes 196616 | tf_op jit(solution)/shard_map/ppermute | solution.py:305
  63.2 4.6 %collective-permute-start.19 = (bf16[32,1024]{1,0:T(8,128)(2,1)S(1)}, bf16[32,1024]{1,0:T(8,128)(2,1)S(1)}, u32[]{:S(2)}, u32[]{:S(2)}) collective-permute-start(bf16[32,1024]{1,0:T(8,128)(2,1)S(1)} %get-tuple-element.66), channel_id=1, source_target_pairs={{0,64},{64,128},{128,192},{192,0},{1,65},{65,129},{129,193},{193,1... | collective-permute-start | bytes 196616 | tf_op jit(solution)/shard_map/ppermute | solution.py:305
  68.8 34.3 %collective-permute-start.22 = (bf16[4,128,1536]{2,1,0:T(8,128)(2,1)S(1)}, bf16[4,128,1536]{2,1,0:T(8,128)(2,1)}, u32[]{:S(2)}, u32[]{:S(2)}) collective-permute-start(bf16[4,128,1536]{2,1,0:T(8,128)(2,1)S(1)} %constant_dynamic-update-slice_fusion), channel_id=1, source_target_pairs={{0,1},{1,0},{2,3},{3,2},{4,5},{5,4},{6,7},{7,6},{8,9},{9,8},{10,11... | collective-permute-start | bytes 4718600 | tf_op jit(solution)/shard_map/ppermute | solution.py:437
  86.8 0.9 copy-start.3
  87.7 15.3 %all-to-all-start = ((bf16[8,360,128]{2,1,0:T(8,128)(2,1)}), bf16[8,360,128]{2,1,0:T(8,128)(2,1)S(1)}, u32[]{:S(2)}, u32[]{:S(2)}) async-start(bf16[8,360,128]{2,1,0:T(8,128)(2,1)} %copy-done.3), calls=%async_computation | async-start | bytes 1474560 | tf_op jit(solution)/shard_map/all_to_all | solution.py:467
  107.2 19.1 %all-to-all-start.1 = ((bf16[4,360,384]{2,1,0:T(8,128)(2,1)}), bf16[4,360,384]{2,1,0:T(8,128)(2,1)S(1)}, u32[]{:S(2)}, u32[]{:S(2)}) async-start(bf16[4,360,384]{2,1,0:T(8,128)(2,1)} %weight_term.1), calls=%async_computation.1 | async-start | bytes 2211840 | tf_op jit(solution)/shard_map/all_to_all | solution.py:477
  110.7 3.4 %collective-permute-start.25 = (bf16[40,1024]{1,0:T(8,128)(2,1)S(1)}, bf16[40,1024]{1,0:T(8,128)(2,1)S(1)}, u32[]{:S(2)}, u32[]{:S(2)}) collective-permute-start(bf16[40,1024]{1,0:T(8,128)(2,1)S(1)} %convert_element_type.86), channel_id=1, source_target_pairs={{0,48},{16,0},{32,16},{48,32},{1,49},{17,1},{33,17},{49,33},{2,50}... | collective-permute-start | bytes 245768 | tf_op jit(solution)/shard_map/ppermute | solution.py:305
  111.6 5.0 %collective-permute-start.24 = (bf16[40,1024]{1,0:T(8,128)(2,1)S(1)}, bf16[40,1024]{1,0:T(8,128)(2,1)S(1)}, u32[]{:S(2)}, u32[]{:S(2)}) collective-permute-start(bf16[40,1024]{1,0:T(8,128)(2,1)S(1)} %convert_element_type.86), channel_id=1, source_target_pairs={{0,32},{16,48},{32,0},{48,16},{1,33},{17,49},{33,1},{49,17},{2,34}... | collective-permute-start | bytes 245768 | tf_op jit(solution)/shard_map/ppermute | solution.py:305
  111.6 6.5 %collective-permute-start.23 = (bf16[40,1024]{1,0:T(8,128)(2,1)S(1)}, bf16[40,1024]{1,0:T(8,128)(2,1)S(1)}, u32[]{:S(2)}, u32[]{:S(2)}) collective-permute-start(bf16[40,1024]{1,0:T(8,128)(2,1)S(1)} %convert_element_type.86), channel_id=1, source_target_pairs={{0,16},{16,32},{32,48},{48,0},{1,17},{17,33},{33,49},{49,1},{2,18}... | collective-permute-start | bytes 245768 | tf_op jit(solution)/shard_map/ppermute | solution.py:305
  118.1 4.8 %collective-permute-start.28 = (bf16[40,1024]{1,0:T(8,128)(2,1)S(1)}, bf16[40,1024]{1,0:T(8,128)(2,1)S(1)}, u32[]{:S(2)}, u32[]{:S(2)}) collective-permute-start(bf16[40,1024]{1,0:T(8,128)(2,1)S(1)} %add_convert_fusion.2), channel_id=1, source_target_pairs={{0,12},{4,0},{8,4},{12,8},{1,13},{5,1},{9,5},{13,9},{2,14},{6,2},{... | collective-permute-start | bytes 245768 | tf_op jit(solution)/shard_map/ppermute | solution.py:305
  120.6 5.1 %collective-permute-start.27 = (bf16[40,1024]{1,0:T(8,128)(2,1)S(1)}, bf16[40,1024]{1,0:T(8,128)(2,1)S(1)}, u32[]{:S(2)}, u32[]{:S(2)}) collective-permute-start(bf16[40,1024]{1,0:T(8,128)(2,1)S(1)} %add_convert_fusion.2), channel_id=1, source_target_pairs={{0,8},{4,12},{8,0},{12,4},{1,9},{5,13},{9,1},{13,5},{2,10},{6,14},... | collective-permute-start | bytes 245768 | tf_op jit(solution)/shard_map/ppermute | solution.py:305
  120.6 5.7 %collective-permute-start.26 = (bf16[40,1024]{1,0:T(8,128)(2,1)S(1)}, bf16[40,1024]{1,0:T(8,128)(2,1)S(1)}, u32[]{:S(2)}, u32[]{:S(2)}) collective-permute-start(bf16[40,1024]{1,0:T(8,128)(2,1)S(1)} %add_convert_fusion.2), channel_id=1, source_target_pairs={{0,4},{4,8},{8,12},{12,0},{1,5},{5,9},{9,13},{13,1},{2,6},{6,10},{... | collective-permute-start | bytes 245768 | tf_op jit(solution)/shard_map/ppermute | solution.py:305
  126.3 3.6 %collective-permute-start.31 = (bf16[40,1024]{1,0:T(8,128)(2,1)S(1)}, bf16[40,1024]{1,0:T(8,128)(2,1)S(1)}, u32[]{:S(2)}, u32[]{:S(2)}) collective-permute-start(bf16[40,1024]{1,0:T(8,128)(2,1)S(1)} %add_convert_fusion.1), channel_id=1, source_target_pairs={{0,192},{64,0},{128,64},{192,128},{1,193},{65,1},{129,65},{193,129... | collective-permute-start | bytes 245768 | tf_op jit(solution)/shard_map/ppermute | solution.py:305
  128.2 4.9 %collective-permute-start.30 = (bf16[40,1024]{1,0:T(8,128)(2,1)S(1)}, bf16[40,1024]{1,0:T(8,128)(2,1)S(1)}, u32[]{:S(2)}, u32[]{:S(2)}) collective-permute-start(bf16[40,1024]{1,0:T(8,128)(2,1)S(1)} %add_convert_fusion.1), channel_id=1, source_target_pairs={{0,128},{64,192},{128,0},{192,64},{1,129},{65,193},{129,1},{193,65... | collective-permute-start | bytes 245768 | tf_op jit(solution)/shard_map/ppermute | solution.py:305
  128.8 5.0 %collective-permute-start.29 = (bf16[40,1024]{1,0:T(8,128)(2,1)S(1)}, bf16[40,1024]{1,0:T(8,128)(2,1)S(1)}, u32[]{:S(2)}, u32[]{:S(2)}) collective-permute-start(bf16[40,1024]{1,0:T(8,128)(2,1)S(1)} %add_convert_fusion.1), channel_id=1, source_target_pairs={{0,64},{64,128},{128,192},{192,0},{1,65},{65,129},{129,193},{193,1... | collective-permute-start | bytes 245768 | tf_op jit(solution)/shard_map/ppermute | solution.py:305
  133.9 25.7 %collective-permute-start.34 = (bf16[40,1024]{1,0:T(8,128)(2,1)S(1)}, bf16[40,1024]{1,0:T(8,128)(2,1)S(1)}, u32[]{:S(2)}, u32[]{:S(2)}) collective-permute-start(bf16[40,1024]{1,0:T(8,128)(2,1)S(1)} %add_convert_fusion), channel_id=1, source_target_pairs={{0,3},{1,0},{2,1},{3,2},{4,7},{5,4},{6,5},{7,6},{8,11},{9,8},{10,9... | collective-permute-start | bytes 245768 | tf_op jit(solution)/shard_map/ppermute | solution.py:305
  139.8 19.9 %collective-permute-start.33 = (bf16[40,1024]{1,0:T(8,128)(2,1)S(1)}, bf16[40,1024]{1,0:T(8,128)(2,1)S(1)}, u32[]{:S(2)}, u32[]{:S(2)}) collective-permute-start(bf16[40,1024]{1,0:T(8,128)(2,1)S(1)} %add_convert_fusion), channel_id=1, source_target_pairs={{0,2},{1,3},{2,0},{3,1},{4,6},{5,7},{6,4},{7,5},{8,10},{9,11},{10,... | collective-permute-start | bytes 245768 | tf_op jit(solution)/shard_map/ppermute | solution.py:305
  145.0 14.6 %collective-permute-start.32 = (bf16[40,1024]{1,0:T(8,128)(2,1)S(1)}, bf16[40,1024]{1,0:T(8,128)(2,1)S(1)}, u32[]{:S(2)}, u32[]{:S(2)}) collective-permute-start(bf16[40,1024]{1,0:T(8,128)(2,1)S(1)} %add_convert_fusion), channel_id=1, source_target_pairs={{0,1},{1,2},{2,3},{3,0},{4,5},{5,6},{6,7},{7,4},{8,9},{9,10},{10,1... | collective-permute-start | bytes 245768 | tf_op jit(solution)/shard_map/ppermute | solution.py:305
  152.8 6.9 %copy-start.7 = (f32[15,16]{0,1:T(8,128)S(1)}, f32[15,16]{0,1:T(8,128)}, u32[]{:S(2)}) copy-start(f32[15,16]{0,1:T(8,128)} %copy-done.6) | copy-start | bytes 2884
  153.9 18.0 %all-to-all-start.2 = ((bf16[32,24,180]{2,1,0:T(8,128)(2,1)}), bf16[32,24,180]{2,1,0:T(8,128)(2,1)S(1)}, u32[]{:S(2)}, u32[]{:S(2)}) async-start(bf16[32,24,180]{2,1,0:T(8,128)(2,1)} %split_rows.1), calls=%async_computation.2 | async-start | bytes 786432 | tf_op jit(solution)/shard_map/all_to_all | solution.py:487

commit v3 on v2

--- a/solution.py
+++ b/solution.py
@@ -21,28 +21,33 @@
     return a.astype(BF16).astype(F32)
 
 
-def project(tp, tk, tn, wt, taps, cott, cotnt, zf, mix, cots, us, dls, acc, turn):
-    step = pl.program_id(0)
-    rows = jnp.concatenate([tp[...], tk[...], tn[...]], axis=0)
-    part = lax.dot_general(rows, wt[...], NT, preferred_element_type=F32)
-
-    @pl.when(step == 0)
-    def _():
-        acc[...] = part
-
-    @pl.when(step > 0)
-    def _():
-        acc[...] += part
-
-    @pl.when(step == pl.num_programs(0) - 1)
-    def _():
-        width, own = cott.shape
+def project(
+    tp, tk, tn, wt, taps, cott, cotnt, zf, mix, cots, us, dls, acc, turn, wbuf, sems,
+):
+    steps, _, kblk = wbuf.shape
+    copies = [
+        pltpu.make_async_copy(wt.at[:, pl.ds(k * kblk, kblk)], wbuf.at[k], sems.at[k])
+        for k in range(steps)
+    ]
+    for copy in copies:
+        copy.start()
+    width, own = cott.shape
+    turn[...] = jnp.zeros(turn.shape, F32)
+    turn[0:width, 0:own] = cott[...].astype(F32)
+    turn[0:width, own : own + HALO] = cotnt[0:width, :].astype(F32)
+    for k in range(steps):
+        cols = slice(k * kblk, (k + 1) * kblk)
+        rows = jnp.concatenate([tp[:, cols], tk[:, cols], tn[:, cols]], axis=0)
+        copies[k].wait()
+        part = lax.dot_general(rows, wbuf[k], NT, preferred_element_type=F32)
+        if k == 0:
+            acc[...] = part
+        else:
+            acc[...] += part
+    if True:
         for g in range(3):
             zf[:, g * PADC : g * PADC + width] = rounded(acc[:, g * width : (g + 1) * width])
             zf[:, g * PADC + width : (g + 1) * PADC] = jnp.zeros((zf.shape[0], PADC - width), F32)
-        turn[...] = jnp.zeros(turn.shape, F32)
-        turn[0:width, 0:own] = cott[...].astype(F32)
-        turn[0:width, own : own + HALO] = cotnt[...].astype(F32)
 
         def tile(ct, carry):
             lane = pl.multiple_of(ct * 128, 128)
@@ -66,32 +71,54 @@
         lax.fori_loop(0, PADC // 128, tile, 0)
 
 
-def first_params(rates, residues, amp, out, held):
+def prepare(feats, cott, rates, residues, amp, conv, head, tail, block, taps, held, turn):
     count = rates.shape[0]
+    width, own = cott.shape
+    depth = feats.shape[1]
+    head[:, 0:depth] = feats[0:HALO, :]
+    turn[...] = jnp.zeros(turn.shape, F32)
+    turn[0:width, :] = cott[...].astype(F32)
+    for c in range(PADC // 128):
+        part = turn[c * 128 : (c + 1) * 128, :].T[0:HALO]
+        head[:, depth + c * 128 : depth + (c + 1) * 128] = part.astype(BF16)
+    tail[...] = feats[own - HALO :, :]
     held[...] = jnp.zeros(held.shape, F32)
-    held[0:count, 0:MODES] = rates[...]
-    held[0:count, MODES : 2 * MODES] = residues[...] * amp[...]
-    out[...] = held[...].T[0 : 2 * MODES, 0:count]
-
-
-def placed(place, refs, held, goal):
-    me = place[0]
-    wide = refs[0].shape[1]
-    total = None
-    for d, ref in enumerate(refs):
-        held[...] = jnp.zeros(held.shape, F32)
-        held[:, 0:wide] = ref[...]
-        part = pltpu.roll(held[...], lax.rem(me + (4 - d), 4) * wide, 1)
-        total = part if total is None else total + part
-    return total[:, 0:goal]
-
-
-def join_params(place, r0, r1, r2, r3, out, held):
-    out[...] = placed(place, (r0, r1, r2, r3), held, out.shape[1])
-
-
-def end_states(place, r0, r1, r2, r3, us, dls, rates, gains, es, ends, endb, ut, dt, held):
-    joined = placed(place, (r0, r1, r2, r3), held, PADC)
+    for j in range(count):
+        row, lane = j // 4, (j % 4) * 2 * MODES
+        held[row : row + 1, lane : lane + MODES] = rates[j : j + 1, :]
+        held[row : row + 1, lane + MODES : lane + 2 * MODES] = residues[j : j + 1, :] * amp[j : j + 1, :]
+    block[...] = jnp.broadcast_to(held[...][None], block.shape)
+    taps[...] = jnp.zeros(taps.shape, F32)
+    for g in range(3):
+        taps[0:7, g * PADC : g * PADC + width] = conv[:, g * width : (g + 1) * width]
+
+
+def joined_params(blocks, order, left):
+    row = lax.broadcasted_iota(jnp.int32, (PADC, PADC), 0)
+    col = lax.broadcasted_iota(jnp.int32, (PADC, PADC), 1)
+    goal = 15 * lax.bitwise_and(row, 63) + lax.shift_right_logical(row, 6)
+    order[...] = jnp.where((goal == col) & (row < 960), 1.0, 0.0).astype(BF16)
+    left[...] = jnp.zeros(left.shape, F32)
+    count = blocks.shape[0]
+    for c in range(4):
+        flipped = blocks[:, c, :].T
+        for p in range(4):
+            j = 4 * c + p
+            if j < 15:
+                left[:, j * count : (j + 1) * count] = flipped[p * 2 * MODES : (p + 1) * 2 * MODES, :]
+    rest = left[...]
+    parts = []
+    for _ in range(3):
+        part = rest.astype(BF16)
+        parts.append(part)
+        rest = rest - part.astype(F32)
+    out = jnp.dot(jnp.concatenate(parts, axis=0), order[...], preferred_element_type=F32)
+    size = 2 * MODES
+    return out[0:size] + out[size : 2 * size] + out[2 * size : 3 * size]
+
+
+def end_states(blocks, us, dls, rates, gains, es, ends, endb, ut, dt, left, order):
+    joined = joined_params(blocks, order, left)
     rates[...] = joined[0:MODES]
     gains[...] = joined[MODES : 2 * MODES]
     sub = lax.broadcasted_iota(jnp.int32, (8, 128), 0)
@@ -324,72 +351,51 @@
     scale = 1.0 / math.sqrt(4 * count * own)
     smem = pl.BlockSpec(memory_space=pltpu.SMEM)
     vm = pl.BlockSpec(memory_space=pltpu.VMEM)
-    each = width // count
     amp_mine = jnp.sqrt(-jnp.expm1(-2.0 * rates))
-    held = pl.pallas_call(
-        first_params,
-        in_specs=[vm] * 3,
-        out_specs=vm,
-        out_shape=jax.ShapeDtypeStruct((2 * MODES, each), F32),
-        scratch_shapes=[pltpu.VMEM((128, 128), F32)],
-        compiler_params=params(4),
-        name="first_params",
-    )(rates, residues, amp_mine)
-    early = None
-    for ax, me in (("y", yi), ("zl", zi)):
-        blocks = [held] + [ring(held, ax, d) for d in (1, 2, 3)]
-        each = 4 * each
-        held = pl.pallas_call(
-            join_params,
-            in_specs=[smem] + [vm] * 4,
-            out_specs=vm,
-            out_shape=jax.ShapeDtypeStruct((2 * MODES, each), F32),
-            scratch_shapes=[pltpu.VMEM((2 * MODES, 256), F32)],
-            compiler_params=params(4),
-            name="join_params",
-        )(me.reshape(1), *blocks)
-        if early is None:
-            early = held
-    blocks = [held] + [ring(held, "x", d) for d in (1, 2, 3)]
-    taps = jnp.pad(conv_taps.reshape(7, 3, width), ((0, 1), (0, 0), (0, PADC - width)))
-    taps = taps.reshape(8, 3 * PADC)
-    tprev = lax.ppermute(feats[own - HALO :], ctx, [(i, i + 1) for i in range(count - 1)])
-    firsts = jnp.concatenate([feats[:HALO], cot[:HALO]], axis=1)
-    nexts = lax.ppermute(firsts, ctx, [(i, i - 1) for i in range(1, count)])
+    head, tail, block, taps = pl.pallas_call(
+        prepare,
+        in_specs=[vm] * 6,
+        out_specs=[vm] * 4,
+        out_shape=[
+            jax.ShapeDtypeStruct((HALO, depth + PADC), BF16),
+            jax.ShapeDtypeStruct((HALO, depth), BF16),
+            jax.ShapeDtypeStruct((count, 8, 128), F32),
+            jax.ShapeDtypeStruct((8, 3 * PADC), F32),
+        ],
+        scratch_shapes=[pltpu.VMEM((8, 128), F32), pltpu.VMEM((PADC, own), F32)],
+        compiler_params=params(8),
+        name="prepare",
+    )(feats, cot.T, rates, residues, amp_mine, conv_taps)
+    blocks = lax.all_to_all(block, ctx, split_axis=0, concat_axis=0, tiled=True)
+    tprev = lax.ppermute(tail, ctx, [(i, i + 1) for i in range(count - 1)])
+    nexts = lax.ppermute(head, ctx, [(i, i - 1) for i in range(1, count)])
     tnext = nexts[:, :depth]
     cnext = nexts[:, depth:].T
 
     kblk = 256
-
-    def whole(shape):
-        return pl.BlockSpec(shape, lambda k: (0,) * len(shape))
 
     ext_rows = own + 2 * HALO
     shapes = [(ext_rows, 3 * PADC), (3, EXT, PADC), (EXT, PADC), (EXT, PADC), (EXT, PADC)]
     zf, mix, cots, us, dls = pl.pallas_call(
         project,
-        grid=(depth // kblk,),
-        in_specs=[
-            pl.BlockSpec((HALO, kblk), lambda k: (0, k)),
-            pl.BlockSpec((own, kblk), lambda k: (0, k)),
-            pl.BlockSpec((HALO, kblk), lambda k: (0, k)),
-            pl.BlockSpec((chans, kblk), lambda k: (0, k)),
-            whole((8, 3 * PADC)),
-            whole((width, own)),
-            whole((width, HALO)),
+        in_specs=[vm] * 3 + [pl.BlockSpec(memory_space=pl.ANY)] + [vm] * 3,
+        out_specs=[vm] * 5,
+        out_shape=[jax.ShapeDtypeStruct(s, F32) for s in shapes],
+        scratch_shapes=[
+            pltpu.VMEM((ext_rows, chans), F32),
+            pltpu.VMEM((PADC, 256), F32),
+            pltpu.VMEM((depth // kblk, chans, kblk), BF16),
+            pltpu.SemaphoreType.DMA((depth // kblk,)),
         ],
-        out_specs=[whole(s) for s in shapes],
-        out_shape=[jax.ShapeDtypeStruct(s, F32) for s in shapes],
-        scratch_shapes=[pltpu.VMEM((ext_rows, chans), F32), pltpu.VMEM((PADC, 256), F32)],
-        compiler_params=params(24),
+        compiler_params=params(46),
         cost_estimate=pl.CostEstimate(flops=1500000000, bytes_accessed=14000000, transcendentals=0),
         name="project",
     )(tprev, feats, tnext, w_in.T, taps, cot.T, cnext)
 
-    *blocks, us, dls = lax.optimization_barrier((*blocks, us, dls))
+    blocks, us, dls = lax.optimization_barrier((blocks, us, dls))
     rate, gain, es, ends, endb = pl.pallas_call(
         end_states,
-        in_specs=[smem] + [vm] * 6,
+        in_specs=[vm] * 3,
         out_specs=[vm] * 5,
         out_shape=[
             jax.ShapeDtypeStruct((MODES, PADC), F32),
@@ -402,13 +408,14 @@
             pltpu.VMEM((EXT, 128), F32),
             pltpu.VMEM((EXT, 128), F32),
             pltpu.VMEM((2 * MODES, PADC), F32),
+            pltpu.VMEM((PADC, PADC), BF16),
         ],
-        compiler_params=params(12),
+        compiler_params=params(16),
         cost_estimate=pl.CostEstimate(flops=20000000, bytes_accessed=3000000, transcendentals=0),
         name="end_states",
-    )(xi.reshape(1), *blocks, us, dls)
-
-    mine, _ = lax.optimization_barrier((feats, early))
+    )(blocks, us, dls)
+
+    mine, _ = lax.optimization_barrier((feats, tprev))
     pair = lax.ppermute(mine, "y", [(i, i ^ 1) for i in range(4)])
     two = jnp.stack([mine, pair], axis=0)
 
@@ -464,7 +471,14 @@
     )(jnp.stack([xi, zi, yi]), zf, mix, es, *prefixes, taps, rate, gain, cots, us, dls)
     output = outt.T
 
+    def summed(a, ax):
+        short = a.astype(BF16)
+        parts = [short] + [ring(short, ax, d) for d in (1, 2, 3)]
+        return sum(p.astype(F32) for p in parts)
+
     arrived = lax.all_to_all(dzb, ("y", "core"), split_axis=0, concat_axis=0, tiled=True)
+    sums = summed(sums, "x")
+    arrived, sums = lax.optimization_barrier((arrived, sums))
     term = pl.pallas_call(
         weight_term,
         in_specs=[smem] + [vm] * 3,
@@ -475,6 +489,10 @@
         name="weight_term",
     )(jnp.stack([yi, ci]), arrived, ours.reshape(2, 2 * own, depth), theirs.reshape(2, 2 * own, depth))
     got = lax.all_to_all(term, "x", 0, 0, tiled=True)
+    dz, sums, _ = lax.optimization_barrier((dz, sums, term))
+    sums = summed(sums, "zl")
+    grad_feats = lax.dot_general(dz, w_in, NT, preferred_element_type=F32).astype(BF16)
+    got, sums, grad_feats = lax.optimization_barrier((got, sums, grad_feats))
     blocks = pl.pallas_call(
         split_rows,
         in_specs=[vm],
@@ -485,15 +503,11 @@
         name="split_rows",
     )(got)
     last = lax.all_to_all(blocks, ("zl", "y", "zh"), 0, 0, tiled=True)
+    sums, _ = lax.optimization_barrier((sums, blocks))
+    sums = summed(summed(sums, "y"), ("zh", "core"))
     last = jnp.sum(last.reshape(4, 4, 2, fblk, piece).astype(F32), axis=(0, 2)) * scale
     grad_weight = last.transpose(1, 0, 2).reshape(fblk, 4 * piece).astype(BF16)
 
-    for ax, behind in (("zl", term), ("y", got), ("x", None), (("zh", "core"), None)):
-        short = sums.astype(BF16)
-        parts = [short] + [ring(short, ax, d) for d in (1, 2, 3)]
-        if behind is not None:
-            *parts, _ = lax.optimization_barrier((*parts, behind))
-        sums = sum(p.astype(F32) for p in parts)
     grad_taps = sums[:24].reshape(3, 8, PADC)[:, :7, :width].transpose(1, 0, 2).reshape(7, chans)
     grad_taps = grad_taps * scale
     index = (xi * 4 + zi) * 4 + yi
@@ -501,8 +515,6 @@
     chosen = lax.dynamic_slice_in_dim(sums[24:, :width], index * held_chans, held_chans, axis=1)
     grad_residues = amp_mine * chosen.T * scale
 
-    dz, _ = lax.optimization_barrier((dz, term))
-    grad_feats = lax.dot_general(dz, w_in, NT, preferred_element_type=F32).astype(BF16)
     return (output[None], grad_feats[None], grad_weight, grad_taps, grad_residues)
 
 

time: 173 us -> 174 us (level)
  the two profiles are of different devices: /device:TPU:1 before, /device:TPU:32 now
where the time goes in v3:
time: 174 us; the launch traced here: 172 us
  starting transfers between devices  65.9 us (38%)
  waiting for transfers between devices  56.2 us (32%)
  Pallas kernels  25.9 us (15%)
  local copies, waits for them, and re-layouts  16.2 us (9%)
  matrix products  5.64 us (3%)
    ppermute x21, starting transfers between devices, ring(): return lax.ppermute(a, ax, [(i, (i + d) % 4) for i in range(4)])  29.6 us
    ppermute x21, waiting for transfers between devices, ring(): return lax.ppermute(a, ax, [(i, (i + d) % 4) for i in range(4)])  18.3 us
    all_to_all x1, waiting for transfers between devices, local(): last = lax.all_to_all(blocks, ('zl', 'y', 'zh'), 0, 0, tiled=True)  14.7 us
    unnamed x42, local copies, waits for them, and re-layouts  13.2 us
    all_to_all x1, starting transfers between devices, local(): blocks = lax.all_to_all(block, ctx, split_axis=0, concat_axis=0, tiled=True)  11.7 us
    all_to_all x1, starting transfers between devices, local(): last = lax.all_to_all(blocks, ('zl', 'y', 'zh'), 0, 0, tiled=True)  8.79 us
    pallas_call x1, Pallas kernels, local(): pl.pallas_call(finish, in_specs=[smem] + [vm] * 12, out_specs=[vm] * 4, o...  8.77 us
    ppermute x1, waiting for transfers between devices, local(): nexts = lax.ppermute(head, ctx, [(i, i - 1) for i in range(1, count)])  8.51 us
  transfers between devices with their start and end apart: 30, of which 18 were waited for; matrix products, arithmetic and copies ran while one was open for 5% of the time, Pallas kernels for 11%

profile of v3, /device:TPU:32, one launch (start us, length us, event | category | flops | bytes accessed | tf_op | source)
XLA Modules:
  0.0 172.4 jit_solution(7785173120625442587)
XLA Ops:
  1.5 1.0 copy-done
  2.5 0.9 copy-done.10
  3.5 0.9 copy-done.15
  5.7 0.9 prepare.1
  6.7 11.7 %all-to-all-start = ((f32[64,8,128]{2,1,0:T(8,128)}), f32[64,8,128]{2,1,0:T(8,128)S(1)}, u32[]{:S(2)}, u32[]{:S(2)}) async-start(f32[64,8,128]{2,1,0:T(8,128)} %get-tuple-element.50), calls=%async_computation | async-start | bytes 524288 | tf_op jit(solution)/shard_map/all_to_all | solution.py:369
  18.3 3.4 %collective-permute-start = (bf16[16,1536]{1,0:T(8,128)(2,1)S(1)}, bf16[16,1536]{1,0:T(8,128)(2,1)S(1)}, u32[]{:S(2)}, u32[]{:S(2)}) collective-permute-start(bf16[16,1536]{1,0:T(8,128)(2,1)S(1)} %get-tuple-element.45), channel_id=1, source_target_pairs={{0,4},{4,8},{8,12},{12,16},{16,20},{20,24},{24,28},{28,32},{32,36}... | collective-permute-start | bytes 147464 | tf_op jit(solution)/shard_map/ppermute | solution.py:370
  21.7 4.9 %collective-permute-done.tp = bf16[16,1536]{1,0:T(8,128)(2,1)S(1)} collective-permute-done((bf16[16,1536]{1,0:T(8,128)(2,1)S(1)}, bf16[16,1536]{1,0:T(8,128)(2,1)S(1)}, u32[]{:S(2)}, u32[]{:S(2)}) %collective-permute-start) | collective-permute-done | bytes 49184 | tf_op jit(solution)/shard_map/ppermute | solution.py:370
  26.6 3.4 %collective-permute-start.1 = (bf16[16,2560]{1,0:T(8,128)(2,1)S(1)}, bf16[16,2560]{1,0:T(8,128)(2,1)S(1)}, u32[]{:S(2)}, u32[]{:S(2)}) collective-permute-start(bf16[16,2560]{1,0:T(8,128)(2,1)S(1)} %get-tuple-element.46), channel_id=1, source_target_pairs={{4,0},{8,4},{12,8},{16,12},{20,16},{24,20},{28,24},{32,28},{36,32}... | collective-permute-start | bytes 245768 | tf_op jit(solution)/shard_map/ppermute | solution.py:371
  30.0 8.5 %collective-permute-done.1 = bf16[16,2560]{1,0:T(8,128)(2,1)S(1)} collective-permute-done((bf16[16,2560]{1,0:T(8,128)(2,1)S(1)}, bf16[16,2560]{1,0:T(8,128)(2,1)S(1)}, u32[]{:S(2)}, u32[]{:S(2)}) %collective-permute-start.1) | collective-permute-done | bytes 81952 | tf_op jit(solution)/shard_map/ppermute | solution.py:371
  38.7 7.2 %project.1 = (f32[160,3072]{1,0:T(8,128)S(1)}, f32[3,136,1024]{2,1,0:T(8,128)S(1)}, f32[136,1024]{1,0:T(8,128)S(1)}, f32[136,1024]{1,0:T(8,128)S(1)}, f32[136,1024]{1,0:T(8,128)S(1)}) custom-call(bf16[16,1536]{1,0:T(8,128)(2,1)S(1)} %collective-permute-done.tp, bf16[128,1536]{1,0:T(8,128)(2,1)S(1)} %bitcast.35, bf16[16,1536]{1,0:T(8,128)(2,1)S(1)} %slice.20.tn, ...), custom_call_target="tpu_custom_call" | custom-call | flops 1500000000 | bytes 14000000 | tf_op jit(solution)/shard_map/project/pallas_call | solution.py:379
  45.9 1.3 copy-done.4
  47.2 1.2 copy-done.6
  49.1 2.6 %end_states.1 = (f32[16,1024]{1,0:T(8,128)S(1)}, f32[16,1024]{1,0:T(8,128)S(1)}, f32[2,16,8,1024]{3,2,1,0:T(8,128)S(1)}, f32[32,1024]{1,0:T(8,128)S(1)}, bf16[32,1024]{1,0:T(8,128)(2,1)S(1)}) custom-call(f32[64,8,128]{2,1,0:T(8,128)S(1)} %all-to-all-done.blocks, f32[136,1024]{1,0:T(8,128)S(1)} %get-tuple-element.54.us, f32[136,1024]{1,0:T(8,128)S(1)} %get-tuple-element.55.dls), custom_call_target="tpu_custom_call" | custom-call | flops 20000000 | bytes 3000000 | tf_op jit(solution)/shard_map/end_states/pallas_call | solution.py:396
  51.9 1.6 collective-permute-start.3
  53.5 1.1 collective-permute-start.2
  55.4 1.1 pad_maximum_fusion
  56.4 1.3 collective-permute-done.3.r2
  57.7 1.2 collective-permute-done.2.r1
  59.2 2.0 %collective-permute-start.9 = (bf16[2,128,1536]{2,1,0:T(8,128)(2,1)S(1)}, bf16[2,128,1536]{2,1,0:T(8,128)(2,1)}, u32[]{:S(2)}, u32[]{:S(2)}) collective-permute-start(bf16[2,128,1536]{2,1,0:T(8,128)(2,1)S(1)} %pad_maximum_fusion), channel_id=1, source_target_pairs={{0,12},{4,8},{8,4},{12,0},{1,13},{5,9},{9,5},{13,1},{2,14},{6,10},... | collective-permute-start | bytes 2359304 | tf_op jit(solution)/shard_map/ppermute | solution.py:441
  61.1 4.6 %collective-permute-start.6 = (bf16[32,1024]{1,0:T(8,128)(2,1)S(1)}, bf16[32,1024]{1,0:T(8,128)(2,1)S(1)}, u32[]{:S(2)}, u32[]{:S(2)}) collective-permute-start(bf16[32,1024]{1,0:T(8,128)(2,1)S(1)} %get-tuple-element.62), channel_id=1, source_target_pairs={{0,32},{16,48},{32,0},{48,16},{1,33},{17,49},{33,1},{49,17},{2,34}... | collective-permute-start | bytes 196616 | tf_op jit(solution)/shard_map/ppermute | solution.py:332
  66.7 2.2 %collective-permute-done.6.r2 = bf16[32,1024]{1,0:T(8,128)(2,1)S(1)} collective-permute-done((bf16[32,1024]{1,0:T(8,128)(2,1)S(1)}, bf16[32,1024]{1,0:T(8,128)(2,1)S(1)}, u32[]{:S(2)}, u32[]{:S(2)}) %collective-permute-start.6) | collective-permute-done | bytes 65568 | tf_op jit(solution)/shard_map/ppermute | solution.py:332
  68.8 1.2 collective-permute-done.5.r1
  70.3 2.8 %collective-permute-start.12 = (bf16[32,1024]{1,0:T(8,128)(2,1)S(1)}, bf16[32,1024]{1,0:T(8,128)(2,1)S(1)}, u32[]{:S(2)}, u32[]{:S(2)}) collective-permute-start(bf16[32,1024]{1,0:T(8,128)(2,1)S(1)} %get-tuple-element.67), channel_id=1, source_target_pairs={{0,192},{64,0},{128,64},{192,128},{1,193},{65,1},{129,65},{193,129... | collective-permute-start | bytes 196616 | tf_op jit(solution)/shard_map/ppermute | solution.py:332
  74.9 3.9 %collective-permute-done.11.r2 = bf16[32,1024]{1,0:T(8,128)(2,1)S(1)} collective-permute-done((bf16[32,1024]{1,0:T(8,128)(2,1)S(1)}, bf16[32,1024]{1,0:T(8,128)(2,1)S(1)}, u32[]{:S(2)}, u32[]{:S(2)}) %collective-permute-start.11) | collective-permute-done | bytes 65568 | tf_op jit(solution)/shard_map/ppermute | solution.py:332
  80.3 1.2 constant_dynamic-update-slice_fusion
  81.7 1.4 copy-done.7
  83.1 1.1 copy-done.14
  84.1 8.8 %finish.1 = (bf16[960,128]{1,0:T(8,128)(2,1)}, bf16[128,2880]{1,0:T(8,128)(2,1)S(1)}, bf16[8,360,128]{2,1,0:T(8,128)(2,1)S(1)}, f32[40,1024]{1,0:T(8,128)S(1)}) custom-call(s32[3]{0:T(128)S(1)} %pad_add_fusion.place, f32[160,3072]{1,0:T(8,128)S(1)} %copy-done.5, f32[3,136,1024]{2,1,0:T(8,128)S(1)} %copy-done.7, f32[2,16,8,1024]{3,2,1,0:T(8,128)S(1)} %copy-done.9, ...), custom_call_target="tpu_custom_call" | custom-call | flops 200000000 | bytes 10000000 | tf_op jit(solution)/shard_map/finish/pallas_call | solution.py:446
  93.8 3.5 %all-to-all-start.1 = ((bf16[8,360,128]{2,1,0:T(8,128)(2,1)}), bf16[8,360,128]{2,1,0:T(8,128)(2,1)S(1)}, u32[]{:S(2)}, u32[]{:S(2)}) async-start(bf16[8,360,128]{2,1,0:T(8,128)(2,1)} %copy-done.12), calls=%async_computation.1 | async-start | bytes 1474560 | tf_op jit(solution)/shard_map/all_to_all | solution.py:479
  97.4 1.4 collective-permute-start.14
  98.9 3.1 %collective-permute-start.15 = (bf16[40,1024]{1,0:T(8,128)(2,1)S(1)}, bf16[40,1024]{1,0:T(8,128)(2,1)S(1)}, u32[]{:S(2)}, u32[]{:S(2)}) collective-permute-start(bf16[40,1024]{1,0:T(8,128)(2,1)S(1)} %convert_element_type.78), channel_id=1, source_target_pairs={{0,192},{64,0},{128,64},{192,128},{1,193},{65,1},{129,65},{193,129... | collective-permute-start | bytes 245768 | tf_op jit(solution)/shard_map/ppermute | solution.py:332
  102.1 2.1 %collective-permute-done.14 = bf16[40,1024]{1,0:T(8,128)(2,1)S(1)} collective-permute-done((bf16[40,1024]{1,0:T(8,128)(2,1)S(1)}, bf16[40,1024]{1,0:T(8,128)(2,1)S(1)}, u32[]{:S(2)}, u32[]{:S(2)}) %collective-permute-start.14) | collective-permute-done | bytes 81952 | tf_op jit(solution)/shard_map/ppermute | solution.py:332
  104.2 1.3 collective-permute-done.13
  105.6 4.3 %all-to-all-done.1.arrived = bf16[8,360,128]{2,1,0:T(8,128)(2,1)S(1)} async-done(((bf16[8,360,128]{2,1,0:T(8,128)(2,1)}), bf16[8,360,128]{2,1,0:T(8,128)(2,1)S(1)}, u32[]{:S(2)}, u32[]{:S(2)}) %all-to-all-start.1) | async-done | bytes 737312 | tf_op jit(solution)/shard_map/all_to_all | solution.py:479
  109.9 4.2 %weight_term.1 = bf16[4,360,384]{2,1,0:T(8,128)(2,1)} custom-call(s32[2]{0:T(128)S(1)} %pad_add_fusion.1.place, bf16[8,360,128]{2,1,0:T(8,128)(2,1)S(1)} %all-to-all-done.1.arrived, bf16[2,256,1536]{2,1,0:T(8,128)(2,1)S(1)} %bitcast.36, bf16[2,256,1536]{2,1,0:T(8,128)(2,1)} %bitcast.14.theirs), custom_call_target="tpu_custom_call" | custom-call | flops 1200000000 | bytes 6000000 | tf_op jit(solution)/shard_map/weight_term/pallas_call | solution.py:482
  114.1 3.5 %all-to-all-start.2 = ((bf16[4,360,384]{2,1,0:T(8,128)(2,1)}), bf16[4,360,384]{2,1,0:T(8,128)(2,1)S(1)}, u32[]{:S(2)}, u32[]{:S(2)}) async-start(bf16[4,360,384]{2,1,0:T(8,128)(2,1)} %weight_term.1), calls=%async_computation.2 | async-start | bytes 2211840 | tf_op jit(solution)/shard_map/all_to_all | solution.py:491
  117.6 1.9 %collective-permute-start.18 = (bf16[40,1024]{1,0:T(8,128)(2,1)S(1)}, bf16[40,1024]{1,0:T(8,128)(2,1)S(1)}, u32[]{:S(2)}, u32[]{:S(2)}) collective-permute-start(bf16[40,1024]{1,0:T(8,128)(2,1)S(1)} %convert_add_fusion.2), channel_id=1, source_target_pairs={{0,32},{16,48},{32,0},{48,16},{1,33},{17,49},{33,1},{49,17},{2,34}... | collective-permute-start | bytes 245768 | tf_op jit(solution)/shard_map/ppermute | solution.py:332
  119.5 1.5 collective-permute-start.17
  121.5 5.6 %convolution_convert_fusion = bf16[128,1536]{1,0:T(8,128)(2,1)} fusion(bf16[128,2880]{1,0:T(8,128)(2,1)S(1)} %get-tuple-element.80, bf16[1536,2880]{0,1:T(8,128)(2,1)} %param.7), kind=kOutput, calls=%fused_computation | convolution fusion | flops 1132658688 | bytes 9977856 | tf_op jit(solution)/shard_map/dot_general | solution.py:494
  127.9 5.5 %all-to-all-done.2.got = bf16[4,360,384]{2,1,0:T(8,128)(2,1)S(1)} async-done(((bf16[4,360,384]{2,1,0:T(8,128)(2,1)}), bf16[4,360,384]{2,1,0:T(8,128)(2,1)S(1)}, u32[]{:S(2)}, u32[]{:S(2)}) %all-to-all-start.2) | async-done | bytes 1105952 | tf_op jit(solution)/shard_map/all_to_all | solution.py:491
  133.4 1.1 split_rows.1
  135.0 1.4 collective-permute-start.20
  136.5 1.8 %collective-permute-start.22 = (bf16[40,1024]{1,0:T(8,128)(2,1)S(1)}, bf16[40,1024]{1,0:T(8,128)(2,1)S(1)}, u32[]{:S(2)}, u32[]{:S(2)}) collective-permute-start(bf16[40,1024]{1,0:T(8,128)(2,1)S(1)} %convert_add_fusion.1), channel_id=1, source_target_pairs={{0,12},{4,0},{8,4},{12,8},{1,13},{5,1},{9,5},{13,9},{2,14},{6,2},{... | collective-permute-start | bytes 245768 | tf_op jit(solution)/shard_map/ppermute | solution.py:332
  138.2 2.2 %collective-permute-done.21 = bf16[40,1024]{1,0:T(8,128)(2,1)S(1)} collective-permute-done((bf16[40,1024]{1,0:T(8,128)(2,1)S(1)}, bf16[40,1024]{1,0:T(8,128)(2,1)S(1)}, u32[]{:S(2)}, u32[]{:S(2)}) %collective-permute-start.21) | collective-permute-done | bytes 81952 | tf_op jit(solution)/shard_map/ppermute | solution.py:332
  141.3 2.0 %collective-permute-start.25 = (bf16[40,1024]{1,0:T(8,128)(2,1)S(1)}, bf16[40,1024]{1,0:T(8,128)(2,1)S(1)}, u32[]{:S(2)}, u32[]{:S(2)}) collective-permute-start(bf16[40,1024]{1,0:T(8,128)(2,1)S(1)} %add_convert_fusion), channel_id=1, source_target_pairs={{0,3},{1,0},{2,1},{3,2},{4,7},{5,4},{6,5},{7,6},{8,11},{9,8},{10,9... | collective-permute-start | bytes 245768 | tf_op jit(solution)/shard_map/ppermute | solution.py:332
  143.3 2.9 %collective-permute-start.24 = (bf16[40,1024]{1,0:T(8,128)(2,1)S(1)}, bf16[40,1024]{1,0:T(8,128)(2,1)S(1)}, u32[]{:S(2)}, u32[]{:S(2)}) collective-permute-start(bf16[40,1024]{1,0:T(8,128)(2,1)S(1)} %add_convert_fusion), channel_id=1, source_target_pairs={{0,2},{1,3},{2,0},{3,1},{4,6},{5,7},{6,4},{7,5},{8,10},{9,11},{10,... | collective-permute-start | bytes 245768 | tf_op jit(solution)/shard_map/ppermute | solution.py:332
  146.3 8.8 %all-to-all-start.3 = ((bf16[32,24,180]{2,1,0:T(8,128)(2,1)}), bf16[32,24,180]{2,1,0:T(8,128)(2,1)S(1)}, u32[]{:S(2)}, u32[]{:S(2)}) async-start(bf16[32,24,180]{2,1,0:T(8,128)(2,1)} %split_rows.1), calls=%async_computation.3 | async-start | bytes 786432 | tf_op jit(solution)/shard_map/all_to_all | solution.py:505
  156.9 14.7 %all-to-all-done.3 = bf16[32,24,180]{2,1,0:T(8,128)(2,1)S(1)} async-done(((bf16[32,24,180]{2,1,0:T(8,128)(2,1)}), bf16[32,24,180]{2,1,0:T(8,128)(2,1)S(1)}, u32[]{:S(2)}, u32[]{:S(2)}) %all-to-all-start.3) | async-done | bytes 276512 | tf_op jit(solution)/shard_map/all_to_all | solution.py:505
  (87 shorter events, 15.4 us)
Async XLA Ops:
  1.5 1.0 copy-start
  2.5 0.9 copy-start.10
  3.5 0.9 copy-start.15
  4.3 0.7 copy-start.16
  5.7 32.9 %copy-start.1 = (bf16[1,128,1536]{2,1,0:T(8,128)(2,1)S(1)}, bf16[1,128,1536]{2,1,0:T(8,128)(2,1)}, u32[]{:S(2)}) copy-start(bf16[1,128,1536]{2,1,0:T(8,128)(2,1)} %param.6) | copy-start | bytes 1179652
  5.7 33.0 %copy-start.11 = (bf16[1,128,960]{1,2,0:T(8,128)(2,1)S(1)}, bf16[1,128,960]{1,2,0:T(8,128)(2,1)}, u32[]{:S(2)}) copy-start(bf16[1,128,960]{1,2,0:T(8,128)(2,1)} %param.11) | copy-start | bytes 737284
  6.7 42.5 %all-to-all-start = ((f32[64,8,128]{2,1,0:T(8,128)}), f32[64,8,128]{2,1,0:T(8,128)S(1)}, u32[]{:S(2)}, u32[]{:S(2)}) async-start(f32[64,8,128]{2,1,0:T(8,128)} %get-tuple-element.50), calls=%async_computation | async-start | bytes 524288 | tf_op jit(solution)/shard_map/all_to_all | solution.py:369
  18.3 8.2 %collective-permute-start = (bf16[16,1536]{1,0:T(8,128)(2,1)S(1)}, bf16[16,1536]{1,0:T(8,128)(2,1)S(1)}, u32[]{:S(2)}, u32[]{:S(2)}) collective-permute-start(bf16[16,1536]{1,0:T(8,128)(2,1)S(1)} %get-tuple-element.45), channel_id=1, source_target_pairs={{0,4},{4,8},{8,12},{12,16},{16,20},{20,24},{24,28},{28,32},{32,36}... | collective-permute-start | bytes 147464 | tf_op jit(solution)/shard_map/ppermute | solution.py:370
  26.6 28.0 %collective-permute-start.8 = (bf16[128,1536]{1,0:T(8,128)(2,1)}, bf16[128,1536]{1,0:T(8,128)(2,1)S(1)}, u32[]{:S(2)}, u32[]{:S(2)}) collective-permute-start(bf16[128,1536]{1,0:T(8,128)(2,1)} %bitcast.33), channel_id=1, source_target_pairs={{0,4},{4,0},{8,12},{12,8},{1,5},{5,1},{9,13},{13,9},{2,6},{6,2},{1... | collective-permute-start | bytes 1179656 | tf_op jit(solution)/shard_map/ppermute | solution.py:419
  26.6 11.9 %collective-permute-start.1 = (bf16[16,2560]{1,0:T(8,128)(2,1)S(1)}, bf16[16,2560]{1,0:T(8,128)(2,1)S(1)}, u32[]{:S(2)}, u32[]{:S(2)}) collective-permute-start(bf16[16,2560]{1,0:T(8,128)(2,1)S(1)} %get-tuple-element.46), channel_id=1, source_target_pairs={{4,0},{8,4},{12,8},{16,12},{20,16},{24,20},{28,24},{32,28},{36,32}... | collective-permute-start | bytes 245768 | tf_op jit(solution)/shard_map/ppermute | solution.py:371
  45.9 1.3 copy-start.4
  47.2 1.2 copy-start.6
  48.3 0.8 copy-start.13
  49.1 10.0 %copy-start.2 = (f32[136,1024]{1,0:T(8,128)}, f32[136,1024]{1,0:T(8,128)S(1)}, u32[]{:S(2)}) copy-start(f32[136,1024]{1,0:T(8,128)S(1)} %get-tuple-element.55.dls) | copy-start | bytes 1671172
  51.8 7.4 %copy-start.8 = (f32[2,16,8,1024]{3,2,1,0:T(8,128)}, f32[2,16,8,1024]{3,2,1,0:T(8,128)S(1)}, u32[]{:S(2)}) copy-start(f32[2,16,8,1024]{3,2,1,0:T(8,128)S(1)} %get-tuple-element.56.es) | copy-start | bytes 3145732
  51.8 4.6 %collective-permute-start.4 = (bf16[32,1024]{1,0:T(8,128)(2,1)S(1)}, bf16[32,1024]{1,0:T(8,128)(2,1)S(1)}, u32[]{:S(2)}, u32[]{:S(2)}) collective-permute-start(bf16[32,1024]{1,0:T(8,128)(2,1)S(1)} %get-tuple-element.58), channel_id=1, source_target_pairs={{0,12},{4,0},{8,4},{12,8},{1,13},{5,1},{9,5},{13,9},{2,14},{6,2},{... | collective-permute-start | bytes 196616 | tf_op jit(solution)/shard_map/ppermute | solution.py:332
  51.9 5.9 %collective-permute-start.3 = (bf16[32,1024]{1,0:T(8,128)(2,1)S(1)}, bf16[32,1024]{1,0:T(8,128)(2,1)S(1)}, u32[]{:S(2)}, u32[]{:S(2)}) collective-permute-start(bf16[32,1024]{1,0:T(8,128)(2,1)S(1)} %get-tuple-element.58), channel_id=1, source_target_pairs={{0,8},{4,12},{8,0},{12,4},{1,9},{5,13},{9,1},{13,5},{2,10},{6,14},... | collective-permute-start | bytes 196616 | tf_op jit(solution)/shard_map/ppermute | solution.py:332
  53.5 5.5 %collective-permute-start.2 = (bf16[32,1024]{1,0:T(8,128)(2,1)S(1)}, bf16[32,1024]{1,0:T(8,128)(2,1)S(1)}, u32[]{:S(2)}, u32[]{:S(2)}) collective-permute-start(bf16[32,1024]{1,0:T(8,128)(2,1)S(1)} %get-tuple-element.58), channel_id=1, source_target_pairs={{0,4},{4,8},{8,12},{12,0},{1,5},{5,9},{9,13},{13,1},{2,6},{6,10},{... | collective-permute-start | bytes 196616 | tf_op jit(solution)/shard_map/ppermute | solution.py:332
  54.6 0.7 copy-start.18
  59.2 21.1 %collective-permute-start.9 = (bf16[2,128,1536]{2,1,0:T(8,128)(2,1)S(1)}, bf16[2,128,1536]{2,1,0:T(8,128)(2,1)}, u32[]{:S(2)}, u32[]{:S(2)}) collective-permute-start(bf16[2,128,1536]{2,1,0:T(8,128)(2,1)S(1)} %pad_maximum_fusion), channel_id=1, source_target_pairs={{0,12},{4,8},{8,4},{12,0},{1,13},{5,9},{9,5},{13,1},{2,14},{6,10},... | collective-permute-start | bytes 2359304 | tf_op jit(solution)/shard_map/ppermute | solution.py:441
  61.1 5.5 %collective-permute-start.7 = (bf16[32,1024]{1,0:T(8,128)(2,1)S(1)}, bf16[32,1024]{1,0:T(8,128)(2,1)S(1)}, u32[]{:S(2)}, u32[]{:S(2)}) collective-permute-start(bf16[32,1024]{1,0:T(8,128)(2,1)S(1)} %get-tuple-element.62), channel_id=1, source_target_pairs={{0,48},{16,0},{32,16},{48,32},{1,49},{17,1},{33,17},{49,33},{2,50}... | collective-permute-start | bytes 196616 | tf_op jit(solution)/shard_map/ppermute | solution.py:332
  61.1 7.7 %collective-permute-start.6 = (bf16[32,1024]{1,0:T(8,128)(2,1)S(1)}, bf16[32,1024]{1,0:T(8,128)(2,1)S(1)}, u32[]{:S(2)}, u32[]{:S(2)}) collective-permute-start(bf16[32,1024]{1,0:T(8,128)(2,1)S(1)} %get-tuple-element.62), channel_id=1, source_target_pairs={{0,32},{16,48},{32,0},{48,16},{1,33},{17,49},{33,1},{49,17},{2,34}... | collective-permute-start | bytes 196616 | tf_op jit(solution)/shard_map/ppermute | solution.py:332
  65.8 4.3 %collective-permute-start.5 = (bf16[32,1024]{1,0:T(8,128)(2,1)S(1)}, bf16[32,1024]{1,0:T(8,128)(2,1)S(1)}, u32[]{:S(2)}, u32[]{:S(2)}) collective-permute-start(bf16[32,1024]{1,0:T(8,128)(2,1)S(1)} %get-tuple-element.62), channel_id=1, source_target_pairs={{0,16},{16,32},{32,48},{48,0},{1,17},{17,33},{33,49},{49,1},{2,18}... | collective-permute-start | bytes 196616 | tf_op jit(solution)/shard_map/ppermute | solution.py:332
  70.0 11.6 %copy-start.9 = (f32[2,16,8,1024]{3,2,1,0:T(8,128)S(1)}, f32[2,16,8,1024]{3,2,1,0:T(8,128)}, u32[]{:S(2)}) copy-start(f32[2,16,8,1024]{3,2,1,0:T(8,128)} %copy-done.8) | copy-start | bytes 3145732
  70.2 11.4 %copy-start.3 = (f32[136,1024]{1,0:T(8,128)S(1)}, f32[136,1024]{1,0:T(8,128)}, u32[]{:S(2)}) copy-start(f32[136,1024]{1,0:T(8,128)} %copy-done.2) | copy-start | bytes 1671172
  70.2 11.4 %copy-start.5 = (f32[160,3072]{1,0:T(8,128)S(1)}, f32[160,3072]{1,0:T(8,128)}, u32[]{:S(2)}) copy-start(f32[160,3072]{1,0:T(8,128)} %copy-done.4) | copy-start | bytes 5898244
  70.3 4.7 %collective-permute-start.12 = (bf16[32,1024]{1,0:T(8,128)(2,1)S(1)}, bf16[32,1024]{1,0:T(8,128)(2,1)S(1)}, u32[]{:S(2)}, u32[]{:S(2)}) collective-permute-start(bf16[32,1024]{1,0:T(8,128)(2,1)S(1)} %get-tuple-element.67), channel_id=1, source_target_pairs={{0,192},{64,0},{128,64},{192,128},{1,193},{65,1},{129,65},{193,129... | collective-permute-start | bytes 196616 | tf_op jit(solution)/shard_map/ppermute | solution.py:332
  73.0 5.8 %collective-permute-start.11 = (bf16[32,1024]{1,0:T(8,128)(2,1)S(1)}, bf16[32,1024]{1,0:T(8,128)(2,1)S(1)}, u32[]{:S(2)}, u32[]{:S(2)}) collective-permute-start(bf16[32,1024]{1,0:T(8,128)(2,1)S(1)} %get-tuple-element.67), channel_id=1, source_target_pairs={{0,128},{64,192},{128,0},{192,64},{1,129},{65,193},{129,1},{193,65... | collective-permute-start | bytes 196616 | tf_op jit(solution)/shard_map/ppermute | solution.py:332
  73.9 5.6 %collective-permute-start.10 = (bf16[32,1024]{1,0:T(8,128)(2,1)S(1)}, bf16[32,1024]{1,0:T(8,128)(2,1)S(1)}, u32[]{:S(2)}, u32[]{:S(2)}) collective-permute-start(bf16[32,1024]{1,0:T(8,128)(2,1)S(1)} %get-tuple-element.67), channel_id=1, source_target_pairs={{0,64},{64,128},{128,192},{192,0},{1,65},{65,129},{129,193},{193,1... | collective-permute-start | bytes 196616 | tf_op jit(solution)/shard_map/ppermute | solution.py:332
  81.5 28.4 %collective-permute-start.16 = (bf16[4,128,1536]{2,1,0:T(8,128)(2,1)S(1)}, bf16[4,128,1536]{2,1,0:T(8,128)(2,1)}, u32[]{:S(2)}, u32[]{:S(2)}) collective-permute-start(bf16[4,128,1536]{2,1,0:T(8,128)(2,1)S(1)} %constant_dynamic-update-slice_fusion), channel_id=1, source_target_pairs={{0,1},{1,0},{2,3},{3,2},{4,5},{5,4},{6,7},{7,6},{8,9},{9,8},{10,11... | collective-permute-start | bytes 4718600 | tf_op jit(solution)/shard_map/ppermute | solution.py:444
  81.6 1.4 copy-start.7
  83.1 1.1 copy-start.14
  92.9 0.9 copy-start.12
  93.8 16.1 %all-to-all-start.1 = ((bf16[8,360,128]{2,1,0:T(8,128)(2,1)}), bf16[8,360,128]{2,1,0:T(8,128)(2,1)S(1)}, u32[]{:S(2)}, u32[]{:S(2)}) async-start(bf16[8,360,128]{2,1,0:T(8,128)(2,1)} %copy-done.12), calls=%async_computation.1 | async-start | bytes 1474560 | tf_op jit(solution)/shard_map/all_to_all | solution.py:479
  97.4 6.8 %collective-permute-start.14 = (bf16[40,1024]{1,0:T(8,128)(2,1)S(1)}, bf16[40,1024]{1,0:T(8,128)(2,1)S(1)}, u32[]{:S(2)}, u32[]{:S(2)}) collective-permute-start(bf16[40,1024]{1,0:T(8,128)(2,1)S(1)} %convert_element_type.78), channel_id=1, source_target_pairs={{0,128},{64,192},{128,0},{192,64},{1,129},{65,193},{129,1},{193,65... | collective-permute-start | bytes 245768 | tf_op jit(solution)/shard_map/ppermute | solution.py:332
  98.8 6.7 %collective-permute-start.13 = (bf16[40,1024]{1,0:T(8,128)(2,1)S(1)}, bf16[40,1024]{1,0:T(8,128)(2,1)S(1)}, u32[]{:S(2)}, u32[]{:S(2)}) collective-permute-start(bf16[40,1024]{1,0:T(8,128)(2,1)S(1)} %convert_element_type.78), channel_id=1, source_target_pairs={{0,64},{64,128},{128,192},{192,0},{1,65},{65,129},{129,193},{193,1... | collective-permute-start | bytes 245768 | tf_op jit(solution)/shard_map/ppermute | solution.py:332
  98.9 6.6 %collective-permute-start.15 = (bf16[40,1024]{1,0:T(8,128)(2,1)S(1)}, bf16[40,1024]{1,0:T(8,128)(2,1)S(1)}, u32[]{:S(2)}, u32[]{:S(2)}) collective-permute-start(bf16[40,1024]{1,0:T(8,128)(2,1)S(1)} %convert_element_type.78), channel_id=1, source_target_pairs={{0,192},{64,0},{128,64},{192,128},{1,193},{65,1},{129,65},{193,129... | collective-permute-start | bytes 245768 | tf_op jit(solution)/shard_map/ppermute | solution.py:332
  114.1 19.3 %all-to-all-start.2 = ((bf16[4,360,384]{2,1,0:T(8,128)(2,1)}), bf16[4,360,384]{2,1,0:T(8,128)(2,1)S(1)}, u32[]{:S(2)}, u32[]{:S(2)}) async-start(bf16[4,360,384]{2,1,0:T(8,128)(2,1)} %weight_term.1), calls=%async_computation.2 | async-start | bytes 2211840 | tf_op jit(solution)/shard_map/all_to_all | solution.py:491
  117.6 9.6 %collective-permute-start.18 = (bf16[40,1024]{1,0:T(8,128)(2,1)S(1)}, bf16[40,1024]{1,0:T(8,128)(2,1)S(1)}, u32[]{:S(2)}, u32[]{:S(2)}) collective-permute-start(bf16[40,1024]{1,0:T(8,128)(2,1)S(1)} %convert_add_fusion.2), channel_id=1, source_target_pairs={{0,32},{16,48},{32,0},{48,16},{1,33},{17,49},{33,1},{49,17},{2,34}... | collective-permute-start | bytes 245768 | tf_op jit(solution)/shard_map/ppermute | solution.py:332
  119.5 7.7 %collective-permute-start.17 = (bf16[40,1024]{1,0:T(8,128)(2,1)S(1)}, bf16[40,1024]{1,0:T(8,128)(2,1)S(1)}, u32[]{:S(2)}, u32[]{:S(2)}) collective-permute-start(bf16[40,1024]{1,0:T(8,128)(2,1)S(1)} %convert_add_fusion.2), channel_id=1, source_target_pairs={{0,16},{16,32},{32,48},{48,0},{1,17},{17,33},{33,49},{49,1},{2,18}... | collective-permute-start | bytes 245768 | tf_op jit(solution)/shard_map/ppermute | solution.py:332
  121.0 6.9 %collective-permute-start.19 = (bf16[40,1024]{1,0:T(8,128)(2,1)S(1)}, bf16[40,1024]{1,0:T(8,128)(2,1)S(1)}, u32[]{:S(2)}, u32[]{:S(2)}) collective-permute-start(bf16[40,1024]{1,0:T(8,128)(2,1)S(1)} %convert_add_fusion.2), channel_id=1, source_target_pairs={{0,48},{16,0},{32,16},{48,32},{1,49},{17,1},{33,17},{49,33},{2,50}... | collective-permute-start | bytes 245768 | tf_op jit(solution)/shard_map/ppermute | solution.py:332
  134.4 6.0 %collective-permute-start.21 = (bf16[40,1024]{1,0:T(8,128)(2,1)S(1)}, bf16[40,1024]{1,0:T(8,128)(2,1)S(1)}, u32[]{:S(2)}, u32[]{:S(2)}) collective-permute-start(bf16[40,1024]{1,0:T(8,128)(2,1)S(1)} %convert_add_fusion.1), channel_id=1, source_target_pairs={{0,8},{4,12},{8,0},{12,4},{1,9},{5,13},{9,1},{13,5},{2,10},{6,14},... | collective-permute-start | bytes 245768 | tf_op jit(solution)/shard_map/ppermute | solution.py:332
  135.0 6.3 %collective-permute-start.20 = (bf16[40,1024]{1,0:T(8,128)(2,1)S(1)}, bf16[40,1024]{1,0:T(8,128)(2,1)S(1)}, u32[]{:S(2)}, u32[]{:S(2)}) collective-permute-start(bf16[40,1024]{1,0:T(8,128)(2,1)S(1)} %convert_add_fusion.1), channel_id=1, source_target_pairs={{0,4},{4,8},{8,12},{12,0},{1,5},{5,9},{9,13},{13,1},{2,6},{6,10},{... | collective-permute-start | bytes 245768 | tf_op jit(solution)/shard_map/ppermute | solution.py:332
  136.5 4.8 %collective-permute-start.22 = (bf16[40,1024]{1,0:T(8,128)(2,1)S(1)}, bf16[40,1024]{1,0:T(8,128)(2,1)S(1)}, u32[]{:S(2)}, u32[]{:S(2)}) collective-permute-start(bf16[40,1024]{1,0:T(8,128)(2,1)S(1)} %convert_add_fusion.1), channel_id=1, source_target_pairs={{0,12},{4,0},{8,4},{12,8},{1,13},{5,1},{9,5},{13,9},{2,14},{6,2},{... | collective-permute-start | bytes 245768 | tf_op jit(solution)/shard_map/ppermute | solution.py:332
  141.3 13.8 %collective-permute-start.25 = (bf16[40,1024]{1,0:T(8,128)(2,1)S(1)}, bf16[40,1024]{1,0:T(8,128)(2,1)S(1)}, u32[]{:S(2)}, u32[]{:S(2)}) collective-permute-start(bf16[40,1024]{1,0:T(8,128)(2,1)S(1)} %add_convert_fusion), channel_id=1, source_target_pairs={{0,3},{1,0},{2,1},{3,2},{4,7},{5,4},{6,5},{7,6},{8,11},{9,8},{10,9... | collective-permute-start | bytes 245768 | tf_op jit(solution)/shard_map/ppermute | solution.py:332
  143.3 11.9 %collective-permute-start.24 = (bf16[40,1024]{1,0:T(8,128)(2,1)S(1)}, bf16[40,1024]{1,0:T(8,128)(2,1)S(1)}, u32[]{:S(2)}, u32[]{:S(2)}) collective-permute-start(bf16[40,1024]{1,0:T(8,128)(2,1)S(1)} %add_convert_fusion), channel_id=1, source_target_pairs={{0,2},{1,3},{2,0},{3,1},{4,6},{5,7},{6,4},{7,5},{8,10},{9,11},{10,... | collective-permute-start | bytes 245768 | tf_op jit(solution)/shard_map/ppermute | solution.py:332
  146.2 9.0 %collective-permute-start.23 = (bf16[40,1024]{1,0:T(8,128)(2,1)S(1)}, bf16[40,1024]{1,0:T(8,128)(2,1)S(1)}, u32[]{:S(2)}, u32[]{:S(2)}) collective-permute-start(bf16[40,1024]{1,0:T(8,128)(2,1)S(1)} %add_convert_fusion), channel_id=1, source_target_pairs={{0,1},{1,2},{2,3},{3,0},{4,5},{5,6},{6,7},{7,4},{8,9},{9,10},{10,1... | collective-permute-start | bytes 245768 | tf_op jit(solution)/shard_map/ppermute | solution.py:332
  146.3 25.2 %all-to-all-start.3 = ((bf16[32,24,180]{2,1,0:T(8,128)(2,1)}), bf16[32,24,180]{2,1,0:T(8,128)(2,1)S(1)}, u32[]{:S(2)}, u32[]{:S(2)}) async-start(bf16[32,24,180]{2,1,0:T(8,128)(2,1)} %split_rows.1), calls=%async_computation.3 | async-start | bytes 786432 | tf_op jit(solution)/shard_map/all_to_all | solution.py:505
  (1 other events, 0.7 us)

commit v4 on v3

v4 whole, which is shorter than its diff:
```python
import math

import jax
import jax.numpy as jnp
from jax import lax
from jax.experimental import pallas as pl
from jax.experimental.pallas import tpu as pltpu
from jax.sharding import Mesh, PartitionSpec as P

F32 = jnp.float32
BF16 = jnp.bfloat16
HALO = 16
EXT = 136
SEG = 17
PADC = 1024
MODES = 16
NT = (((1,), (1,)), ((), ()))


def rounded(a):
    return a.astype(BF16).astype(F32)


def project(
    tp, tk, nexts, wt, taps, cott, zf_out, mix_out, cots_out, us, dls,
    acc, turn, wbuf, zf, mix, cots, sems, zsem, tsems,
):
    steps, _, kblk = wbuf.shape
    copies = [
        pltpu.make_async_copy(wt.at[:, pl.ds(k * kblk, kblk)], wbuf.at[k], sems.at[k])
        for k in range(steps)
    ]
    for copy in copies:
        copy.start()
    width, own = cott.shape
    depth = tk.shape[1]
    turn[...] = jnp.zeros(turn.shape, F32)
    turn[0:width, :] = cott[...].astype(F32)
    for g in range(3):
        zf[g, :, width:] = jnp.zeros((zf.shape[1], PADC - width), F32)
    for k in range(steps):
        cols = slice(k * kblk, (k + 1) * kblk)
        rows = jnp.concatenate([tp[:, cols], tk[:, cols], nexts[:, cols]], axis=0)
        copies[k].wait()
        part = lax.dot_general(rows, wbuf[k], NT, preferred_element_type=F32)
        if k == 0:
            acc[...] = part
        elif k < steps - 1:
            acc[...] += part
        else:
            total = acc[...] + part
            for g in range(3):
                zf[g, :, 0:width] = rounded(total[:, g * width : (g + 1) * width])
    zcopy = pltpu.make_async_copy(zf, zf_out, zsem)
    zcopy.start()

    def out_copies(ct):
        lanes = pl.ds(pl.multiple_of(ct * 128, 128), 128)
        return (
            pltpu.make_async_copy(mix.at[:, :, lanes], mix_out.at[:, :, lanes], tsems.at[0, ct]),
            pltpu.make_async_copy(cots.at[:, lanes], cots_out.at[:, lanes], tsems.at[1, ct]),
        )

    def tile(ct, carry):
        lane = pl.multiple_of(ct * 128, 128)
        lanes = pl.ds(lane, 128)
        mixed = []
        for g in range(3):
            total = taps[g, 0:1, lanes] * zf[g, pl.ds(HALO, EXT), lanes]
            for j in range(1, 7):
                total = total + taps[g, j : j + 1, lanes] * zf[g, pl.ds(HALO - j, EXT), lanes]
            mix[g, :, lanes] = total
            mixed.append(total)
        after = nexts[:, pl.ds(pl.multiple_of(depth + lane, 128), 128)].astype(F32)
        cot = jnp.concatenate([turn[lanes, :].T, after[0 : EXT - 128]], axis=0)
        cots[:, lanes] = cot
        us[:, lanes] = rounded(mixed[1] * mixed[2])
        dls[:, lanes] = rounded(cot * mixed[0])
        for copy in out_copies(ct):
            copy.start()
        return carry

    lax.fori_loop(0, PADC // 128, tile, 0)
    zcopy.wait()
    for ct in range(PADC // 128):
        for copy in out_copies(ct):
            copy.wait()


def one_minus_exp(x):
    series = jnp.ones_like(x)
    for n in range(13, 1, -1):
        series = 1.0 - series * x * (1.0 / n)
    return jnp.where(x < 0.5, x * series, 1.0 - jnp.exp(-x))


def prepare(
    feats, cott, rates, residues, conv, head, tail, block, taps, amp,
    held, turn, cbuf, rbuf, sbuf, vbuf, sems,
):
    count = rates.shape[0]
    width, own = cott.shape
    depth = feats.shape[1]
    copies = [
        pltpu.make_async_copy(rates, rbuf, sems.at[0]),
        pltpu.make_async_copy(residues, sbuf, sems.at[1]),
        pltpu.make_async_copy(cott, cbuf, sems.at[2]),
        pltpu.make_async_copy(conv, vbuf, sems.at[3]),
        pltpu.make_async_copy(feats.at[pl.ds(0, HALO)], head.at[:, pl.ds(0, depth)], sems.at[4]),
        pltpu.make_async_copy(feats.at[pl.ds(own - HALO, HALO)], tail, sems.at[5]),
    ]
    for copy in copies:
        copy.start()
    held[...] = jnp.zeros(held.shape, F32)
    turn[...] = jnp.zeros(turn.shape, F32)
    taps[...] = jnp.zeros(taps.shape, F32)
    copies[0].wait()
    copies[1].wait()
    size = jnp.sqrt(one_minus_exp(2.0 * rbuf[...]))
    amp[...] = size
    rate = rbuf[...]
    gain = sbuf[...] * size
    for j in range(count):
        row, lane = j // 4, (j % 4) * 2 * MODES
        held[row : row + 1, lane : lane + MODES] = rate[j : j + 1, :]
        held[row : row + 1, lane + MODES : lane + 2 * MODES] = gain[j : j + 1, :]
    block[...] = jnp.broadcast_to(held[...][None], block.shape)
    copies[2].wait()
    turn[0:width, :] = cbuf[...].astype(F32)
    for c in range(PADC // 128):
        part = turn[c * 128 : (c + 1) * 128, :].T[0:HALO]
        head[:, depth + c * 128 : depth + (c + 1) * 128] = part.astype(BF16)
    copies[3].wait()
    for g in range(3):
        taps[g, 0:7, 0:width] = vbuf[:, g * width : (g + 1) * width]
    copies[4].wait()
    copies[5].wait()


def joined_params(blocks, order, left):
    row = lax.broadcasted_iota(jnp.int32, (PADC, PADC), 0)
    col = lax.broadcasted_iota(jnp.int32, (PADC, PADC), 1)
    goal = 15 * lax.bitwise_and(row, 63) + lax.shift_right_logical(row, 6)
    order[...] = jnp.where((goal == col) & (row < 960), 1.0, 0.0).astype(BF16)
    left[...] = jnp.zeros(left.shape, F32)
    count = blocks.shape[0]
    for c in range(4):
        flipped = blocks[:, c, :].T
        for p in range(4):
            j = 4 * c + p
            if j < 15:
                left[:, j * count : (j + 1) * count] = flipped[p * 2 * MODES : (p + 1) * 2 * MODES, :]
    rest = left[...]
    parts = []
    for _ in range(3):
        part = rest.astype(BF16)
        parts.append(part)
        rest = rest - part.astype(F32)
    out = jnp.dot(jnp.concatenate(parts, axis=0), order[...], preferred_element_type=F32)
    size = 2 * MODES
    return out[0:size] + out[size : 2 * size] + out[2 * size : 3 * size]


def end_states(blocks, us, dls, rates, gains, es, ends, endb, ut, dt, left, order):
    joined = joined_params(blocks, order, left)
    rates[...] = joined[0:MODES]
    gains[...] = joined[MODES : 2 * MODES]
    sub = lax.broadcasted_iota(jnp.int32, (8, 128), 0)
    subf = sub.astype(F32)
    fdepth = jnp.where(sub == 7, 0.0, (EXT - 8 - SEG) - SEG * subf)
    bdepth = jnp.where(sub == 0, 0.0, SEG * subf - 8.0)

    def tile(ct, carry):
        lanes = pl.ds(pl.multiple_of(ct * 128, 128), 128)
        ut[...] = us[:, lanes]
        dt[...] = dls[:, lanes]
        rate = rates[:, lanes]
        decay = jnp.exp(-rate)
        for half in range(2):
            ks = range(half * 8, half * 8 + 8)
            al = [jnp.broadcast_to(decay[k : k + 1, :], (8, 128)) for k in ks]
            rl = [jnp.broadcast_to(rate[k : k + 1, :], (8, 128)) for k in ks]
            st = [jnp.zeros((8, 128), F32)] * 8
            snap = st
            for t in range(SEG):
                uv = ut[pl.ds(t, 8, stride=SEG), :]
                st = [a * s + uv for a, s in zip(al, st)]
                if t == 8:
                    snap = st
            for i, k in enumerate(ks):
                es[0, k, :, lanes] = st[i]
                full = jnp.where(sub == 7, snap[i], st[i]) * jnp.exp(-rl[i] * fdepth)
                ends[k : k + 1, lanes] = jnp.sum(full, axis=0, keepdims=True)
            st = [jnp.zeros((8, 128), F32)] * 8
            for t in range(SEG - 1, -1, -1):
                dv = dt[pl.ds(t, 8, stride=SEG), :]
                st = [a * s + dv for a, s in zip(al, st)]
                if t == 8:
                    snap = st
            for i, k in enumerate(ks):
                es[1, k, :, lanes] = st[i]
                full = jnp.where(sub == 0, snap[i], st[i]) * jnp.exp(-rl[i] * bdepth)
                ends[MODES + k : MODES + k + 1, lanes] = jnp.sum(full, axis=0, keepdims=True)
        return carry

    lax.fori_loop(0, PADC // 128, tile, 0)
    endb[...] = ends[...].astype(BF16)


def make_level(span):
    def level(place, own, r1, r2, r3, rates, total, totalb, prefix):
        me = place[0]
        rate = rates[...] * float(span)
        before = jnp.zeros((MODES, PADC), F32)
        after = before
        whole_f = before
        whole_b = before
        for d, ref in enumerate((own, r1, r2, r3)):
            m = lax.rem(me + (4 - d), 4)
            f = ref[0:MODES, :].astype(F32)
            b = ref[MODES : 2 * MODES, :].astype(F32)
            whole_f = whole_f + f * jnp.exp(-rate * (3 - m).astype(F32))
            whole_b = whole_b + b * jnp.exp(-rate * m.astype(F32))
            if d > 0:
                gf = me - 1 - m
                gb = m - me - 1
                wf = jnp.exp(-rate * jnp.maximum(gf, 0).astype(F32))
                wb = jnp.exp(-rate * jnp.maximum(gb, 0).astype(F32))
                before = before + jnp.where(gf >= 0, 1.0, 0.0) * (wf * f)
                after = after + jnp.where(gb >= 0, 1.0, 0.0) * (wb * b)
        prefix[0:MODES, :] = before
        prefix[MODES : 2 * MODES, :] = after
        total[0:MODES, :] = whole_f
        total[MODES : 2 * MODES, :] = whole_b
        totalb[0:MODES, :] = whole_f.astype(BF16)
        totalb[MODES : 2 * MODES, :] = whole_b.astype(BF16)

    return level


def finish(
    place, zf, mix, es, py, pz, px, taps, rates, reff, cots,
    outt, dz, dzb, sums, inc, ut, dt, longs, dps, dms, dzt,
):
    own = dz.shape[1]
    rate = rates[...]
    for back in range(2):
        part = pl.ds(back * MODES, MODES)
        near, mid = place[2], place[1]
        if back:
            near, mid = 3 - near, 3 - mid
        far = pz[part, :] + jnp.exp(-rate * (4 * own * mid).astype(F32)) * px[part, :]
        inc[part, :] = py[part, :] + jnp.exp(-rate * (own * near).astype(F32)) * far
    sub = lax.broadcasted_iota(jnp.int32, (8, 128), 0)
    ut[...] = rounded(mix[1] * mix[2])
    dt[...] = rounded(cots[...] * mix[0])
    decay = jnp.exp(-rate)
    gain = reff[...]
    for half in range(2):
        ks = range(half * 8, half * 8 + 8)
        al = [jnp.broadcast_to(decay[k : k + 1, :], (8, 128)) for k in ks]
        gl = [jnp.broadcast_to(gain[k : k + 1, :], (8, 128)) for k in ks]
        rl = [jnp.broadcast_to(rate[k : k + 1, :], (8, 128)) for k in ks]
        fwd = []
        bwd = []
        for i, k in enumerate(ks):
            jump = [jnp.exp(-float(SEG * m) * rl[i]) for m in (1, 2, 4)]
            x = jnp.where(sub == 0, inc[k : k + 1, :], pltpu.roll(es[0, k], 1, 0))
            for m, d in zip((1, 2, 4), jump):
                x = x + jnp.where(sub >= m, pltpu.roll(x, m, 0) * d, 0.0)
            fwd.append(x)
            x = jnp.where(
                sub == 7, inc[MODES + k : MODES + k + 1, :], pltpu.roll(es[1, k], 7, 0)
            )
            for m, d in zip((1, 2, 4), jump):
                x = x + jnp.where(sub < 8 - m, pltpu.roll(x, 8 - m, 0) * d, 0.0)
            bwd.append(x)
        gr = [jnp.zeros((8, 128), F32)] * 8
        st = fwd
        for t in range(SEG):
            uv = ut[pl.ds(t, 8, stride=SEG), :]
            dv = dt[pl.ds(t, 8, stride=SEG), :]
            if t >= 9:
                dv = jnp.where(sub < 7, dv, 0.0)
            st = [a * s + uv for a, s in zip(al, st)]
            gr = [q + dv * s for q, s in zip(gr, st)]
            total = sum(g * s for g, s in zip(gl, st))
            if half:
                total = total + longs[pl.ds(t, 8, stride=SEG), :]
            longs[pl.ds(t, 8, stride=SEG), :] = total
        for i, k in enumerate(ks):
            sums[24 + k : 25 + k, :] = jnp.sum(gr[i], axis=0, keepdims=True)
        st = bwd
        for t in range(SEG - 1, -1, -1):
            dv = dt[pl.ds(t, 8, stride=SEG), :]
            st = [a * s + dv for a, s in zip(al, st)]
            total = sum(g * s for g, s in zip(gl, st))
            if half:
                total = total + dps[pl.ds(t, 8, stride=SEG), :]
            dps[pl.ds(t, 8, stride=SEG), :] = total
    long_out = rounded(longs[...])
    dprod = rounded(dps[...])
    outt[...] = (mix[0, 0:own, :] * long_out[0:own]).T.astype(BF16)
    dms[0] = rounded(cots[...] * long_out)
    dms[1] = rounded(dprod * mix[2])
    dms[2] = rounded(dprod * mix[1])
    ct = pl.program_id(0)
    for g in range(3):
        mine = dms[g, 0:own, :]
        total = taps[g, 0:1, :] * mine
        sums[8 * g : 8 * g + 1, :] = jnp.sum(mine * zf[g, pl.ds(HALO, own), :], axis=0, keepdims=True)
        for j in range(1, 7):
            total = total + taps[g, j : j + 1, :] * dms[g, pl.ds(j, own), :]
            sums[8 * g + j : 8 * g + j + 1, :] = jnp.sum(
                mine * zf[g, pl.ds(HALO - j, own), :], axis=0, keepdims=True
            )
        sums[8 * g + 7 : 8 * g + 8, :] = jnp.zeros((1, 128), F32)
        dz[g] = total.astype(BF16)
        dzt[g, pl.ds(pl.multiple_of(ct * 128, 128), 128), :] = total.T

    @pl.when(ct == pl.num_programs(0) - 1)
    def _():
        piece = dzb.shape[1] // 2
        width = 16 * piece // 3
        for b in range(8):
            both = []
            for h in range(2):
                off = h * 8 * piece + (b % 2) * 4 * piece + (b // 2) * piece
                g, low = off // width, off % width
                size = min(piece, width - low)
                both.append(dzt[g, low : low + size, :])
                if size < piece:
                    both.append(dzt[g + 1, 0 : piece - size, :])
            dzb[b] = jnp.concatenate(both, axis=0).astype(BF16)


def token_grads(dz, wt, out, acc):
    g = pl.program_id(0)
    part = jnp.dot(dz[0, :, 0 : wt.shape[0]], wt[...], preferred_element_type=F32)

    @pl.when(g == 0)
    def _():
        acc[...] = part

    @pl.when(g > 0)
    def _():
        acc[...] += part

    @pl.when(g == pl.num_programs(0) - 1)
    def _():
        out[...] = acc[...].astype(BF16)


def weight_term(place, arrived, *refs):
    *tokens, term = refs
    me = place[0]
    core = place[1]
    chunk = term.shape[2]
    slots = (me, lax.bitwise_xor(me, 1), 3 - me, lax.bitwise_xor(3 - me, 1))
    pairs = []
    for half, c in ((0, core), (1, 1 - core)):
        for p in (0, 2):
            left = [arrived[slots[p + i] * 2 + c] for i in range(2)]
            pairs.append((jnp.concatenate(left, axis=1), tokens[4 * half + p : 4 * half + p + 2]))
    for j in range(4):
        total = None
        cols = slice(j * chunk, (j + 1) * chunk)
        for left, (one, two) in pairs:
            right = jnp.concatenate([one[:, cols], two[:, cols]], axis=0)
            part = jnp.dot(left, right, preferred_element_type=F32)
            total = part if total is None else total + part
        term[j] = total.astype(BF16)


def split_rows(got, blocks, turn):
    chans = got.shape[1]
    fblk = blocks.shape[1]
    piece = blocks.shape[2]
    turn[0:chans, :] = (
        got[0].astype(F32) + got[1].astype(F32) + got[2].astype(F32) + got[3].astype(F32)
    )
    turn[chans:, :] = jnp.zeros((turn.shape[0] - chans, turn.shape[1]), F32)
    flipped = turn[...].T
    for q in range(16):
        for h in range(2):
            part = flipped[q * fblk : (q + 1) * fblk, h * piece : (h + 1) * piece]
            blocks[2 * q + h] = part.astype(BF16)


def ring(a, ax, d):
    return lax.ppermute(a, ax, [(i, (i + d) % 4) for i in range(4)])


def params(mb):
    return pltpu.CompilerParams(vmem_limit_bytes=mb * 1024 * 1024)


def local(tokens, w_in, conv_taps, residues, rates, cotangent):
    feats = tokens[0]
    cot = cotangent[0]
    own, width = cot.shape
    depth = feats.shape[1]
    chans = 3 * width
    count = 64
    piece = chans // 16
    fblk = depth // count
    xi, zi, yi = lax.axis_index("x"), lax.axis_index("zl"), lax.axis_index("y")
    ci = lax.axis_index("core")
    ctx = ("x", "zl", "y")
    scale = 1.0 / math.sqrt(4 * count * own)
    smem = pl.BlockSpec(memory_space=pltpu.SMEM)
    vm = pl.BlockSpec(memory_space=pltpu.VMEM)
    anywhere = pl.BlockSpec(memory_space=pl.ANY)
    head, tail, block, taps, amp_mine = pl.pallas_call(
        prepare,
        in_specs=[anywhere] * 5,
        out_specs=[vm] * 5,
        out_shape=[
            jax.ShapeDtypeStruct((HALO, depth + PADC), BF16),
            jax.ShapeDtypeStruct((HALO, depth), BF16),
            jax.ShapeDtypeStruct((count, 8, 128), F32),
            jax.ShapeDtypeStruct((3, 8, PADC), F32),
            jax.ShapeDtypeStruct(rates.shape, F32),
        ],
        scratch_shapes=[
            pltpu.VMEM((8, 128), F32),
            pltpu.VMEM((PADC, own), F32),
            pltpu.VMEM((width, own), BF16),
            pltpu.VMEM(rates.shape, F32),
            pltpu.VMEM(rates.shape, F32),
            pltpu.VMEM(conv_taps.shape, F32),
            pltpu.SemaphoreType.DMA((6,)),
        ],
        compiler_params=params(60),
        name="prepare",
    )(feats, cot.T, rates, residues, conv_taps)
    tprev = lax.ppermute(tail, ctx, [(i, i + 1) for i in range(count - 1)])
    nexts = lax.ppermute(head, ctx, [(i, i - 1) for i in range(1, count)])
    block, tprev, nexts = lax.optimization_barrier((block, tprev, nexts))
    blocks = lax.all_to_all(block, ctx, split_axis=0, concat_axis=0, tiled=True)

    kblk = 256
    ext_rows = own + 2 * HALO
    shapes = [(3, ext_rows, PADC), (3, EXT, PADC), (EXT, PADC), (EXT, PADC), (EXT, PADC)]
    zf, mix, cots, us, dls = pl.pallas_call(
        project,
        in_specs=[vm] * 3 + [anywhere] + [vm] * 2,
        out_specs=[anywhere] * 3 + [vm] * 2,
        out_shape=[jax.ShapeDtypeStruct(s, F32) for s in shapes],
        scratch_shapes=[
            pltpu.VMEM((ext_rows, chans), F32),
            pltpu.VMEM((PADC, own), F32),
            pltpu.VMEM((depth // kblk, chans, kblk), BF16),
            pltpu.VMEM(shapes[0], F32),
            pltpu.VMEM(shapes[1], F32),
            pltpu.VMEM(shapes[2], F32),
            pltpu.SemaphoreType.DMA((depth // kblk,)),
            pltpu.SemaphoreType.DMA,
            pltpu.SemaphoreType.DMA((2, PADC // 128)),
        ],
        compiler_params=params(48),
        cost_estimate=pl.CostEstimate(flops=1500000000, bytes_accessed=14000000, transcendentals=0),
        name="project",
    )(tprev, feats, nexts, w_in.T, taps, cot.T)

    blocks, us, dls = lax.optimization_barrier((blocks, us, dls))
    rate, gain, es, ends, endb = pl.pallas_call(
        end_states,
        in_specs=[vm] * 3,
        out_specs=[vm] * 5,
        out_shape=[
            jax.ShapeDtypeStruct((MODES, PADC), F32),
            jax.ShapeDtypeStruct((MODES, PADC), F32),
            jax.ShapeDtypeStruct((2, MODES, 8, PADC), F32),
            jax.ShapeDtypeStruct((2 * MODES, PADC), F32),
            jax.ShapeDtypeStruct((2 * MODES, PADC), BF16),
        ],
        scratch_shapes=[
            pltpu.VMEM((EXT, 128), F32),
            pltpu.VMEM((EXT, 128), F32),
            pltpu.VMEM((2 * MODES, PADC), F32),
            pltpu.VMEM((PADC, PADC), BF16),
        ],
        compiler_params=params(16),
        cost_estimate=pl.CostEstimate(flops=20000000, bytes_accessed=3000000, transcendentals=0),
        name="end_states",
    )(blocks, us, dls)

    prefixes = []
    total, sent = ends, endb
    for ax, me, span in (("y", yi, own), ("zl", zi, 4 * own), ("x", xi, 16 * own)):
        near = [ring(sent, ax, d) for d in (1, 2, 3)]
        total, sent, prefix = pl.pallas_call(
            make_level(span),
            in_specs=[smem] + [vm] * 5,
            out_specs=[vm] * 3,
            out_shape=[
                jax.ShapeDtypeStruct((2 * MODES, PADC), F32),
                jax.ShapeDtypeStruct((2 * MODES, PADC), BF16),
                jax.ShapeDtypeStruct((2 * MODES, PADC), F32),
            ],
            compiler_params=params(8),
            name="level",
        )(me.reshape(1), total, *near, rate)
        prefixes.append(prefix)
        if ax == "y":
            mine, _ = lax.optimization_barrier((feats, sent))
            pair = lax.ppermute(mine, "y", [(i, i ^ 1) for i in range(4)])
            opposite = lax.ppermute(mine, "y", [(i, 3 - i) for i in range(4)])
        elif ax == "zl":
            pair, opposite, _ = lax.optimization_barrier((pair, opposite, sent))
            far = lax.ppermute(pair, "y", [(i, 3 - i) for i in range(4)])

    def tiles(shape):
        lead = len(shape) - 1
        return pl.BlockSpec(shape, lambda k: (0,) * lead + (k,))

    outt, dz, dzb, sums = pl.pallas_call(
        finish,
        grid=(PADC // 128,),
        in_specs=[
            smem,
            tiles((3, ext_rows, 128)),
            tiles((3, EXT, 128)),
            tiles((2, MODES, 8, 128)),
            tiles((2 * MODES, 128)),
            tiles((2 * MODES, 128)),
            tiles((2 * MODES, 128)),
            tiles((3, 8, 128)),
            tiles((MODES, 128)),
            tiles((MODES, 128)),
            tiles((EXT, 128)),
        ],
        out_specs=[
            pl.BlockSpec((128, own), lambda k: (k, 0)),
            tiles((3, own, 128)),
            pl.BlockSpec((8, 2 * piece, own), lambda k: (0, 0, 0)),
            tiles((40, 128)),
        ],
        out_shape=[
            jax.ShapeDtypeStruct((width, own), BF16),
            jax.ShapeDtypeStruct((3, own, PADC), BF16),
            jax.ShapeDtypeStruct((8, 2 * piece, own), BF16),
            jax.ShapeDtypeStruct((40, PADC), F32),
        ],
        scratch_shapes=[
            pltpu.VMEM((2 * MODES, 128), F32),
            pltpu.VMEM((EXT, 128), F32),
            pltpu.VMEM((EXT, 128), F32),
            pltpu.VMEM((EXT, 128), F32),
            pltpu.VMEM((EXT, 128), F32),
            pltpu.VMEM((3, EXT, 128), F32),
            pltpu.VMEM((3, PADC, own), F32),
        ],
        compiler_params=params(40),
        cost_estimate=pl.CostEstimate(flops=200000000, bytes_accessed=10000000, transcendentals=0),
        name="finish",
    )(jnp.stack([xi, zi, yi]), zf, mix, es, *prefixes, taps, rate, gain, cots)
    output = outt.T
    blocks_of = [mine, pair, opposite, far]
    theirs = [lax.ppermute(a, "core", [(0, 1), (1, 0)]) for a in blocks_of]

    def summed(a, ax):
        short = a.astype(BF16)
        parts = [short] + [ring(short, ax, d) for d in (1, 2, 3)]
        return sum(p.astype(F32) for p in parts)

    arrived = lax.all_to_all(dzb, ("y", "core"), split_axis=0, concat_axis=0, tiled=True)
    sums = summed(sums, "x")
    arrived, sums = lax.optimization_barrier((arrived, sums))
    term = pl.pallas_call(
        weight_term,
        in_specs=[smem] + [vm] * 9,
        out_specs=vm,
        out_shape=jax.ShapeDtypeStruct((4, 2 * piece, depth // 4), BF16),
        compiler_params=params(24),
        cost_estimate=pl.CostEstimate(flops=1200000000, bytes_accessed=6000000, transcendentals=0),
        name="weight_term",
    )(jnp.stack([yi, ci]), arrived, *blocks_of, *theirs)
    got = lax.all_to_all(term, "x", 0, 0, tiled=True)
    sums, _ = lax.optimization_barrier((sums, term))
    sums = summed(summed(sums, "zl"), "y")
    got, sums = lax.optimization_barrier((got, sums))
    blocks = pl.pallas_call(
        split_rows,
        in_specs=[vm],
        out_specs=vm,
        out_shape=jax.ShapeDtypeStruct((32, fblk, piece), BF16),
        scratch_shapes=[pltpu.VMEM((384, depth // 4), F32)],
        compiler_params=params(12),
        name="split_rows",
    )(got)
    last = lax.all_to_all(blocks, ("zl", "y", "zh"), 0, 0, tiled=True)
    sums, dz, _ = lax.optimization_barrier((sums, dz, blocks))
    sums = summed(sums, ("zh", "core"))
    grad_feats = pl.pallas_call(
        token_grads,
        grid=(3,),
        in_specs=[
            pl.BlockSpec((1, own, PADC), lambda g: (g, 0, 0)),
            pl.BlockSpec((width, depth), lambda g: (g, 0)),
        ],
        out_specs=pl.BlockSpec((own, depth), lambda g: (0, 0)),
        out_shape=jax.ShapeDtypeStruct((own, depth), BF16),
        scratch_shapes=[pltpu.VMEM((own, depth), F32)],
        compiler_params=params(24),
        cost_estimate=pl.CostEstimate(flops=1200000000, bytes_accessed=11000000, transcendentals=0),
        name="token_grads",
    )(dz, w_in.T)
    last = jnp.sum(last.reshape(4, 4, 2, fblk, piece).astype(F32), axis=(0, 2)) * scale
    grad_weight = last.transpose(1, 0, 2).reshape(fblk, 4 * piece).astype(BF16)

    grad_taps = sums[:24].reshape(3, 8, PADC)[:, :7, :width].transpose(1, 0, 2).reshape(7, chans)
    grad_taps = grad_taps * scale
    index = (xi * 4 + zi) * 4 + yi
    held_chans = width // count
    chosen = lax.dynamic_slice_in_dim(sums[24:, :width], index * held_chans, held_chans, axis=1)
    grad_residues = amp_mine * chosen.T * scale

    return (output[None], grad_feats[None], grad_weight, grad_taps, grad_residues)


def solution(mesh):
    fine = Mesh(mesh.devices.reshape(4, 4, 4, 2, 2), ("x", "zl", "y", "zh", "core"))
    ctx = ("x", "zl", "y")
    dp = ("zh", "core")
    in_specs = (P(dp, ctx, None), P(), P(), P(ctx, None), P(ctx, None), P(dp, ctx, None))
    out_specs = (P(dp, ctx, None), P(dp, ctx, None), P(ctx, dp), P(), P(ctx, None))
    return jax.shard_map(local, mesh=fine, in_specs=in_specs, out_specs=out_specs, check_vma=False)
```

time: 174 us -> 180 us (1.034)
  the two profiles are of different devices: /device:TPU:32 before, /device:TPU:1 now
where the time goes in v4:
time: 180 us; the launch traced here: 179 us
  starting transfers between devices  79 us (44%)
  waiting for transfers between devices  36 us (20%)
  Pallas kernels  33.9 us (19%)
  local copies, waits for them, and re-layouts  27.9 us (16%)
    ppermute x21, waiting for transfers between devices, ring(): return lax.ppermute(a, ax, [(i, (i + d) % 4) for i in range(4)])  34.5 us
    ppermute x21, starting transfers between devices, ring(): return lax.ppermute(a, ax, [(i, (i + d) % 4) for i in range(4)])  29.3 us
    unnamed x64, local copies, waits for them, and re-layouts  26.2 us
    all_to_all x1, starting transfers between devices, local(): blocks = lax.all_to_all(block, ctx, split_axis=0, concat_axis=0, tiled=True)  17 us
    all_to_all x1, starting transfers between devices, local(): lax.all_to_all(dzb, ('y', 'core'), split_axis=0, concat_axis=0, tiled=True)  11 us
    pallas_call x1, Pallas kernels, local(): pl.pallas_call(finish, grid=(PADC // 128,), in_specs=[smem, tiles((3, ext...  9.3 us
    pallas_call x1, Pallas kernels, local(): pl.pallas_call(project, in_specs=[vm] * 3 + [anywhere] + [vm] * 2, out_sp...  7.92 us
    all_to_all x1, starting transfers between devices, local(): last = lax.all_to_all(blocks, ('zl', 'y', 'zh'), 0, 0, tiled=True)  7.49 us
  transfers between devices with their start and end apart: 34, of which 19 were waited for; matrix products, arithmetic and copies ran while one was open for 2% of the time, Pallas kernels for 12%

profile of v4, /device:TPU:1, one launch (start us, length us, event | category | flops | bytes accessed | tf_op | source)
XLA Modules:
  0.0 179.0 jit_solution(5997126959359833265)
XLA Ops:
  0.6 2.0 %prepare.1 = (bf16[16,2560]{1,0:T(8,128)(2,1)}, bf16[16,1536]{1,0:T(8,128)(2,1)}, f32[64,8,128]{2,1,0:T(8,128)}, f32[3,8,1024]{2,1,0:T(8,128)}, f32[15,16]{1,0:T(8,128)}) custom-call(bf16[128,1536]{1,0:T(8,128)(2,1)} %bitcast.28, bf16[960,128]{1,0:T(8,128)(2,1)} %bitcast.34, f32[15,16]{1,0:T(8,128)} %rates.1, f32[15,16]{1,0:T(8,128)} %residues.1, f32[7,2880]{1,0:T(8,128)} %conv.1), custom_call_target="tpu_custom_call" | custom-call | tf_op jit(solution)/shard_map/prepare/pallas_call | solution.py:414
  2.7 1.3 collective-permute-start.1
  4.0 4.7 %collective-permute-start = (bf16[16,1536]{1,0:T(8,128)(2,1)}, bf16[16,1536]{1,0:T(8,128)(2,1)S(1)}, u32[]{:S(2)}, u32[]{:S(2)}) collective-permute-start(bf16[16,1536]{1,0:T(8,128)(2,1)} %get-tuple-element.48), channel_id=1, source_target_pairs={{0,4},{4,8},{8,12},{12,16},{16,20},{20,24},{24,28},{28,32},{32,36}... | collective-permute-start | bytes 147464 | tf_op jit(solution)/shard_map/ppermute | solution.py:437
  8.6 1.5 collective-permute-done.tp
  10.1 17.0 %all-to-all-start = ((f32[64,8,128]{2,1,0:T(8,128)}), f32[64,8,128]{2,1,0:T(8,128)S(1)}, u32[]{:S(2)}, u32[]{:S(2)}) async-start(f32[64,8,128]{2,1,0:T(8,128)} %get-tuple-element.55), calls=%async_computation | async-start | bytes 524288 | tf_op jit(solution)/shard_map/all_to_all | solution.py:440
  27.1 1.0 copy-done.1
  28.1 0.9 copy-done.7
  29.9 7.9 %project.1 = (f32[3,160,1024]{2,1,0:T(8,128)S(1)}, f32[3,136,1024]{2,1,0:T(8,128)S(1)}, f32[136,1024]{1,0:T(8,128)S(1)}, f32[136,1024]{1,0:T(8,128)S(1)}, f32[136,1024]{1,0:T(8,128)S(1)}) custom-call(bf16[16,1536]{1,0:T(8,128)(2,1)S(1)} %collective-permute-done.tp, bf16[128,1536]{1,0:T(8,128)(2,1)S(1)} %bitcast.29, ...), custom_call_target="tpu_custom_call" | custom-call | flops 1500000000 | bytes 14000000 | tf_op jit(solution)/shard_map/project/pallas_call | solution.py:445
  37.9 1.2 copy-done.3
  40.7 1.1 copy-done.16
  41.8 3.2 %end_states.1 = (f32[16,1024]{1,0:T(8,128)S(1)}, f32[16,1024]{1,0:T(8,128)S(1)}, f32[2,16,8,1024]{3,2,1,0:T(8,128)S(1)}, f32[32,1024]{1,0:T(8,128)S(1)}, bf16[32,1024]{1,0:T(8,128)(2,1)}) custom-call(f32[64,8,128]{2,1,0:T(8,128)S(1)} %all-to-all-done.blocks, f32[136,1024]{1,0:T(8,128)S(1)} %get-tuple-element.59.us, f32[136,1024]{1,0:T(8,128)S(1)} %copy-done.16), custom_call_target="tpu_custom_call" | custom-call | flops 20000000 | bytes 3000000 | tf_op jit(solution)/shard_map/end_states/pallas_call | solution.py:467
  45.1 1.0 copy-done.5
  46.7 2.2 %collective-permute-start.4 = (bf16[32,1024]{1,0:T(8,128)(2,1)}, bf16[32,1024]{1,0:T(8,128)(2,1)}, u32[]{:S(2)}, u32[]{:S(2)}) collective-permute-start(bf16[32,1024]{1,0:T(8,128)(2,1)} %get-tuple-element.63), channel_id=1, source_target_pairs={{0,12},{4,0},{8,4},{12,8},{1,13},{5,1},{9,5},{13,9},{2,14},{6,2},{... | collective-permute-start | bytes 196616 | tf_op jit(solution)/shard_map/ppermute | solution.py:391
  50.6 3.3 %collective-permute-done.3.r2 = bf16[32,1024]{1,0:T(8,128)(2,1)} collective-permute-done((bf16[32,1024]{1,0:T(8,128)(2,1)}, bf16[32,1024]{1,0:T(8,128)(2,1)}, u32[]{:S(2)}, u32[]{:S(2)}) %collective-permute-start.3) | collective-permute-done | bytes 65568 | tf_op jit(solution)/shard_map/ppermute | solution.py:391
  54.5 0.9 copy-done.28
  55.5 1.6 level.3
  59.1 3.0 %collective-permute-start.7 = (bf16[32,1024]{1,0:T(8,128)(2,1)}, bf16[32,1024]{1,0:T(8,128)(2,1)}, u32[]{:S(2)}, u32[]{:S(2)}) collective-permute-start(bf16[32,1024]{1,0:T(8,128)(2,1)} %get-tuple-element.67), channel_id=1, source_target_pairs={{0,48},{16,0},{32,16},{48,32},{1,49},{17,1},{33,17},{49,33},{2,50}... | collective-permute-start | bytes 196616 | tf_op jit(solution)/shard_map/ppermute | solution.py:391
  62.7 1.1 collective-permute-done.7.r3
  63.8 2.7 %collective-permute-done.6.r2 = bf16[32,1024]{1,0:T(8,128)(2,1)} collective-permute-done((bf16[32,1024]{1,0:T(8,128)(2,1)}, bf16[32,1024]{1,0:T(8,128)(2,1)}, u32[]{:S(2)}, u32[]{:S(2)}) %collective-permute-start.6) | collective-permute-done | bytes 65568 | tf_op jit(solution)/shard_map/ppermute | solution.py:391
  66.5 0.9 collective-permute-done.5.r1
  67.4 0.9 copy-done.26
  68.3 1.1 level.4
  71.4 2.0 %collective-permute-start.16 = (bf16[128,1536]{1,0:T(8,128)(2,1)}, bf16[128,1536]{1,0:T(8,128)(2,1)}, u32[]{:S(2)}, u32[]{:S(2)}) collective-permute-start(bf16[128,1536]{1,0:T(8,128)(2,1)} %collective-permute-done.14.refs_1_), channel_id=1, source_target_pairs={{0,12},{4,8},{8,4},{12,0},{1,13},{5,9},{9,5},{13,1},{2,14},{6,10},... | collective-permute-start | bytes 1179656 | tf_op jit(solution)/shard_map/ppermute | solution.py:512
  73.3 2.7 %collective-permute-start.10 = (bf16[32,1024]{1,0:T(8,128)(2,1)}, bf16[32,1024]{1,0:T(8,128)(2,1)S(1)}, u32[]{:S(2)}, u32[]{:S(2)}) collective-permute-start(bf16[32,1024]{1,0:T(8,128)(2,1)} %copy-done.29), channel_id=1, source_target_pairs={{0,192},{64,0},{128,64},{192,128},{1,193},{65,1},{129,65},{193,129... | collective-permute-start | bytes 196616 | tf_op jit(solution)/shard_map/ppermute | solution.py:391
  77.7 3.2 %collective-permute-done.9.r2 = bf16[32,1024]{1,0:T(8,128)(2,1)S(1)} collective-permute-done((bf16[32,1024]{1,0:T(8,128)(2,1)}, bf16[32,1024]{1,0:T(8,128)(2,1)S(1)}, u32[]{:S(2)}, u32[]{:S(2)}) %collective-permute-start.9) | collective-permute-done | bytes 65568 | tf_op jit(solution)/shard_map/ppermute | solution.py:391
  83.3 1.4 copy-done.4
  84.7 1.1 copy-done.14
  88.5 9.3 %finish.1 = (bf16[960,128]{1,0:T(8,128)(2,1)}, bf16[3,128,1024]{2,1,0:T(8,128)(2,1)S(1)}, bf16[8,360,128]{2,1,0:T(8,128)(2,1)S(1)}, f32[40,1024]{1,0:T(8,128)S(1)}) custom-call(s32[3]{0:T(128)S(1)} %pad_add_fusion.place, f32[3,160,1024]{2,1,0:T(8,128)S(1)} %get-tuple-element.53.zf, f32[3,136,1024]{2,1,0:T(8,128)S(1)} %copy-done.4, ...), custom_call_target="tpu_custom_call" | custom-call | flops 200000000 | bytes 10000000 | tf_op jit(solution)/shard_map/finish/pallas_call | solution.py:518
  100.3 11.0 %all-to-all-start.1 = ((bf16[8,360,128]{2,1,0:T(8,128)(2,1)}), bf16[8,360,128]{2,1,0:T(8,128)(2,1)S(1)}, u32[]{:S(2)}, u32[]{:S(2)}) async-start(bf16[8,360,128]{2,1,0:T(8,128)(2,1)} %copy-done.10), calls=%async_computation.1 | async-start | bytes 1474560 | tf_op jit(solution)/shard_map/all_to_all | solution.py:568
  111.2 0.9 convert_element_type.75
  112.2 1.2 collective-permute-start.12
  113.8 3.9 %collective-permute-done.12 = bf16[40,1024]{1,0:T(8,128)(2,1)S(1)} collective-permute-done((bf16[40,1024]{1,0:T(8,128)(2,1)S(1)}, bf16[40,1024]{1,0:T(8,128)(2,1)S(1)}, u32[]{:S(2)}, u32[]{:S(2)}) %collective-permute-start.12) | collective-permute-done | bytes 81952 | tf_op jit(solution)/shard_map/ppermute | solution.py:391
  117.8 1.3 collective-permute-start.19
  119.9 3.5 %collective-permute-done.13 = bf16[40,1024]{1,0:T(8,128)(2,1)S(1)} collective-permute-done((bf16[40,1024]{1,0:T(8,128)(2,1)S(1)}, bf16[40,1024]{1,0:T(8,128)(2,1)S(1)}, u32[]{:S(2)}, u32[]{:S(2)}) %collective-permute-start.13) | collective-permute-done | bytes 81952 | tf_op jit(solution)/shard_map/ppermute | solution.py:391
  123.5 4.0 %weight_term.1 = bf16[4,360,384]{2,1,0:T(8,128)(2,1)} custom-call(s32[2]{0:T(128)S(1)} %pad_add_fusion.1.place, bf16[8,360,128]{2,1,0:T(8,128)(2,1)S(1)} %all-to-all-done.1.arrived, bf16[128,1536]{1,0:T(8,128)(2,1)S(1)} %bitcast.33, bf16[128,1536]{1,0:T(8,128)(2,1)} %collective-permute-done.14.refs_1_, bf16[128,1536]{1,0:T(8,128)(2,1)} %collective-permute-done.15.refs_2_, ...), custom_call_target="tpu_custom_call" | custom-call | flops 1200000000 | bytes 6000000 | tf_op jit(solution)/shard_map/weight_term/pallas_call | solution.py:571
  127.6 3.7 %all-to-all-start.2 = ((bf16[4,360,384]{2,1,0:T(8,128)(2,1)}), bf16[4,360,384]{2,1,0:T(8,128)(2,1)S(1)}, u32[]{:S(2)}, u32[]{:S(2)}) async-start(bf16[4,360,384]{2,1,0:T(8,128)(2,1)} %weight_term.1), calls=%async_computation.2 | async-start | bytes 2211840 | tf_op jit(solution)/shard_map/all_to_all | solution.py:580
  131.2 0.9 collective-permute-start.22
  132.4 3.0 %collective-permute-start.23 = (bf16[40,1024]{1,0:T(8,128)(2,1)S(1)}, bf16[40,1024]{1,0:T(8,128)(2,1)S(1)}, u32[]{:S(2)}, u32[]{:S(2)}) collective-permute-start(bf16[40,1024]{1,0:T(8,128)(2,1)S(1)} %convert_add_fusion.2), channel_id=1, source_target_pairs={{0,48},{16,0},{32,16},{48,32},{1,49},{17,1},{33,17},{49,33},{2,50}... | collective-permute-start | bytes 245768 | tf_op jit(solution)/shard_map/ppermute | solution.py:391
  135.6 1.9 %collective-permute-done.21 = bf16[40,1024]{1,0:T(8,128)(2,1)S(1)} collective-permute-done((bf16[40,1024]{1,0:T(8,128)(2,1)S(1)}, bf16[40,1024]{1,0:T(8,128)(2,1)S(1)}, u32[]{:S(2)}, u32[]{:S(2)}) %collective-permute-start.21) | collective-permute-done | bytes 81952 | tf_op jit(solution)/shard_map/ppermute | solution.py:391
  137.5 2.8 %collective-permute-start.26 = (bf16[40,1024]{1,0:T(8,128)(2,1)S(1)}, bf16[40,1024]{1,0:T(8,128)(2,1)S(1)}, u32[]{:S(2)}, u32[]{:S(2)}) collective-permute-start(bf16[40,1024]{1,0:T(8,128)(2,1)S(1)} %add_convert_fusion), channel_id=1, source_target_pairs={{0,12},{4,0},{8,4},{12,8},{1,13},{5,1},{9,5},{13,9},{2,14},{6,2},{... | collective-permute-start | bytes 245768 | tf_op jit(solution)/shard_map/ppermute | solution.py:391
  141.7 3.6 %collective-permute-done.25 = bf16[40,1024]{1,0:T(8,128)(2,1)S(1)} collective-permute-done((bf16[40,1024]{1,0:T(8,128)(2,1)S(1)}, bf16[40,1024]{1,0:T(8,128)(2,1)S(1)}, u32[]{:S(2)}, u32[]{:S(2)}) %collective-permute-start.25) | collective-permute-done | bytes 81952 | tf_op jit(solution)/shard_map/ppermute | solution.py:391
  146.3 1.1 split_rows.1
  147.3 7.5 %all-to-all-start.3 = ((bf16[32,24,180]{2,1,0:T(8,128)(2,1)}), bf16[32,24,180]{2,1,0:T(8,128)(2,1)S(1)}, u32[]{:S(2)}, u32[]{:S(2)}) async-start(bf16[32,24,180]{2,1,0:T(8,128)(2,1)} %split_rows.1), calls=%async_computation.3 | async-start | bytes 786432 | tf_op jit(solution)/shard_map/all_to_all | solution.py:593
  154.8 5.2 %collective-permute-start.28 = (bf16[40,1024]{1,0:T(8,128)(2,1)S(1)}, bf16[40,1024]{1,0:T(8,128)(2,1)S(1)}, u32[]{:S(2)}, u32[]{:S(2)}) collective-permute-start(bf16[40,1024]{1,0:T(8,128)(2,1)S(1)} %convert_add_fusion.1), channel_id=1, source_target_pairs={{0,2},{1,3},{2,0},{3,1},{4,6},{5,7},{6,4},{7,5},{8,10},{9,11},{10,... | collective-permute-start | bytes 245768 | tf_op jit(solution)/shard_map/ppermute | solution.py:391
  160.1 4.0 %collective-permute-start.27 = (bf16[40,1024]{1,0:T(8,128)(2,1)S(1)}, bf16[40,1024]{1,0:T(8,128)(2,1)S(1)}, u32[]{:S(2)}, u32[]{:S(2)}) collective-permute-start(bf16[40,1024]{1,0:T(8,128)(2,1)S(1)} %convert_add_fusion.1), channel_id=1, source_target_pairs={{0,1},{1,2},{2,3},{3,0},{4,5},{5,6},{6,7},{7,4},{8,9},{9,10},{10,1... | collective-permute-start | bytes 245768 | tf_op jit(solution)/shard_map/ppermute | solution.py:391
  164.2 3.5 %copy-done = bf16[1536,2880]{0,1:T(8,128)(2,1)S(1)} copy-done((bf16[1536,2880]{0,1:T(8,128)(2,1)S(1)}, bf16[1536,2880]{0,1:T(8,128)(2,1)}, u32[]{:S(2)}) %copy-start) | copy-done | bytes 8847384
  167.7 2.8 %token_grads.1 = bf16[128,1536]{1,0:T(8,128)(2,1)} custom-call(bf16[3,128,1024]{2,1,0:T(8,128)(2,1)S(1)} %copy-done.9, bf16[2880,1536]{1,0:T(8,128)(2,1)S(1)} %bitcast.27), custom_call_target="tpu_custom_call" | custom-call | flops 1200000000 | bytes 11000000 | tf_op jit(solution)/shard_map/token_grads/pallas_call | solution.py:596
  170.5 6.0 %collective-permute-done.29 = bf16[40,1024]{1,0:T(8,128)(2,1)S(1)} collective-permute-done((bf16[40,1024]{1,0:T(8,128)(2,1)S(1)}, bf16[40,1024]{1,0:T(8,128)(2,1)S(1)}, u32[]{:S(2)}, u32[]{:S(2)}) %collective-permute-start.29) | collective-permute-done | bytes 81952 | tf_op jit(solution)/shard_map/ppermute | solution.py:391
  (111 shorter events, 26.0 us)
Async XLA Ops:
  2.7 7.4 %collective-permute-start.1 = (bf16[16,2560]{1,0:T(8,128)(2,1)}, bf16[16,2560]{1,0:T(8,128)(2,1)S(1)}, u32[]{:S(2)}, u32[]{:S(2)}) collective-permute-start(bf16[16,2560]{1,0:T(8,128)(2,1)} %get-tuple-element.49), channel_id=1, source_target_pairs={{4,0},{8,4},{12,8},{16,12},{20,16},{24,20},{28,24},{32,28},{36,32}... | collective-permute-start | bytes 245768 | tf_op jit(solution)/shard_map/ppermute | solution.py:438
  4.0 6.1 %collective-permute-start = (bf16[16,1536]{1,0:T(8,128)(2,1)}, bf16[16,1536]{1,0:T(8,128)(2,1)S(1)}, u32[]{:S(2)}, u32[]{:S(2)}) collective-permute-start(bf16[16,1536]{1,0:T(8,128)(2,1)} %get-tuple-element.48), channel_id=1, source_target_pairs={{0,4},{4,8},{8,12},{12,16},{16,20},{20,24},{24,28},{28,32},{32,36}... | collective-permute-start | bytes 147464 | tf_op jit(solution)/shard_map/ppermute | solution.py:437
  10.1 30.6 %all-to-all-start = ((f32[64,8,128]{2,1,0:T(8,128)}), f32[64,8,128]{2,1,0:T(8,128)S(1)}, u32[]{:S(2)}, u32[]{:S(2)}) async-start(f32[64,8,128]{2,1,0:T(8,128)} %get-tuple-element.55), calls=%async_computation | async-start | bytes 524288 | tf_op jit(solution)/shard_map/all_to_all | solution.py:440
  27.1 1.0 copy-start.1
  28.1 0.9 copy-start.7
  37.9 1.2 copy-start.3
  40.7 17.7 %copy-start.2 = (bf16[1,128,1536]{2,1,0:T(8,128)(2,1)S(1)}, bf16[1,128,1536]{2,1,0:T(8,128)(2,1)}, u32[]{:S(2)}) copy-start(bf16[1,128,1536]{2,1,0:T(8,128)(2,1)} %param.6) | copy-start | bytes 1179652
  40.7 1.1 copy-start.16
  45.1 1.0 copy-start.5
  46.7 36.6 %copy-start.6 = (f32[2,16,8,1024]{3,2,1,0:T(8,128)S(1)}, f32[2,16,8,1024]{3,2,1,0:T(8,128)}, u32[]{:S(2)}) copy-start(f32[2,16,8,1024]{3,2,1,0:T(8,128)} %copy-done.5) | copy-start | bytes 3145732
  46.7 3.9 %collective-permute-start.4 = (bf16[32,1024]{1,0:T(8,128)(2,1)}, bf16[32,1024]{1,0:T(8,128)(2,1)}, u32[]{:S(2)}, u32[]{:S(2)}) collective-permute-start(bf16[32,1024]{1,0:T(8,128)(2,1)} %get-tuple-element.63), channel_id=1, source_target_pairs={{0,12},{4,0},{8,4},{12,8},{1,13},{5,1},{9,5},{13,9},{2,14},{6,2},{... | collective-permute-start | bytes 196616 | tf_op jit(solution)/shard_map/ppermute | solution.py:391
  48.9 5.0 %collective-permute-start.3 = (bf16[32,1024]{1,0:T(8,128)(2,1)}, bf16[32,1024]{1,0:T(8,128)(2,1)}, u32[]{:S(2)}, u32[]{:S(2)}) collective-permute-start(bf16[32,1024]{1,0:T(8,128)(2,1)} %get-tuple-element.63), channel_id=1, source_target_pairs={{0,8},{4,12},{8,0},{12,4},{1,9},{5,13},{9,1},{13,5},{2,10},{6,14},... | collective-permute-start | bytes 196616 | tf_op jit(solution)/shard_map/ppermute | solution.py:391
  49.5 5.1 %collective-permute-start.2 = (bf16[32,1024]{1,0:T(8,128)(2,1)}, bf16[32,1024]{1,0:T(8,128)(2,1)}, u32[]{:S(2)}, u32[]{:S(2)}) collective-permute-start(bf16[32,1024]{1,0:T(8,128)(2,1)} %get-tuple-element.63), channel_id=1, source_target_pairs={{0,4},{4,8},{8,12},{12,0},{1,5},{5,9},{9,13},{13,1},{2,6},{6,10},{... | collective-permute-start | bytes 196616 | tf_op jit(solution)/shard_map/ppermute | solution.py:391
  54.5 0.9 copy-start.28
  58.4 13.0 %collective-permute-start.15 = (bf16[128,1536]{1,0:T(8,128)(2,1)S(1)}, bf16[128,1536]{1,0:T(8,128)(2,1)}, u32[]{:S(2)}, u32[]{:S(2)}) collective-permute-start(bf16[128,1536]{1,0:T(8,128)(2,1)S(1)} %bitcast.30), channel_id=1, source_target_pairs={{0,12},{4,8},{8,4},{12,0},{1,13},{5,9},{9,5},{13,1},{2,14},{6,10},... | collective-permute-start | bytes 1179656 | tf_op jit(solution)/shard_map/ppermute | solution.py:509
  58.7 12.7 %collective-permute-start.14 = (bf16[128,1536]{1,0:T(8,128)(2,1)S(1)}, bf16[128,1536]{1,0:T(8,128)(2,1)}, u32[]{:S(2)}, u32[]{:S(2)}) collective-permute-start(bf16[128,1536]{1,0:T(8,128)(2,1)S(1)} %bitcast.31), channel_id=1, source_target_pairs={{0,4},{4,0},{8,12},{12,8},{1,5},{5,1},{9,13},{13,9},{2,6},{6,2},{1... | collective-permute-start | bytes 1179656 | tf_op jit(solution)/shard_map/ppermute | solution.py:508
  59.1 4.6 %collective-permute-start.7 = (bf16[32,1024]{1,0:T(8,128)(2,1)}, bf16[32,1024]{1,0:T(8,128)(2,1)}, u32[]{:S(2)}, u32[]{:S(2)}) collective-permute-start(bf16[32,1024]{1,0:T(8,128)(2,1)} %get-tuple-element.67), channel_id=1, source_target_pairs={{0,48},{16,0},{32,16},{48,32},{1,49},{17,1},{33,17},{49,33},{2,50}... | collective-permute-start | bytes 196616 | tf_op jit(solution)/shard_map/ppermute | solution.py:391
  62.1 4.3 %collective-permute-start.6 = (bf16[32,1024]{1,0:T(8,128)(2,1)}, bf16[32,1024]{1,0:T(8,128)(2,1)}, u32[]{:S(2)}, u32[]{:S(2)}) collective-permute-start(bf16[32,1024]{1,0:T(8,128)(2,1)} %get-tuple-element.67), channel_id=1, source_target_pairs={{0,32},{16,48},{32,0},{48,16},{1,33},{17,49},{33,1},{49,17},{2,34}... | collective-permute-start | bytes 196616 | tf_op jit(solution)/shard_map/ppermute | solution.py:391
  62.1 5.3 %collective-permute-start.5 = (bf16[32,1024]{1,0:T(8,128)(2,1)}, bf16[32,1024]{1,0:T(8,128)(2,1)}, u32[]{:S(2)}, u32[]{:S(2)}) collective-permute-start(bf16[32,1024]{1,0:T(8,128)(2,1)} %get-tuple-element.67), channel_id=1, source_target_pairs={{0,16},{16,32},{32,48},{48,0},{1,17},{17,33},{33,49},{49,1},{2,18}... | collective-permute-start | bytes 196616 | tf_op jit(solution)/shard_map/ppermute | solution.py:391
  71.4 47.7 %collective-permute-start.16 = (bf16[128,1536]{1,0:T(8,128)(2,1)}, bf16[128,1536]{1,0:T(8,128)(2,1)}, u32[]{:S(2)}, u32[]{:S(2)}) collective-permute-start(bf16[128,1536]{1,0:T(8,128)(2,1)} %collective-permute-done.14.refs_1_), channel_id=1, source_target_pairs={{0,12},{4,8},{8,4},{12,0},{1,13},{5,9},{9,5},{13,1},{2,14},{6,10},... | collective-permute-start | bytes 1179656 | tf_op jit(solution)/shard_map/ppermute | solution.py:512
  73.3 4.4 %collective-permute-start.10 = (bf16[32,1024]{1,0:T(8,128)(2,1)}, bf16[32,1024]{1,0:T(8,128)(2,1)S(1)}, u32[]{:S(2)}, u32[]{:S(2)}) collective-permute-start(bf16[32,1024]{1,0:T(8,128)(2,1)} %copy-done.29), channel_id=1, source_target_pairs={{0,192},{64,0},{128,64},{192,128},{1,193},{65,1},{129,65},{193,129... | collective-permute-start | bytes 196616 | tf_op jit(solution)/shard_map/ppermute | solution.py:391
  76.1 4.9 %collective-permute-start.9 = (bf16[32,1024]{1,0:T(8,128)(2,1)}, bf16[32,1024]{1,0:T(8,128)(2,1)S(1)}, u32[]{:S(2)}, u32[]{:S(2)}) collective-permute-start(bf16[32,1024]{1,0:T(8,128)(2,1)} %copy-done.29), channel_id=1, source_target_pairs={{0,128},{64,192},{128,0},{192,64},{1,129},{65,193},{129,1},{193,65... | collective-permute-start | bytes 196616 | tf_op jit(solution)/shard_map/ppermute | solution.py:391
  76.4 5.2 %collective-permute-start.8 = (bf16[32,1024]{1,0:T(8,128)(2,1)}, bf16[32,1024]{1,0:T(8,128)(2,1)S(1)}, u32[]{:S(2)}, u32[]{:S(2)}) collective-permute-start(bf16[32,1024]{1,0:T(8,128)(2,1)} %copy-done.29), channel_id=1, source_target_pairs={{0,64},{64,128},{128,192},{192,0},{1,65},{65,129},{129,193},{193,1... | collective-permute-start | bytes 196616 | tf_op jit(solution)/shard_map/ppermute | solution.py:391
  83.3 1.4 copy-start.4
  84.7 1.1 copy-start.14
  100.3 23.2 %copy-start.12 = (f32[40,1024]{1,0:T(8,128)S(1)}, f32[40,1024]{1,0:T(8,128)}, u32[]{:S(2)}) copy-start(f32[40,1024]{1,0:T(8,128)} %copy-done.11) | copy-start | bytes 491524
  100.3 23.2 %all-to-all-start.1 = ((bf16[8,360,128]{2,1,0:T(8,128)(2,1)}), bf16[8,360,128]{2,1,0:T(8,128)(2,1)S(1)}, u32[]{:S(2)}, u32[]{:S(2)}) async-start(bf16[8,360,128]{2,1,0:T(8,128)(2,1)} %copy-done.10), calls=%async_computation.1 | async-start | bytes 1474560 | tf_op jit(solution)/shard_map/all_to_all | solution.py:568
  112.2 5.6 %collective-permute-start.12 = (bf16[40,1024]{1,0:T(8,128)(2,1)S(1)}, bf16[40,1024]{1,0:T(8,128)(2,1)S(1)}, u32[]{:S(2)}, u32[]{:S(2)}) collective-permute-start(bf16[40,1024]{1,0:T(8,128)(2,1)S(1)} %convert_element_type.75), channel_id=1, source_target_pairs={{0,128},{64,192},{128,0},{192,64},{1,129},{65,193},{129,1},{193,65... | collective-permute-start | bytes 245768 | tf_op jit(solution)/shard_map/ppermute | solution.py:391
  113.3 6.5 %collective-permute-start.11 = (bf16[40,1024]{1,0:T(8,128)(2,1)S(1)}, bf16[40,1024]{1,0:T(8,128)(2,1)S(1)}, u32[]{:S(2)}, u32[]{:S(2)}) collective-permute-start(bf16[40,1024]{1,0:T(8,128)(2,1)S(1)} %convert_element_type.75), channel_id=1, source_target_pairs={{0,64},{64,128},{128,192},{192,0},{1,65},{65,129},{129,193},{193,1... | collective-permute-start | bytes 245768 | tf_op jit(solution)/shard_map/ppermute | solution.py:391
  113.3 10.2 %collective-permute-start.17 = (bf16[128,1536]{1,0:T(8,128)(2,1)S(1)}, bf16[128,1536]{1,0:T(8,128)(2,1)S(1)}, u32[]{:S(2)}, u32[]{:S(2)}) collective-permute-start(bf16[128,1536]{1,0:T(8,128)(2,1)S(1)} %bitcast.32), channel_id=1, source_target_pairs={{0,1},{1,0},{2,3},{3,2},{4,5},{5,4},{6,7},{7,6},{8,9},{9,8},{10,11... | collective-permute-start | bytes 1179656 | tf_op jit(solution)/shard_map/ppermute | solution.py:561
  113.8 9.7 %collective-permute-start.18 = (bf16[128,1536]{1,0:T(8,128)(2,1)}, bf16[128,1536]{1,0:T(8,128)(2,1)S(1)}, u32[]{:S(2)}, u32[]{:S(2)}) collective-permute-start(bf16[128,1536]{1,0:T(8,128)(2,1)} %collective-permute-done.14.refs_1_), channel_id=1, source_target_pairs={{0,1},{1,0},{2,3},{3,2},{4,5},{5,4},{6,7},{7,6},{8,9},{9,8},{10,11... | collective-permute-start | bytes 1179656 | tf_op jit(solution)/shard_map/ppermute | solution.py:561
  117.8 5.7 %collective-permute-start.19 = (bf16[128,1536]{1,0:T(8,128)(2,1)}, bf16[128,1536]{1,0:T(8,128)(2,1)S(1)}, u32[]{:S(2)}, u32[]{:S(2)}) collective-permute-start(bf16[128,1536]{1,0:T(8,128)(2,1)} %collective-permute-done.15.refs_2_), channel_id=1, source_target_pairs={{0,1},{1,0},{2,3},{3,2},{4,5},{5,4},{6,7},{7,6},{8,9},{9,8},{10,11... | collective-permute-start | bytes 1179656 | tf_op jit(solution)/shard_map/ppermute | solution.py:561
  119.1 4.4 %collective-permute-start.20 = (bf16[128,1536]{1,0:T(8,128)(2,1)}, bf16[128,1536]{1,0:T(8,128)(2,1)S(1)}, u32[]{:S(2)}, u32[]{:S(2)}) collective-permute-start(bf16[128,1536]{1,0:T(8,128)(2,1)} %collective-permute-done.16.refs_3_), channel_id=1, source_target_pairs={{0,1},{1,0},{2,3},{3,2},{4,5},{5,4},{6,7},{7,6},{8,9},{9,8},{10,11... | collective-permute-start | bytes 1179656 | tf_op jit(solution)/shard_map/ppermute | solution.py:561
  119.8 3.6 %collective-permute-start.13 = (bf16[40,1024]{1,0:T(8,128)(2,1)S(1)}, bf16[40,1024]{1,0:T(8,128)(2,1)S(1)}, u32[]{:S(2)}, u32[]{:S(2)}) collective-permute-start(bf16[40,1024]{1,0:T(8,128)(2,1)S(1)} %convert_element_type.75), channel_id=1, source_target_pairs={{0,192},{64,0},{128,64},{192,128},{1,193},{65,1},{129,65},{193,129... | collective-permute-start | bytes 245768 | tf_op jit(solution)/shard_map/ppermute | solution.py:391
  127.6 13.8 %copy-start.30 = (f32[15,16]{1,0:T(8,128)S(1)}, f32[15,16]{1,0:T(8,128)}, u32[]{:S(2)}) copy-start(f32[15,16]{1,0:T(8,128)} %get-tuple-element.88) | copy-start | bytes 2884
  127.6 18.7 %all-to-all-start.2 = ((bf16[4,360,384]{2,1,0:T(8,128)(2,1)}), bf16[4,360,384]{2,1,0:T(8,128)(2,1)S(1)}, u32[]{:S(2)}, u32[]{:S(2)}) async-start(bf16[4,360,384]{2,1,0:T(8,128)(2,1)} %weight_term.1), calls=%async_computation.2 | async-start | bytes 2211840 | tf_op jit(solution)/shard_map/all_to_all | solution.py:580
  131.2 33.0 %copy-start.9 = (bf16[3,128,1024]{2,1,0:T(8,128)(2,1)S(1)}, bf16[3,128,1024]{2,1,0:T(8,128)(2,1)}, u32[]{:S(2)}) copy-start(bf16[3,128,1024]{2,1,0:T(8,128)(2,1)} %copy-done.8) | copy-start | bytes 2359300
  131.2 4.3 %collective-permute-start.22 = (bf16[40,1024]{1,0:T(8,128)(2,1)S(1)}, bf16[40,1024]{1,0:T(8,128)(2,1)S(1)}, u32[]{:S(2)}, u32[]{:S(2)}) collective-permute-start(bf16[40,1024]{1,0:T(8,128)(2,1)S(1)} %convert_add_fusion.2), channel_id=1, source_target_pairs={{0,32},{16,48},{32,0},{48,16},{1,33},{17,49},{33,1},{49,17},{2,34}... | collective-permute-start | bytes 245768 | tf_op jit(solution)/shard_map/ppermute | solution.py:391
  132.2 5.3 %collective-permute-start.21 = (bf16[40,1024]{1,0:T(8,128)(2,1)S(1)}, bf16[40,1024]{1,0:T(8,128)(2,1)S(1)}, u32[]{:S(2)}, u32[]{:S(2)}) collective-permute-start(bf16[40,1024]{1,0:T(8,128)(2,1)S(1)} %convert_add_fusion.2), channel_id=1, source_target_pairs={{0,16},{16,32},{32,48},{48,0},{1,17},{17,33},{33,49},{49,1},{2,18}... | collective-permute-start | bytes 245768 | tf_op jit(solution)/shard_map/ppermute | solution.py:391
  132.4 5.1 %collective-permute-start.23 = (bf16[40,1024]{1,0:T(8,128)(2,1)S(1)}, bf16[40,1024]{1,0:T(8,128)(2,1)S(1)}, u32[]{:S(2)}, u32[]{:S(2)}) collective-permute-start(bf16[40,1024]{1,0:T(8,128)(2,1)S(1)} %convert_add_fusion.2), channel_id=1, source_target_pairs={{0,48},{16,0},{32,16},{48,32},{1,49},{17,1},{33,17},{49,33},{2,50}... | collective-permute-start | bytes 245768 | tf_op jit(solution)/shard_map/ppermute | solution.py:391
  137.5 4.2 %collective-permute-start.26 = (bf16[40,1024]{1,0:T(8,128)(2,1)S(1)}, bf16[40,1024]{1,0:T(8,128)(2,1)S(1)}, u32[]{:S(2)}, u32[]{:S(2)}) collective-permute-start(bf16[40,1024]{1,0:T(8,128)(2,1)S(1)} %add_convert_fusion), channel_id=1, source_target_pairs={{0,12},{4,0},{8,4},{12,8},{1,13},{5,1},{9,5},{13,9},{2,14},{6,2},{... | collective-permute-start | bytes 245768 | tf_op jit(solution)/shard_map/ppermute | solution.py:391
  140.3 5.1 %collective-permute-start.25 = (bf16[40,1024]{1,0:T(8,128)(2,1)S(1)}, bf16[40,1024]{1,0:T(8,128)(2,1)S(1)}, u32[]{:S(2)}, u32[]{:S(2)}) collective-permute-start(bf16[40,1024]{1,0:T(8,128)(2,1)S(1)} %add_convert_fusion), channel_id=1, source_target_pairs={{0,8},{4,12},{8,0},{12,4},{1,9},{5,13},{9,1},{13,5},{2,10},{6,14},... | collective-permute-start | bytes 245768 | tf_op jit(solution)/shard_map/ppermute | solution.py:391
  140.8 5.4 %collective-permute-start.24 = (bf16[40,1024]{1,0:T(8,128)(2,1)S(1)}, bf16[40,1024]{1,0:T(8,128)(2,1)S(1)}, u32[]{:S(2)}, u32[]{:S(2)}) collective-permute-start(bf16[40,1024]{1,0:T(8,128)(2,1)S(1)} %add_convert_fusion), channel_id=1, source_target_pairs={{0,4},{4,8},{8,12},{12,0},{1,5},{5,9},{9,13},{13,1},{2,6},{6,10},{... | collective-permute-start | bytes 245768 | tf_op jit(solution)/shard_map/ppermute | solution.py:391
  147.3 30.8 %all-to-all-start.3 = ((bf16[32,24,180]{2,1,0:T(8,128)(2,1)}), bf16[32,24,180]{2,1,0:T(8,128)(2,1)S(1)}, u32[]{:S(2)}, u32[]{:S(2)}) async-start(bf16[32,24,180]{2,1,0:T(8,128)(2,1)} %split_rows.1), calls=%async_computation.3 | async-start | bytes 786432 | tf_op jit(solution)/shard_map/all_to_all | solution.py:593
  154.8 15.7 %collective-permute-start.28 = (bf16[40,1024]{1,0:T(8,128)(2,1)S(1)}, bf16[40,1024]{1,0:T(8,128)(2,1)S(1)}, u32[]{:S(2)}, u32[]{:S(2)}) collective-permute-start(bf16[40,1024]{1,0:T(8,128)(2,1)S(1)} %convert_add_fusion.1), channel_id=1, source_target_pairs={{0,2},{1,3},{2,0},{3,1},{4,6},{5,7},{6,4},{7,5},{8,10},{9,11},{10,... | collective-permute-start | bytes 245768 | tf_op jit(solution)/shard_map/ppermute | solution.py:391
  160.1 10.4 %collective-permute-start.27 = (bf16[40,1024]{1,0:T(8,128)(2,1)S(1)}, bf16[40,1024]{1,0:T(8,128)(2,1)S(1)}, u32[]{:S(2)}, u32[]{:S(2)}) collective-permute-start(bf16[40,1024]{1,0:T(8,128)(2,1)S(1)} %convert_add_fusion.1), channel_id=1, source_target_pairs={{0,1},{1,2},{2,3},{3,0},{4,5},{5,6},{6,7},{7,4},{8,9},{9,10},{10,1... | collective-permute-start | bytes 245768 | tf_op jit(solution)/shard_map/ppermute | solution.py:391
  164.1 12.4 %collective-permute-start.29 = (bf16[40,1024]{1,0:T(8,128)(2,1)S(1)}, bf16[40,1024]{1,0:T(8,128)(2,1)S(1)}, u32[]{:S(2)}, u32[]{:S(2)}) collective-permute-start(bf16[40,1024]{1,0:T(8,128)(2,1)S(1)} %convert_add_fusion.1), channel_id=1, source_target_pairs={{0,3},{1,0},{2,1},{3,2},{4,7},{5,4},{6,5},{7,6},{8,11},{9,8},{10,9... | collective-permute-start | bytes 245768 | tf_op jit(solution)/shard_map/ppermute | solution.py:391
  164.2 3.5 %copy-start = (bf16[1536,2880]{0,1:T(8,128)(2,1)S(1)}, bf16[1536,2880]{0,1:T(8,128)(2,1)}, u32[]{:S(2)}) copy-start(bf16[1536,2880]{0,1:T(8,128)(2,1)} %param.7) | copy-start | bytes 26542084
  (17 other events, 13.4 us)

commit v5 on v4

--- a/solution.py
+++ b/solution.py
@@ -22,22 +22,28 @@
 
 
 def project(
-    tp, tk, nexts, wt, taps, cott, zf_out, mix_out, cots_out, us, dls,
-    acc, turn, wbuf, zf, mix, cots, sems, zsem, tsems,
+    tp, nexts, taps, feats, cott, wt, zf_out, mix_out, cots_out, us, dls,
+    acc, turn, wbuf, zf, mix, cots, tk, cbuf, sems, zsem, tsems, isems,
 ):
     steps, _, kblk = wbuf.shape
+    arrivals = [
+        pltpu.make_async_copy(feats, tk, isems.at[0]),
+        pltpu.make_async_copy(cott, cbuf, isems.at[1]),
+    ]
+    arrivals[0].start()
     copies = [
         pltpu.make_async_copy(wt.at[:, pl.ds(k * kblk, kblk)], wbuf.at[k], sems.at[k])
         for k in range(steps)
     ]
     for copy in copies:
         copy.start()
+    arrivals[1].start()
     width, own = cott.shape
     depth = tk.shape[1]
     turn[...] = jnp.zeros(turn.shape, F32)
-    turn[0:width, :] = cott[...].astype(F32)
     for g in range(3):
         zf[g, :, width:] = jnp.zeros((zf.shape[1], PADC - width), F32)
+    arrivals[0].wait()
     for k in range(steps):
         cols = slice(k * kblk, (k + 1) * kblk)
         rows = jnp.concatenate([tp[:, cols], tk[:, cols], nexts[:, cols]], axis=0)
@@ -53,6 +59,8 @@
                 zf[g, :, 0:width] = rounded(total[:, g * width : (g + 1) * width])
     zcopy = pltpu.make_async_copy(zf, zf_out, zsem)
     zcopy.start()
+    arrivals[1].wait()
+    turn[0:width, :] = cbuf[...].astype(F32)
 
     def out_copies(ct):
         lanes = pl.ds(pl.multiple_of(ct * 128, 128), 128)
@@ -118,13 +126,9 @@
     copies[1].wait()
     size = jnp.sqrt(one_minus_exp(2.0 * rbuf[...]))
     amp[...] = size
-    rate = rbuf[...]
-    gain = sbuf[...] * size
-    for j in range(count):
-        row, lane = j // 4, (j % 4) * 2 * MODES
-        held[row : row + 1, lane : lane + MODES] = rate[j : j + 1, :]
-        held[row : row + 1, lane + MODES : lane + 2 * MODES] = gain[j : j + 1, :]
-    block[...] = jnp.broadcast_to(held[...][None], block.shape)
+    held[0:count, 0:MODES] = rbuf[...]
+    held[0:count, MODES : 2 * MODES] = sbuf[...] * size
+    block[...] = held[...].T[0 : 2 * MODES, 0:count]
     copies[2].wait()
     turn[0:width, :] = cbuf[...].astype(F32)
     for c in range(PADC // 128):
@@ -137,32 +141,26 @@
     copies[5].wait()
 
 
-def joined_params(blocks, order, left):
-    row = lax.broadcasted_iota(jnp.int32, (PADC, PADC), 0)
-    col = lax.broadcasted_iota(jnp.int32, (PADC, PADC), 1)
-    goal = 15 * lax.bitwise_and(row, 63) + lax.shift_right_logical(row, 6)
-    order[...] = jnp.where((goal == col) & (row < 960), 1.0, 0.0).astype(BF16)
-    left[...] = jnp.zeros(left.shape, F32)
-    count = blocks.shape[0]
-    for c in range(4):
-        flipped = blocks[:, c, :].T
-        for p in range(4):
-            j = 4 * c + p
-            if j < 15:
-                left[:, j * count : (j + 1) * count] = flipped[p * 2 * MODES : (p + 1) * 2 * MODES, :]
-    rest = left[...]
-    parts = []
-    for _ in range(3):
-        part = rest.astype(BF16)
-        parts.append(part)
-        rest = rest - part.astype(F32)
-    out = jnp.dot(jnp.concatenate(parts, axis=0), order[...], preferred_element_type=F32)
-    size = 2 * MODES
-    return out[0:size] + out[size : 2 * size] + out[2 * size : 3 * size]
-
-
-def end_states(blocks, us, dls, rates, gains, es, ends, endb, ut, dt, left, order):
-    joined = joined_params(blocks, order, left)
+def placed(me, refs, held, goal):
+    wide = refs[0].shape[1]
+    total = None
+    for d, ref in enumerate(refs):
+        held[...] = jnp.zeros(held.shape, F32)
+        held[:, 0:wide] = ref[...]
+        part = pltpu.roll(held[...], lax.rem(me + (4 - d), 4) * wide, 1)
+        total = part if total is None else total + part
+    return total[:, 0:goal]
+
+
+def make_join(axis):
+    def join_params(place, r0, r1, r2, r3, out, held):
+        out[...] = placed(place[axis], (r0, r1, r2, r3), held, out.shape[1])
+
+    return join_params
+
+
+def end_states(place, r0, r1, r2, r3, us, dls, rates, gains, es, ends, endb, ut, dt, held):
+    joined = placed(place[0], (r0, r1, r2, r3), held, PADC)
     rates[...] = joined[0:MODES]
     gains[...] = joined[MODES : 2 * MODES]
     sub = lax.broadcasted_iota(jnp.int32, (8, 128), 0)
@@ -207,9 +205,9 @@
     endb[...] = ends[...].astype(BF16)
 
 
-def make_level(span):
+def make_level(axis, span):
     def level(place, own, r1, r2, r3, rates, total, totalb, prefix):
-        me = place[0]
+        me = place[axis]
         rate = rates[...] * float(span)
         before = jnp.zeros((MODES, PADC), F32)
         after = before
@@ -240,7 +238,7 @@
 
 def finish(
     place, zf, mix, es, py, pz, px, taps, rates, reff, cots,
-    outt, dz, dzb, sums, inc, ut, dt, longs, dps, dms, dzt,
+    outt, dz, dzb, sumb, sums, inc, ut, dt, longs, dps, dms, dzt,
 ):
     own = dz.shape[1]
     rate = rates[...]
@@ -318,6 +316,8 @@
         dz[g] = total.astype(BF16)
         dzt[g, pl.ds(pl.multiple_of(ct * 128, 128), 128), :] = total.T
 
+    sumb[...] = sums[...].astype(BF16)
+
     @pl.when(ct == pl.num_programs(0) - 1)
     def _():
         piece = dzb.shape[1] // 2
@@ -353,8 +353,8 @@
 
 def weight_term(place, arrived, *refs):
     *tokens, term = refs
-    me = place[0]
-    core = place[1]
+    me = place[2]
+    core = place[3]
     chunk = term.shape[2]
     slots = (me, lax.bitwise_xor(me, 1), 3 - me, lax.bitwise_xor(3 - me, 1))
     pairs = []
@@ -387,12 +387,46 @@
             blocks[2 * q + h] = part.astype(BF16)
 
 
+def make_sum(final):
+    def add_parts(p0, p1, p2, p3, out):
+        total = p0[...].astype(F32) + p1[...].astype(F32) + p2[...].astype(F32) + p3[...].astype(F32)
+        out[...] = total.astype(BF16)
+
+    def close_sums(place, amp, p0, p1, p2, p3, grad_taps, grad_res, held):
+        total = p0[...].astype(F32) + p1[...].astype(F32) + p2[...].astype(F32) + p3[...].astype(F32)
+        total = total * final
+        width = grad_taps.shape[1] // 3
+        for g in range(3):
+            grad_taps[:, g * width : (g + 1) * width] = total[8 * g : 8 * g + 7, 0:width]
+        count = grad_res.shape[0]
+        index = (place[0] * 4 + place[1]) * 4 + place[2]
+        moved = pltpu.roll(total[24:40, :], lax.rem(PADC - index * count, PADC), 1)
+        held[...] = jnp.zeros(held.shape, F32)
+        held[0:MODES, :] = moved[:, 0:128]
+        grad_res[...] = held[...].T[0:count, 0:MODES] * amp[...]
+
+    return close_sums if final else add_parts
+
+
+def make_close(scale):
+    def close_weight(last, out):
+        fblk, piece = last.shape[1:]
+        for y in range(4):
+            total = jnp.zeros((fblk, piece), F32)
+            for z in range(4):
+                for h in range(2):
+                    total = total + last[(z * 4 + y) * 2 + h].astype(F32)
+            out[:, y * piece : (y + 1) * piece] = (total * scale).astype(BF16)
+
+    return close_weight
+
+
 def ring(a, ax, d):
     return lax.ppermute(a, ax, [(i, (i + d) % 4) for i in range(4)])
 
 
 def params(mb):
-    return pltpu.CompilerParams(vmem_limit_bytes=mb * 1024 * 1024)
+    return pltpu.CompilerParams(vmem_limit_bytes=int(mb * 1024 * 1024))
 
 
 def local(tokens, w_in, conv_taps, residues, rates, cotangent):
@@ -405,7 +439,8 @@
     piece = chans // 16
     fblk = depth // count
     xi, zi, yi = lax.axis_index("x"), lax.axis_index("zl"), lax.axis_index("y")
-    ci = lax.axis_index("core")
+    place = jnp.stack([xi, zi, yi, lax.axis_index("core")]).astype(jnp.int32)
+    feats, cot, rates, place = lax.optimization_barrier((feats, cot, rates, place))
     ctx = ("x", "zl", "y")
     scale = 1.0 / math.sqrt(4 * count * own)
     smem = pl.BlockSpec(memory_space=pltpu.SMEM)
@@ -418,12 +453,12 @@
         out_shape=[
             jax.ShapeDtypeStruct((HALO, depth + PADC), BF16),
             jax.ShapeDtypeStruct((HALO, depth), BF16),
-            jax.ShapeDtypeStruct((count, 8, 128), F32),
+            jax.ShapeDtypeStruct((2 * MODES, width // count), F32),
             jax.ShapeDtypeStruct((3, 8, PADC), F32),
             jax.ShapeDtypeStruct(rates.shape, F32),
         ],
         scratch_shapes=[
-            pltpu.VMEM((8, 128), F32),
+            pltpu.VMEM((128, 128), F32),
             pltpu.VMEM((PADC, own), F32),
             pltpu.VMEM((width, own), BF16),
             pltpu.VMEM(rates.shape, F32),
@@ -431,20 +466,32 @@
             pltpu.VMEM(conv_taps.shape, F32),
             pltpu.SemaphoreType.DMA((6,)),
         ],
-        compiler_params=params(60),
+        compiler_params=params(56),
         name="prepare",
     )(feats, cot.T, rates, residues, conv_taps)
     tprev = lax.ppermute(tail, ctx, [(i, i + 1) for i in range(count - 1)])
     nexts = lax.ppermute(head, ctx, [(i, i - 1) for i in range(1, count)])
-    block, tprev, nexts = lax.optimization_barrier((block, tprev, nexts))
-    blocks = lax.all_to_all(block, ctx, split_axis=0, concat_axis=0, tiled=True)
+    held, each = block, width // count
+    for axis, ax in ((2, "y"), (1, "zl")):
+        blocks = [held] + [ring(held, ax, d) for d in (1, 2, 3)]
+        each = 4 * each
+        held = pl.pallas_call(
+            make_join(axis),
+            in_specs=[smem] + [vm] * 4,
+            out_specs=vm,
+            out_shape=jax.ShapeDtypeStruct((2 * MODES, each), F32),
+            scratch_shapes=[pltpu.VMEM((2 * MODES, 256), F32)],
+            compiler_params=params(4),
+            name="join_params",
+        )(place, *blocks)
+    blocks = [held] + [ring(held, "x", d) for d in (1, 2, 3)]
 
     kblk = 256
     ext_rows = own + 2 * HALO
     shapes = [(3, ext_rows, PADC), (3, EXT, PADC), (EXT, PADC), (EXT, PADC), (EXT, PADC)]
     zf, mix, cots, us, dls = pl.pallas_call(
         project,
-        in_specs=[vm] * 3 + [anywhere] + [vm] * 2,
+        in_specs=[vm] * 3 + [anywhere] * 3,
         out_specs=[anywhere] * 3 + [vm] * 2,
         out_shape=[jax.ShapeDtypeStruct(s, F32) for s in shapes],
         scratch_shapes=[
@@ -454,19 +501,22 @@
             pltpu.VMEM(shapes[0], F32),
             pltpu.VMEM(shapes[1], F32),
             pltpu.VMEM(shapes[2], F32),
+            pltpu.VMEM((own, depth), BF16),
+            pltpu.VMEM((width, own), BF16),
             pltpu.SemaphoreType.DMA((depth // kblk,)),
             pltpu.SemaphoreType.DMA,
             pltpu.SemaphoreType.DMA((2, PADC // 128)),
-        ],
-        compiler_params=params(48),
+            pltpu.SemaphoreType.DMA((2,)),
+        ],
+        compiler_params=params(51),
         cost_estimate=pl.CostEstimate(flops=1500000000, bytes_accessed=14000000, transcendentals=0),
         name="project",
-    )(tprev, feats, nexts, w_in.T, taps, cot.T)
-
-    blocks, us, dls = lax.optimization_barrier((blocks, us, dls))
+    )(tprev, nexts, taps, feats, cot.T, w_in.T)
+
+    *blocks, us, dls = lax.optimization_barrier((*blocks, us, dls))
     rate, gain, es, ends, endb = pl.pallas_call(
         end_states,
-        in_specs=[vm] * 3,
+        in_specs=[smem] + [vm] * 6,
         out_specs=[vm] * 5,
         out_shape=[
             jax.ShapeDtypeStruct((MODES, PADC), F32),
@@ -479,19 +529,18 @@
             pltpu.VMEM((EXT, 128), F32),
             pltpu.VMEM((EXT, 128), F32),
             pltpu.VMEM((2 * MODES, PADC), F32),
-            pltpu.VMEM((PADC, PADC), BF16),
         ],
         compiler_params=params(16),
         cost_estimate=pl.CostEstimate(flops=20000000, bytes_accessed=3000000, transcendentals=0),
         name="end_states",
-    )(blocks, us, dls)
+    )(place, *blocks, us, dls)
 
     prefixes = []
     total, sent = ends, endb
-    for ax, me, span in (("y", yi, own), ("zl", zi, 4 * own), ("x", xi, 16 * own)):
+    for axis, ax, span in ((2, "y", own), (1, "zl", 4 * own), (0, "x", 16 * own)):
         near = [ring(sent, ax, d) for d in (1, 2, 3)]
         total, sent, prefix = pl.pallas_call(
-            make_level(span),
+            make_level(axis, span),
             in_specs=[smem] + [vm] * 5,
             out_specs=[vm] * 3,
             out_shape=[
@@ -501,7 +550,7 @@
             ],
             compiler_params=params(8),
             name="level",
-        )(me.reshape(1), total, *near, rate)
+        )(place, total, *near, rate)
         prefixes.append(prefix)
         if ax == "y":
             mine, _ = lax.optimization_barrier((feats, sent))
@@ -541,9 +590,10 @@
             jax.ShapeDtypeStruct((width, own), BF16),
             jax.ShapeDtypeStruct((3, own, PADC), BF16),
             jax.ShapeDtypeStruct((8, 2 * piece, own), BF16),
-            jax.ShapeDtypeStruct((40, PADC), F32),
+            jax.ShapeDtypeStruct((40, PADC), BF16),
         ],
         scratch_shapes=[
+            pltpu.VMEM((40, 128), F32),
             pltpu.VMEM((2 * MODES, 128), F32),
             pltpu.VMEM((EXT, 128), F32),
             pltpu.VMEM((EXT, 128), F32),
@@ -552,21 +602,29 @@
             pltpu.VMEM((3, EXT, 128), F32),
             pltpu.VMEM((3, PADC, own), F32),
         ],
-        compiler_params=params(40),
+        compiler_params=params(50),
         cost_estimate=pl.CostEstimate(flops=200000000, bytes_accessed=10000000, transcendentals=0),
         name="finish",
-    )(jnp.stack([xi, zi, yi]), zf, mix, es, *prefixes, taps, rate, gain, cots)
+    )(place, zf, mix, es, *prefixes, taps, rate, gain, cots)
     output = outt.T
     blocks_of = [mine, pair, opposite, far]
     theirs = [lax.ppermute(a, "core", [(0, 1), (1, 0)]) for a in blocks_of]
 
+    def spread(a, ax):
+        return [a] + [ring(a, ax, d) for d in (1, 2, 3)]
+
     def summed(a, ax):
-        short = a.astype(BF16)
-        parts = [short] + [ring(short, ax, d) for d in (1, 2, 3)]
-        return sum(p.astype(F32) for p in parts)
+        return pl.pallas_call(
+            make_sum(None),
+            in_specs=[vm] * 4,
+            out_specs=vm,
+            out_shape=jax.ShapeDtypeStruct((40, PADC), BF16),
+            compiler_params=params(4),
+            name="add_parts",
+        )(*spread(a, ax))
 
     arrived = lax.all_to_all(dzb, ("y", "core"), split_axis=0, concat_axis=0, tiled=True)
-    sums = summed(sums, "x")
+    sums = summed(sums, "zl")
     arrived, sums = lax.optimization_barrier((arrived, sums))
     term = pl.pallas_call(
         weight_term,
@@ -576,10 +634,10 @@
         compiler_params=params(24),
         cost_estimate=pl.CostEstimate(flops=1200000000, bytes_accessed=6000000, transcendentals=0),
         name="weight_term",
-    )(jnp.stack([yi, ci]), arrived, *blocks_of, *theirs)
+    )(place, arrived, *blocks_of, *theirs)
     got = lax.all_to_all(term, "x", 0, 0, tiled=True)
     sums, _ = lax.optimization_barrier((sums, term))
-    sums = summed(summed(sums, "zl"), "y")
+    sums = summed(summed(sums, "y"), ("zh", "core"))
     got, sums = lax.optimization_barrier((got, sums))
     blocks = pl.pallas_call(
         split_rows,
@@ -592,7 +650,7 @@
     )(got)
     last = lax.all_to_all(blocks, ("zl", "y", "zh"), 0, 0, tiled=True)
     sums, dz, _ = lax.optimization_barrier((sums, dz, blocks))
-    sums = summed(sums, ("zh", "core"))
+    parts = spread(sums, "x")
     grad_feats = pl.pallas_call(
         token_grads,
         grid=(3,),
@@ -603,20 +661,30 @@
         out_specs=pl.BlockSpec((own, depth), lambda g: (0, 0)),
         out_shape=jax.ShapeDtypeStruct((own, depth), BF16),
         scratch_shapes=[pltpu.VMEM((own, depth), F32)],
-        compiler_params=params(24),
+        compiler_params=params(57),
         cost_estimate=pl.CostEstimate(flops=1200000000, bytes_accessed=11000000, transcendentals=0),
         name="token_grads",
     )(dz, w_in.T)
-    last = jnp.sum(last.reshape(4, 4, 2, fblk, piece).astype(F32), axis=(0, 2)) * scale
-    grad_weight = last.transpose(1, 0, 2).reshape(fblk, 4 * piece).astype(BF16)
-
-    grad_taps = sums[:24].reshape(3, 8, PADC)[:, :7, :width].transpose(1, 0, 2).reshape(7, chans)
-    grad_taps = grad_taps * scale
-    index = (xi * 4 + zi) * 4 + yi
-    held_chans = width // count
-    chosen = lax.dynamic_slice_in_dim(sums[24:, :width], index * held_chans, held_chans, axis=1)
-    grad_residues = amp_mine * chosen.T * scale
-
+    grad_taps, grad_residues = pl.pallas_call(
+        make_sum(scale),
+        in_specs=[smem] + [vm] * 5,
+        out_specs=[vm] * 2,
+        out_shape=[
+            jax.ShapeDtypeStruct((7, chans), F32),
+            jax.ShapeDtypeStruct(rates.shape, F32),
+        ],
+        scratch_shapes=[pltpu.VMEM((128, 128), F32)],
+        compiler_params=params(4),
+        name="close_sums",
+    )(place, amp_mine, *parts)
+    grad_weight = pl.pallas_call(
+        make_close(scale),
+        in_specs=[vm],
+        out_specs=vm,
+        out_shape=jax.ShapeDtypeStruct((fblk, 4 * piece), BF16),
+        compiler_params=params(4),
+        name="close_weight",
+    )(last)
     return (output[None], grad_feats[None], grad_weight, grad_taps, grad_residues)
 
 

time: 180 us -> 171 us (0.950)
  the two profiles are of different devices: /device:TPU:1 before, /device:TPU:32 now
where the time goes in v5:
time: 171 us; the launch traced here: 170 us
  starting transfers between devices  77.2 us (45%)
  waiting for transfers between devices  45.3 us (26%)
  Pallas kernels  39.7 us (23%)
  local copies, waits for them, and re-layouts  6.61 us (4%)
    ppermute x30, starting transfers between devices, ring(): return lax.ppermute(a, ax, [(i, (i + d) % 4) for i in range(4)])  51.3 us
    ppermute x30, waiting for transfers between devices, ring(): return lax.ppermute(a, ax, [(i, (i + d) % 4) for i in range(4)])  42.3 us
    pallas_call x1, Pallas kernels, local(): pl.pallas_call(finish, grid=(PADC // 128,), in_specs=[smem, tiles((3, ext...  9.81 us
    all_to_all x1, starting transfers between devices, local(): last = lax.all_to_all(blocks, ('zl', 'y', 'zh'), 0, 0, tiled=True)  8.42 us
    pallas_call x1, Pallas kernels, local(): pl.pallas_call(project, in_specs=[vm] * 3 + [anywhere] * 3, out_specs=[an...  8.29 us
    unnamed x22, local copies, waits for them, and re-layouts  6.61 us
    pallas_call x1, Pallas kernels, local(): pl.pallas_call(token_grads, grid=(3,), in_specs=[pl.BlockSpec((1, own, PA...  6.01 us
    ppermute x1, starting transfers between devices, local(): nexts = lax.ppermute(head, ctx, [(i, i - 1) for i in range(1, count)])  4.47 us
  transfers between devices with their start and end apart: 42, of which 21 were waited for; matrix products, arithmetic and copies ran while one was open for 0% of the time, Pallas kernels for 17%

profile of v5, /device:TPU:32, one launch (start us, length us, event | category | flops | bytes accessed | tf_op | source)
XLA Modules:
  0.0 169.7 jit_solution(14431302266039590857)
XLA Ops:
  0.7 1.9 %prepare.1 = (bf16[16,2560]{1,0:T(8,128)(2,1)}, bf16[16,1536]{1,0:T(8,128)(2,1)}, f32[32,15]{1,0:T(8,128)}, f32[3,8,1024]{2,1,0:T(8,128)}, f32[15,16]{1,0:T(8,128)}) custom-call(bf16[128,1536]{1,0:T(8,128)(2,1)} %bitcast.12, bf16[960,128]{1,0:T(8,128)(2,1)} %bitcast.18, f32[15,16]{1,0:T(8,128)} %rates, f32[15,16]{1,0:T(8,128)} %residues.1, f32[7,2880]{1,0:T(8,128)} %conv.1), custom_call_target="tpu_custom_call" | custom-call | tf_op jit(solution)/shard_map/prepare/pallas_call | solution.py:449
  2.7 4.5 %collective-permute-start.1 = (bf16[16,2560]{1,0:T(8,128)(2,1)}, bf16[16,2560]{1,0:T(8,128)(2,1)S(1)}, u32[]{:S(2)}, u32[]{:S(2)}) collective-permute-start(bf16[16,2560]{1,0:T(8,128)(2,1)} %get-tuple-element.58), channel_id=1, source_target_pairs={{4,0},{8,4},{12,8},{16,12},{20,16},{24,20},{28,24},{32,28},{36,32}... | collective-permute-start | bytes 245768 | tf_op jit(solution)/shard_map/ppermute | solution.py:473
  7.1 1.9 %collective-permute-start = (bf16[16,1536]{1,0:T(8,128)(2,1)}, bf16[16,1536]{1,0:T(8,128)(2,1)S(1)}, u32[]{:S(2)}, u32[]{:S(2)}) collective-permute-start(bf16[16,1536]{1,0:T(8,128)(2,1)} %get-tuple-element.57), channel_id=1, source_target_pairs={{0,4},{4,8},{8,12},{12,16},{16,20},{20,24},{24,28},{28,32},{32,36}... | collective-permute-start | bytes 147464 | tf_op jit(solution)/shard_map/ppermute | solution.py:472
  9.1 4.7 %collective-permute-start.4 = (f32[32,15]{1,0:T(8,128)}, f32[32,15]{1,0:T(8,128)S(1)}, u32[]{:S(2)}, u32[]{:S(2)}) collective-permute-start(f32[32,15]{1,0:T(8,128)} %get-tuple-element.62.r0), channel_id=1, source_target_pairs={{0,12},{4,0},{8,4},{12,8},{1,13},{5,1},{9,5},{13,9},{2,14},{6,2},{... | collective-permute-start | bytes 5768 | tf_op jit(solution)/shard_map/ppermute | solution.py:425
  15.4 3.8 %collective-permute-done.3.r2 = f32[32,15]{1,0:T(8,128)S(1)} collective-permute-done((f32[32,15]{1,0:T(8,128)}, f32[32,15]{1,0:T(8,128)S(1)}, u32[]{:S(2)}, u32[]{:S(2)}) %collective-permute-start.3) | collective-permute-done | bytes 1952 | tf_op jit(solution)/shard_map/ppermute | solution.py:425
  20.7 6.0 %collective-permute-start.6 = (f32[32,60]{1,0:T(8,128)S(1)}, f32[32,60]{1,0:T(8,128)S(1)}, u32[]{:S(2)}, u32[]{:S(2)}) collective-permute-start(f32[32,60]{1,0:T(8,128)S(1)} %join_params.2.r0), channel_id=1, source_target_pairs={{0,32},{16,48},{32,0},{48,16},{1,33},{17,49},{33,1},{49,17},{2,34}... | collective-permute-start | bytes 23048 | tf_op jit(solution)/shard_map/ppermute | solution.py:425
  26.7 2.8 %collective-permute-start.5 = (f32[32,60]{1,0:T(8,128)S(1)}, f32[32,60]{1,0:T(8,128)S(1)}, u32[]{:S(2)}, u32[]{:S(2)}) collective-permute-start(f32[32,60]{1,0:T(8,128)S(1)} %join_params.2.r0), channel_id=1, source_target_pairs={{0,16},{16,32},{32,48},{48,0},{1,17},{17,33},{33,49},{49,1},{2,18}... | collective-permute-start | bytes 23048 | tf_op jit(solution)/shard_map/ppermute | solution.py:425
  29.5 1.4 collective-permute-done.5.r1
  31.7 3.5 %collective-permute-start.9 = (f32[32,240]{1,0:T(8,128)S(1)}, f32[32,240]{1,0:T(8,128)S(1)}, u32[]{:S(2)}, u32[]{:S(2)}) collective-permute-start(f32[32,240]{1,0:T(8,128)S(1)} %join_params.3.r0), channel_id=1, source_target_pairs={{0,128},{64,192},{128,0},{192,64},{1,129},{65,193},{129,1},{193,65... | collective-permute-start | bytes 92168 | tf_op jit(solution)/shard_map/ppermute | solution.py:425
  36.2 1.0 copy-done
  39.0 8.3 %project.1 = (f32[3,160,1024]{2,1,0:T(8,128)}, f32[3,136,1024]{2,1,0:T(8,128)}, f32[136,1024]{1,0:T(8,128)S(1)}, f32[136,1024]{1,0:T(8,128)S(1)}, f32[136,1024]{1,0:T(8,128)S(1)}) custom-call(bf16[16,1536]{1,0:T(8,128)(2,1)S(1)} %collective-permute-done.tp, bf16[16,2560]{1,0:T(8,128)(2,1)S(1)} %collective-permute-done.1.nexts, f32[3,8,1024]{2,1,0:T(8,128)S(1)} %copy-done.4, ...), custom_call_target="tpu_custom_call" | custom-call | flops 1500000000 | bytes 14000000 | tf_op jit(solution)/shard_map/project/pallas_call | solution.py:492
  47.3 2.6 %end_states.1 = (f32[16,1024]{1,0:T(8,128)S(1)}, f32[16,1024]{1,0:T(8,128)S(1)}, f32[2,16,8,1024]{3,2,1,0:T(8,128)S(1)}, f32[32,1024]{1,0:T(8,128)S(1)}, bf16[32,1024]{1,0:T(8,128)(2,1)S(1)}) custom-call(s32[4]{0:T(128)S(1)} %pad_add_fusion.place, f32[32,240]{1,0:T(8,128)S(1)} %join_params.3.r0, f32[32,240]{1,0:T(8,128)S(1)} %collective-permute-done.8.r1, ...), custom_call_target="tpu_custom_call" | custom-call | flops 20000000 | bytes 3000000 | tf_op jit(solution)/shard_map/end_states/pallas_call | solution.py:517
  50.7 1.4 collective-permute-start.12
  52.1 1.3 collective-permute-start.11
  54.2 2.2 %collective-permute-done.12.r2 = bf16[32,1024]{1,0:T(8,128)(2,1)S(1)} collective-permute-done((bf16[32,1024]{1,0:T(8,128)(2,1)S(1)}, bf16[32,1024]{1,0:T(8,128)(2,1)S(1)}, u32[]{:S(2)}, u32[]{:S(2)}) %collective-permute-start.12) | collective-permute-done | bytes 65568 | tf_op jit(solution)/shard_map/ppermute | solution.py:425
  56.5 1.7 %collective-permute-done.11.r1 = bf16[32,1024]{1,0:T(8,128)(2,1)S(1)} collective-permute-done((bf16[32,1024]{1,0:T(8,128)(2,1)S(1)}, bf16[32,1024]{1,0:T(8,128)(2,1)S(1)}, u32[]{:S(2)}, u32[]{:S(2)}) %collective-permute-start.11) | collective-permute-done | bytes 65568 | tf_op jit(solution)/shard_map/ppermute | solution.py:425
  58.9 1.5 collective-permute-start.24
  60.5 2.6 %collective-permute-start.16 = (bf16[32,1024]{1,0:T(8,128)(2,1)S(1)}, bf16[32,1024]{1,0:T(8,128)(2,1)S(1)}, u32[]{:S(2)}, u32[]{:S(2)}) collective-permute-start(bf16[32,1024]{1,0:T(8,128)(2,1)S(1)} %get-tuple-element.77), channel_id=1, source_target_pairs={{0,48},{16,0},{32,16},{48,32},{1,49},{17,1},{33,17},{49,33},{2,50}... | collective-permute-start | bytes 196616 | tf_op jit(solution)/shard_map/ppermute | solution.py:425
  63.1 1.0 collective-permute-start.15
  64.1 1.0 collective-permute-start.14
  65.1 3.1 %collective-permute-done.15.r2 = bf16[32,1024]{1,0:T(8,128)(2,1)S(1)} collective-permute-done((bf16[32,1024]{1,0:T(8,128)(2,1)S(1)}, bf16[32,1024]{1,0:T(8,128)(2,1)S(1)}, u32[]{:S(2)}, u32[]{:S(2)}) %collective-permute-start.15) | collective-permute-done | bytes 65568 | tf_op jit(solution)/shard_map/ppermute | solution.py:425
  69.1 1.8 %collective-permute-done.24.refs_2_ = bf16[128,1536]{1,0:T(8,128)(2,1)S(1)} collective-permute-done((bf16[128,1536]{1,0:T(8,128)(2,1)S(1)}, bf16[128,1536]{1,0:T(8,128)(2,1)S(1)}, u32[]{:S(2)}, u32[]{:S(2)}) %collective-permute-start.24) | collective-permute-done | bytes 393248 | tf_op jit(solution)/shard_map/ppermute | solution.py:558
  70.9 1.2 collective-permute-start.25
  72.2 2.3 %collective-permute-start.19 = (bf16[32,1024]{1,0:T(8,128)(2,1)S(1)}, bf16[32,1024]{1,0:T(8,128)(2,1)S(1)}, u32[]{:S(2)}, u32[]{:S(2)}) collective-permute-start(bf16[32,1024]{1,0:T(8,128)(2,1)S(1)} %get-tuple-element.80), channel_id=1, source_target_pairs={{0,192},{64,0},{128,64},{192,128},{1,193},{65,1},{129,65},{193,129... | collective-permute-start | bytes 196616 | tf_op jit(solution)/shard_map/ppermute | solution.py:425
  75.4 1.7 collective-permute-done.19.r3
  77.0 3.4 %collective-permute-done.18.r2 = bf16[32,1024]{1,0:T(8,128)(2,1)S(1)} collective-permute-done((bf16[32,1024]{1,0:T(8,128)(2,1)S(1)}, bf16[32,1024]{1,0:T(8,128)(2,1)S(1)}, u32[]{:S(2)}, u32[]{:S(2)}) %collective-permute-start.18) | collective-permute-done | bytes 65568 | tf_op jit(solution)/shard_map/ppermute | solution.py:425
  80.7 1.3 level.5
  82.0 9.8 %finish.1 = (bf16[960,128]{1,0:T(8,128)(2,1)}, bf16[3,128,1024]{2,1,0:T(8,128)(2,1)S(1)}, bf16[8,360,128]{2,1,0:T(8,128)(2,1)}, bf16[40,1024]{1,0:T(8,128)(2,1)S(1)}) custom-call(s32[4]{0:T(128)S(1)} %pad_add_fusion.place, f32[3,160,1024]{2,1,0:T(8,128)} %get-tuple-element.60.zf, f32[3,136,1024]{2,1,0:T(8,128)} %get-tuple-element.61.mix, ...), custom_call_target="tpu_custom_call" | custom-call | flops 200000000 | bytes 10000000 | tf_op jit(solution)/shard_map/finish/pallas_call | solution.py:567
  93.4 3.5 %all-to-all-start = ((bf16[8,360,128]{2,1,0:T(8,128)(2,1)}), bf16[8,360,128]{2,1,0:T(8,128)(2,1)S(1)}, u32[]{:S(2)}, u32[]{:S(2)}) async-start(bf16[8,360,128]{2,1,0:T(8,128)(2,1)} %get-tuple-element.85), calls=%async_computation | async-start | bytes 1474560 | tf_op jit(solution)/shard_map/all_to_all | solution.py:626
  98.0 2.7 %collective-permute-start.22 = (bf16[40,1024]{1,0:T(8,128)(2,1)}, bf16[40,1024]{1,0:T(8,128)(2,1)S(1)}, u32[]{:S(2)}, u32[]{:S(2)}) collective-permute-start(bf16[40,1024]{1,0:T(8,128)(2,1)} %copy-done.7), channel_id=1, source_target_pairs={{0,48},{16,0},{32,16},{48,32},{1,49},{17,1},{33,17},{49,33},{2,50}... | collective-permute-start | bytes 245768 | tf_op jit(solution)/shard_map/ppermute | solution.py:425
  100.7 2.9 %collective-permute-done.22.p3 = bf16[40,1024]{1,0:T(8,128)(2,1)S(1)} collective-permute-done((bf16[40,1024]{1,0:T(8,128)(2,1)}, bf16[40,1024]{1,0:T(8,128)(2,1)S(1)}, u32[]{:S(2)}, u32[]{:S(2)}) %collective-permute-start.22) | collective-permute-done | bytes 81952 | tf_op jit(solution)/shard_map/ppermute | solution.py:425
  103.6 2.7 %collective-permute-start.21 = (bf16[40,1024]{1,0:T(8,128)(2,1)}, bf16[40,1024]{1,0:T(8,128)(2,1)S(1)}, u32[]{:S(2)}, u32[]{:S(2)}) collective-permute-start(bf16[40,1024]{1,0:T(8,128)(2,1)} %copy-done.7), channel_id=1, source_target_pairs={{0,32},{16,48},{32,0},{48,16},{1,33},{17,49},{33,1},{49,17},{2,34}... | collective-permute-start | bytes 245768 | tf_op jit(solution)/shard_map/ppermute | solution.py:425
  106.3 3.4 %collective-permute-done.21.p2 = bf16[40,1024]{1,0:T(8,128)(2,1)S(1)} collective-permute-done((bf16[40,1024]{1,0:T(8,128)(2,1)}, bf16[40,1024]{1,0:T(8,128)(2,1)S(1)}, u32[]{:S(2)}, u32[]{:S(2)}) %collective-permute-start.21) | collective-permute-done | bytes 81952 | tf_op jit(solution)/shard_map/ppermute | solution.py:425
  109.7 1.3 collective-permute-start.20
  111.0 3.8 %collective-permute-done.20.p1 = bf16[40,1024]{1,0:T(8,128)(2,1)S(1)} collective-permute-done((bf16[40,1024]{1,0:T(8,128)(2,1)}, bf16[40,1024]{1,0:T(8,128)(2,1)S(1)}, u32[]{:S(2)}, u32[]{:S(2)}) %collective-permute-start.20) | collective-permute-done | bytes 81952 | tf_op jit(solution)/shard_map/ppermute | solution.py:425
  116.4 3.8 %weight_term.1 = bf16[4,360,384]{2,1,0:T(8,128)(2,1)} custom-call(s32[4]{0:T(128)S(1)} %pad_add_fusion.place, bf16[8,360,128]{2,1,0:T(8,128)(2,1)S(1)} %all-to-all-done.arrived, bf16[128,1536]{1,0:T(8,128)(2,1)S(1)} %bitcast.17, bf16[128,1536]{1,0:T(8,128)(2,1)S(1)} %collective-permute-done.23.refs_1_, ...), custom_call_target="tpu_custom_call" | custom-call | flops 1200000000 | bytes 6000000 | tf_op jit(solution)/shard_map/weight_term/pallas_call | solution.py:629
  120.2 3.7 %all-to-all-start.1 = ((bf16[4,360,384]{2,1,0:T(8,128)(2,1)}), bf16[4,360,384]{2,1,0:T(8,128)(2,1)S(1)}, u32[]{:S(2)}, u32[]{:S(2)}) async-start(bf16[4,360,384]{2,1,0:T(8,128)(2,1)} %weight_term.1), calls=%async_computation.1 | async-start | bytes 2211840 | tf_op jit(solution)/shard_map/all_to_all | solution.py:638
  123.8 2.8 %collective-permute-start.32 = (bf16[40,1024]{1,0:T(8,128)(2,1)S(1)}, bf16[40,1024]{1,0:T(8,128)(2,1)S(1)}, u32[]{:S(2)}, u32[]{:S(2)}) collective-permute-start(bf16[40,1024]{1,0:T(8,128)(2,1)S(1)} %copy-done.6), channel_id=1, source_target_pairs={{0,12},{4,0},{8,4},{12,8},{1,13},{5,1},{9,5},{13,9},{2,14},{6,2},{... | collective-permute-start | bytes 245768 | tf_op jit(solution)/shard_map/ppermute | solution.py:425
  129.1 3.5 %collective-permute-done.31.p2 = bf16[40,1024]{1,0:T(8,128)(2,1)S(1)} collective-permute-done((bf16[40,1024]{1,0:T(8,128)(2,1)S(1)}, bf16[40,1024]{1,0:T(8,128)(2,1)S(1)}, u32[]{:S(2)}, u32[]{:S(2)}) %collective-permute-start.31) | collective-permute-done | bytes 81952 | tf_op jit(solution)/shard_map/ppermute | solution.py:425
  133.5 1.8 %collective-permute-start.35 = (bf16[40,1024]{1,0:T(8,128)(2,1)S(1)}, bf16[40,1024]{1,0:T(8,128)(2,1)S(1)}, u32[]{:S(2)}, u32[]{:S(2)}) collective-permute-start(bf16[40,1024]{1,0:T(8,128)(2,1)S(1)} %add_parts.4.p0), channel_id=1, source_target_pairs={{0,3},{1,0},{2,1},{3,2},{4,7},{5,4},{6,5},{7,6},{8,11},{9,8},{10,9... | collective-permute-start | bytes 245768 | tf_op jit(solution)/shard_map/ppermute | solution.py:425
  135.3 2.9 %collective-permute-start.34 = (bf16[40,1024]{1,0:T(8,128)(2,1)S(1)}, bf16[40,1024]{1,0:T(8,128)(2,1)S(1)}, u32[]{:S(2)}, u32[]{:S(2)}) collective-permute-start(bf16[40,1024]{1,0:T(8,128)(2,1)S(1)} %add_parts.4.p0), channel_id=1, source_target_pairs={{0,2},{1,3},{2,0},{3,1},{4,6},{5,7},{6,4},{7,5},{8,10},{9,11},{10,... | collective-permute-start | bytes 245768 | tf_op jit(solution)/shard_map/ppermute | solution.py:425
  138.3 6.9 %collective-permute-done.34.p2 = bf16[40,1024]{1,0:T(8,128)(2,1)S(1)} collective-permute-done((bf16[40,1024]{1,0:T(8,128)(2,1)S(1)}, bf16[40,1024]{1,0:T(8,128)(2,1)S(1)}, u32[]{:S(2)}, u32[]{:S(2)}) %collective-permute-start.34) | collective-permute-done | bytes 81952 | tf_op jit(solution)/shard_map/ppermute | solution.py:425
  146.1 1.0 split_rows.1
  147.2 8.4 %all-to-all-start.2 = ((bf16[32,24,180]{2,1,0:T(8,128)(2,1)}), bf16[32,24,180]{2,1,0:T(8,128)(2,1)S(1)}, u32[]{:S(2)}, u32[]{:S(2)}) async-start(bf16[32,24,180]{2,1,0:T(8,128)(2,1)} %split_rows.1), calls=%async_computation.2 | async-start | bytes 786432 | tf_op jit(solution)/shard_map/all_to_all | solution.py:651
  155.6 3.2 %collective-permute-start.38 = (bf16[40,1024]{1,0:T(8,128)(2,1)S(1)}, bf16[40,1024]{1,0:T(8,128)(2,1)S(1)}, u32[]{:S(2)}, u32[]{:S(2)}) collective-permute-start(bf16[40,1024]{1,0:T(8,128)(2,1)S(1)} %add_parts.5.p0), channel_id=1, source_target_pairs={{0,192},{64,0},{128,64},{192,128},{1,193},{65,1},{129,65},{193,129... | collective-permute-start | bytes 245768 | tf_op jit(solution)/shard_map/ppermute | solution.py:425
  160.5 6.0 %token_grads.1 = bf16[128,1536]{1,0:T(8,128)(2,1)} custom-call(bf16[3,128,1024]{2,1,0:T(8,128)(2,1)} %copy-done.3, bf16[2880,1536]{1,0:T(8,128)(2,1)} %bitcast.21), custom_call_target="tpu_custom_call" | custom-call | flops 1200000000 | bytes 11000000 | tf_op jit(solution)/shard_map/token_grads/pallas_call | solution.py:654
  166.5 1.3 close_sums.1
  167.8 1.1 all-to-all-done.2.last
  (76 shorter events, 22.3 us)
Async XLA Ops:
  2.7 33.5 %collective-permute-start.1 = (bf16[16,2560]{1,0:T(8,128)(2,1)}, bf16[16,2560]{1,0:T(8,128)(2,1)S(1)}, u32[]{:S(2)}, u32[]{:S(2)}) collective-permute-start(bf16[16,2560]{1,0:T(8,128)(2,1)} %get-tuple-element.58), channel_id=1, source_target_pairs={{4,0},{8,4},{12,8},{16,12},{20,16},{24,20},{28,24},{32,28},{36,32}... | collective-permute-start | bytes 245768 | tf_op jit(solution)/shard_map/ppermute | solution.py:473
  7.1 29.0 %collective-permute-start = (bf16[16,1536]{1,0:T(8,128)(2,1)}, bf16[16,1536]{1,0:T(8,128)(2,1)S(1)}, u32[]{:S(2)}, u32[]{:S(2)}) collective-permute-start(bf16[16,1536]{1,0:T(8,128)(2,1)} %get-tuple-element.57), channel_id=1, source_target_pairs={{0,4},{4,8},{8,12},{12,16},{16,20},{20,24},{24,28},{28,32},{32,36}... | collective-permute-start | bytes 147464 | tf_op jit(solution)/shard_map/ppermute | solution.py:472
  9.1 6.3 %collective-permute-start.4 = (f32[32,15]{1,0:T(8,128)}, f32[32,15]{1,0:T(8,128)S(1)}, u32[]{:S(2)}, u32[]{:S(2)}) collective-permute-start(f32[32,15]{1,0:T(8,128)} %get-tuple-element.62.r0), channel_id=1, source_target_pairs={{0,12},{4,0},{8,4},{12,8},{1,13},{5,1},{9,5},{13,9},{2,14},{6,2},{... | collective-permute-start | bytes 5768 | tf_op jit(solution)/shard_map/ppermute | solution.py:425
  13.7 5.5 %collective-permute-start.3 = (f32[32,15]{1,0:T(8,128)}, f32[32,15]{1,0:T(8,128)S(1)}, u32[]{:S(2)}, u32[]{:S(2)}) collective-permute-start(f32[32,15]{1,0:T(8,128)} %get-tuple-element.62.r0), channel_id=1, source_target_pairs={{0,8},{4,12},{8,0},{12,4},{1,9},{5,13},{9,1},{13,5},{2,10},{6,14},... | collective-permute-start | bytes 5768 | tf_op jit(solution)/shard_map/ppermute | solution.py:425
  13.7 5.5 %collective-permute-start.2 = (f32[32,15]{1,0:T(8,128)}, f32[32,15]{1,0:T(8,128)S(1)}, u32[]{:S(2)}, u32[]{:S(2)}) collective-permute-start(f32[32,15]{1,0:T(8,128)} %get-tuple-element.62.r0), channel_id=1, source_target_pairs={{0,4},{4,8},{8,12},{12,0},{1,5},{5,9},{9,13},{13,1},{2,6},{6,10},{... | collective-permute-start | bytes 5768 | tf_op jit(solution)/shard_map/ppermute | solution.py:425
  20.6 9.0 %collective-permute-start.7 = (f32[32,60]{1,0:T(8,128)S(1)}, f32[32,60]{1,0:T(8,128)S(1)}, u32[]{:S(2)}, u32[]{:S(2)}) collective-permute-start(f32[32,60]{1,0:T(8,128)S(1)} %join_params.2.r0), channel_id=1, source_target_pairs={{0,48},{16,0},{32,16},{48,32},{1,49},{17,1},{33,17},{49,33},{2,50}... | collective-permute-start | bytes 23048 | tf_op jit(solution)/shard_map/ppermute | solution.py:425
  20.7 8.8 %collective-permute-start.6 = (f32[32,60]{1,0:T(8,128)S(1)}, f32[32,60]{1,0:T(8,128)S(1)}, u32[]{:S(2)}, u32[]{:S(2)}) collective-permute-start(f32[32,60]{1,0:T(8,128)S(1)} %join_params.2.r0), channel_id=1, source_target_pairs={{0,32},{16,48},{32,0},{48,16},{1,33},{17,49},{33,1},{49,17},{2,34}... | collective-permute-start | bytes 23048 | tf_op jit(solution)/shard_map/ppermute | solution.py:425
  26.7 4.3 %collective-permute-start.5 = (f32[32,60]{1,0:T(8,128)S(1)}, f32[32,60]{1,0:T(8,128)S(1)}, u32[]{:S(2)}, u32[]{:S(2)}) collective-permute-start(f32[32,60]{1,0:T(8,128)S(1)} %join_params.2.r0), channel_id=1, source_target_pairs={{0,16},{16,32},{32,48},{48,0},{1,17},{17,33},{33,49},{49,1},{2,18}... | collective-permute-start | bytes 23048 | tf_op jit(solution)/shard_map/ppermute | solution.py:425
  31.6 15.7 %collective-permute-start.10 = (f32[32,240]{1,0:T(8,128)S(1)}, f32[32,240]{1,0:T(8,128)S(1)}, u32[]{:S(2)}, u32[]{:S(2)}) collective-permute-start(f32[32,240]{1,0:T(8,128)S(1)} %join_params.3.r0), channel_id=1, source_target_pairs={{0,192},{64,0},{128,64},{192,128},{1,193},{65,1},{129,65},{193,129... | collective-permute-start | bytes 92168 | tf_op jit(solution)/shard_map/ppermute | solution.py:425
  31.7 15.6 %collective-permute-start.9 = (f32[32,240]{1,0:T(8,128)S(1)}, f32[32,240]{1,0:T(8,128)S(1)}, u32[]{:S(2)}, u32[]{:S(2)}) collective-permute-start(f32[32,240]{1,0:T(8,128)S(1)} %join_params.3.r0), channel_id=1, source_target_pairs={{0,128},{64,192},{128,0},{192,64},{1,129},{65,193},{129,1},{193,65... | collective-permute-start | bytes 92168 | tf_op jit(solution)/shard_map/ppermute | solution.py:425
  35.3 12.1 %collective-permute-start.8 = (f32[32,240]{1,0:T(8,128)S(1)}, f32[32,240]{1,0:T(8,128)S(1)}, u32[]{:S(2)}, u32[]{:S(2)}) collective-permute-start(f32[32,240]{1,0:T(8,128)S(1)} %join_params.3.r0), channel_id=1, source_target_pairs={{0,64},{64,128},{128,192},{192,0},{1,65},{65,129},{129,193},{193,1... | collective-permute-start | bytes 92168 | tf_op jit(solution)/shard_map/ppermute | solution.py:425
  36.1 1.0 copy-start
  37.1 0.9 copy-start.2
  49.9 4.3 %collective-permute-start.13 = (bf16[32,1024]{1,0:T(8,128)(2,1)S(1)}, bf16[32,1024]{1,0:T(8,128)(2,1)S(1)}, u32[]{:S(2)}, u32[]{:S(2)}) collective-permute-start(bf16[32,1024]{1,0:T(8,128)(2,1)S(1)} %get-tuple-element.73), channel_id=1, source_target_pairs={{0,12},{4,0},{8,4},{12,8},{1,13},{5,1},{9,5},{13,9},{2,14},{6,2},{... | collective-permute-start | bytes 196616 | tf_op jit(solution)/shard_map/ppermute | solution.py:425
  50.7 5.8 %collective-permute-start.12 = (bf16[32,1024]{1,0:T(8,128)(2,1)S(1)}, bf16[32,1024]{1,0:T(8,128)(2,1)S(1)}, u32[]{:S(2)}, u32[]{:S(2)}) collective-permute-start(bf16[32,1024]{1,0:T(8,128)(2,1)S(1)} %get-tuple-element.73), channel_id=1, source_target_pairs={{0,8},{4,12},{8,0},{12,4},{1,9},{5,13},{9,1},{13,5},{2,10},{6,14},... | collective-permute-start | bytes 196616 | tf_op jit(solution)/shard_map/ppermute | solution.py:425
  52.1 6.1 %collective-permute-start.11 = (bf16[32,1024]{1,0:T(8,128)(2,1)S(1)}, bf16[32,1024]{1,0:T(8,128)(2,1)S(1)}, u32[]{:S(2)}, u32[]{:S(2)}) collective-permute-start(bf16[32,1024]{1,0:T(8,128)(2,1)S(1)} %get-tuple-element.73), channel_id=1, source_target_pairs={{0,4},{4,8},{8,12},{12,0},{1,5},{5,9},{9,13},{13,1},{2,6},{6,10},{... | collective-permute-start | bytes 196616 | tf_op jit(solution)/shard_map/ppermute | solution.py:425
  58.9 12.0 %collective-permute-start.24 = (bf16[128,1536]{1,0:T(8,128)(2,1)S(1)}, bf16[128,1536]{1,0:T(8,128)(2,1)S(1)}, u32[]{:S(2)}, u32[]{:S(2)}) collective-permute-start(bf16[128,1536]{1,0:T(8,128)(2,1)S(1)} %bitcast.14), channel_id=1, source_target_pairs={{0,12},{4,8},{8,4},{12,0},{1,13},{5,9},{9,5},{13,1},{2,14},{6,10},... | collective-permute-start | bytes 1179656 | tf_op jit(solution)/shard_map/ppermute | solution.py:558
  60.4 10.5 %collective-permute-start.23 = (bf16[128,1536]{1,0:T(8,128)(2,1)S(1)}, bf16[128,1536]{1,0:T(8,128)(2,1)S(1)}, u32[]{:S(2)}, u32[]{:S(2)}) collective-permute-start(bf16[128,1536]{1,0:T(8,128)(2,1)S(1)} %bitcast.15), channel_id=1, source_target_pairs={{0,4},{4,0},{8,12},{12,8},{1,5},{5,1},{9,13},{13,9},{2,6},{6,2},{1... | collective-permute-start | bytes 1179656 | tf_op jit(solution)/shard_map/ppermute | solution.py:557
  60.5 4.7 %collective-permute-start.16 = (bf16[32,1024]{1,0:T(8,128)(2,1)S(1)}, bf16[32,1024]{1,0:T(8,128)(2,1)S(1)}, u32[]{:S(2)}, u32[]{:S(2)}) collective-permute-start(bf16[32,1024]{1,0:T(8,128)(2,1)S(1)} %get-tuple-element.77), channel_id=1, source_target_pairs={{0,48},{16,0},{32,16},{48,32},{1,49},{17,1},{33,17},{49,33},{2,50}... | collective-permute-start | bytes 196616 | tf_op jit(solution)/shard_map/ppermute | solution.py:425
  63.1 5.2 %collective-permute-start.15 = (bf16[32,1024]{1,0:T(8,128)(2,1)S(1)}, bf16[32,1024]{1,0:T(8,128)(2,1)S(1)}, u32[]{:S(2)}, u32[]{:S(2)}) collective-permute-start(bf16[32,1024]{1,0:T(8,128)(2,1)S(1)} %get-tuple-element.77), channel_id=1, source_target_pairs={{0,32},{16,48},{32,0},{48,16},{1,33},{17,49},{33,1},{49,17},{2,34}... | collective-permute-start | bytes 196616 | tf_op jit(solution)/shard_map/ppermute | solution.py:425
  64.1 4.3 %collective-permute-start.14 = (bf16[32,1024]{1,0:T(8,128)(2,1)S(1)}, bf16[32,1024]{1,0:T(8,128)(2,1)S(1)}, u32[]{:S(2)}, u32[]{:S(2)}) collective-permute-start(bf16[32,1024]{1,0:T(8,128)(2,1)S(1)} %get-tuple-element.77), channel_id=1, source_target_pairs={{0,16},{16,32},{32,48},{48,0},{1,17},{17,33},{33,49},{49,1},{2,18}... | collective-permute-start | bytes 196616 | tf_op jit(solution)/shard_map/ppermute | solution.py:425
  70.9 26.9 %collective-permute-start.25 = (bf16[128,1536]{1,0:T(8,128)(2,1)S(1)}, bf16[128,1536]{1,0:T(8,128)(2,1)S(1)}, u32[]{:S(2)}, u32[]{:S(2)}) collective-permute-start(bf16[128,1536]{1,0:T(8,128)(2,1)S(1)} %collective-permute-done.23.refs_1_), channel_id=1, source_target_pairs={{0,12},{4,8},{8,4},{12,0},{1,13},{5,9},{9,5},{13,1},{2,14},{6,10},... | collective-permute-start | bytes 1179656 | tf_op jit(solution)/shard_map/ppermute | solution.py:561
  72.2 4.9 %collective-permute-start.19 = (bf16[32,1024]{1,0:T(8,128)(2,1)S(1)}, bf16[32,1024]{1,0:T(8,128)(2,1)S(1)}, u32[]{:S(2)}, u32[]{:S(2)}) collective-permute-start(bf16[32,1024]{1,0:T(8,128)(2,1)S(1)} %get-tuple-element.80), channel_id=1, source_target_pairs={{0,192},{64,0},{128,64},{192,128},{1,193},{65,1},{129,65},{193,129... | collective-permute-start | bytes 196616 | tf_op jit(solution)/shard_map/ppermute | solution.py:425
  74.5 5.9 %collective-permute-start.18 = (bf16[32,1024]{1,0:T(8,128)(2,1)S(1)}, bf16[32,1024]{1,0:T(8,128)(2,1)S(1)}, u32[]{:S(2)}, u32[]{:S(2)}) collective-permute-start(bf16[32,1024]{1,0:T(8,128)(2,1)S(1)} %get-tuple-element.80), channel_id=1, source_target_pairs={{0,128},{64,192},{128,0},{192,64},{1,129},{65,193},{129,1},{193,65... | collective-permute-start | bytes 196616 | tf_op jit(solution)/shard_map/ppermute | solution.py:425
  74.5 6.2 %collective-permute-start.17 = (bf16[32,1024]{1,0:T(8,128)(2,1)S(1)}, bf16[32,1024]{1,0:T(8,128)(2,1)S(1)}, u32[]{:S(2)}, u32[]{:S(2)}) collective-permute-start(bf16[32,1024]{1,0:T(8,128)(2,1)S(1)} %get-tuple-element.80), channel_id=1, source_target_pairs={{0,64},{64,128},{128,192},{192,0},{1,65},{65,129},{129,193},{193,1... | collective-permute-start | bytes 196616 | tf_op jit(solution)/shard_map/ppermute | solution.py:425
  82.0 14.9 %copy-start.1 = (bf16[1,128,1536]{2,1,0:T(8,128)(2,1)S(1)}, bf16[1,128,1536]{2,1,0:T(8,128)(2,1)}, u32[]{:S(2)}) copy-start(bf16[1,128,1536]{2,1,0:T(8,128)(2,1)} %param.6) | copy-start | bytes 1179652
  91.8 0.9 copy-start.3
  93.4 23.0 %all-to-all-start = ((bf16[8,360,128]{2,1,0:T(8,128)(2,1)}), bf16[8,360,128]{2,1,0:T(8,128)(2,1)S(1)}, u32[]{:S(2)}, u32[]{:S(2)}) async-start(bf16[8,360,128]{2,1,0:T(8,128)(2,1)} %get-tuple-element.85), calls=%async_computation | async-start | bytes 1474560 | tf_op jit(solution)/shard_map/all_to_all | solution.py:626
  96.9 19.4 %collective-permute-start.26 = (bf16[128,1536]{1,0:T(8,128)(2,1)S(1)}, bf16[128,1536]{1,0:T(8,128)(2,1)S(1)}, u32[]{:S(2)}, u32[]{:S(2)}) collective-permute-start(bf16[128,1536]{1,0:T(8,128)(2,1)S(1)} %bitcast.16), channel_id=1, source_target_pairs={{0,1},{1,0},{2,3},{3,2},{4,5},{5,4},{6,7},{7,6},{8,9},{9,8},{10,11... | collective-permute-start | bytes 1179656 | tf_op jit(solution)/shard_map/ppermute | solution.py:611
  97.3 19.0 %collective-permute-start.27 = (bf16[128,1536]{1,0:T(8,128)(2,1)S(1)}, bf16[128,1536]{1,0:T(8,128)(2,1)S(1)}, u32[]{:S(2)}, u32[]{:S(2)}) collective-permute-start(bf16[128,1536]{1,0:T(8,128)(2,1)S(1)} %collective-permute-done.23.refs_1_), channel_id=1, source_target_pairs={{0,1},{1,0},{2,3},{3,2},{4,5},{5,4},{6,7},{7,6},{8,9},{9,8},{10,11... | collective-permute-start | bytes 1179656 | tf_op jit(solution)/shard_map/ppermute | solution.py:611
  97.5 18.8 %collective-permute-start.28 = (bf16[128,1536]{1,0:T(8,128)(2,1)S(1)}, bf16[128,1536]{1,0:T(8,128)(2,1)S(1)}, u32[]{:S(2)}, u32[]{:S(2)}) collective-permute-start(bf16[128,1536]{1,0:T(8,128)(2,1)S(1)} %collective-permute-done.24.refs_2_), channel_id=1, source_target_pairs={{0,1},{1,0},{2,3},{3,2},{4,5},{5,4},{6,7},{7,6},{8,9},{9,8},{10,11... | collective-permute-start | bytes 1179656 | tf_op jit(solution)/shard_map/ppermute | solution.py:611
  97.8 18.5 %collective-permute-start.29 = (bf16[128,1536]{1,0:T(8,128)(2,1)S(1)}, bf16[128,1536]{1,0:T(8,128)(2,1)}, u32[]{:S(2)}, u32[]{:S(2)}) collective-permute-start(bf16[128,1536]{1,0:T(8,128)(2,1)S(1)} %collective-permute-done.25.refs_3_), channel_id=1, source_target_pairs={{0,1},{1,0},{2,3},{3,2},{4,5},{5,4},{6,7},{7,6},{8,9},{9,8},{10,11... | collective-permute-start | bytes 1179656 | tf_op jit(solution)/shard_map/ppermute | solution.py:611
  98.0 5.6 %collective-permute-start.22 = (bf16[40,1024]{1,0:T(8,128)(2,1)}, bf16[40,1024]{1,0:T(8,128)(2,1)S(1)}, u32[]{:S(2)}, u32[]{:S(2)}) collective-permute-start(bf16[40,1024]{1,0:T(8,128)(2,1)} %copy-done.7), channel_id=1, source_target_pairs={{0,48},{16,0},{32,16},{48,32},{1,49},{17,1},{33,17},{49,33},{2,50}... | collective-permute-start | bytes 245768 | tf_op jit(solution)/shard_map/ppermute | solution.py:425
  103.6 6.1 %collective-permute-start.21 = (bf16[40,1024]{1,0:T(8,128)(2,1)}, bf16[40,1024]{1,0:T(8,128)(2,1)S(1)}, u32[]{:S(2)}, u32[]{:S(2)}) collective-permute-start(bf16[40,1024]{1,0:T(8,128)(2,1)} %copy-done.7), channel_id=1, source_target_pairs={{0,32},{16,48},{32,0},{48,16},{1,33},{17,49},{33,1},{49,17},{2,34}... | collective-permute-start | bytes 245768 | tf_op jit(solution)/shard_map/ppermute | solution.py:425
  109.7 5.1 %collective-permute-start.20 = (bf16[40,1024]{1,0:T(8,128)(2,1)}, bf16[40,1024]{1,0:T(8,128)(2,1)S(1)}, u32[]{:S(2)}, u32[]{:S(2)}) collective-permute-start(bf16[40,1024]{1,0:T(8,128)(2,1)} %copy-done.7), channel_id=1, source_target_pairs={{0,16},{16,32},{32,48},{48,0},{1,17},{17,33},{33,49},{49,1},{2,18}... | collective-permute-start | bytes 245768 | tf_op jit(solution)/shard_map/ppermute | solution.py:425
  120.2 3.7 %copy-start.6 = (bf16[40,1024]{1,0:T(8,128)(2,1)S(1)}, bf16[40,1024]{1,0:T(8,128)(2,1)}, u32[]{:S(2)}) copy-start(bf16[40,1024]{1,0:T(8,128)(2,1)} %copy-done.5) | copy-start | bytes 245764
  120.2 25.9 %all-to-all-start.1 = ((bf16[4,360,384]{2,1,0:T(8,128)(2,1)}), bf16[4,360,384]{2,1,0:T(8,128)(2,1)S(1)}, u32[]{:S(2)}, u32[]{:S(2)}) async-start(bf16[4,360,384]{2,1,0:T(8,128)(2,1)} %weight_term.1), calls=%async_computation.1 | async-start | bytes 2211840 | tf_op jit(solution)/shard_map/all_to_all | solution.py:638
  123.8 5.2 %collective-permute-start.32 = (bf16[40,1024]{1,0:T(8,128)(2,1)S(1)}, bf16[40,1024]{1,0:T(8,128)(2,1)S(1)}, u32[]{:S(2)}, u32[]{:S(2)}) collective-permute-start(bf16[40,1024]{1,0:T(8,128)(2,1)S(1)} %copy-done.6), channel_id=1, source_target_pairs={{0,12},{4,0},{8,4},{12,8},{1,13},{5,1},{9,5},{13,9},{2,14},{6,2},{... | collective-permute-start | bytes 245768 | tf_op jit(solution)/shard_map/ppermute | solution.py:425
  126.6 6.0 %collective-permute-start.31 = (bf16[40,1024]{1,0:T(8,128)(2,1)S(1)}, bf16[40,1024]{1,0:T(8,128)(2,1)S(1)}, u32[]{:S(2)}, u32[]{:S(2)}) collective-permute-start(bf16[40,1024]{1,0:T(8,128)(2,1)S(1)} %copy-done.6), channel_id=1, source_target_pairs={{0,8},{4,12},{8,0},{12,4},{1,9},{5,13},{9,1},{13,5},{2,10},{6,14},... | collective-permute-start | bytes 245768 | tf_op jit(solution)/shard_map/ppermute | solution.py:425
  127.5 6.0 %collective-permute-start.30 = (bf16[40,1024]{1,0:T(8,128)(2,1)S(1)}, bf16[40,1024]{1,0:T(8,128)(2,1)S(1)}, u32[]{:S(2)}, u32[]{:S(2)}) collective-permute-start(bf16[40,1024]{1,0:T(8,128)(2,1)S(1)} %copy-done.6), channel_id=1, source_target_pairs={{0,4},{4,8},{8,12},{12,0},{1,5},{5,9},{9,13},{13,1},{2,6},{6,10},{... | collective-permute-start | bytes 245768 | tf_op jit(solution)/shard_map/ppermute | solution.py:425
  133.5 4.8 %collective-permute-start.35 = (bf16[40,1024]{1,0:T(8,128)(2,1)S(1)}, bf16[40,1024]{1,0:T(8,128)(2,1)S(1)}, u32[]{:S(2)}, u32[]{:S(2)}) collective-permute-start(bf16[40,1024]{1,0:T(8,128)(2,1)S(1)} %add_parts.4.p0), channel_id=1, source_target_pairs={{0,3},{1,0},{2,1},{3,2},{4,7},{5,4},{6,5},{7,6},{8,11},{9,8},{10,9... | collective-permute-start | bytes 245768 | tf_op jit(solution)/shard_map/ppermute | solution.py:425
  135.3 9.9 %collective-permute-start.34 = (bf16[40,1024]{1,0:T(8,128)(2,1)S(1)}, bf16[40,1024]{1,0:T(8,128)(2,1)S(1)}, u32[]{:S(2)}, u32[]{:S(2)}) collective-permute-start(bf16[40,1024]{1,0:T(8,128)(2,1)S(1)} %add_parts.4.p0), channel_id=1, source_target_pairs={{0,2},{1,3},{2,0},{3,1},{4,6},{5,7},{6,4},{7,5},{8,10},{9,11},{10,... | collective-permute-start | bytes 245768 | tf_op jit(solution)/shard_map/ppermute | solution.py:425
  138.2 7.9 %collective-permute-start.33 = (bf16[40,1024]{1,0:T(8,128)(2,1)S(1)}, bf16[40,1024]{1,0:T(8,128)(2,1)S(1)}, u32[]{:S(2)}, u32[]{:S(2)}) collective-permute-start(bf16[40,1024]{1,0:T(8,128)(2,1)S(1)} %add_parts.4.p0), channel_id=1, source_target_pairs={{0,1},{1,2},{2,3},{3,0},{4,5},{5,6},{6,7},{7,4},{8,9},{9,10},{10,1... | collective-permute-start | bytes 245768 | tf_op jit(solution)/shard_map/ppermute | solution.py:425
  147.2 21.8 %all-to-all-start.2 = ((bf16[32,24,180]{2,1,0:T(8,128)(2,1)}), bf16[32,24,180]{2,1,0:T(8,128)(2,1)S(1)}, u32[]{:S(2)}, u32[]{:S(2)}) async-start(bf16[32,24,180]{2,1,0:T(8,128)(2,1)} %split_rows.1), calls=%async_computation.2 | async-start | bytes 786432 | tf_op jit(solution)/shard_map/all_to_all | solution.py:651
  155.6 10.9 %copy-start.10 = (f32[15,16]{1,0:T(8,128)S(1)}, f32[15,16]{1,0:T(8,128)}, u32[]{:S(2)}) copy-start(f32[15,16]{1,0:T(8,128)} %get-tuple-element.97.amp) | copy-start | bytes 2884
  155.6 10.9 %collective-permute-start.38 = (bf16[40,1024]{1,0:T(8,128)(2,1)S(1)}, bf16[40,1024]{1,0:T(8,128)(2,1)S(1)}, u32[]{:S(2)}, u32[]{:S(2)}) collective-permute-start(bf16[40,1024]{1,0:T(8,128)(2,1)S(1)} %add_parts.5.p0), channel_id=1, source_target_pairs={{0,192},{64,0},{128,64},{192,128},{1,193},{65,1},{129,65},{193,129... | collective-permute-start | bytes 245768 | tf_op jit(solution)/shard_map/ppermute | solution.py:425
  158.8 7.7 %collective-permute-start.37 = (bf16[40,1024]{1,0:T(8,128)(2,1)S(1)}, bf16[40,1024]{1,0:T(8,128)(2,1)S(1)}, u32[]{:S(2)}, u32[]{:S(2)}) collective-permute-start(bf16[40,1024]{1,0:T(8,128)(2,1)S(1)} %add_parts.5.p0), channel_id=1, source_target_pairs={{0,128},{64,192},{128,0},{192,64},{1,129},{65,193},{129,1},{193,65... | collective-permute-start | bytes 245768 | tf_op jit(solution)/shard_map/ppermute | solution.py:425
  159.6 6.9 %collective-permute-start.36 = (bf16[40,1024]{1,0:T(8,128)(2,1)S(1)}, bf16[40,1024]{1,0:T(8,128)(2,1)S(1)}, u32[]{:S(2)}, u32[]{:S(2)}) collective-permute-start(bf16[40,1024]{1,0:T(8,128)(2,1)S(1)} %add_parts.5.p0), channel_id=1, source_target_pairs={{0,64},{64,128},{128,192},{192,0},{1,65},{65,129},{129,193},{193,1... | collective-permute-start | bytes 245768 | tf_op jit(solution)/shard_map/ppermute | solution.py:425
  (5 other events, 3.8 us)

commit v6 on v5

--- a/solution.py
+++ b/solution.py
@@ -21,78 +21,55 @@
     return a.astype(BF16).astype(F32)
 
 
-def project(
-    tp, nexts, taps, feats, cott, wt, zf_out, mix_out, cots_out, us, dls,
-    acc, turn, wbuf, zf, mix, cots, tk, cbuf, sems, zsem, tsems, isems,
-):
-    steps, _, kblk = wbuf.shape
-    arrivals = [
-        pltpu.make_async_copy(feats, tk, isems.at[0]),
-        pltpu.make_async_copy(cott, cbuf, isems.at[1]),
-    ]
-    arrivals[0].start()
-    copies = [
-        pltpu.make_async_copy(wt.at[:, pl.ds(k * kblk, kblk)], wbuf.at[k], sems.at[k])
-        for k in range(steps)
-    ]
-    for copy in copies:
-        copy.start()
-    arrivals[1].start()
-    width, own = cott.shape
-    depth = tk.shape[1]
-    turn[...] = jnp.zeros(turn.shape, F32)
-    for g in range(3):
-        zf[g, :, width:] = jnp.zeros((zf.shape[1], PADC - width), F32)
-    arrivals[0].wait()
-    for k in range(steps):
-        cols = slice(k * kblk, (k + 1) * kblk)
-        rows = jnp.concatenate([tp[:, cols], tk[:, cols], nexts[:, cols]], axis=0)
-        copies[k].wait()
-        part = lax.dot_general(rows, wbuf[k], NT, preferred_element_type=F32)
-        if k == 0:
-            acc[...] = part
-        elif k < steps - 1:
-            acc[...] += part
+def make_project(g):
+    def project(*refs):
+        if g == 0:
+            tp, nexts, taps, feats, wt, cott, zf, mix, cots, tk, wbuf, sems, turn, cbuf, csem = refs
         else:
-            total = acc[...] + part
-            for g in range(3):
-                zf[g, :, 0:width] = rounded(total[:, g * width : (g + 1) * width])
-    zcopy = pltpu.make_async_copy(zf, zf_out, zsem)
-    zcopy.start()
-    arrivals[1].wait()
-    turn[0:width, :] = cbuf[...].astype(F32)
-
-    def out_copies(ct):
-        lanes = pl.ds(pl.multiple_of(ct * 128, 128), 128)
-        return (
-            pltpu.make_async_copy(mix.at[:, :, lanes], mix_out.at[:, :, lanes], tsems.at[0, ct]),
-            pltpu.make_async_copy(cots.at[:, lanes], cots_out.at[:, lanes], tsems.at[1, ct]),
-        )
-
-    def tile(ct, carry):
-        lane = pl.multiple_of(ct * 128, 128)
-        lanes = pl.ds(lane, 128)
-        mixed = []
-        for g in range(3):
-            total = taps[g, 0:1, lanes] * zf[g, pl.ds(HALO, EXT), lanes]
+            tp, nexts, taps, feats, wt, zf, mix, tk, wbuf, sems = refs
+        width = wbuf.shape[0]
+        depth = tk.shape[1]
+        chunks = ((0, 512), (512, width - 512))
+        arrival = pltpu.make_async_copy(feats, tk, sems.at[0])
+        arrival.start()
+        copies = [
+            pltpu.make_async_copy(
+                wt.at[pl.ds(g * width + low, size)], wbuf.at[pl.ds(low, size)], sems.at[1 + i]
+            )
+            for i, (low, size) in enumerate(chunks)
+        ]
+        for copy in copies:
+            copy.start()
+        if g == 0:
+            other = pltpu.make_async_copy(cott, cbuf, csem)
+            other.start()
+        zf[:, width:] = jnp.zeros((zf.shape[0], PADC - width), F32)
+        arrival.wait()
+        rows = jnp.concatenate([tp[...], tk[...], nexts[:, 0:depth]], axis=0)
+        for (low, size), copy in zip(chunks, copies):
+            copy.wait()
+            part = lax.dot_general(rows, wbuf[low : low + size, :], NT, preferred_element_type=F32)
+            zf[:, low : low + size] = rounded(part)
+        if g == 0:
+            other.wait()
+            turn[...] = jnp.zeros(turn.shape, F32)
+            turn[0:width, :] = cbuf[...].astype(F32)
+
+        def tile(ct, carry):
+            lane = pl.multiple_of(ct * 128, 128)
+            lanes = pl.ds(lane, 128)
+            total = taps[g, 0:1, lanes] * zf[pl.ds(HALO, EXT), lanes]
             for j in range(1, 7):
-                total = total + taps[g, j : j + 1, lanes] * zf[g, pl.ds(HALO - j, EXT), lanes]
-            mix[g, :, lanes] = total
-            mixed.append(total)
-        after = nexts[:, pl.ds(pl.multiple_of(depth + lane, 128), 128)].astype(F32)
-        cot = jnp.concatenate([turn[lanes, :].T, after[0 : EXT - 128]], axis=0)
-        cots[:, lanes] = cot
-        us[:, lanes] = rounded(mixed[1] * mixed[2])
-        dls[:, lanes] = rounded(cot * mixed[0])
-        for copy in out_copies(ct):
-            copy.start()
-        return carry
-
-    lax.fori_loop(0, PADC // 128, tile, 0)
-    zcopy.wait()
-    for ct in range(PADC // 128):
-        for copy in out_copies(ct):
-            copy.wait()
+                total = total + taps[g, j : j + 1, lanes] * zf[pl.ds(HALO - j, EXT), lanes]
+            mix[:, lanes] = total
+            if g == 0:
+                after = nexts[:, pl.ds(pl.multiple_of(depth + lane, 128), 128)].astype(F32)
+                cots[:, lanes] = jnp.concatenate([turn[lanes, :].T, after[0 : EXT - 128]], axis=0)
+            return carry
+
+        lax.fori_loop(0, PADC // 128, tile, 0)
+
+    return project
 
 
 def one_minus_exp(x):
@@ -152,15 +129,12 @@
     return total[:, 0:goal]
 
 
-def make_join(axis):
-    def join_params(place, r0, r1, r2, r3, out, held):
-        out[...] = placed(place[axis], (r0, r1, r2, r3), held, out.shape[1])
-
-    return join_params
-
-
-def end_states(place, r0, r1, r2, r3, us, dls, rates, gains, es, ends, endb, ut, dt, held):
-    joined = placed(place[0], (r0, r1, r2, r3), held, PADC)
+def join_params(me, r0, r1, r2, r3, out, held):
+    out[...] = placed(me[0], (r0, r1, r2, r3), held, out.shape[1])
+
+
+def end_states(me, r0, r1, r2, r3, mq, mk, mv, cots, rates, gains, es, ends, endb, ut, dt, held):
+    joined = placed(me[0], (r0, r1, r2, r3), held, PADC)
     rates[...] = joined[0:MODES]
     gains[...] = joined[MODES : 2 * MODES]
     sub = lax.broadcasted_iota(jnp.int32, (8, 128), 0)
@@ -170,8 +144,8 @@
 
     def tile(ct, carry):
         lanes = pl.ds(pl.multiple_of(ct * 128, 128), 128)
-        ut[...] = us[:, lanes]
-        dt[...] = dls[:, lanes]
+        ut[...] = rounded(mk[:, lanes] * mv[:, lanes])
+        dt[...] = rounded(cots[:, lanes] * mq[:, lanes])
         rate = rates[:, lanes]
         decay = jnp.exp(-rate)
         for half in range(2):
@@ -205,9 +179,9 @@
     endb[...] = ends[...].astype(BF16)
 
 
-def make_level(axis, span):
-    def level(place, own, r1, r2, r3, rates, total, totalb, prefix):
-        me = place[axis]
+def make_level(span):
+    def level(index, own, r1, r2, r3, rates, total, totalb, prefix):
+        me = index[0]
         rate = rates[...] * float(span)
         before = jnp.zeros((MODES, PADC), F32)
         after = before
@@ -237,21 +211,21 @@
 
 
 def finish(
-    place, zf, mix, es, py, pz, px, taps, rates, reff, cots,
+    zi, yi, zq, zk, zv, mq, mk, mv, es, py, pz, px, taps, rates, reff, cots,
     outt, dz, dzb, sumb, sums, inc, ut, dt, longs, dps, dms, dzt,
 ):
     own = dz.shape[1]
     rate = rates[...]
     for back in range(2):
         part = pl.ds(back * MODES, MODES)
-        near, mid = place[2], place[1]
+        near, mid = yi[0], zi[0]
         if back:
             near, mid = 3 - near, 3 - mid
         far = pz[part, :] + jnp.exp(-rate * (4 * own * mid).astype(F32)) * px[part, :]
         inc[part, :] = py[part, :] + jnp.exp(-rate * (own * near).astype(F32)) * far
     sub = lax.broadcasted_iota(jnp.int32, (8, 128), 0)
-    ut[...] = rounded(mix[1] * mix[2])
-    dt[...] = rounded(cots[...] * mix[0])
+    ut[...] = rounded(mk[...] * mv[...])
+    dt[...] = rounded(cots[...] * mq[...])
     decay = jnp.exp(-rate)
     gain = reff[...]
     for half in range(2):
@@ -298,19 +272,19 @@
             dps[pl.ds(t, 8, stride=SEG), :] = total
     long_out = rounded(longs[...])
     dprod = rounded(dps[...])
-    outt[...] = (mix[0, 0:own, :] * long_out[0:own]).T.astype(BF16)
+    outt[...] = (mq[0:own, :] * long_out[0:own]).T.astype(BF16)
     dms[0] = rounded(cots[...] * long_out)
-    dms[1] = rounded(dprod * mix[2])
-    dms[2] = rounded(dprod * mix[1])
+    dms[1] = rounded(dprod * mv[...])
+    dms[2] = rounded(dprod * mk[...])
     ct = pl.program_id(0)
-    for g in range(3):
+    for g, zg in enumerate((zq, zk, zv)):
         mine = dms[g, 0:own, :]
         total = taps[g, 0:1, :] * mine
-        sums[8 * g : 8 * g + 1, :] = jnp.sum(mine * zf[g, pl.ds(HALO, own), :], axis=0, keepdims=True)
+        sums[8 * g : 8 * g + 1, :] = jnp.sum(mine * zg[pl.ds(HALO, own), :], axis=0, keepdims=True)
         for j in range(1, 7):
             total = total + taps[g, j : j + 1, :] * dms[g, pl.ds(j, own), :]
             sums[8 * g + j : 8 * g + j + 1, :] = jnp.sum(
-                mine * zf[g, pl.ds(HALO - j, own), :], axis=0, keepdims=True
+                mine * zg[pl.ds(HALO - j, own), :], axis=0, keepdims=True
             )
         sums[8 * g + 7 : 8 * g + 8, :] = jnp.zeros((1, 128), F32)
         dz[g] = total.astype(BF16)
@@ -351,10 +325,10 @@
         out[...] = acc[...].astype(BF16)
 
 
-def weight_term(place, arrived, *refs):
+def weight_term(yi, ci, arrived, *refs):
     *tokens, term = refs
-    me = place[2]
-    core = place[3]
+    me = yi[0]
+    core = ci[0]
     chunk = term.shape[2]
     slots = (me, lax.bitwise_xor(me, 1), 3 - me, lax.bitwise_xor(3 - me, 1))
     pairs = []
@@ -387,25 +361,32 @@
             blocks[2 * q + h] = part.astype(BF16)
 
 
-def make_sum(final):
-    def add_parts(p0, p1, p2, p3, out):
-        total = p0[...].astype(F32) + p1[...].astype(F32) + p2[...].astype(F32) + p3[...].astype(F32)
-        out[...] = total.astype(BF16)
-
-    def close_sums(place, amp, p0, p1, p2, p3, grad_taps, grad_res, held):
-        total = p0[...].astype(F32) + p1[...].astype(F32) + p2[...].astype(F32) + p3[...].astype(F32)
-        total = total * final
+def added(refs):
+    total = refs[0][...].astype(F32)
+    for ref in refs[1:]:
+        total = total + ref[...].astype(F32)
+    return total
+
+
+def add_parts(*refs):
+    refs[-1][...] = added(refs[:-1]).astype(BF16)
+
+
+def make_close_sums(scale):
+    def close_sums(xi, zi, yi, amp, *refs):
+        *parts, grad_taps, grad_res, held = refs
+        total = added(parts) * scale
         width = grad_taps.shape[1] // 3
         for g in range(3):
             grad_taps[:, g * width : (g + 1) * width] = total[8 * g : 8 * g + 7, 0:width]
         count = grad_res.shape[0]
-        index = (place[0] * 4 + place[1]) * 4 + place[2]
+        index = (xi[0] * 4 + zi[0]) * 4 + yi[0]
         moved = pltpu.roll(total[24:40, :], lax.rem(PADC - index * count, PADC), 1)
         held[...] = jnp.zeros(held.shape, F32)
         held[0:MODES, :] = moved[:, 0:128]
         grad_res[...] = held[...].T[0:count, 0:MODES] * amp[...]
 
-    return close_sums if final else add_parts
+    return close_sums
 
 
 def make_close(scale):
@@ -438,13 +419,15 @@
     count = 64
     piece = chans // 16
     fblk = depth // count
-    xi, zi, yi = lax.axis_index("x"), lax.axis_index("zl"), lax.axis_index("y")
-    place = jnp.stack([xi, zi, yi, lax.axis_index("core")]).astype(jnp.int32)
-    feats, cot, rates, place = lax.optimization_barrier((feats, cot, rates, place))
     ctx = ("x", "zl", "y")
     scale = 1.0 / math.sqrt(4 * count * own)
     smem = pl.BlockSpec(memory_space=pltpu.SMEM)
     vm = pl.BlockSpec(memory_space=pltpu.VMEM)
+    names = ("x", "zl", "y", "core")
+    feats, cot, rates, *where = lax.optimization_barrier(
+        (feats, cot, rates, *[lax.axis_index(n) for n in names])
+    )
+    xi, zi, yi, ci = [w.reshape(1) for w in where]
     anywhere = pl.BlockSpec(memory_space=pl.ANY)
     head, tail, block, taps, amp_mine = pl.pallas_call(
         prepare,
@@ -471,52 +454,53 @@
     )(feats, cot.T, rates, residues, conv_taps)
     tprev = lax.ppermute(tail, ctx, [(i, i + 1) for i in range(count - 1)])
     nexts = lax.ppermute(head, ctx, [(i, i - 1) for i in range(1, count)])
+    ext_rows = own + 2 * HALO
+    project_out = [jax.ShapeDtypeStruct((ext_rows, PADC), F32), jax.ShapeDtypeStruct((EXT, PADC), F32)]
+    project_scratch = [
+        pltpu.VMEM((own, depth), BF16),
+        pltpu.VMEM((width, depth), BF16),
+        pltpu.SemaphoreType.DMA((3,)),
+    ]
+    project_cost = pl.CostEstimate(flops=500000000, bytes_accessed=4000000, transcendentals=0)
+    first = [
+        pltpu.VMEM((PADC, own), F32),
+        pltpu.VMEM((width, own), BF16),
+        pltpu.SemaphoreType.DMA,
+    ]
     held, each = block, width // count
-    for axis, ax in ((2, "y"), (1, "zl")):
+    projected = []
+    for g, (me, ax) in enumerate(((yi, "y"), (zi, "zl"), (xi, "x"))):
         blocks = [held] + [ring(held, ax, d) for d in (1, 2, 3)]
+        done = pl.pallas_call(
+            make_project(g),
+            in_specs=[vm] * 3 + [anywhere] * (3 if g == 0 else 2),
+            out_specs=[vm] * (3 if g == 0 else 2),
+            out_shape=project_out + project_out[1:] if g == 0 else project_out,
+            scratch_shapes=project_scratch + first if g == 0 else project_scratch,
+            compiler_params=params((57, 56, 52)[g]),
+            cost_estimate=project_cost,
+            name="project",
+        )(tprev, nexts, taps, feats, w_in.T, *((cot.T,) if g == 0 else ()))
+        *blocks, zg, mg = lax.optimization_barrier((*blocks, done[0], done[1]))
+        projected.append((zg, mg))
+        if g == 0:
+            cots = done[2]
+        if g == 2:
+            break
         each = 4 * each
         held = pl.pallas_call(
-            make_join(axis),
+            join_params,
             in_specs=[smem] + [vm] * 4,
             out_specs=vm,
             out_shape=jax.ShapeDtypeStruct((2 * MODES, each), F32),
             scratch_shapes=[pltpu.VMEM((2 * MODES, 256), F32)],
             compiler_params=params(4),
             name="join_params",
-        )(place, *blocks)
-    blocks = [held] + [ring(held, "x", d) for d in (1, 2, 3)]
-
-    kblk = 256
-    ext_rows = own + 2 * HALO
-    shapes = [(3, ext_rows, PADC), (3, EXT, PADC), (EXT, PADC), (EXT, PADC), (EXT, PADC)]
-    zf, mix, cots, us, dls = pl.pallas_call(
-        project,
-        in_specs=[vm] * 3 + [anywhere] * 3,
-        out_specs=[anywhere] * 3 + [vm] * 2,
-        out_shape=[jax.ShapeDtypeStruct(s, F32) for s in shapes],
-        scratch_shapes=[
-            pltpu.VMEM((ext_rows, chans), F32),
-            pltpu.VMEM((PADC, own), F32),
-            pltpu.VMEM((depth // kblk, chans, kblk), BF16),
-            pltpu.VMEM(shapes[0], F32),
-            pltpu.VMEM(shapes[1], F32),
-            pltpu.VMEM(shapes[2], F32),
-            pltpu.VMEM((own, depth), BF16),
-            pltpu.VMEM((width, own), BF16),
-            pltpu.SemaphoreType.DMA((depth // kblk,)),
-            pltpu.SemaphoreType.DMA,
-            pltpu.SemaphoreType.DMA((2, PADC // 128)),
-            pltpu.SemaphoreType.DMA((2,)),
-        ],
-        compiler_params=params(51),
-        cost_estimate=pl.CostEstimate(flops=1500000000, bytes_accessed=14000000, transcendentals=0),
-        name="project",
-    )(tprev, nexts, taps, feats, cot.T, w_in.T)
-
-    *blocks, us, dls = lax.optimization_barrier((*blocks, us, dls))
+        )(me, *blocks)
+    (zq, mq), (zk, mk), (zv, mv) = projected
     rate, gain, es, ends, endb = pl.pallas_call(
         end_states,
-        in_specs=[smem] + [vm] * 6,
+        in_specs=[smem] + [vm] * 8,
         out_specs=[vm] * 5,
         out_shape=[
             jax.ShapeDtypeStruct((MODES, PADC), F32),
@@ -533,14 +517,14 @@
         compiler_params=params(16),
         cost_estimate=pl.CostEstimate(flops=20000000, bytes_accessed=3000000, transcendentals=0),
         name="end_states",
-    )(place, *blocks, us, dls)
+    )(xi, *blocks, mq, mk, mv, cots)
 
     prefixes = []
     total, sent = ends, endb
-    for axis, ax, span in ((2, "y", own), (1, "zl", 4 * own), (0, "x", 16 * own)):
+    for me, ax, span in ((yi, "y", own), (zi, "zl", 4 * own), (xi, "x", 16 * own)):
         near = [ring(sent, ax, d) for d in (1, 2, 3)]
         total, sent, prefix = pl.pallas_call(
-            make_level(axis, span),
+            make_level(span),
             in_specs=[smem] + [vm] * 5,
             out_specs=[vm] * 3,
             out_shape=[
@@ -550,7 +534,7 @@
             ],
             compiler_params=params(8),
             name="level",
-        )(place, total, *near, rate)
+        )(me, total, *near, rate)
         prefixes.append(prefix)
         if ax == "y":
             mine, _ = lax.optimization_barrier((feats, sent))
@@ -560,6 +544,12 @@
             pair, opposite, _ = lax.optimization_barrier((pair, opposite, sent))
             far = lax.ppermute(pair, "y", [(i, 3 - i) for i in range(4)])
 
+    def swapped(a):
+        return lax.ppermute(a, "core", [(0, 1), (1, 0)])
+
+    theirs = [swapped(a) for a in (mine, pair, opposite)]
+    *theirs, prefixes[2] = lax.optimization_barrier((*theirs, prefixes[2]))
+
     def tiles(shape):
         lead = len(shape) - 1
         return pl.BlockSpec(shape, lambda k: (0,) * lead + (k,))
@@ -569,8 +559,9 @@
         grid=(PADC // 128,),
         in_specs=[
             smem,
-            tiles((3, ext_rows, 128)),
-            tiles((3, EXT, 128)),
+            smem,
+            *[tiles((ext_rows, 128))] * 3,
+            *[tiles((EXT, 128))] * 3,
             tiles((2, MODES, 8, 128)),
             tiles((2 * MODES, 128)),
             tiles((2 * MODES, 128)),
@@ -602,42 +593,45 @@
             pltpu.VMEM((3, EXT, 128), F32),
             pltpu.VMEM((3, PADC, own), F32),
         ],
-        compiler_params=params(50),
+        compiler_params=params(24),
         cost_estimate=pl.CostEstimate(flops=200000000, bytes_accessed=10000000, transcendentals=0),
         name="finish",
-    )(place, zf, mix, es, *prefixes, taps, rate, gain, cots)
+    )(zi, yi, zq, zk, zv, mq, mk, mv, es, *prefixes, taps, rate, gain, cots)
     output = outt.T
     blocks_of = [mine, pair, opposite, far]
-    theirs = [lax.ppermute(a, "core", [(0, 1), (1, 0)]) for a in blocks_of]
+    theirs.append(swapped(far))
 
     def spread(a, ax):
         return [a] + [ring(a, ax, d) for d in (1, 2, 3)]
 
-    def summed(a, ax):
+    def swap(a, ax):
+        return [a, lax.ppermute(a, ax, [(0, 1), (1, 0)])]
+
+    def summed(parts):
         return pl.pallas_call(
-            make_sum(None),
-            in_specs=[vm] * 4,
+            add_parts,
+            in_specs=[vm] * len(parts),
             out_specs=vm,
             out_shape=jax.ShapeDtypeStruct((40, PADC), BF16),
             compiler_params=params(4),
             name="add_parts",
-        )(*spread(a, ax))
+        )(*parts)
 
     arrived = lax.all_to_all(dzb, ("y", "core"), split_axis=0, concat_axis=0, tiled=True)
-    sums = summed(sums, "zl")
+    sums = summed(spread(summed(swap(sums, "core")), "zl"))
     arrived, sums = lax.optimization_barrier((arrived, sums))
     term = pl.pallas_call(
         weight_term,
-        in_specs=[smem] + [vm] * 9,
+        in_specs=[smem] * 2 + [vm] * 9,
         out_specs=vm,
         out_shape=jax.ShapeDtypeStruct((4, 2 * piece, depth // 4), BF16),
         compiler_params=params(24),
         cost_estimate=pl.CostEstimate(flops=1200000000, bytes_accessed=6000000, transcendentals=0),
         name="weight_term",
-    )(place, arrived, *blocks_of, *theirs)
+    )(yi, ci, arrived, *blocks_of, *theirs)
     got = lax.all_to_all(term, "x", 0, 0, tiled=True)
     sums, _ = lax.optimization_barrier((sums, term))
-    sums = summed(summed(sums, "y"), ("zh", "core"))
+    sums = summed(swap(summed(spread(sums, "y")), "zh"))
     got, sums = lax.optimization_barrier((got, sums))
     blocks = pl.pallas_call(
         split_rows,
@@ -661,13 +655,13 @@
         out_specs=pl.BlockSpec((own, depth), lambda g: (0, 0)),
         out_shape=jax.ShapeDtypeStruct((own, depth), BF16),
         scratch_shapes=[pltpu.VMEM((own, depth), F32)],
-        compiler_params=params(57),
+        compiler_params=params(24),
         cost_estimate=pl.CostEstimate(flops=1200000000, bytes_accessed=11000000, transcendentals=0),
         name="token_grads",
     )(dz, w_in.T)
     grad_taps, grad_residues = pl.pallas_call(
-        make_sum(scale),
-        in_specs=[smem] + [vm] * 5,
+        make_close_sums(scale),
+        in_specs=[smem] * 3 + [vm] * 5,
         out_specs=[vm] * 2,
         out_shape=[
             jax.ShapeDtypeStruct((7, chans), F32),
@@ -676,7 +670,7 @@
         scratch_shapes=[pltpu.VMEM((128, 128), F32)],
         compiler_params=params(4),
         name="close_sums",
-    )(place, amp_mine, *parts)
+    )(xi, zi, yi, amp_mine, *parts)
     grad_weight = pl.pallas_call(
         make_close(scale),
         in_specs=[vm],

time: 171 us -> 163 us (0.953)
  waiting for transfers between devices: 45.3 us -> 28.3 us
  starting transfers between devices: 77.2 us -> 85.2 us
    ppermute x30 -> x27, waiting for transfers between devices: 42.3 us -> 21.6 us  [ring(): return lax.ppermute(a, ax, [(i, (i + d) % 4) for i in range(4)])]
    ppermute x4 -> x6, waiting for transfers between devices: 0.01 us -> 6.32 us  [the longest x2 6.31 us: swap(): return [a, lax.ppermute(a, ax, [(0, 1), (1, 0)])]]
    ppermute x4 -> x6, starting transfers between devices: 1.11 us -> 5.78 us  [the longest x2 4.68 us: swap(): return [a, lax.ppermute(a, ax, [(0, 1), (1, 0)])]]
    pallas_call x1, Pallas kernels: 6.01 us -> 2.74 us  [local(): pl.pallas_call(token_grads, grid=(3,), in_specs=[pl.BlockSpec((1, own, PA...]
    pallas_call x13 -> x16, Pallas kernels: 30 us -> 32.5 us  [the longest x3 14.8 us: local(): pl.pallas_call(make_project(g), in_specs=[vm] * 3 + [anywhere] * (3 if g...]
    ppermute x1, waiting for transfers between devices: 1.81 us -> 0.01 us  [local(): opposite = lax.ppermute(mine, 'y', [(i, 3 - i) for i in range(4)])]
    unnamed x22 -> x40, local copies, waits for them, and re-layouts: 6.61 us -> 8.1 us
    ppermute x30 -> x27, starting transfers between devices: 51.3 us -> 52.3 us  [ring(): return lax.ppermute(a, ax, [(i, (i + d) % 4) for i in range(4)])]
  transfers between devices with their start and end apart: 42 -> 41, of which waited for: 21 -> 15; matrix products, arithmetic and copies ran while one was open for 0% -> 0% of each run, Pallas kernels for 17% -> 18%
where the time goes in v6:
time: 163 us; the launch traced here: 162 us
  starting transfers between devices  85.2 us (52%)
  Pallas kernels  39 us (24%)
  waiting for transfers between devices  28.3 us (17%)
  local copies, waits for them, and re-layouts  8.1 us (5%)
    ppermute x27, starting transfers between devices, ring(): return lax.ppermute(a, ax, [(i, (i + d) % 4) for i in range(4)])  52.3 us
    ppermute x27, waiting for transfers between devices, ring(): return lax.ppermute(a, ax, [(i, (i + d) % 4) for i in range(4)])  21.6 us
    pallas_call x3, Pallas kernels, local(): pl.pallas_call(make_project(g), in_specs=[vm] * 3 + [anywhere] * (3 if g...  14.8 us
    pallas_call x1, Pallas kernels, local(): pl.pallas_call(finish, grid=(PADC // 128,), in_specs=[smem, smem, *[tiles...  9.36 us
    all_to_all x1, starting transfers between devices, local(): last = lax.all_to_all(blocks, ('zl', 'y', 'zh'), 0, 0, tiled=True)  8.39 us
    unnamed x40, local copies, waits for them, and re-layouts  8.1 us
    ppermute x2, waiting for transfers between devices, swap(): return [a, lax.ppermute(a, ax, [(0, 1), (1, 0)])]  6.31 us
    ppermute x2, starting transfers between devices, swap(): return [a, lax.ppermute(a, ax, [(0, 1), (1, 0)])]  4.68 us
  transfers between devices with their start and end apart: 41, of which 15 were waited for; matrix products, arithmetic and copies ran while one was open for 0% of the time, Pallas kernels for 18%

profile of v6, /device:TPU:32, one launch (start us, length us, event | category | flops | bytes accessed | tf_op | source)
XLA Modules:
  0.0 161.6 jit_solution(4165878893692744934)
XLA Ops:
  0.6 1.9 %prepare.1 = (bf16[16,2560]{1,0:T(8,128)(2,1)}, bf16[16,1536]{1,0:T(8,128)(2,1)}, f32[32,15]{1,0:T(8,128)}, f32[3,8,1024]{2,1,0:T(8,128)}, f32[15,16]{1,0:T(8,128)}) custom-call(bf16[128,1536]{1,0:T(8,128)(2,1)} %bitcast.16, bf16[960,128]{1,0:T(8,128)(2,1)} %bitcast.24, f32[15,16]{1,0:T(8,128)} %rates, f32[15,16]{1,0:T(8,128)} %residues.1, f32[7,2880]{1,0:T(8,128)} %conv.1), custom_call_target="tpu_custom_call" | custom-call | tf_op jit(solution)/shard_map/prepare/pallas_call | solution.py:432
  2.6 4.5 %collective-permute-start.4 = (bf16[16,2560]{1,0:T(8,128)(2,1)}, bf16[16,2560]{1,0:T(8,128)(2,1)S(1)}, u32[]{:S(2)}, u32[]{:S(2)}) collective-permute-start(bf16[16,2560]{1,0:T(8,128)(2,1)} %get-tuple-element.81), channel_id=1, source_target_pairs={{4,0},{8,4},{12,8},{16,12},{20,16},{24,20},{28,24},{32,28},{36,32}... | collective-permute-start | bytes 245768 | tf_op jit(solution)/shard_map/ppermute | solution.py:456
  7.1 1.9 %collective-permute-start.3 = (bf16[16,1536]{1,0:T(8,128)(2,1)}, bf16[16,1536]{1,0:T(8,128)(2,1)S(1)}, u32[]{:S(2)}, u32[]{:S(2)}) collective-permute-start(bf16[16,1536]{1,0:T(8,128)(2,1)} %get-tuple-element.80), channel_id=1, source_target_pairs={{0,4},{4,8},{8,12},{12,16},{16,20},{20,24},{24,28},{28,32},{32,36}... | collective-permute-start | bytes 147464 | tf_op jit(solution)/shard_map/ppermute | solution.py:455
  9.0 1.1 collective-permute-start
  10.1 5.0 %collective-permute-start.1 = (f32[32,15]{1,0:T(8,128)}, f32[32,15]{1,0:T(8,128)S(1)}, u32[]{:S(2)}, u32[]{:S(2)}) collective-permute-start(f32[32,15]{1,0:T(8,128)} %get-tuple-element.86.r0), channel_id=1, source_target_pairs={{0,8},{4,12},{8,0},{12,4},{1,9},{5,13},{9,1},{13,5},{2,10},{6,14},... | collective-permute-start | bytes 5768 | tf_op jit(solution)/shard_map/ppermute | solution.py:406
  16.1 6.0 %project.3 = (f32[160,1024]{1,0:T(8,128)}, f32[136,1024]{1,0:T(8,128)}, f32[136,1024]{1,0:T(8,128)}) custom-call(bf16[16,1536]{1,0:T(8,128)(2,1)} %copy-done.10, bf16[16,2560]{1,0:T(8,128)(2,1)} %copy-done.6, f32[3,8,1024]{2,1,0:T(8,128)} %get-tuple-element.82.refs_2_.taps, bf16[128,1536]{1,0:T(8,128)(2,1)} %bitcast.17, bf16[2880,1536]{1,0:T(8,128)(2,1)} %bitcast.12, ...), custom_call_target="tpu_custom_call" | custom-call | flops 500000000 | bytes 4000000 | tf_op jit(solution)/shard_map/project/pallas_call | solution.py:474
  22.2 2.0 %collective-permute-start.5 = (f32[32,60]{1,0:T(8,128)S(1)}, f32[32,60]{1,0:T(8,128)S(1)}, u32[]{:S(2)}, u32[]{:S(2)}) collective-permute-start(f32[32,60]{1,0:T(8,128)S(1)} %join_params.2.r0), channel_id=1, source_target_pairs={{0,16},{16,32},{32,48},{48,0},{1,17},{17,33},{33,49},{49,1},{2,18}... | collective-permute-start | bytes 23048 | tf_op jit(solution)/shard_map/ppermute | solution.py:406
  24.2 3.9 %collective-permute-start.6 = (f32[32,60]{1,0:T(8,128)S(1)}, f32[32,60]{1,0:T(8,128)S(1)}, u32[]{:S(2)}, u32[]{:S(2)}) collective-permute-start(f32[32,60]{1,0:T(8,128)S(1)} %join_params.2.r0), channel_id=1, source_target_pairs={{0,32},{16,48},{32,0},{48,16},{1,33},{17,49},{33,1},{49,17},{2,34}... | collective-permute-start | bytes 23048 | tf_op jit(solution)/shard_map/ppermute | solution.py:406
  28.1 1.9 %collective-permute-start.7 = (f32[32,60]{1,0:T(8,128)S(1)}, f32[32,60]{1,0:T(8,128)S(1)}, u32[]{:S(2)}, u32[]{:S(2)}) collective-permute-start(f32[32,60]{1,0:T(8,128)S(1)} %join_params.2.r0), channel_id=1, source_target_pairs={{0,48},{16,0},{32,16},{48,32},{1,49},{17,1},{33,17},{49,33},{2,50}... | collective-permute-start | bytes 23048 | tf_op jit(solution)/shard_map/ppermute | solution.py:406
  30.0 5.4 %project.4 = (f32[160,1024]{1,0:T(8,128)}, f32[136,1024]{1,0:T(8,128)}) custom-call(bf16[16,1536]{1,0:T(8,128)(2,1)} %copy-done.10, bf16[16,2560]{1,0:T(8,128)(2,1)} %copy-done.6, f32[3,8,1024]{2,1,0:T(8,128)} %get-tuple-element.82.refs_2_.taps, bf16[128,1536]{1,0:T(8,128)(2,1)} %bitcast.18, bf16[2880,1536]{1,0:T(8,128)(2,1)} %bitcast.13), custom_call_target="tpu_custom_call" | custom-call | flops 500000000 | bytes 4000000 | tf_op jit(solution)/shard_map/project/pallas_call | solution.py:474
  35.6 5.0 %collective-permute-start.10 = (f32[32,240]{1,0:T(8,128)S(1)}, f32[32,240]{1,0:T(8,128)S(1)}, u32[]{:S(2)}, u32[]{:S(2)}) collective-permute-start(f32[32,240]{1,0:T(8,128)S(1)} %join_params.3.r0), channel_id=1, source_target_pairs={{0,192},{64,0},{128,64},{192,128},{1,193},{65,1},{129,65},{193,129... | collective-permute-start | bytes 92168 | tf_op jit(solution)/shard_map/ppermute | solution.py:406
  40.6 2.0 %collective-permute-start.9 = (f32[32,240]{1,0:T(8,128)S(1)}, f32[32,240]{1,0:T(8,128)S(1)}, u32[]{:S(2)}, u32[]{:S(2)}) collective-permute-start(f32[32,240]{1,0:T(8,128)S(1)} %join_params.3.r0), channel_id=1, source_target_pairs={{0,128},{64,192},{128,0},{192,64},{1,129},{65,193},{129,1},{193,65... | collective-permute-start | bytes 92168 | tf_op jit(solution)/shard_map/ppermute | solution.py:406
  42.6 3.5 %project.5 = (f32[160,1024]{1,0:T(8,128)S(1)}, f32[136,1024]{1,0:T(8,128)S(1)}) custom-call(bf16[16,1536]{1,0:T(8,128)(2,1)S(1)} %copy-done.11, bf16[16,2560]{1,0:T(8,128)(2,1)S(1)} %copy-done.7, f32[3,8,1024]{2,1,0:T(8,128)S(1)} %copy-done.5, bf16[128,1536]{1,0:T(8,128)(2,1)S(1)} %bitcast.19, bf16[2880,1536]{1,0:T(8,128)(2,1)} %bitcast.14), custom_call_target="tpu_custom_call" | custom-call | flops 500000000 | bytes 4000000 | tf_op jit(solution)/shard_map/project/pallas_call | solution.py:474
  46.2 2.2 %end_states.1 = (f32[16,1024]{1,0:T(8,128)S(1)}, f32[16,1024]{1,0:T(8,128)S(1)}, f32[2,16,8,1024]{3,2,1,0:T(8,128)S(1)}, f32[32,1024]{1,0:T(8,128)S(1)}, bf16[32,1024]{1,0:T(8,128)(2,1)S(1)}) custom-call(s32[1]{0:T(128)} %bitcast.6.me.index.xi, f32[32,240]{1,0:T(8,128)S(1)} %join_params.3.r0, f32[32,240]{1,0:T(8,128)S(1)} %collective-permute-done.8.r1, ...), custom_call_target="tpu_custom_call" | custom-call | flops 20000000 | bytes 3000000 | tf_op jit(solution)/shard_map/end_states/pallas_call | solution.py:501
  48.6 3.1 %collective-permute-start.13 = (bf16[32,1024]{1,0:T(8,128)(2,1)S(1)}, bf16[32,1024]{1,0:T(8,128)(2,1)S(1)}, u32[]{:S(2)}, u32[]{:S(2)}) collective-permute-start(bf16[32,1024]{1,0:T(8,128)(2,1)S(1)} %get-tuple-element.111), channel_id=1, source_target_pairs={{0,12},{4,0},{8,4},{12,8},{1,13},{5,1},{9,5},{13,9},{2,14},{6,2},{... | collective-permute-start | bytes 196616 | tf_op jit(solution)/shard_map/ppermute | solution.py:406
  51.7 2.9 %collective-permute-done.11.r1 = bf16[32,1024]{1,0:T(8,128)(2,1)S(1)} collective-permute-done((bf16[32,1024]{1,0:T(8,128)(2,1)S(1)}, bf16[32,1024]{1,0:T(8,128)(2,1)S(1)}, u32[]{:S(2)}, u32[]{:S(2)}) %collective-permute-start.11) | collective-permute-done | bytes 65568 | tf_op jit(solution)/shard_map/ppermute | solution.py:406
  54.6 2.2 %collective-permute-done.13.r3 = bf16[32,1024]{1,0:T(8,128)(2,1)S(1)} collective-permute-done((bf16[32,1024]{1,0:T(8,128)(2,1)S(1)}, bf16[32,1024]{1,0:T(8,128)(2,1)S(1)}, u32[]{:S(2)}, u32[]{:S(2)}) %collective-permute-start.13) | collective-permute-done | bytes 65568 | tf_op jit(solution)/shard_map/ppermute | solution.py:406
  58.7 2.1 %collective-permute-start.14 = (bf16[32,1024]{1,0:T(8,128)(2,1)S(1)}, bf16[32,1024]{1,0:T(8,128)(2,1)S(1)}, u32[]{:S(2)}, u32[]{:S(2)}) collective-permute-start(bf16[32,1024]{1,0:T(8,128)(2,1)S(1)} %get-tuple-element.115), channel_id=1, source_target_pairs={{0,16},{16,32},{32,48},{48,0},{1,17},{17,33},{33,49},{49,1},{2,18}... | collective-permute-start | bytes 196616 | tf_op jit(solution)/shard_map/ppermute | solution.py:406
  60.8 1.8 %collective-permute-start.15 = (bf16[32,1024]{1,0:T(8,128)(2,1)S(1)}, bf16[32,1024]{1,0:T(8,128)(2,1)S(1)}, u32[]{:S(2)}, u32[]{:S(2)}) collective-permute-start(bf16[32,1024]{1,0:T(8,128)(2,1)S(1)} %get-tuple-element.115), channel_id=1, source_target_pairs={{0,32},{16,48},{32,0},{48,16},{1,33},{17,49},{33,1},{49,17},{2,34}... | collective-permute-start | bytes 196616 | tf_op jit(solution)/shard_map/ppermute | solution.py:406
  63.0 3.0 %collective-permute-done.15.r2 = bf16[32,1024]{1,0:T(8,128)(2,1)S(1)} collective-permute-done((bf16[32,1024]{1,0:T(8,128)(2,1)S(1)}, bf16[32,1024]{1,0:T(8,128)(2,1)S(1)}, u32[]{:S(2)}, u32[]{:S(2)}) %collective-permute-start.15) | collective-permute-done | bytes 65568 | tf_op jit(solution)/shard_map/ppermute | solution.py:406
  67.6 2.1 %collective-permute-start.22 = (bf16[32,1024]{1,0:T(8,128)(2,1)S(1)}, bf16[32,1024]{1,0:T(8,128)(2,1)S(1)}, u32[]{:S(2)}, u32[]{:S(2)}) collective-permute-start(bf16[32,1024]{1,0:T(8,128)(2,1)S(1)} %get-tuple-element.118), channel_id=1, source_target_pairs={{0,64},{64,128},{128,192},{192,0},{1,65},{65,129},{129,193},{193,1... | collective-permute-start | bytes 196616 | tf_op jit(solution)/shard_map/ppermute | solution.py:406
  69.7 2.6 %collective-permute-start.23 = (bf16[32,1024]{1,0:T(8,128)(2,1)S(1)}, bf16[32,1024]{1,0:T(8,128)(2,1)S(1)}, u32[]{:S(2)}, u32[]{:S(2)}) collective-permute-start(bf16[32,1024]{1,0:T(8,128)(2,1)S(1)} %get-tuple-element.118), channel_id=1, source_target_pairs={{0,128},{64,192},{128,0},{192,64},{1,129},{65,193},{129,1},{193,65... | collective-permute-start | bytes 196616 | tf_op jit(solution)/shard_map/ppermute | solution.py:406
  73.2 2.4 %collective-permute-start.29 = (bf16[128,1536]{1,0:T(8,128)(2,1)S(1)}, bf16[128,1536]{1,0:T(8,128)(2,1)}, u32[]{:S(2)}, u32[]{:S(2)}) collective-permute-start(bf16[128,1536]{1,0:T(8,128)(2,1)S(1)} %collective-permute-done.18.refs_1_), channel_id=1, source_target_pairs={{0,12},{4,8},{8,4},{12,0},{1,13},{5,9},{9,5},{13,1},{2,14},{6,10},... | collective-permute-start | bytes 1179656 | tf_op jit(solution)/shard_map/ppermute | solution.py:545
  75.8 2.4 %collective-permute-start.24 = (bf16[32,1024]{1,0:T(8,128)(2,1)S(1)}, bf16[32,1024]{1,0:T(8,128)(2,1)S(1)}, u32[]{:S(2)}, u32[]{:S(2)}) collective-permute-start(bf16[32,1024]{1,0:T(8,128)(2,1)S(1)} %get-tuple-element.118), channel_id=1, source_target_pairs={{0,192},{64,0},{128,64},{192,128},{1,193},{65,1},{129,65},{193,129... | collective-permute-start | bytes 196616 | tf_op jit(solution)/shard_map/ppermute | solution.py:406
  78.1 1.9 %collective-permute-done.24.r3 = bf16[32,1024]{1,0:T(8,128)(2,1)S(1)} collective-permute-done((bf16[32,1024]{1,0:T(8,128)(2,1)S(1)}, bf16[32,1024]{1,0:T(8,128)(2,1)S(1)}, u32[]{:S(2)}, u32[]{:S(2)}) %collective-permute-start.24) | collective-permute-done | bytes 65568 | tf_op jit(solution)/shard_map/ppermute | solution.py:406
  81.6 9.4 %finish.1 = (bf16[960,128]{1,0:T(8,128)(2,1)}, bf16[3,128,1024]{2,1,0:T(8,128)(2,1)S(1)}, bf16[8,360,128]{2,1,0:T(8,128)(2,1)}, bf16[40,1024]{1,0:T(8,128)(2,1)S(1)}) custom-call(s32[1]{0:T(128)} %bitcast.2.me.index.zi, s32[1]{0:T(128)} %bitcast.3.me.index.yi, f32[160,1024]{1,0:T(8,128)S(1)} %copy-done.8, f32[160,1024]{1,0:T(8,128)S(1)} %copy-done.9, ...), custom_call_target="tpu_custom_call" | custom-call | flops 200000000 | bytes 10000000 | tf_op jit(solution)/shard_map/finish/pallas_call | solution.py:557
  91.6 4.0 %all-to-all-start = ((bf16[8,360,128]{2,1,0:T(8,128)(2,1)}), bf16[8,360,128]{2,1,0:T(8,128)(2,1)S(1)}, u32[]{:S(2)}, u32[]{:S(2)}) async-start(bf16[8,360,128]{2,1,0:T(8,128)(2,1)} %get-tuple-element.127), calls=%async_computation | async-start | bytes 1474560 | tf_op jit(solution)/shard_map/all_to_all | solution.py:620
  96.1 1.6 collective-permute-done.25.refs_1_
  98.6 1.4 collective-permute-start.26
  100.0 1.8 %collective-permute-start.27 = (bf16[40,1024]{1,0:T(8,128)(2,1)S(1)}, bf16[40,1024]{1,0:T(8,128)(2,1)S(1)}, u32[]{:S(2)}, u32[]{:S(2)}) collective-permute-start(bf16[40,1024]{1,0:T(8,128)(2,1)S(1)} %add_parts.4.refs_0_), channel_id=1, source_target_pairs={{0,32},{16,48},{32,0},{48,16},{1,33},{17,49},{33,1},{49,17},{2,34}... | collective-permute-start | bytes 245768 | tf_op jit(solution)/shard_map/ppermute | solution.py:406
  101.8 1.9 %collective-permute-start.28 = (bf16[40,1024]{1,0:T(8,128)(2,1)S(1)}, bf16[40,1024]{1,0:T(8,128)(2,1)S(1)}, u32[]{:S(2)}, u32[]{:S(2)}) collective-permute-start(bf16[40,1024]{1,0:T(8,128)(2,1)S(1)} %add_parts.4.refs_0_), channel_id=1, source_target_pairs={{0,48},{16,0},{32,16},{48,32},{1,49},{17,1},{33,17},{49,33},{2,50}... | collective-permute-start | bytes 245768 | tf_op jit(solution)/shard_map/ppermute | solution.py:406
  103.7 3.9 %collective-permute-done.27.refs_2_ = bf16[40,1024]{1,0:T(8,128)(2,1)S(1)} collective-permute-done((bf16[40,1024]{1,0:T(8,128)(2,1)S(1)}, bf16[40,1024]{1,0:T(8,128)(2,1)S(1)}, u32[]{:S(2)}, u32[]{:S(2)}) %collective-permute-start.27) | collective-permute-done | bytes 81952 | tf_op jit(solution)/shard_map/ppermute | solution.py:406
  107.6 2.4 %collective-permute-done.28.refs_3_ = bf16[40,1024]{1,0:T(8,128)(2,1)S(1)} collective-permute-done((bf16[40,1024]{1,0:T(8,128)(2,1)S(1)}, bf16[40,1024]{1,0:T(8,128)(2,1)S(1)}, u32[]{:S(2)}, u32[]{:S(2)}) %collective-permute-start.28) | collective-permute-done | bytes 81952 | tf_op jit(solution)/shard_map/ppermute | solution.py:406
  111.7 3.9 %weight_term.1 = bf16[4,360,384]{2,1,0:T(8,128)(2,1)} custom-call(s32[1]{0:T(128)} %bitcast.3.me.index.yi, s32[1]{0:T(128)} %bitcast.9.ci, bf16[8,360,128]{2,1,0:T(8,128)(2,1)S(1)} %all-to-all-done.arrived, bf16[128,1536]{1,0:T(8,128)(2,1)S(1)} %bitcast.23, bf16[128,1536]{1,0:T(8,128)(2,1)S(1)} %collective-permute-done.18.refs_1_, ...), custom_call_target="tpu_custom_call" | custom-call | flops 1200000000 | bytes 6000000 | tf_op jit(solution)/shard_map/weight_term/pallas_call | solution.py:623
  115.6 4.4 %all-to-all-start.1 = ((bf16[4,360,384]{2,1,0:T(8,128)(2,1)}), bf16[4,360,384]{2,1,0:T(8,128)(2,1)S(1)}, u32[]{:S(2)}, u32[]{:S(2)}) async-start(bf16[4,360,384]{2,1,0:T(8,128)(2,1)} %weight_term.1), calls=%async_computation.1 | async-start | bytes 2211840 | tf_op jit(solution)/shard_map/all_to_all | solution.py:632
  119.9 1.7 %collective-permute-start.31 = (bf16[40,1024]{1,0:T(8,128)(2,1)S(1)}, bf16[40,1024]{1,0:T(8,128)(2,1)S(1)}, u32[]{:S(2)}, u32[]{:S(2)}) collective-permute-start(bf16[40,1024]{1,0:T(8,128)(2,1)S(1)} %copy-done.15), channel_id=1, source_target_pairs={{0,4},{4,8},{8,12},{12,0},{1,5},{5,9},{9,13},{13,1},{2,6},{6,10},{... | collective-permute-start | bytes 245768 | tf_op jit(solution)/shard_map/ppermute | solution.py:406
  121.6 2.7 %collective-permute-start.32 = (bf16[40,1024]{1,0:T(8,128)(2,1)S(1)}, bf16[40,1024]{1,0:T(8,128)(2,1)S(1)}, u32[]{:S(2)}, u32[]{:S(2)}) collective-permute-start(bf16[40,1024]{1,0:T(8,128)(2,1)S(1)} %copy-done.15), channel_id=1, source_target_pairs={{0,8},{4,12},{8,0},{12,4},{1,9},{5,13},{9,1},{13,5},{2,10},{6,14},... | collective-permute-start | bytes 245768 | tf_op jit(solution)/shard_map/ppermute | solution.py:406
  124.3 1.4 collective-permute-start.33
  125.8 2.4 %collective-permute-done.32.refs_2_ = bf16[40,1024]{1,0:T(8,128)(2,1)S(1)} collective-permute-done((bf16[40,1024]{1,0:T(8,128)(2,1)S(1)}, bf16[40,1024]{1,0:T(8,128)(2,1)S(1)}, u32[]{:S(2)}, u32[]{:S(2)}) %collective-permute-start.32) | collective-permute-done | bytes 81952 | tf_op jit(solution)/shard_map/ppermute | solution.py:406
  128.8 4.6 %collective-permute-start.34 = (bf16[40,1024]{1,0:T(8,128)(2,1)S(1)}, bf16[40,1024]{1,0:T(8,128)(2,1)S(1)}, u32[]{:S(2)}, u32[]{:S(2)}) collective-permute-start(bf16[40,1024]{1,0:T(8,128)(2,1)S(1)} %add_parts.6.refs_0_), channel_id=1, source_target_pairs={{0,2},{2,0},{1,3},{3,1},{4,6},{6,4},{5,7},{7,5},{8,10},{10,8},{9,1... | collective-permute-start | bytes 245768 | tf_op jit(solution)/shard_map/ppermute | solution.py:608
  133.4 4.7 %collective-permute-done.34.refs_1_ = bf16[40,1024]{1,0:T(8,128)(2,1)S(1)} collective-permute-done((bf16[40,1024]{1,0:T(8,128)(2,1)S(1)}, bf16[40,1024]{1,0:T(8,128)(2,1)S(1)}, u32[]{:S(2)}, u32[]{:S(2)}) %collective-permute-start.34) | collective-permute-done | bytes 81952 | tf_op jit(solution)/shard_map/ppermute | solution.py:608
  138.1 1.1 split_rows.1
  139.2 8.4 %all-to-all-start.2 = ((bf16[32,24,180]{2,1,0:T(8,128)(2,1)}), bf16[32,24,180]{2,1,0:T(8,128)(2,1)S(1)}, u32[]{:S(2)}, u32[]{:S(2)}) async-start(bf16[32,24,180]{2,1,0:T(8,128)(2,1)} %split_rows.1), calls=%async_computation.2 | async-start | bytes 786432 | tf_op jit(solution)/shard_map/all_to_all | solution.py:645
  147.6 2.1 %collective-permute-start.35 = (bf16[40,1024]{1,0:T(8,128)(2,1)S(1)}, bf16[40,1024]{1,0:T(8,128)(2,1)S(1)}, u32[]{:S(2)}, u32[]{:S(2)}) collective-permute-start(bf16[40,1024]{1,0:T(8,128)(2,1)S(1)} %add_parts.7.refs_0_), channel_id=1, source_target_pairs={{0,64},{64,128},{128,192},{192,0},{1,65},{65,129},{129,193},{193,1... | collective-permute-start | bytes 245768 | tf_op jit(solution)/shard_map/ppermute | solution.py:406
  149.7 2.7 %collective-permute-start.36 = (bf16[40,1024]{1,0:T(8,128)(2,1)S(1)}, bf16[40,1024]{1,0:T(8,128)(2,1)S(1)}, u32[]{:S(2)}, u32[]{:S(2)}) collective-permute-start(bf16[40,1024]{1,0:T(8,128)(2,1)S(1)} %add_parts.7.refs_0_), channel_id=1, source_target_pairs={{0,128},{64,192},{128,0},{192,64},{1,129},{65,193},{129,1},{193,65... | collective-permute-start | bytes 245768 | tf_op jit(solution)/shard_map/ppermute | solution.py:406
  152.4 1.5 collective-permute-start.37
  153.8 3.5 %copy-done = bf16[1536,2880]{0,1:T(8,128)(2,1)S(1)} copy-done((bf16[1536,2880]{0,1:T(8,128)(2,1)S(1)}, bf16[1536,2880]{0,1:T(8,128)(2,1)}, u32[]{:S(2)}) %copy-start) | copy-done | bytes 8847384
  157.4 2.7 %token_grads.1 = bf16[128,1536]{1,0:T(8,128)(2,1)} custom-call(bf16[3,128,1024]{2,1,0:T(8,128)(2,1)S(1)} %get-tuple-element.138.dz, bf16[2880,1536]{1,0:T(8,128)(2,1)S(1)} %bitcast.15), custom_call_target="tpu_custom_call" | custom-call | flops 1200000000 | bytes 11000000 | tf_op jit(solution)/shard_map/token_grads/pallas_call | solution.py:648
  (94 shorter events, 13.9 us)
Async XLA Ops:
  2.6 12.8 %collective-permute-start.4 = (bf16[16,2560]{1,0:T(8,128)(2,1)}, bf16[16,2560]{1,0:T(8,128)(2,1)S(1)}, u32[]{:S(2)}, u32[]{:S(2)}) collective-permute-start(bf16[16,2560]{1,0:T(8,128)(2,1)} %get-tuple-element.81), channel_id=1, source_target_pairs={{4,0},{8,4},{12,8},{16,12},{20,16},{24,20},{28,24},{32,28},{36,32}... | collective-permute-start | bytes 245768 | tf_op jit(solution)/shard_map/ppermute | solution.py:456
  7.1 8.3 %collective-permute-start.3 = (bf16[16,1536]{1,0:T(8,128)(2,1)}, bf16[16,1536]{1,0:T(8,128)(2,1)S(1)}, u32[]{:S(2)}, u32[]{:S(2)}) collective-permute-start(bf16[16,1536]{1,0:T(8,128)(2,1)} %get-tuple-element.80), channel_id=1, source_target_pairs={{0,4},{4,8},{8,12},{12,16},{16,20},{20,24},{24,28},{28,32},{32,36}... | collective-permute-start | bytes 147464 | tf_op jit(solution)/shard_map/ppermute | solution.py:455
  9.0 13.0 %collective-permute-start = (f32[32,15]{1,0:T(8,128)}, f32[32,15]{1,0:T(8,128)S(1)}, u32[]{:S(2)}, u32[]{:S(2)}) collective-permute-start(f32[32,15]{1,0:T(8,128)} %get-tuple-element.86.r0), channel_id=1, source_target_pairs={{0,4},{4,8},{8,12},{12,0},{1,5},{5,9},{9,13},{13,1},{2,6},{6,10},{... | collective-permute-start | bytes 5768 | tf_op jit(solution)/shard_map/ppermute | solution.py:406
  10.1 11.9 %collective-permute-start.1 = (f32[32,15]{1,0:T(8,128)}, f32[32,15]{1,0:T(8,128)S(1)}, u32[]{:S(2)}, u32[]{:S(2)}) collective-permute-start(f32[32,15]{1,0:T(8,128)} %get-tuple-element.86.r0), channel_id=1, source_target_pairs={{0,8},{4,12},{8,0},{12,4},{1,9},{5,13},{9,1},{13,5},{2,10},{6,14},... | collective-permute-start | bytes 5768 | tf_op jit(solution)/shard_map/ppermute | solution.py:406
  15.1 6.9 %collective-permute-start.2 = (f32[32,15]{1,0:T(8,128)}, f32[32,15]{1,0:T(8,128)S(1)}, u32[]{:S(2)}, u32[]{:S(2)}) collective-permute-start(f32[32,15]{1,0:T(8,128)} %get-tuple-element.86.r0), channel_id=1, source_target_pairs={{0,12},{4,0},{8,4},{12,8},{1,13},{5,1},{9,5},{13,9},{2,14},{6,2},{... | collective-permute-start | bytes 5768 | tf_op jit(solution)/shard_map/ppermute | solution.py:406
  22.2 20.4 %copy-start.1 = (bf16[1,128,1536]{2,1,0:T(8,128)(2,1)S(1)}, bf16[1,128,1536]{2,1,0:T(8,128)(2,1)}, u32[]{:S(2)}) copy-start(bf16[1,128,1536]{2,1,0:T(8,128)(2,1)} %param.6) | copy-start | bytes 1179652
  22.2 20.4 %copy-start.5 = (f32[3,8,1024]{2,1,0:T(8,128)S(1)}, f32[3,8,1024]{2,1,0:T(8,128)}, u32[]{:S(2)}) copy-start(f32[3,8,1024]{2,1,0:T(8,128)} %get-tuple-element.82.refs_2_.taps) | copy-start | bytes 294916
  22.2 20.4 %copy-start.7 = (bf16[16,2560]{1,0:T(8,128)(2,1)S(1)}, bf16[16,2560]{1,0:T(8,128)(2,1)}, u32[]{:S(2)}) copy-start(bf16[16,2560]{1,0:T(8,128)(2,1)} %copy-done.6) | copy-start | bytes 245764
  22.2 20.4 %copy-start.11 = (bf16[16,1536]{1,0:T(8,128)(2,1)S(1)}, bf16[16,1536]{1,0:T(8,128)(2,1)}, u32[]{:S(2)}) copy-start(bf16[16,1536]{1,0:T(8,128)(2,1)} %copy-done.10) | copy-start | bytes 147460
  22.2 13.2 %collective-permute-start.5 = (f32[32,60]{1,0:T(8,128)S(1)}, f32[32,60]{1,0:T(8,128)S(1)}, u32[]{:S(2)}, u32[]{:S(2)}) collective-permute-start(f32[32,60]{1,0:T(8,128)S(1)} %join_params.2.r0), channel_id=1, source_target_pairs={{0,16},{16,32},{32,48},{48,0},{1,17},{17,33},{33,49},{49,1},{2,18}... | collective-permute-start | bytes 23048 | tf_op jit(solution)/shard_map/ppermute | solution.py:406
  24.2 11.2 %collective-permute-start.6 = (f32[32,60]{1,0:T(8,128)S(1)}, f32[32,60]{1,0:T(8,128)S(1)}, u32[]{:S(2)}, u32[]{:S(2)}) collective-permute-start(f32[32,60]{1,0:T(8,128)S(1)} %join_params.2.r0), channel_id=1, source_target_pairs={{0,32},{16,48},{32,0},{48,16},{1,33},{17,49},{33,1},{49,17},{2,34}... | collective-permute-start | bytes 23048 | tf_op jit(solution)/shard_map/ppermute | solution.py:406
  28.1 7.3 %collective-permute-start.7 = (f32[32,60]{1,0:T(8,128)S(1)}, f32[32,60]{1,0:T(8,128)S(1)}, u32[]{:S(2)}, u32[]{:S(2)}) collective-permute-start(f32[32,60]{1,0:T(8,128)S(1)} %join_params.2.r0), channel_id=1, source_target_pairs={{0,48},{16,0},{32,16},{48,32},{1,49},{17,1},{33,17},{49,33},{2,50}... | collective-permute-start | bytes 23048 | tf_op jit(solution)/shard_map/ppermute | solution.py:406
  35.6 10.5 %collective-permute-start.10 = (f32[32,240]{1,0:T(8,128)S(1)}, f32[32,240]{1,0:T(8,128)S(1)}, u32[]{:S(2)}, u32[]{:S(2)}) collective-permute-start(f32[32,240]{1,0:T(8,128)S(1)} %join_params.3.r0), channel_id=1, source_target_pairs={{0,192},{64,0},{128,64},{192,128},{1,193},{65,1},{129,65},{193,129... | collective-permute-start | bytes 92168 | tf_op jit(solution)/shard_map/ppermute | solution.py:406
  40.6 5.5 %collective-permute-start.8 = (f32[32,240]{1,0:T(8,128)S(1)}, f32[32,240]{1,0:T(8,128)S(1)}, u32[]{:S(2)}, u32[]{:S(2)}) collective-permute-start(f32[32,240]{1,0:T(8,128)S(1)} %join_params.3.r0), channel_id=1, source_target_pairs={{0,64},{64,128},{128,192},{192,0},{1,65},{65,129},{129,193},{193,1... | collective-permute-start | bytes 92168 | tf_op jit(solution)/shard_map/ppermute | solution.py:406
  40.6 5.5 %collective-permute-start.9 = (f32[32,240]{1,0:T(8,128)S(1)}, f32[32,240]{1,0:T(8,128)S(1)}, u32[]{:S(2)}, u32[]{:S(2)}) collective-permute-start(f32[32,240]{1,0:T(8,128)S(1)} %join_params.3.r0), channel_id=1, source_target_pairs={{0,128},{64,192},{128,0},{192,64},{1,129},{65,193},{129,1},{193,65... | collective-permute-start | bytes 92168 | tf_op jit(solution)/shard_map/ppermute | solution.py:406
  46.2 35.4 %copy-start.9 = (f32[160,1024]{1,0:T(8,128)S(1)}, f32[160,1024]{1,0:T(8,128)}, u32[]{:S(2)}) copy-start(f32[160,1024]{1,0:T(8,128)} %get-tuple-element.92.zk) | copy-start | bytes 1966084
  48.4 33.2 %copy-start.8 = (f32[160,1024]{1,0:T(8,128)S(1)}, f32[160,1024]{1,0:T(8,128)}, u32[]{:S(2)}) copy-start(f32[160,1024]{1,0:T(8,128)} %get-tuple-element.85.zq) | copy-start | bytes 1966084
  48.4 6.3 %collective-permute-start.11 = (bf16[32,1024]{1,0:T(8,128)(2,1)S(1)}, bf16[32,1024]{1,0:T(8,128)(2,1)S(1)}, u32[]{:S(2)}, u32[]{:S(2)}) collective-permute-start(bf16[32,1024]{1,0:T(8,128)(2,1)S(1)} %get-tuple-element.111), channel_id=1, source_target_pairs={{0,4},{4,8},{8,12},{12,0},{1,5},{5,9},{9,13},{13,1},{2,6},{6,10},{... | collective-permute-start | bytes 196616 | tf_op jit(solution)/shard_map/ppermute | solution.py:406
  48.6 6.1 %collective-permute-start.12 = (bf16[32,1024]{1,0:T(8,128)(2,1)S(1)}, bf16[32,1024]{1,0:T(8,128)(2,1)S(1)}, u32[]{:S(2)}, u32[]{:S(2)}) collective-permute-start(bf16[32,1024]{1,0:T(8,128)(2,1)S(1)} %get-tuple-element.111), channel_id=1, source_target_pairs={{0,8},{4,12},{8,0},{12,4},{1,9},{5,13},{9,1},{13,5},{2,10},{6,14},... | collective-permute-start | bytes 196616 | tf_op jit(solution)/shard_map/ppermute | solution.py:406
  48.6 8.3 %collective-permute-start.13 = (bf16[32,1024]{1,0:T(8,128)(2,1)S(1)}, bf16[32,1024]{1,0:T(8,128)(2,1)S(1)}, u32[]{:S(2)}, u32[]{:S(2)}) collective-permute-start(bf16[32,1024]{1,0:T(8,128)(2,1)S(1)} %get-tuple-element.111), channel_id=1, source_target_pairs={{0,12},{4,0},{8,4},{12,8},{1,13},{5,1},{9,5},{13,9},{2,14},{6,2},{... | collective-permute-start | bytes 196616 | tf_op jit(solution)/shard_map/ppermute | solution.py:406
  57.0 9.9 %collective-permute-start.18 = (bf16[128,1536]{1,0:T(8,128)(2,1)S(1)}, bf16[128,1536]{1,0:T(8,128)(2,1)S(1)}, u32[]{:S(2)}, u32[]{:S(2)}) collective-permute-start(bf16[128,1536]{1,0:T(8,128)(2,1)S(1)} %bitcast.20), channel_id=1, source_target_pairs={{0,4},{4,0},{8,12},{12,8},{1,5},{5,1},{9,13},{13,9},{2,6},{6,2},{1... | collective-permute-start | bytes 1179656 | tf_op jit(solution)/shard_map/ppermute | solution.py:541
  58.0 9.0 %collective-permute-start.19 = (bf16[128,1536]{1,0:T(8,128)(2,1)S(1)}, bf16[128,1536]{1,0:T(8,128)(2,1)S(1)}, u32[]{:S(2)}, u32[]{:S(2)}) collective-permute-start(bf16[128,1536]{1,0:T(8,128)(2,1)S(1)} %bitcast.21), channel_id=1, source_target_pairs={{0,12},{4,8},{8,4},{12,0},{1,13},{5,9},{9,5},{13,1},{2,14},{6,10},... | collective-permute-start | bytes 1179656 | tf_op jit(solution)/shard_map/ppermute | solution.py:542
  58.7 4.3 %collective-permute-start.14 = (bf16[32,1024]{1,0:T(8,128)(2,1)S(1)}, bf16[32,1024]{1,0:T(8,128)(2,1)S(1)}, u32[]{:S(2)}, u32[]{:S(2)}) collective-permute-start(bf16[32,1024]{1,0:T(8,128)(2,1)S(1)} %get-tuple-element.115), channel_id=1, source_target_pairs={{0,16},{16,32},{32,48},{48,0},{1,17},{17,33},{33,49},{49,1},{2,18}... | collective-permute-start | bytes 196616 | tf_op jit(solution)/shard_map/ppermute | solution.py:406
  60.8 5.2 %collective-permute-start.15 = (bf16[32,1024]{1,0:T(8,128)(2,1)S(1)}, bf16[32,1024]{1,0:T(8,128)(2,1)S(1)}, u32[]{:S(2)}, u32[]{:S(2)}) collective-permute-start(bf16[32,1024]{1,0:T(8,128)(2,1)S(1)} %get-tuple-element.115), channel_id=1, source_target_pairs={{0,32},{16,48},{32,0},{48,16},{1,33},{17,49},{33,1},{49,17},{2,34}... | collective-permute-start | bytes 196616 | tf_op jit(solution)/shard_map/ppermute | solution.py:406
  62.5 4.3 %collective-permute-start.16 = (bf16[32,1024]{1,0:T(8,128)(2,1)S(1)}, bf16[32,1024]{1,0:T(8,128)(2,1)S(1)}, u32[]{:S(2)}, u32[]{:S(2)}) collective-permute-start(bf16[32,1024]{1,0:T(8,128)(2,1)S(1)} %get-tuple-element.115), channel_id=1, source_target_pairs={{0,48},{16,0},{32,16},{48,32},{1,49},{17,1},{33,17},{49,33},{2,50}... | collective-permute-start | bytes 196616 | tf_op jit(solution)/shard_map/ppermute | solution.py:406
  63.0 17.9 %collective-permute-start.17 = (bf16[128,1536]{1,0:T(8,128)(2,1)S(1)}, bf16[128,1536]{1,0:T(8,128)(2,1)S(1)}, u32[]{:S(2)}, u32[]{:S(2)}) collective-permute-start(bf16[128,1536]{1,0:T(8,128)(2,1)S(1)} %bitcast.22), channel_id=1, source_target_pairs={{0,1},{1,0},{2,3},{3,2},{4,5},{5,4},{6,7},{7,6},{8,9},{9,8},{10,11... | collective-permute-start | bytes 1179656 | tf_op jit(solution)/shard_map/ppermute | solution.py:548
  67.0 13.8 %collective-permute-start.20 = (bf16[128,1536]{1,0:T(8,128)(2,1)S(1)}, bf16[128,1536]{1,0:T(8,128)(2,1)S(1)}, u32[]{:S(2)}, u32[]{:S(2)}) collective-permute-start(bf16[128,1536]{1,0:T(8,128)(2,1)S(1)} %collective-permute-done.18.refs_1_), channel_id=1, source_target_pairs={{0,1},{1,0},{2,3},{3,2},{4,5},{5,4},{6,7},{7,6},{8,9},{9,8},{10,11... | collective-permute-start | bytes 1179656 | tf_op jit(solution)/shard_map/ppermute | solution.py:548
  67.1 13.7 %collective-permute-start.21 = (bf16[128,1536]{1,0:T(8,128)(2,1)S(1)}, bf16[128,1536]{1,0:T(8,128)(2,1)S(1)}, u32[]{:S(2)}, u32[]{:S(2)}) collective-permute-start(bf16[128,1536]{1,0:T(8,128)(2,1)S(1)} %collective-permute-done.19.refs_2_), channel_id=1, source_target_pairs={{0,1},{1,0},{2,3},{3,2},{4,5},{5,4},{6,7},{7,6},{8,9},{9,8},{10,11... | collective-permute-start | bytes 1179656 | tf_op jit(solution)/shard_map/ppermute | solution.py:548
  67.6 5.6 %collective-permute-start.22 = (bf16[32,1024]{1,0:T(8,128)(2,1)S(1)}, bf16[32,1024]{1,0:T(8,128)(2,1)S(1)}, u32[]{:S(2)}, u32[]{:S(2)}) collective-permute-start(bf16[32,1024]{1,0:T(8,128)(2,1)S(1)} %get-tuple-element.118), channel_id=1, source_target_pairs={{0,64},{64,128},{128,192},{192,0},{1,65},{65,129},{129,193},{193,1... | collective-permute-start | bytes 196616 | tf_op jit(solution)/shard_map/ppermute | solution.py:406
  69.7 6.1 %collective-permute-start.23 = (bf16[32,1024]{1,0:T(8,128)(2,1)S(1)}, bf16[32,1024]{1,0:T(8,128)(2,1)S(1)}, u32[]{:S(2)}, u32[]{:S(2)}) collective-permute-start(bf16[32,1024]{1,0:T(8,128)(2,1)S(1)} %get-tuple-element.118), channel_id=1, source_target_pairs={{0,128},{64,192},{128,0},{192,64},{1,129},{65,193},{129,1},{193,65... | collective-permute-start | bytes 196616 | tf_op jit(solution)/shard_map/ppermute | solution.py:406
  73.2 22.4 %collective-permute-start.29 = (bf16[128,1536]{1,0:T(8,128)(2,1)S(1)}, bf16[128,1536]{1,0:T(8,128)(2,1)}, u32[]{:S(2)}, u32[]{:S(2)}) collective-permute-start(bf16[128,1536]{1,0:T(8,128)(2,1)S(1)} %collective-permute-done.18.refs_1_), channel_id=1, source_target_pairs={{0,12},{4,8},{8,4},{12,0},{1,13},{5,9},{9,5},{13,1},{2,14},{6,10},... | collective-permute-start | bytes 1179656 | tf_op jit(solution)/shard_map/ppermute | solution.py:545
  75.8 4.3 %collective-permute-start.24 = (bf16[32,1024]{1,0:T(8,128)(2,1)S(1)}, bf16[32,1024]{1,0:T(8,128)(2,1)S(1)}, u32[]{:S(2)}, u32[]{:S(2)}) collective-permute-start(bf16[32,1024]{1,0:T(8,128)(2,1)S(1)} %get-tuple-element.118), channel_id=1, source_target_pairs={{0,192},{64,0},{128,64},{192,128},{1,193},{65,1},{129,65},{193,129... | collective-permute-start | bytes 196616 | tf_op jit(solution)/shard_map/ppermute | solution.py:406
  91.6 19.1 %all-to-all-start = ((bf16[8,360,128]{2,1,0:T(8,128)(2,1)}), bf16[8,360,128]{2,1,0:T(8,128)(2,1)S(1)}, u32[]{:S(2)}, u32[]{:S(2)}) async-start(bf16[8,360,128]{2,1,0:T(8,128)(2,1)} %get-tuple-element.127), calls=%async_computation | async-start | bytes 1474560 | tf_op jit(solution)/shard_map/all_to_all | solution.py:620
  95.5 15.1 %collective-permute-start.30 = (bf16[128,1536]{1,0:T(8,128)(2,1)}, bf16[128,1536]{1,0:T(8,128)(2,1)}, u32[]{:S(2)}, u32[]{:S(2)}) collective-permute-start(bf16[128,1536]{1,0:T(8,128)(2,1)} %collective-permute-done.29.refs_3_), channel_id=1, source_target_pairs={{0,1},{1,0},{2,3},{3,2},{4,5},{5,4},{6,7},{7,6},{8,9},{9,8},{10,11... | collective-permute-start | bytes 1179656 | tf_op jit(solution)/shard_map/ppermute | solution.py:548
  96.0 1.7 %collective-permute-start.25 = (bf16[40,1024]{1,0:T(8,128)(2,1)}, bf16[40,1024]{1,0:T(8,128)(2,1)S(1)}, u32[]{:S(2)}, u32[]{:S(2)}) collective-permute-start(bf16[40,1024]{1,0:T(8,128)(2,1)} %copy-done.16), channel_id=1, source_target_pairs={{0,1},{1,0},{2,3},{3,2},{4,5},{5,4},{6,7},{7,6},{8,9},{9,8},{10,11... | collective-permute-start | bytes 245768 | tf_op jit(solution)/shard_map/ppermute | solution.py:608
  98.6 5.1 %collective-permute-start.26 = (bf16[40,1024]{1,0:T(8,128)(2,1)S(1)}, bf16[40,1024]{1,0:T(8,128)(2,1)S(1)}, u32[]{:S(2)}, u32[]{:S(2)}) collective-permute-start(bf16[40,1024]{1,0:T(8,128)(2,1)S(1)} %add_parts.4.refs_0_), channel_id=1, source_target_pairs={{0,16},{16,32},{32,48},{48,0},{1,17},{17,33},{33,49},{49,1},{2,18}... | collective-permute-start | bytes 245768 | tf_op jit(solution)/shard_map/ppermute | solution.py:406
  100.0 7.6 %collective-permute-start.27 = (bf16[40,1024]{1,0:T(8,128)(2,1)S(1)}, bf16[40,1024]{1,0:T(8,128)(2,1)S(1)}, u32[]{:S(2)}, u32[]{:S(2)}) collective-permute-start(bf16[40,1024]{1,0:T(8,128)(2,1)S(1)} %add_parts.4.refs_0_), channel_id=1, source_target_pairs={{0,32},{16,48},{32,0},{48,16},{1,33},{17,49},{33,1},{49,17},{2,34}... | collective-permute-start | bytes 245768 | tf_op jit(solution)/shard_map/ppermute | solution.py:406
  101.8 8.1 %collective-permute-start.28 = (bf16[40,1024]{1,0:T(8,128)(2,1)S(1)}, bf16[40,1024]{1,0:T(8,128)(2,1)S(1)}, u32[]{:S(2)}, u32[]{:S(2)}) collective-permute-start(bf16[40,1024]{1,0:T(8,128)(2,1)S(1)} %add_parts.4.refs_0_), channel_id=1, source_target_pairs={{0,48},{16,0},{32,16},{48,32},{1,49},{17,1},{33,17},{49,33},{2,50}... | collective-permute-start | bytes 245768 | tf_op jit(solution)/shard_map/ppermute | solution.py:406
  115.6 22.6 %all-to-all-start.1 = ((bf16[4,360,384]{2,1,0:T(8,128)(2,1)}), bf16[4,360,384]{2,1,0:T(8,128)(2,1)S(1)}, u32[]{:S(2)}, u32[]{:S(2)}) async-start(bf16[4,360,384]{2,1,0:T(8,128)(2,1)} %weight_term.1), calls=%async_computation.1 | async-start | bytes 2211840 | tf_op jit(solution)/shard_map/all_to_all | solution.py:632
  119.9 5.8 %collective-permute-start.31 = (bf16[40,1024]{1,0:T(8,128)(2,1)S(1)}, bf16[40,1024]{1,0:T(8,128)(2,1)S(1)}, u32[]{:S(2)}, u32[]{:S(2)}) collective-permute-start(bf16[40,1024]{1,0:T(8,128)(2,1)S(1)} %copy-done.15), channel_id=1, source_target_pairs={{0,4},{4,8},{8,12},{12,0},{1,5},{5,9},{9,13},{13,1},{2,6},{6,10},{... | collective-permute-start | bytes 245768 | tf_op jit(solution)/shard_map/ppermute | solution.py:406
  121.6 6.5 %collective-permute-start.32 = (bf16[40,1024]{1,0:T(8,128)(2,1)S(1)}, bf16[40,1024]{1,0:T(8,128)(2,1)S(1)}, u32[]{:S(2)}, u32[]{:S(2)}) collective-permute-start(bf16[40,1024]{1,0:T(8,128)(2,1)S(1)} %copy-done.15), channel_id=1, source_target_pairs={{0,8},{4,12},{8,0},{12,4},{1,9},{5,13},{9,1},{13,5},{2,10},{6,14},... | collective-permute-start | bytes 245768 | tf_op jit(solution)/shard_map/ppermute | solution.py:406
  124.3 4.4 %collective-permute-start.33 = (bf16[40,1024]{1,0:T(8,128)(2,1)S(1)}, bf16[40,1024]{1,0:T(8,128)(2,1)S(1)}, u32[]{:S(2)}, u32[]{:S(2)}) collective-permute-start(bf16[40,1024]{1,0:T(8,128)(2,1)S(1)} %copy-done.15), channel_id=1, source_target_pairs={{0,12},{4,0},{8,4},{12,8},{1,13},{5,1},{9,5},{13,9},{2,14},{6,2},{... | collective-permute-start | bytes 245768 | tf_op jit(solution)/shard_map/ppermute | solution.py:406
  128.8 9.3 %collective-permute-start.34 = (bf16[40,1024]{1,0:T(8,128)(2,1)S(1)}, bf16[40,1024]{1,0:T(8,128)(2,1)S(1)}, u32[]{:S(2)}, u32[]{:S(2)}) collective-permute-start(bf16[40,1024]{1,0:T(8,128)(2,1)S(1)} %add_parts.6.refs_0_), channel_id=1, source_target_pairs={{0,2},{2,0},{1,3},{3,1},{4,6},{6,4},{5,7},{7,5},{8,10},{10,8},{9,1... | collective-permute-start | bytes 245768 | tf_op jit(solution)/shard_map/ppermute | solution.py:608
  139.2 20.9 %copy-start.19 = (f32[15,16]{1,0:T(8,128)S(1)}, f32[15,16]{1,0:T(8,128)}, u32[]{:S(2)}) copy-start(f32[15,16]{1,0:T(8,128)} %get-tuple-element.139.amp) | copy-start | bytes 2884
  139.2 21.7 %all-to-all-start.2 = ((bf16[32,24,180]{2,1,0:T(8,128)(2,1)}), bf16[32,24,180]{2,1,0:T(8,128)(2,1)S(1)}, u32[]{:S(2)}, u32[]{:S(2)}) async-start(bf16[32,24,180]{2,1,0:T(8,128)(2,1)} %split_rows.1), calls=%async_computation.2 | async-start | bytes 786432 | tf_op jit(solution)/shard_map/all_to_all | solution.py:645
  147.6 12.5 %collective-permute-start.35 = (bf16[40,1024]{1,0:T(8,128)(2,1)S(1)}, bf16[40,1024]{1,0:T(8,128)(2,1)S(1)}, u32[]{:S(2)}, u32[]{:S(2)}) collective-permute-start(bf16[40,1024]{1,0:T(8,128)(2,1)S(1)} %add_parts.7.refs_0_), channel_id=1, source_target_pairs={{0,64},{64,128},{128,192},{192,0},{1,65},{65,129},{129,193},{193,1... | collective-permute-start | bytes 245768 | tf_op jit(solution)/shard_map/ppermute | solution.py:406
  149.7 10.4 %collective-permute-start.36 = (bf16[40,1024]{1,0:T(8,128)(2,1)S(1)}, bf16[40,1024]{1,0:T(8,128)(2,1)S(1)}, u32[]{:S(2)}, u32[]{:S(2)}) collective-permute-start(bf16[40,1024]{1,0:T(8,128)(2,1)S(1)} %add_parts.7.refs_0_), channel_id=1, source_target_pairs={{0,128},{64,192},{128,0},{192,64},{1,129},{65,193},{129,1},{193,65... | collective-permute-start | bytes 245768 | tf_op jit(solution)/shard_map/ppermute | solution.py:406
  152.4 7.7 %collective-permute-start.37 = (bf16[40,1024]{1,0:T(8,128)(2,1)S(1)}, bf16[40,1024]{1,0:T(8,128)(2,1)S(1)}, u32[]{:S(2)}, u32[]{:S(2)}) collective-permute-start(bf16[40,1024]{1,0:T(8,128)(2,1)S(1)} %add_parts.7.refs_0_), channel_id=1, source_target_pairs={{0,192},{64,0},{128,64},{192,128},{1,193},{65,1},{129,65},{193,129... | collective-permute-start | bytes 245768 | tf_op jit(solution)/shard_map/ppermute | solution.py:406
  (13 other events, 50.9 us)

commit v7 on v6

--- a/solution.py
+++ b/solution.py
@@ -23,51 +23,31 @@
 
 def make_project(g):
     def project(*refs):
-        if g == 0:
-            tp, nexts, taps, feats, wt, cott, zf, mix, cots, tk, wbuf, sems, turn, cbuf, csem = refs
+        if g < 2:
+            *ins, wt, zf, mix, wnext, sem = refs
+            coming = pltpu.make_async_copy(wt.at[pl.ds((g + 1) * wnext.shape[0], wnext.shape[0])], wnext, sem)
+            coming.start()
         else:
-            tp, nexts, taps, feats, wt, zf, mix, tk, wbuf, sems = refs
-        width = wbuf.shape[0]
-        depth = tk.shape[1]
-        chunks = ((0, 512), (512, width - 512))
-        arrival = pltpu.make_async_copy(feats, tk, sems.at[0])
-        arrival.start()
-        copies = [
-            pltpu.make_async_copy(
-                wt.at[pl.ds(g * width + low, size)], wbuf.at[pl.ds(low, size)], sems.at[1 + i]
-            )
-            for i, (low, size) in enumerate(chunks)
-        ]
-        for copy in copies:
-            copy.start()
-        if g == 0:
-            other = pltpu.make_async_copy(cott, cbuf, csem)
-            other.start()
+            *ins, zf, mix = refs
+        tp, nexts, taps, tk, w = ins
+        width, depth = w.shape
         zf[:, width:] = jnp.zeros((zf.shape[0], PADC - width), F32)
-        arrival.wait()
         rows = jnp.concatenate([tp[...], tk[...], nexts[:, 0:depth]], axis=0)
-        for (low, size), copy in zip(chunks, copies):
-            copy.wait()
-            part = lax.dot_general(rows, wbuf[low : low + size, :], NT, preferred_element_type=F32)
+        for low, size in ((0, 512), (512, width - 512)):
+            part = lax.dot_general(rows, w[low : low + size, :], NT, preferred_element_type=F32)
             zf[:, low : low + size] = rounded(part)
-        if g == 0:
-            other.wait()
-            turn[...] = jnp.zeros(turn.shape, F32)
-            turn[0:width, :] = cbuf[...].astype(F32)
 
         def tile(ct, carry):
-            lane = pl.multiple_of(ct * 128, 128)
-            lanes = pl.ds(lane, 128)
+            lanes = pl.ds(pl.multiple_of(ct * 128, 128), 128)
             total = taps[g, 0:1, lanes] * zf[pl.ds(HALO, EXT), lanes]
             for j in range(1, 7):
                 total = total + taps[g, j : j + 1, lanes] * zf[pl.ds(HALO - j, EXT), lanes]
             mix[:, lanes] = total
-            if g == 0:
-                after = nexts[:, pl.ds(pl.multiple_of(depth + lane, 128), 128)].astype(F32)
-                cots[:, lanes] = jnp.concatenate([turn[lanes, :].T, after[0 : EXT - 128]], axis=0)
             return carry
 
         lax.fori_loop(0, PADC // 128, tile, 0)
+        if g < 2:
+            coming.wait()
 
     return project
 
@@ -80,7 +60,7 @@
 
 
 def prepare(
-    feats, cott, rates, residues, conv, head, tail, block, taps, amp,
+    feats, cott, rates, residues, conv, wt, head, tail, block, taps, amp, tokens, cots, wfirst,
     held, turn, cbuf, rbuf, sbuf, vbuf, sems,
 ):
     count = rates.shape[0]
@@ -93,6 +73,8 @@
         pltpu.make_async_copy(conv, vbuf, sems.at[3]),
         pltpu.make_async_copy(feats.at[pl.ds(0, HALO)], head.at[:, pl.ds(0, depth)], sems.at[4]),
         pltpu.make_async_copy(feats.at[pl.ds(own - HALO, HALO)], tail, sems.at[5]),
+        pltpu.make_async_copy(feats, tokens, sems.at[6]),
+        pltpu.make_async_copy(wt.at[pl.ds(0, width)], wfirst, sems.at[7]),
     ]
     for copy in copies:
         copy.start()
@@ -109,13 +91,14 @@
     copies[2].wait()
     turn[0:width, :] = cbuf[...].astype(F32)
     for c in range(PADC // 128):
-        part = turn[c * 128 : (c + 1) * 128, :].T[0:HALO]
-        head[:, depth + c * 128 : depth + (c + 1) * 128] = part.astype(BF16)
+        part = turn[c * 128 : (c + 1) * 128, :].T
+        cots[:, c * 128 : (c + 1) * 128] = part
+        head[:, depth + c * 128 : depth + (c + 1) * 128] = part[0:HALO].astype(BF16)
     copies[3].wait()
     for g in range(3):
         taps[g, 0:7, 0:width] = vbuf[:, g * width : (g + 1) * width]
-    copies[4].wait()
-    copies[5].wait()
+    for copy in copies[4:]:
+        copy.wait()
 
 
 def placed(me, refs, held, goal):
@@ -133,7 +116,7 @@
     out[...] = placed(me[0], (r0, r1, r2, r3), held, out.shape[1])
 
 
-def end_states(me, r0, r1, r2, r3, mq, mk, mv, cots, rates, gains, es, ends, endb, ut, dt, held):
+def end_states(me, r0, r1, r2, r3, mq, mk, mv, cown, nexts, cots, rates, gains, es, ends, endb, ut, dt, held):
     joined = placed(me[0], (r0, r1, r2, r3), held, PADC)
     rates[...] = joined[0:MODES]
     gains[...] = joined[MODES : 2 * MODES]
@@ -145,7 +128,11 @@
     def tile(ct, carry):
         lanes = pl.ds(pl.multiple_of(ct * 128, 128), 128)
         ut[...] = rounded(mk[:, lanes] * mv[:, lanes])
-        dt[...] = rounded(cots[:, lanes] * mq[:, lanes])
+        lane = pl.multiple_of(nexts.shape[1] - PADC + ct * 128, 128)
+        after = nexts[:, pl.ds(lane, 128)].astype(F32)
+        cot = jnp.concatenate([cown[:, lanes], after[0 : EXT - 128]], axis=0)
+        cots[:, lanes] = cot
+        dt[...] = rounded(cot * mq[:, lanes])
         rate = rates[:, lanes]
         decay = jnp.exp(-rate)
         for half in range(2):
@@ -429,16 +416,19 @@
     )
     xi, zi, yi, ci = [w.reshape(1) for w in where]
     anywhere = pl.BlockSpec(memory_space=pl.ANY)
-    head, tail, block, taps, amp_mine = pl.pallas_call(
+    head, tail, block, taps, amp_mine, tk, cown, wg = pl.pallas_call(
         prepare,
-        in_specs=[anywhere] * 5,
-        out_specs=[vm] * 5,
+        in_specs=[anywhere] * 6,
+        out_specs=[vm] * 8,
         out_shape=[
             jax.ShapeDtypeStruct((HALO, depth + PADC), BF16),
             jax.ShapeDtypeStruct((HALO, depth), BF16),
             jax.ShapeDtypeStruct((2 * MODES, width // count), F32),
             jax.ShapeDtypeStruct((3, 8, PADC), F32),
             jax.ShapeDtypeStruct(rates.shape, F32),
+            jax.ShapeDtypeStruct((own, depth), BF16),
+            jax.ShapeDtypeStruct((own, PADC), F32),
+            jax.ShapeDtypeStruct((width, depth), BF16),
         ],
         scratch_shapes=[
             pltpu.VMEM((128, 128), F32),
@@ -447,46 +437,36 @@
             pltpu.VMEM(rates.shape, F32),
             pltpu.VMEM(rates.shape, F32),
             pltpu.VMEM(conv_taps.shape, F32),
-            pltpu.SemaphoreType.DMA((6,)),
-        ],
-        compiler_params=params(56),
+            pltpu.SemaphoreType.DMA((8,)),
+        ],
+        compiler_params=params(54),
         name="prepare",
-    )(feats, cot.T, rates, residues, conv_taps)
+    )(feats, cot.T, rates, residues, conv_taps, w_in.T)
     tprev = lax.ppermute(tail, ctx, [(i, i + 1) for i in range(count - 1)])
     nexts = lax.ppermute(head, ctx, [(i, i - 1) for i in range(1, count)])
     ext_rows = own + 2 * HALO
     project_out = [jax.ShapeDtypeStruct((ext_rows, PADC), F32), jax.ShapeDtypeStruct((EXT, PADC), F32)]
-    project_scratch = [
-        pltpu.VMEM((own, depth), BF16),
-        pltpu.VMEM((width, depth), BF16),
-        pltpu.SemaphoreType.DMA((3,)),
-    ]
     project_cost = pl.CostEstimate(flops=500000000, bytes_accessed=4000000, transcendentals=0)
-    first = [
-        pltpu.VMEM((PADC, own), F32),
-        pltpu.VMEM((width, own), BF16),
-        pltpu.SemaphoreType.DMA,
-    ]
     held, each = block, width // count
     projected = []
     for g, (me, ax) in enumerate(((yi, "y"), (zi, "zl"), (xi, "x"))):
         blocks = [held] + [ring(held, ax, d) for d in (1, 2, 3)]
+        more = g < 2
         done = pl.pallas_call(
             make_project(g),
-            in_specs=[vm] * 3 + [anywhere] * (3 if g == 0 else 2),
-            out_specs=[vm] * (3 if g == 0 else 2),
-            out_shape=project_out + project_out[1:] if g == 0 else project_out,
-            scratch_shapes=project_scratch + first if g == 0 else project_scratch,
-            compiler_params=params((57, 56, 52)[g]),
+            in_specs=[vm] * 5 + [anywhere] * more,
+            out_specs=[vm] * (2 + more),
+            out_shape=project_out + [jax.ShapeDtypeStruct((width, depth), BF16)] * more,
+            scratch_shapes=[pltpu.SemaphoreType.DMA] * more,
+            compiler_params=params((50, 50, 50)[g]),
             cost_estimate=project_cost,
             name="project",
-        )(tprev, nexts, taps, feats, w_in.T, *((cot.T,) if g == 0 else ()))
+        )(tprev, nexts, taps, tk, wg, *[w_in.T] * more)
         *blocks, zg, mg = lax.optimization_barrier((*blocks, done[0], done[1]))
         projected.append((zg, mg))
-        if g == 0:
-            cots = done[2]
         if g == 2:
             break
+        wg = done[2]
         each = 4 * each
         held = pl.pallas_call(
             join_params,
@@ -498,11 +478,12 @@
             name="join_params",
         )(me, *blocks)
     (zq, mq), (zk, mk), (zv, mv) = projected
-    rate, gain, es, ends, endb = pl.pallas_call(
+    cots, rate, gain, es, ends, endb = pl.pallas_call(
         end_states,
-        in_specs=[smem] + [vm] * 8,
-        out_specs=[vm] * 5,
+        in_specs=[smem] + [vm] * 9,
+        out_specs=[vm] * 6,
         out_shape=[
+            jax.ShapeDtypeStruct((EXT, PADC), F32),
             jax.ShapeDtypeStruct((MODES, PADC), F32),
             jax.ShapeDtypeStruct((MODES, PADC), F32),
             jax.ShapeDtypeStruct((2, MODES, 8, PADC), F32),
@@ -517,7 +498,7 @@
         compiler_params=params(16),
         cost_estimate=pl.CostEstimate(flops=20000000, bytes_accessed=3000000, transcendentals=0),
         name="end_states",
-    )(xi, *blocks, mq, mk, mv, cots)
+    )(xi, *blocks, mq, mk, mv, cown, nexts)
 
     prefixes = []
     total, sent = ends, endb
@@ -536,19 +517,15 @@
             name="level",
         )(me, total, *near, rate)
         prefixes.append(prefix)
-        if ax == "y":
+        if ax == "zl":
             mine, _ = lax.optimization_barrier((feats, sent))
             pair = lax.ppermute(mine, "y", [(i, i ^ 1) for i in range(4)])
             opposite = lax.ppermute(mine, "y", [(i, 3 - i) for i in range(4)])
-        elif ax == "zl":
-            pair, opposite, _ = lax.optimization_barrier((pair, opposite, sent))
-            far = lax.ppermute(pair, "y", [(i, 3 - i) for i in range(4)])
+    pair, opposite, prefixes[2] = lax.optimization_barrier((pair, opposite, prefixes[2]))
+    far = lax.ppermute(pair, "y", [(i, 3 - i) for i in range(4)])
 
     def swapped(a):
         return lax.ppermute(a, "core", [(0, 1), (1, 0)])
-
-    theirs = [swapped(a) for a in (mine, pair, opposite)]
-    *theirs, prefixes[2] = lax.optimization_barrier((*theirs, prefixes[2]))
 
     def tiles(shape):
         lead = len(shape) - 1
@@ -599,7 +576,9 @@
     )(zi, yi, zq, zk, zv, mq, mk, mv, es, *prefixes, taps, rate, gain, cots)
     output = outt.T
     blocks_of = [mine, pair, opposite, far]
-    theirs.append(swapped(far))
+    mine, pair, opposite, _ = lax.optimization_barrier((mine, pair, opposite, sums))
+    blocks_of = [mine, pair, opposite, far]
+    theirs = [swapped(a) for a in blocks_of]
 
     def spread(a, ax):
         return [a] + [ring(a, ax, d) for d in (1, 2, 3)]
@@ -618,7 +597,25 @@
         )(*parts)
 
     arrived = lax.all_to_all(dzb, ("y", "core"), split_axis=0, concat_axis=0, tiled=True)
-    sums = summed(spread(summed(swap(sums, "core")), "zl"))
+    sums = summed(swap(sums, "core"))
+    *theirs, sums = lax.optimization_barrier((*theirs, sums))
+    parts = spread(sums, "zl")
+    grad_feats = pl.pallas_call(
+        token_grads,
+        grid=(3,),
+        in_specs=[
+            pl.BlockSpec((1, own, PADC), lambda g: (g, 0, 0)),
+            pl.BlockSpec((width, depth), lambda g: (g, 0)),
+        ],
+        out_specs=pl.BlockSpec((own, depth), lambda g: (0, 0)),
+        out_shape=jax.ShapeDtypeStruct((own, depth), BF16),
+        scratch_shapes=[pltpu.VMEM((own, depth), F32)],
+        compiler_params=params(57),
+        cost_estimate=pl.CostEstimate(flops=1200000000, bytes_accessed=11000000, transcendentals=0),
+        name="token_grads",
+    )(dz, w_in.T)
+    *parts, grad_feats = lax.optimization_barrier((*parts, grad_feats))
+    sums = summed(parts)
     arrived, sums = lax.optimization_barrier((arrived, sums))
     term = pl.pallas_call(
         weight_term,
@@ -643,22 +640,8 @@
         name="split_rows",
     )(got)
     last = lax.all_to_all(blocks, ("zl", "y", "zh"), 0, 0, tiled=True)
-    sums, dz, _ = lax.optimization_barrier((sums, dz, blocks))
+    sums, _ = lax.optimization_barrier((sums, blocks))
     parts = spread(sums, "x")
-    grad_feats = pl.pallas_call(
-        token_grads,
-        grid=(3,),
-        in_specs=[
-            pl.BlockSpec((1, own, PADC), lambda g: (g, 0, 0)),
-            pl.BlockSpec((width, depth), lambda g: (g, 0)),
-        ],
-        out_specs=pl.BlockSpec((own, depth), lambda g: (0, 0)),
-        out_shape=jax.ShapeDtypeStruct((own, depth), BF16),
-        scratch_shapes=[pltpu.VMEM((own, depth), F32)],
-        compiler_params=params(24),
-        cost_estimate=pl.CostEstimate(flops=1200000000, bytes_accessed=11000000, transcendentals=0),
-        name="token_grads",
-    )(dz, w_in.T)
     grad_taps, grad_residues = pl.pallas_call(
         make_close_sums(scale),
         in_specs=[smem] * 3 + [vm] * 5,

time: 163 us -> 165 us (1.012)
  Pallas kernels: 39 us -> 42.7 us
    pallas_call x1, Pallas kernels: 2.74 us -> 6.01 us  [local(): pl.pallas_call(token_grads, grid=(3,), in_specs=[pl.BlockSpec((1, own, PA...]
    ppermute x27, waiting for transfers between devices: 21.6 us -> 18.6 us  [ring(): return lax.ppermute(a, ax, [(i, (i + d) % 4) for i in range(4)])]
    all_to_all x1, waiting for transfers between devices: 0.01 us -> 2.61 us  [local(): last = lax.all_to_all(blocks, ('zl', 'y', 'zh'), 0, 0, tiled=True)]
    ppermute x27, starting transfers between devices: 52.3 us -> 50.5 us  [ring(): return lax.ppermute(a, ax, [(i, (i + d) % 4) for i in range(4)])]
    unnamed x40 -> x26, local copies, waits for them, and re-layouts: 8.1 us -> 7.58 us
  transfers between devices with their start and end apart: 41 -> 41, of which waited for: 15 -> 19; matrix products, arithmetic and copies ran while one was open for 0% -> 0% of each run, Pallas kernels for 18% -> 19%
where the time goes in v7:
time: 165 us; the launch traced here: 164 us
  starting transfers between devices  83.9 us (51%)
  Pallas kernels  42.7 us (26%)
  waiting for transfers between devices  28.8 us (17%)
  local copies, waits for them, and re-layouts  7.58 us (5%)
    ppermute x27, starting transfers between devices, ring(): return lax.ppermute(a, ax, [(i, (i + d) % 4) for i in range(4)])  50.5 us
    ppermute x27, waiting for transfers between devices, ring(): return lax.ppermute(a, ax, [(i, (i + d) % 4) for i in range(4)])  18.6 us
    pallas_call x3, Pallas kernels, local(): pl.pallas_call(make_project(g), in_specs=[vm] * 5 + [anywhere] * more, ou...  14.1 us
    pallas_call x1, Pallas kernels, local(): pl.pallas_call(finish, grid=(PADC // 128,), in_specs=[smem, smem, *[tiles...  9.34 us
    all_to_all x1, starting transfers between devices, local(): last = lax.all_to_all(blocks, ('zl', 'y', 'zh'), 0, 0, tiled=True)  8.58 us
    unnamed x26, local copies, waits for them, and re-layouts  7.58 us
    ppermute x2, waiting for transfers between devices, swap(): return [a, lax.ppermute(a, ax, [(0, 1), (1, 0)])]  6.06 us
    pallas_call x1, Pallas kernels, local(): pl.pallas_call(token_grads, grid=(3,), in_specs=[pl.BlockSpec((1, own, PA...  6.01 us
  transfers between devices with their start and end apart: 41, of which 19 were waited for; matrix products, arithmetic and copies ran while one was open for 0% of the time, Pallas kernels for 19%

profile of v7, /device:TPU:32, one launch (start us, length us, event | category | flops | bytes accessed | tf_op | source)
XLA Modules:
  0.0 164.0 jit_solution(12315144475898647685)
XLA Ops:
  0.6 4.3 %prepare.1 = (bf16[16,2560]{1,0:T(8,128)(2,1)}, bf16[16,1536]{1,0:T(8,128)(2,1)}, f32[32,15]{1,0:T(8,128)}, f32[3,8,1024]{2,1,0:T(8,128)}, f32[15,16]{1,0:T(8,12...) custom-call(bf16[128,1536]{1,0:T(8,128)(2,1)} %bitcast.12, ...), custom_call_target="tpu_custom_call" | custom-call | tf_op jit(solution)/shard_map/prepare/pallas_call | solution.py:419
  4.9 4.5 %collective-permute-start.4 = (bf16[16,2560]{1,0:T(8,128)(2,1)}, bf16[16,2560]{1,0:T(8,128)(2,1)S(1)}, u32[]{:S(2)}, u32[]{:S(2)}) collective-permute-start(bf16[16,2560]{1,0:T(8,128)(2,1)} %get-tuple-element.95), channel_id=1, source_target_pairs={{4,0},{8,4},{12,8},{16,12},{20,16},{24,20},{28,24},{32,28},{36,32}... | collective-permute-start | bytes 245768 | tf_op jit(solution)/shard_map/ppermute | solution.py:446
  9.4 1.9 %collective-permute-start.3 = (bf16[16,1536]{1,0:T(8,128)(2,1)}, bf16[16,1536]{1,0:T(8,128)(2,1)S(1)}, u32[]{:S(2)}, u32[]{:S(2)}) collective-permute-start(bf16[16,1536]{1,0:T(8,128)(2,1)} %get-tuple-element.94), channel_id=1, source_target_pairs={{0,4},{4,8},{8,12},{12,16},{16,20},{20,24},{24,28},{28,32},{32,36}... | collective-permute-start | bytes 147464 | tf_op jit(solution)/shard_map/ppermute | solution.py:445
  11.3 1.1 collective-permute-start
  12.4 5.0 %collective-permute-start.1 = (f32[32,15]{1,0:T(8,128)}, f32[32,15]{1,0:T(8,128)S(1)}, u32[]{:S(2)}, u32[]{:S(2)}) collective-permute-start(f32[32,15]{1,0:T(8,128)} %get-tuple-element.102.r0), channel_id=1, source_target_pairs={{0,8},{4,12},{8,0},{12,4},{1,9},{5,13},{9,1},{13,5},{2,10},{6,14},... | collective-permute-start | bytes 5768 | tf_op jit(solution)/shard_map/ppermute | solution.py:393
  17.7 1.0 copy-done
  19.6 5.3 %project.3 = (f32[160,1024]{1,0:T(8,128)S(1)}, f32[136,1024]{1,0:T(8,128)S(1)}, bf16[960,1536]{1,0:T(8,128)(2,1)}) custom-call(bf16[16,1536]{1,0:T(8,128)(2,1)S(1)} %collective-permute-done.3.refs_0_, bf16[16,2560]{1,0:T(8,128)(2,1)S(1)} %collective-permute-done.4.refs_1_.nexts, f32[3,8,1024]{2,1,0:T(8,128)S(1)} %copy-done.1, bf16[128,1536]{1,0:T(8,128)(2,1)S(1)} %copy-done, ...), custom_call_target="tpu_custom_call" | custom-call | flops 500000000 | bytes 4000000 | tf_op jit(solution)/shard_map/project/pallas_call | solution.py:455
  25.1 2.0 %collective-permute-start.5 = (f32[32,60]{1,0:T(8,128)S(1)}, f32[32,60]{1,0:T(8,128)S(1)}, u32[]{:S(2)}, u32[]{:S(2)}) collective-permute-start(f32[32,60]{1,0:T(8,128)S(1)} %join_params.2.r0), channel_id=1, source_target_pairs={{0,16},{16,32},{32,48},{48,0},{1,17},{17,33},{33,49},{49,1},{2,18}... | collective-permute-start | bytes 23048 | tf_op jit(solution)/shard_map/ppermute | solution.py:393
  27.1 3.9 %collective-permute-start.6 = (f32[32,60]{1,0:T(8,128)S(1)}, f32[32,60]{1,0:T(8,128)S(1)}, u32[]{:S(2)}, u32[]{:S(2)}) collective-permute-start(f32[32,60]{1,0:T(8,128)S(1)} %join_params.2.r0), channel_id=1, source_target_pairs={{0,32},{16,48},{32,0},{48,16},{1,33},{17,49},{33,1},{49,17},{2,34}... | collective-permute-start | bytes 23048 | tf_op jit(solution)/shard_map/ppermute | solution.py:393
  31.0 1.9 %collective-permute-start.7 = (f32[32,60]{1,0:T(8,128)S(1)}, f32[32,60]{1,0:T(8,128)S(1)}, u32[]{:S(2)}, u32[]{:S(2)}) collective-permute-start(f32[32,60]{1,0:T(8,128)S(1)} %join_params.2.r0), channel_id=1, source_target_pairs={{0,48},{16,0},{32,16},{48,32},{1,49},{17,1},{33,17},{49,33},{2,50}... | collective-permute-start | bytes 23048 | tf_op jit(solution)/shard_map/ppermute | solution.py:393
  32.9 5.3 %project.4 = (f32[160,1024]{1,0:T(8,128)S(1)}, f32[136,1024]{1,0:T(8,128)S(1)}, bf16[960,1536]{1,0:T(8,128)(2,1)}) custom-call(bf16[16,1536]{1,0:T(8,128)(2,1)S(1)} %collective-permute-done.3.refs_0_, bf16[16,2560]{1,0:T(8,128)(2,1)S(1)} %collective-permute-done.4.refs_1_.nexts, f32[3,8,1024]{2,1,0:T(8,128)S(1)} %copy-done.1, bf16[128,1536]{1,0:T(8,128)(2,1)S(1)} %copy-done, ...), custom_call_target="tpu_custom_call" | custom-call | flops 500000000 | bytes 4000000 | tf_op jit(solution)/shard_map/project/pallas_call | solution.py:455
  38.3 5.0 %collective-permute-start.10 = (f32[32,240]{1,0:T(8,128)S(1)}, f32[32,240]{1,0:T(8,128)S(1)}, u32[]{:S(2)}, u32[]{:S(2)}) collective-permute-start(f32[32,240]{1,0:T(8,128)S(1)} %join_params.3.r0), channel_id=1, source_target_pairs={{0,192},{64,0},{128,64},{192,128},{1,193},{65,1},{129,65},{193,129... | collective-permute-start | bytes 92168 | tf_op jit(solution)/shard_map/ppermute | solution.py:393
  43.4 2.0 %collective-permute-start.9 = (f32[32,240]{1,0:T(8,128)S(1)}, f32[32,240]{1,0:T(8,128)S(1)}, u32[]{:S(2)}, u32[]{:S(2)}) collective-permute-start(f32[32,240]{1,0:T(8,128)S(1)} %join_params.3.r0), channel_id=1, source_target_pairs={{0,128},{64,192},{128,0},{192,64},{1,129},{65,193},{129,1},{193,65... | collective-permute-start | bytes 92168 | tf_op jit(solution)/shard_map/ppermute | solution.py:393
  45.4 3.5 %project.5 = (f32[160,1024]{1,0:T(8,128)S(1)}, f32[136,1024]{1,0:T(8,128)S(1)}) custom-call(bf16[16,1536]{1,0:T(8,128)(2,1)S(1)} %collective-permute-done.3.refs_0_, bf16[16,2560]{1,0:T(8,128)(2,1)S(1)} %collective-permute-done.4.refs_1_.nexts, f32[3,8,1024]{2,1,0:T(8,128)S(1)} %copy-done.1, bf16[128,1536]{1,0:T(8,128)(2,1)S(1)} %copy-done, ...), custom_call_target="tpu_custom_call" | custom-call | flops 500000000 | bytes 4000000 | tf_op jit(solution)/shard_map/project/pallas_call | solution.py:455
  48.9 2.2 %end_states.1 = (f32[136,1024]{1,0:T(8,128)S(1)}, f32[16,1024]{1,0:T(8,128)S(1)}, f32[16,1024]{1,0:T(8,128)S(1)}, f32[2,16,8,1024]{3,2,1,0:T(8,128)S(1)}, f32[32...) custom-call(s32[1]{0:T(128)} %bitcast.6.me.index.xi, f32[32,240]{1,0:T(8,128)S(1)} %join_params.3.r0, ...), custom_call_target="tpu_custom_call" | custom-call | flops 20000000 | bytes 3000000 | tf_op jit(solution)/shard_map/end_states/pallas_call | solution.py:481
  51.3 3.1 %collective-permute-start.13 = (bf16[32,1024]{1,0:T(8,128)(2,1)S(1)}, bf16[32,1024]{1,0:T(8,128)(2,1)S(1)}, u32[]{:S(2)}, u32[]{:S(2)}) collective-permute-start(bf16[32,1024]{1,0:T(8,128)(2,1)S(1)} %get-tuple-element.129), channel_id=1, source_target_pairs={{0,12},{4,0},{8,4},{12,8},{1,13},{5,1},{9,5},{13,9},{2,14},{6,2},{... | collective-permute-start | bytes 196616 | tf_op jit(solution)/shard_map/ppermute | solution.py:393
  54.4 2.9 %collective-permute-done.11.r1 = bf16[32,1024]{1,0:T(8,128)(2,1)S(1)} collective-permute-done((bf16[32,1024]{1,0:T(8,128)(2,1)S(1)}, bf16[32,1024]{1,0:T(8,128)(2,1)S(1)}, u32[]{:S(2)}, u32[]{:S(2)}) %collective-permute-start.11) | collective-permute-done | bytes 65568 | tf_op jit(solution)/shard_map/ppermute | solution.py:393
  58.4 2.3 %collective-permute-start.14 = (bf16[32,1024]{1,0:T(8,128)(2,1)S(1)}, bf16[32,1024]{1,0:T(8,128)(2,1)S(1)}, u32[]{:S(2)}, u32[]{:S(2)}) collective-permute-start(bf16[32,1024]{1,0:T(8,128)(2,1)S(1)} %get-tuple-element.133), channel_id=1, source_target_pairs={{0,16},{16,32},{32,48},{48,0},{1,17},{17,33},{33,49},{49,1},{2,18}... | collective-permute-start | bytes 196616 | tf_op jit(solution)/shard_map/ppermute | solution.py:393
  60.7 1.8 %collective-permute-start.15 = (bf16[32,1024]{1,0:T(8,128)(2,1)S(1)}, bf16[32,1024]{1,0:T(8,128)(2,1)S(1)}, u32[]{:S(2)}, u32[]{:S(2)}) collective-permute-start(bf16[32,1024]{1,0:T(8,128)(2,1)S(1)} %get-tuple-element.133), channel_id=1, source_target_pairs={{0,32},{16,48},{32,0},{48,16},{1,33},{17,49},{33,1},{49,17},{2,34}... | collective-permute-start | bytes 196616 | tf_op jit(solution)/shard_map/ppermute | solution.py:393
  62.9 2.9 %collective-permute-done.15.r2 = bf16[32,1024]{1,0:T(8,128)(2,1)S(1)} collective-permute-done((bf16[32,1024]{1,0:T(8,128)(2,1)S(1)}, bf16[32,1024]{1,0:T(8,128)(2,1)S(1)}, u32[]{:S(2)}, u32[]{:S(2)}) %collective-permute-start.15) | collective-permute-done | bytes 65568 | tf_op jit(solution)/shard_map/ppermute | solution.py:393
  67.0 1.4 collective-permute-start.17
  68.4 1.2 collective-permute-start.18
  69.5 2.1 %collective-permute-start.19 = (bf16[32,1024]{1,0:T(8,128)(2,1)S(1)}, bf16[32,1024]{1,0:T(8,128)(2,1)S(1)}, u32[]{:S(2)}, u32[]{:S(2)}) collective-permute-start(bf16[32,1024]{1,0:T(8,128)(2,1)S(1)} %get-tuple-element.135), channel_id=1, source_target_pairs={{0,64},{64,128},{128,192},{192,0},{1,65},{65,129},{129,193},{193,1... | collective-permute-start | bytes 196616 | tf_op jit(solution)/shard_map/ppermute | solution.py:393
  71.6 2.5 %collective-permute-start.20 = (bf16[32,1024]{1,0:T(8,128)(2,1)S(1)}, bf16[32,1024]{1,0:T(8,128)(2,1)S(1)}, u32[]{:S(2)}, u32[]{:S(2)}) collective-permute-start(bf16[32,1024]{1,0:T(8,128)(2,1)S(1)} %get-tuple-element.135), channel_id=1, source_target_pairs={{0,128},{64,192},{128,0},{192,64},{1,129},{65,193},{129,1},{193,65... | collective-permute-start | bytes 196616 | tf_op jit(solution)/shard_map/ppermute | solution.py:393
  75.0 2.4 %collective-permute-done.20.r2 = bf16[32,1024]{1,0:T(8,128)(2,1)S(1)} collective-permute-done((bf16[32,1024]{1,0:T(8,128)(2,1)S(1)}, bf16[32,1024]{1,0:T(8,128)(2,1)S(1)}, u32[]{:S(2)}, u32[]{:S(2)}) %collective-permute-start.20) | collective-permute-done | bytes 65568 | tf_op jit(solution)/shard_map/ppermute | solution.py:393
  79.2 1.3 collective-permute-done.18.refs_2_
  81.3 9.3 %finish.1 = (bf16[960,128]{1,0:T(8,128)(2,1)}, bf16[3,128,1024]{2,1,0:T(8,128)(2,1)S(1)}, bf16[8,360,128]{2,1,0:T(8,128)(2,1)}, bf16[40,1024]{1,0:T(8,128)(2,1)S(1)}) custom-call(s32[1]{0:T(128)} %bitcast.2.me.index.zi, s32[1]{0:T(128)} %bitcast.3.me.index.yi, f32[160,1024]{1,0:T(8,128)S(1)} %get-tuple-element.101.zq, ...), custom_call_target="tpu_custom_call" | custom-call | flops 200000000 | bytes 10000000 | tf_op jit(solution)/shard_map/finish/pallas_call | solution.py:534
  92.2 3.6 %all-to-all-start = ((bf16[8,360,128]{2,1,0:T(8,128)(2,1)}), bf16[8,360,128]{2,1,0:T(8,128)(2,1)S(1)}, u32[]{:S(2)}, u32[]{:S(2)}) async-start(bf16[8,360,128]{2,1,0:T(8,128)(2,1)} %get-tuple-element.153), calls=%async_computation | async-start | bytes 1474560 | tf_op jit(solution)/shard_map/all_to_all | solution.py:599
  97.4 1.3 collective-permute-done.27.refs_1_
  100.6 3.1 %collective-permute-start.29 = (bf16[40,1024]{1,0:T(8,128)(2,1)S(1)}, bf16[40,1024]{1,0:T(8,128)(2,1)S(1)}, u32[]{:S(2)}, u32[]{:S(2)}) collective-permute-start(bf16[40,1024]{1,0:T(8,128)(2,1)S(1)} %add_parts.4.refs_0_), channel_id=1, source_target_pairs={{0,32},{16,48},{32,0},{48,16},{1,33},{17,49},{33,1},{49,17},{2,34}... | collective-permute-start | bytes 245768 | tf_op jit(solution)/shard_map/ppermute | solution.py:393
  103.7 2.0 %collective-permute-start.30 = (bf16[40,1024]{1,0:T(8,128)(2,1)S(1)}, bf16[40,1024]{1,0:T(8,128)(2,1)S(1)}, u32[]{:S(2)}, u32[]{:S(2)}) collective-permute-start(bf16[40,1024]{1,0:T(8,128)(2,1)S(1)} %add_parts.4.refs_0_), channel_id=1, source_target_pairs={{0,48},{16,0},{32,16},{48,32},{1,49},{17,1},{33,17},{49,33},{2,50}... | collective-permute-start | bytes 245768 | tf_op jit(solution)/shard_map/ppermute | solution.py:393
  105.7 6.0 %token_grads.1 = bf16[128,1536]{1,0:T(8,128)(2,1)} custom-call(bf16[3,128,1024]{2,1,0:T(8,128)(2,1)} %copy-done.3, bf16[2880,1536]{1,0:T(8,128)(2,1)} %bitcast.20), custom_call_target="tpu_custom_call" | custom-call | flops 1200000000 | bytes 11000000 | tf_op jit(solution)/shard_map/token_grads/pallas_call | solution.py:603
  113.7 2.8 %weight_term.1 = bf16[4,360,384]{2,1,0:T(8,128)(2,1)} custom-call(s32[1]{0:T(128)} %bitcast.3.me.index.yi, s32[1]{0:T(128)} %bitcast.10.ci, bf16[8,360,128]{2,1,0:T(8,128)(2,1)S(1)} %all-to-all-done.arrived, bf16[128,1536]{1,0:T(8,128)(2,1)S(1)} %bitcast.16, bf16[128,1536]{1,0:T(8,128)(2,1)S(1)} %collective-permute-done.17.refs_1_, ...), custom_call_target="tpu_custom_call" | custom-call | flops 1200000000 | bytes 6000000 | tf_op jit(solution)/shard_map/weight_term/pallas_call | solution.py:620
  116.5 5.2 %all-to-all-start.1 = ((bf16[4,360,384]{2,1,0:T(8,128)(2,1)}), bf16[4,360,384]{2,1,0:T(8,128)(2,1)S(1)}, u32[]{:S(2)}, u32[]{:S(2)}) async-start(bf16[4,360,384]{2,1,0:T(8,128)(2,1)} %weight_term.1), calls=%async_computation.1 | async-start | bytes 2211840 | tf_op jit(solution)/shard_map/all_to_all | solution.py:629
  121.7 1.7 %collective-permute-start.31 = (bf16[40,1024]{1,0:T(8,128)(2,1)}, bf16[40,1024]{1,0:T(8,128)(2,1)S(1)}, u32[]{:S(2)}, u32[]{:S(2)}) collective-permute-start(bf16[40,1024]{1,0:T(8,128)(2,1)} %copy-done.7), channel_id=1, source_target_pairs={{0,4},{4,8},{8,12},{12,0},{1,5},{5,9},{9,13},{13,1},{2,6},{6,10},{... | collective-permute-start | bytes 245768 | tf_op jit(solution)/shard_map/ppermute | solution.py:393
  123.4 2.7 %collective-permute-start.32 = (bf16[40,1024]{1,0:T(8,128)(2,1)}, bf16[40,1024]{1,0:T(8,128)(2,1)S(1)}, u32[]{:S(2)}, u32[]{:S(2)}) collective-permute-start(bf16[40,1024]{1,0:T(8,128)(2,1)} %copy-done.7), channel_id=1, source_target_pairs={{0,8},{4,12},{8,0},{12,4},{1,9},{5,13},{9,1},{13,5},{2,10},{6,14},... | collective-permute-start | bytes 245768 | tf_op jit(solution)/shard_map/ppermute | solution.py:393
  126.1 1.4 collective-permute-start.33
  127.6 2.5 %collective-permute-done.32.refs_2_ = bf16[40,1024]{1,0:T(8,128)(2,1)S(1)} collective-permute-done((bf16[40,1024]{1,0:T(8,128)(2,1)}, bf16[40,1024]{1,0:T(8,128)(2,1)S(1)}, u32[]{:S(2)}, u32[]{:S(2)}) %collective-permute-start.32) | collective-permute-done | bytes 81952 | tf_op jit(solution)/shard_map/ppermute | solution.py:393
  131.6 4.6 %collective-permute-start.34 = (bf16[40,1024]{1,0:T(8,128)(2,1)S(1)}, bf16[40,1024]{1,0:T(8,128)(2,1)S(1)}, u32[]{:S(2)}, u32[]{:S(2)}) collective-permute-start(bf16[40,1024]{1,0:T(8,128)(2,1)S(1)} %add_parts.6.refs_0_), channel_id=1, source_target_pairs={{0,2},{2,0},{1,3},{3,1},{4,6},{6,4},{5,7},{7,5},{8,10},{10,8},{9,1... | collective-permute-start | bytes 245768 | tf_op jit(solution)/shard_map/ppermute | solution.py:587
  136.2 4.7 %collective-permute-done.34.refs_1_ = bf16[40,1024]{1,0:T(8,128)(2,1)S(1)} collective-permute-done((bf16[40,1024]{1,0:T(8,128)(2,1)S(1)}, bf16[40,1024]{1,0:T(8,128)(2,1)S(1)}, u32[]{:S(2)}, u32[]{:S(2)}) %collective-permute-start.34) | collective-permute-done | bytes 81952 | tf_op jit(solution)/shard_map/ppermute | solution.py:587
  141.0 1.1 split_rows.1
  142.1 8.6 %all-to-all-start.2 = ((bf16[32,24,180]{2,1,0:T(8,128)(2,1)}), bf16[32,24,180]{2,1,0:T(8,128)(2,1)S(1)}, u32[]{:S(2)}, u32[]{:S(2)}) async-start(bf16[32,24,180]{2,1,0:T(8,128)(2,1)} %split_rows.1), calls=%async_computation.2 | async-start | bytes 786432 | tf_op jit(solution)/shard_map/all_to_all | solution.py:642
  150.6 2.1 %collective-permute-start.35 = (bf16[40,1024]{1,0:T(8,128)(2,1)S(1)}, bf16[40,1024]{1,0:T(8,128)(2,1)S(1)}, u32[]{:S(2)}, u32[]{:S(2)}) collective-permute-start(bf16[40,1024]{1,0:T(8,128)(2,1)S(1)} %add_parts.7.refs_0_), channel_id=1, source_target_pairs={{0,64},{64,128},{128,192},{192,0},{1,65},{65,129},{129,193},{193,1... | collective-permute-start | bytes 245768 | tf_op jit(solution)/shard_map/ppermute | solution.py:393
  152.7 2.7 %collective-permute-start.36 = (bf16[40,1024]{1,0:T(8,128)(2,1)S(1)}, bf16[40,1024]{1,0:T(8,128)(2,1)S(1)}, u32[]{:S(2)}, u32[]{:S(2)}) collective-permute-start(bf16[40,1024]{1,0:T(8,128)(2,1)S(1)} %add_parts.7.refs_0_), channel_id=1, source_target_pairs={{0,128},{64,192},{128,0},{192,64},{1,129},{65,193},{129,1},{193,65... | collective-permute-start | bytes 245768 | tf_op jit(solution)/shard_map/ppermute | solution.py:393
  155.4 1.5 collective-permute-start.37
  156.9 1.8 %collective-permute-done.36.refs_2_ = bf16[40,1024]{1,0:T(8,128)(2,1)S(1)} collective-permute-done((bf16[40,1024]{1,0:T(8,128)(2,1)S(1)}, bf16[40,1024]{1,0:T(8,128)(2,1)S(1)}, u32[]{:S(2)}, u32[]{:S(2)}) %collective-permute-start.36) | collective-permute-done | bytes 81952 | tf_op jit(solution)/shard_map/ppermute | solution.py:393
  158.7 1.1 collective-permute-done.37.refs_3_
  160.6 2.6 %all-to-all-done.2.last = bf16[32,24,180]{2,1,0:T(8,128)(2,1)S(1)} async-done(((bf16[32,24,180]{2,1,0:T(8,128)(2,1)}), bf16[32,24,180]{2,1,0:T(8,128)(2,1)S(1)}, u32[]{:S(2)}, u32[]{:S(2)}) %all-to-all-start.2) | async-done | bytes 276512 | tf_op jit(solution)/shard_map/all_to_all | solution.py:642
  (80 shorter events, 17.8 us)
Async XLA Ops:
  4.9 12.8 %collective-permute-start.4 = (bf16[16,2560]{1,0:T(8,128)(2,1)}, bf16[16,2560]{1,0:T(8,128)(2,1)S(1)}, u32[]{:S(2)}, u32[]{:S(2)}) collective-permute-start(bf16[16,2560]{1,0:T(8,128)(2,1)} %get-tuple-element.95), channel_id=1, source_target_pairs={{4,0},{8,4},{12,8},{16,12},{20,16},{24,20},{28,24},{32,28},{36,32}... | collective-permute-start | bytes 245768 | tf_op jit(solution)/shard_map/ppermute | solution.py:446
  9.4 8.3 %collective-permute-start.3 = (bf16[16,1536]{1,0:T(8,128)(2,1)}, bf16[16,1536]{1,0:T(8,128)(2,1)S(1)}, u32[]{:S(2)}, u32[]{:S(2)}) collective-permute-start(bf16[16,1536]{1,0:T(8,128)(2,1)} %get-tuple-element.94), channel_id=1, source_target_pairs={{0,4},{4,8},{8,12},{12,16},{16,20},{20,24},{24,28},{28,32},{32,36}... | collective-permute-start | bytes 147464 | tf_op jit(solution)/shard_map/ppermute | solution.py:445
  11.3 13.6 %collective-permute-start = (f32[32,15]{1,0:T(8,128)}, f32[32,15]{1,0:T(8,128)S(1)}, u32[]{:S(2)}, u32[]{:S(2)}) collective-permute-start(f32[32,15]{1,0:T(8,128)} %get-tuple-element.102.r0), channel_id=1, source_target_pairs={{0,4},{4,8},{8,12},{12,0},{1,5},{5,9},{9,13},{13,1},{2,6},{6,10},{... | collective-permute-start | bytes 5768 | tf_op jit(solution)/shard_map/ppermute | solution.py:393
  12.4 12.5 %collective-permute-start.1 = (f32[32,15]{1,0:T(8,128)}, f32[32,15]{1,0:T(8,128)S(1)}, u32[]{:S(2)}, u32[]{:S(2)}) collective-permute-start(f32[32,15]{1,0:T(8,128)} %get-tuple-element.102.r0), channel_id=1, source_target_pairs={{0,8},{4,12},{8,0},{12,4},{1,9},{5,13},{9,1},{13,5},{2,10},{6,14},... | collective-permute-start | bytes 5768 | tf_op jit(solution)/shard_map/ppermute | solution.py:393
  17.4 7.5 %collective-permute-start.2 = (f32[32,15]{1,0:T(8,128)}, f32[32,15]{1,0:T(8,128)S(1)}, u32[]{:S(2)}, u32[]{:S(2)}) collective-permute-start(f32[32,15]{1,0:T(8,128)} %get-tuple-element.102.r0), channel_id=1, source_target_pairs={{0,12},{4,0},{8,4},{12,8},{1,13},{5,1},{9,5},{13,9},{2,14},{6,2},{... | collective-permute-start | bytes 5768 | tf_op jit(solution)/shard_map/ppermute | solution.py:393
  17.7 1.0 copy-start
  19.6 5.4 %copy-start.11 = (f32[32,15]{1,0:T(8,128)S(1)}, f32[32,15]{1,0:T(8,128)}, u32[]{:S(2)}) copy-start(f32[32,15]{1,0:T(8,128)} %get-tuple-element.102.r0) | copy-start | bytes 5764
  25.1 13.1 %collective-permute-start.5 = (f32[32,60]{1,0:T(8,128)S(1)}, f32[32,60]{1,0:T(8,128)S(1)}, u32[]{:S(2)}, u32[]{:S(2)}) collective-permute-start(f32[32,60]{1,0:T(8,128)S(1)} %join_params.2.r0), channel_id=1, source_target_pairs={{0,16},{16,32},{32,48},{48,0},{1,17},{17,33},{33,49},{49,1},{2,18}... | collective-permute-start | bytes 23048 | tf_op jit(solution)/shard_map/ppermute | solution.py:393
  27.1 11.1 %collective-permute-start.6 = (f32[32,60]{1,0:T(8,128)S(1)}, f32[32,60]{1,0:T(8,128)S(1)}, u32[]{:S(2)}, u32[]{:S(2)}) collective-permute-start(f32[32,60]{1,0:T(8,128)S(1)} %join_params.2.r0), channel_id=1, source_target_pairs={{0,32},{16,48},{32,0},{48,16},{1,33},{17,49},{33,1},{49,17},{2,34}... | collective-permute-start | bytes 23048 | tf_op jit(solution)/shard_map/ppermute | solution.py:393
  31.0 7.2 %collective-permute-start.7 = (f32[32,60]{1,0:T(8,128)S(1)}, f32[32,60]{1,0:T(8,128)S(1)}, u32[]{:S(2)}, u32[]{:S(2)}) collective-permute-start(f32[32,60]{1,0:T(8,128)S(1)} %join_params.2.r0), channel_id=1, source_target_pairs={{0,48},{16,0},{32,16},{48,32},{1,49},{17,1},{33,17},{49,33},{2,50}... | collective-permute-start | bytes 23048 | tf_op jit(solution)/shard_map/ppermute | solution.py:393
  38.2 10.7 %copy-start.4 = (f32[128,1024]{1,0:T(8,128)S(1)}, f32[128,1024]{1,0:T(8,128)}, u32[]{:S(2)}) copy-start(f32[128,1024]{1,0:T(8,128)} %get-tuple-element.126.cown) | copy-start | bytes 1572868
  38.3 10.5 %collective-permute-start.10 = (f32[32,240]{1,0:T(8,128)S(1)}, f32[32,240]{1,0:T(8,128)S(1)}, u32[]{:S(2)}, u32[]{:S(2)}) collective-permute-start(f32[32,240]{1,0:T(8,128)S(1)} %join_params.3.r0), channel_id=1, source_target_pairs={{0,192},{64,0},{128,64},{192,128},{1,193},{65,1},{129,65},{193,129... | collective-permute-start | bytes 92168 | tf_op jit(solution)/shard_map/ppermute | solution.py:393
  43.4 5.5 %collective-permute-start.8 = (f32[32,240]{1,0:T(8,128)S(1)}, f32[32,240]{1,0:T(8,128)S(1)}, u32[]{:S(2)}, u32[]{:S(2)}) collective-permute-start(f32[32,240]{1,0:T(8,128)S(1)} %join_params.3.r0), channel_id=1, source_target_pairs={{0,64},{64,128},{128,192},{192,0},{1,65},{65,129},{129,193},{193,1... | collective-permute-start | bytes 92168 | tf_op jit(solution)/shard_map/ppermute | solution.py:393
  43.4 5.5 %collective-permute-start.9 = (f32[32,240]{1,0:T(8,128)S(1)}, f32[32,240]{1,0:T(8,128)S(1)}, u32[]{:S(2)}, u32[]{:S(2)}) collective-permute-start(f32[32,240]{1,0:T(8,128)S(1)} %join_params.3.r0), channel_id=1, source_target_pairs={{0,128},{64,192},{128,0},{192,64},{1,129},{65,193},{129,1},{193,65... | collective-permute-start | bytes 92168 | tf_op jit(solution)/shard_map/ppermute | solution.py:393
  45.4 21.6 %copy-start.2 = (bf16[1,128,1536]{2,1,0:T(8,128)(2,1)S(1)}, bf16[1,128,1536]{2,1,0:T(8,128)(2,1)}, u32[]{:S(2)}) copy-start(bf16[1,128,1536]{2,1,0:T(8,128)(2,1)} %param.6) | copy-start | bytes 1179652
  51.1 6.3 %collective-permute-start.11 = (bf16[32,1024]{1,0:T(8,128)(2,1)S(1)}, bf16[32,1024]{1,0:T(8,128)(2,1)S(1)}, u32[]{:S(2)}, u32[]{:S(2)}) collective-permute-start(bf16[32,1024]{1,0:T(8,128)(2,1)S(1)} %get-tuple-element.129), channel_id=1, source_target_pairs={{0,4},{4,8},{8,12},{12,0},{1,5},{5,9},{9,13},{13,1},{2,6},{6,10},{... | collective-permute-start | bytes 196616 | tf_op jit(solution)/shard_map/ppermute | solution.py:393
  51.3 6.1 %collective-permute-start.12 = (bf16[32,1024]{1,0:T(8,128)(2,1)S(1)}, bf16[32,1024]{1,0:T(8,128)(2,1)S(1)}, u32[]{:S(2)}, u32[]{:S(2)}) collective-permute-start(bf16[32,1024]{1,0:T(8,128)(2,1)S(1)} %get-tuple-element.129), channel_id=1, source_target_pairs={{0,8},{4,12},{8,0},{12,4},{1,9},{5,13},{9,1},{13,5},{2,10},{6,14},... | collective-permute-start | bytes 196616 | tf_op jit(solution)/shard_map/ppermute | solution.py:393
  51.3 6.9 %collective-permute-start.13 = (bf16[32,1024]{1,0:T(8,128)(2,1)S(1)}, bf16[32,1024]{1,0:T(8,128)(2,1)S(1)}, u32[]{:S(2)}, u32[]{:S(2)}) collective-permute-start(bf16[32,1024]{1,0:T(8,128)(2,1)S(1)} %get-tuple-element.129), channel_id=1, source_target_pairs={{0,12},{4,0},{8,4},{12,8},{1,13},{5,1},{9,5},{13,9},{2,14},{6,2},{... | collective-permute-start | bytes 196616 | tf_op jit(solution)/shard_map/ppermute | solution.py:393
  58.4 4.5 %collective-permute-start.14 = (bf16[32,1024]{1,0:T(8,128)(2,1)S(1)}, bf16[32,1024]{1,0:T(8,128)(2,1)S(1)}, u32[]{:S(2)}, u32[]{:S(2)}) collective-permute-start(bf16[32,1024]{1,0:T(8,128)(2,1)S(1)} %get-tuple-element.133), channel_id=1, source_target_pairs={{0,16},{16,32},{32,48},{48,0},{1,17},{17,33},{33,49},{49,1},{2,18}... | collective-permute-start | bytes 196616 | tf_op jit(solution)/shard_map/ppermute | solution.py:393
  60.7 5.2 %collective-permute-start.15 = (bf16[32,1024]{1,0:T(8,128)(2,1)S(1)}, bf16[32,1024]{1,0:T(8,128)(2,1)S(1)}, u32[]{:S(2)}, u32[]{:S(2)}) collective-permute-start(bf16[32,1024]{1,0:T(8,128)(2,1)S(1)} %get-tuple-element.133), channel_id=1, source_target_pairs={{0,32},{16,48},{32,0},{48,16},{1,33},{17,49},{33,1},{49,17},{2,34}... | collective-permute-start | bytes 196616 | tf_op jit(solution)/shard_map/ppermute | solution.py:393
  62.5 4.3 %collective-permute-start.16 = (bf16[32,1024]{1,0:T(8,128)(2,1)S(1)}, bf16[32,1024]{1,0:T(8,128)(2,1)S(1)}, u32[]{:S(2)}, u32[]{:S(2)}) collective-permute-start(bf16[32,1024]{1,0:T(8,128)(2,1)S(1)} %get-tuple-element.133), channel_id=1, source_target_pairs={{0,48},{16,0},{32,16},{48,32},{1,49},{17,1},{33,17},{49,33},{2,50}... | collective-permute-start | bytes 196616 | tf_op jit(solution)/shard_map/ppermute | solution.py:393
  67.0 12.2 %collective-permute-start.17 = (bf16[128,1536]{1,0:T(8,128)(2,1)S(1)}, bf16[128,1536]{1,0:T(8,128)(2,1)S(1)}, u32[]{:S(2)}, u32[]{:S(2)}) collective-permute-start(bf16[128,1536]{1,0:T(8,128)(2,1)S(1)} %bitcast.13), channel_id=1, source_target_pairs={{0,4},{4,0},{8,12},{12,8},{1,5},{5,1},{9,13},{13,9},{2,6},{6,2},{1... | collective-permute-start | bytes 1179656 | tf_op jit(solution)/shard_map/ppermute | solution.py:522
  68.4 12.1 %collective-permute-start.18 = (bf16[128,1536]{1,0:T(8,128)(2,1)S(1)}, bf16[128,1536]{1,0:T(8,128)(2,1)S(1)}, u32[]{:S(2)}, u32[]{:S(2)}) collective-permute-start(bf16[128,1536]{1,0:T(8,128)(2,1)S(1)} %bitcast.14), channel_id=1, source_target_pairs={{0,12},{4,8},{8,4},{12,0},{1,13},{5,9},{9,5},{13,1},{2,14},{6,10},... | collective-permute-start | bytes 1179656 | tf_op jit(solution)/shard_map/ppermute | solution.py:523
  69.5 5.5 %collective-permute-start.19 = (bf16[32,1024]{1,0:T(8,128)(2,1)S(1)}, bf16[32,1024]{1,0:T(8,128)(2,1)S(1)}, u32[]{:S(2)}, u32[]{:S(2)}) collective-permute-start(bf16[32,1024]{1,0:T(8,128)(2,1)S(1)} %get-tuple-element.135), channel_id=1, source_target_pairs={{0,64},{64,128},{128,192},{192,0},{1,65},{65,129},{129,193},{193,1... | collective-permute-start | bytes 196616 | tf_op jit(solution)/shard_map/ppermute | solution.py:393
  71.6 5.8 %collective-permute-start.20 = (bf16[32,1024]{1,0:T(8,128)(2,1)S(1)}, bf16[32,1024]{1,0:T(8,128)(2,1)S(1)}, u32[]{:S(2)}, u32[]{:S(2)}) collective-permute-start(bf16[32,1024]{1,0:T(8,128)(2,1)S(1)} %get-tuple-element.135), channel_id=1, source_target_pairs={{0,128},{64,192},{128,0},{192,64},{1,129},{65,193},{129,1},{193,65... | collective-permute-start | bytes 196616 | tf_op jit(solution)/shard_map/ppermute | solution.py:393
  74.1 4.3 %collective-permute-start.21 = (bf16[32,1024]{1,0:T(8,128)(2,1)S(1)}, bf16[32,1024]{1,0:T(8,128)(2,1)S(1)}, u32[]{:S(2)}, u32[]{:S(2)}) collective-permute-start(bf16[32,1024]{1,0:T(8,128)(2,1)S(1)} %get-tuple-element.135), channel_id=1, source_target_pairs={{0,192},{64,0},{128,64},{192,128},{1,193},{65,1},{129,65},{193,129... | collective-permute-start | bytes 196616 | tf_op jit(solution)/shard_map/ppermute | solution.py:393
  80.4 16.4 %collective-permute-start.25 = (bf16[128,1536]{1,0:T(8,128)(2,1)S(1)}, bf16[128,1536]{1,0:T(8,128)(2,1)S(1)}, u32[]{:S(2)}, u32[]{:S(2)}) collective-permute-start(bf16[128,1536]{1,0:T(8,128)(2,1)S(1)} %collective-permute-done.17.refs_1_), channel_id=1, source_target_pairs={{0,12},{4,8},{8,4},{12,0},{1,13},{5,9},{9,5},{13,1},{2,14},{6,10},... | collective-permute-start | bytes 1179656 | tf_op jit(solution)/shard_map/ppermute | solution.py:525
  90.7 0.9 copy-start.3
  92.2 20.5 %all-to-all-start = ((bf16[8,360,128]{2,1,0:T(8,128)(2,1)}), bf16[8,360,128]{2,1,0:T(8,128)(2,1)S(1)}, u32[]{:S(2)}, u32[]{:S(2)}) async-start(bf16[8,360,128]{2,1,0:T(8,128)(2,1)} %get-tuple-element.153), calls=%async_computation | async-start | bytes 1474560 | tf_op jit(solution)/shard_map/all_to_all | solution.py:599
  95.8 3.8 %collective-permute-start.22 = (bf16[128,1536]{1,0:T(8,128)(2,1)S(1)}, bf16[128,1536]{1,0:T(8,128)(2,1)S(1)}, u32[]{:S(2)}, u32[]{:S(2)}) collective-permute-start(bf16[128,1536]{1,0:T(8,128)(2,1)S(1)} %bitcast.15), channel_id=1, source_target_pairs={{0,1},{1,0},{2,3},{3,2},{4,5},{5,4},{6,7},{7,6},{8,9},{9,8},{10,11... | collective-permute-start | bytes 1179656 | tf_op jit(solution)/shard_map/ppermute | solution.py:528
  96.3 3.3 %collective-permute-start.23 = (bf16[128,1536]{1,0:T(8,128)(2,1)S(1)}, bf16[128,1536]{1,0:T(8,128)(2,1)S(1)}, u32[]{:S(2)}, u32[]{:S(2)}) collective-permute-start(bf16[128,1536]{1,0:T(8,128)(2,1)S(1)} %collective-permute-done.17.refs_1_), channel_id=1, source_target_pairs={{0,1},{1,0},{2,3},{3,2},{4,5},{5,4},{6,7},{7,6},{8,9},{9,8},{10,11... | collective-permute-start | bytes 1179656 | tf_op jit(solution)/shard_map/ppermute | solution.py:528
  96.4 3.2 %collective-permute-start.24 = (bf16[128,1536]{1,0:T(8,128)(2,1)S(1)}, bf16[128,1536]{1,0:T(8,128)(2,1)S(1)}, u32[]{:S(2)}, u32[]{:S(2)}) collective-permute-start(bf16[128,1536]{1,0:T(8,128)(2,1)S(1)} %collective-permute-done.18.refs_2_), channel_id=1, source_target_pairs={{0,1},{1,0},{2,3},{3,2},{4,5},{5,4},{6,7},{7,6},{8,9},{9,8},{10,11... | collective-permute-start | bytes 1179656 | tf_op jit(solution)/shard_map/ppermute | solution.py:528
  96.9 2.8 %collective-permute-start.26 = (bf16[128,1536]{1,0:T(8,128)(2,1)S(1)}, bf16[128,1536]{1,0:T(8,128)(2,1)S(1)}, u32[]{:S(2)}, u32[]{:S(2)}) collective-permute-start(bf16[128,1536]{1,0:T(8,128)(2,1)S(1)} %collective-permute-done.25.refs_3_), channel_id=1, source_target_pairs={{0,1},{1,0},{2,3},{3,2},{4,5},{5,4},{6,7},{7,6},{8,9},{9,8},{10,11... | collective-permute-start | bytes 1179656 | tf_op jit(solution)/shard_map/ppermute | solution.py:528
  96.9 1.8 %collective-permute-start.27 = (bf16[40,1024]{1,0:T(8,128)(2,1)}, bf16[40,1024]{1,0:T(8,128)(2,1)S(1)}, u32[]{:S(2)}, u32[]{:S(2)}) collective-permute-start(bf16[40,1024]{1,0:T(8,128)(2,1)} %copy-done.9), channel_id=1, source_target_pairs={{0,1},{1,0},{2,3},{3,2},{4,5},{5,4},{6,7},{7,6},{8,9},{9,8},{10,11... | collective-permute-start | bytes 245768 | tf_op jit(solution)/shard_map/ppermute | solution.py:587
  100.4 11.4 %collective-permute-start.28 = (bf16[40,1024]{1,0:T(8,128)(2,1)S(1)}, bf16[40,1024]{1,0:T(8,128)(2,1)S(1)}, u32[]{:S(2)}, u32[]{:S(2)}) collective-permute-start(bf16[40,1024]{1,0:T(8,128)(2,1)S(1)} %add_parts.4.refs_0_), channel_id=1, source_target_pairs={{0,16},{16,32},{32,48},{48,0},{1,17},{17,33},{33,49},{49,1},{2,18}... | collective-permute-start | bytes 245768 | tf_op jit(solution)/shard_map/ppermute | solution.py:393
  100.6 11.1 %collective-permute-start.29 = (bf16[40,1024]{1,0:T(8,128)(2,1)S(1)}, bf16[40,1024]{1,0:T(8,128)(2,1)S(1)}, u32[]{:S(2)}, u32[]{:S(2)}) collective-permute-start(bf16[40,1024]{1,0:T(8,128)(2,1)S(1)} %add_parts.4.refs_0_), channel_id=1, source_target_pairs={{0,32},{16,48},{32,0},{48,16},{1,33},{17,49},{33,1},{49,17},{2,34}... | collective-permute-start | bytes 245768 | tf_op jit(solution)/shard_map/ppermute | solution.py:393
  103.7 8.3 %collective-permute-start.30 = (bf16[40,1024]{1,0:T(8,128)(2,1)S(1)}, bf16[40,1024]{1,0:T(8,128)(2,1)S(1)}, u32[]{:S(2)}, u32[]{:S(2)}) collective-permute-start(bf16[40,1024]{1,0:T(8,128)(2,1)S(1)} %add_parts.4.refs_0_), channel_id=1, source_target_pairs={{0,48},{16,0},{32,16},{48,32},{1,49},{17,1},{33,17},{49,33},{2,50}... | collective-permute-start | bytes 245768 | tf_op jit(solution)/shard_map/ppermute | solution.py:393
  112.7 1.0 copy-start.6
  116.5 43.4 %copy-start.12 = (f32[15,16]{1,0:T(8,128)S(1)}, f32[15,16]{1,0:T(8,128)}, u32[]{:S(2)}) copy-start(f32[15,16]{1,0:T(8,128)} %get-tuple-element.166.amp) | copy-start | bytes 2884
  116.5 24.5 %all-to-all-start.1 = ((bf16[4,360,384]{2,1,0:T(8,128)(2,1)}), bf16[4,360,384]{2,1,0:T(8,128)(2,1)S(1)}, u32[]{:S(2)}, u32[]{:S(2)}) async-start(bf16[4,360,384]{2,1,0:T(8,128)(2,1)} %weight_term.1), calls=%async_computation.1 | async-start | bytes 2211840 | tf_op jit(solution)/shard_map/all_to_all | solution.py:629
  121.7 5.9 %collective-permute-start.31 = (bf16[40,1024]{1,0:T(8,128)(2,1)}, bf16[40,1024]{1,0:T(8,128)(2,1)S(1)}, u32[]{:S(2)}, u32[]{:S(2)}) collective-permute-start(bf16[40,1024]{1,0:T(8,128)(2,1)} %copy-done.7), channel_id=1, source_target_pairs={{0,4},{4,8},{8,12},{12,0},{1,5},{5,9},{9,13},{13,1},{2,6},{6,10},{... | collective-permute-start | bytes 245768 | tf_op jit(solution)/shard_map/ppermute | solution.py:393
  123.4 6.7 %collective-permute-start.32 = (bf16[40,1024]{1,0:T(8,128)(2,1)}, bf16[40,1024]{1,0:T(8,128)(2,1)S(1)}, u32[]{:S(2)}, u32[]{:S(2)}) collective-permute-start(bf16[40,1024]{1,0:T(8,128)(2,1)} %copy-done.7), channel_id=1, source_target_pairs={{0,8},{4,12},{8,0},{12,4},{1,9},{5,13},{9,1},{13,5},{2,10},{6,14},... | collective-permute-start | bytes 245768 | tf_op jit(solution)/shard_map/ppermute | solution.py:393
  126.1 4.7 %collective-permute-start.33 = (bf16[40,1024]{1,0:T(8,128)(2,1)}, bf16[40,1024]{1,0:T(8,128)(2,1)S(1)}, u32[]{:S(2)}, u32[]{:S(2)}) collective-permute-start(bf16[40,1024]{1,0:T(8,128)(2,1)} %copy-done.7), channel_id=1, source_target_pairs={{0,12},{4,0},{8,4},{12,8},{1,13},{5,1},{9,5},{13,9},{2,14},{6,2},{... | collective-permute-start | bytes 245768 | tf_op jit(solution)/shard_map/ppermute | solution.py:393
  131.6 9.3 %collective-permute-start.34 = (bf16[40,1024]{1,0:T(8,128)(2,1)S(1)}, bf16[40,1024]{1,0:T(8,128)(2,1)S(1)}, u32[]{:S(2)}, u32[]{:S(2)}) collective-permute-start(bf16[40,1024]{1,0:T(8,128)(2,1)S(1)} %add_parts.6.refs_0_), channel_id=1, source_target_pairs={{0,2},{2,0},{1,3},{3,1},{4,6},{6,4},{5,7},{7,5},{8,10},{10,8},{9,1... | collective-permute-start | bytes 245768 | tf_op jit(solution)/shard_map/ppermute | solution.py:587
  142.1 21.2 %all-to-all-start.2 = ((bf16[32,24,180]{2,1,0:T(8,128)(2,1)}), bf16[32,24,180]{2,1,0:T(8,128)(2,1)S(1)}, u32[]{:S(2)}, u32[]{:S(2)}) async-start(bf16[32,24,180]{2,1,0:T(8,128)(2,1)} %split_rows.1), calls=%async_computation.2 | async-start | bytes 786432 | tf_op jit(solution)/shard_map/all_to_all | solution.py:642
  150.6 6.2 %collective-permute-start.35 = (bf16[40,1024]{1,0:T(8,128)(2,1)S(1)}, bf16[40,1024]{1,0:T(8,128)(2,1)S(1)}, u32[]{:S(2)}, u32[]{:S(2)}) collective-permute-start(bf16[40,1024]{1,0:T(8,128)(2,1)S(1)} %add_parts.7.refs_0_), channel_id=1, source_target_pairs={{0,64},{64,128},{128,192},{192,0},{1,65},{65,129},{129,193},{193,1... | collective-permute-start | bytes 245768 | tf_op jit(solution)/shard_map/ppermute | solution.py:393
  152.7 6.0 %collective-permute-start.36 = (bf16[40,1024]{1,0:T(8,128)(2,1)S(1)}, bf16[40,1024]{1,0:T(8,128)(2,1)S(1)}, u32[]{:S(2)}, u32[]{:S(2)}) collective-permute-start(bf16[40,1024]{1,0:T(8,128)(2,1)S(1)} %add_parts.7.refs_0_), channel_id=1, source_target_pairs={{0,128},{64,192},{128,0},{192,64},{1,129},{65,193},{129,1},{193,65... | collective-permute-start | bytes 245768 | tf_op jit(solution)/shard_map/ppermute | solution.py:393
  155.4 4.4 %collective-permute-start.37 = (bf16[40,1024]{1,0:T(8,128)(2,1)S(1)}, bf16[40,1024]{1,0:T(8,128)(2,1)S(1)}, u32[]{:S(2)}, u32[]{:S(2)}) collective-permute-start(bf16[40,1024]{1,0:T(8,128)(2,1)S(1)} %add_parts.7.refs_0_), channel_id=1, source_target_pairs={{0,192},{64,0},{128,64},{192,128},{1,193},{65,1},{129,65},{193,129... | collective-permute-start | bytes 245768 | tf_op jit(solution)/shard_map/ppermute | solution.py:393
  (6 other events, 4.7 us)

commit v8 on v7

--- a/solution.py
+++ b/solution.py
@@ -21,12 +21,26 @@
     return a.astype(BF16).astype(F32)
 
 
+PARTS = 12
+
+
+def part_copies(src, base, dst, sems):
+    size = dst.shape[0] // PARTS
+    return [
+        pltpu.make_async_copy(
+            src.at[pl.ds(base + i * size, size)], dst.at[pl.ds(i * size, size)], sems.at[i]
+        )
+        for i in range(PARTS)
+    ]
+
+
 def make_project(g):
     def project(*refs):
         if g < 2:
-            *ins, wt, zf, mix, wnext, sem = refs
-            coming = pltpu.make_async_copy(wt.at[pl.ds((g + 1) * wnext.shape[0], wnext.shape[0])], wnext, sem)
-            coming.start()
+            *ins, wt, zf, mix, wnext, sems = refs
+            coming = part_copies(wt, (g + 1) * wnext.shape[0], wnext, sems)
+            for copy in coming:
+                copy.start()
         else:
             *ins, zf, mix = refs
         tp, nexts, taps, tk, w = ins
@@ -47,7 +61,8 @@
 
         lax.fori_loop(0, PADC // 128, tile, 0)
         if g < 2:
-            coming.wait()
+            for copy in coming:
+                copy.wait()
 
     return project
 
@@ -61,7 +76,7 @@
 
 def prepare(
     feats, cott, rates, residues, conv, wt, head, tail, block, taps, amp, tokens, cots, wfirst,
-    held, turn, cbuf, rbuf, sbuf, vbuf, sems,
+    held, turn, cbuf, rbuf, sbuf, vbuf, sems, wsems,
 ):
     count = rates.shape[0]
     width, own = cott.shape
@@ -74,7 +89,7 @@
         pltpu.make_async_copy(feats.at[pl.ds(0, HALO)], head.at[:, pl.ds(0, depth)], sems.at[4]),
         pltpu.make_async_copy(feats.at[pl.ds(own - HALO, HALO)], tail, sems.at[5]),
         pltpu.make_async_copy(feats, tokens, sems.at[6]),
-        pltpu.make_async_copy(wt.at[pl.ds(0, width)], wfirst, sems.at[7]),
+        *part_copies(wt, 0, wfirst, wsems),
     ]
     for copy in copies:
         copy.start()
@@ -295,21 +310,22 @@
             dzb[b] = jnp.concatenate(both, axis=0).astype(BF16)
 
 
-def token_grads(dz, wt, out, acc):
-    g = pl.program_id(0)
-    part = jnp.dot(dz[0, :, 0 : wt.shape[0]], wt[...], preferred_element_type=F32)
-
-    @pl.when(g == 0)
-    def _():
-        acc[...] = part
-
-    @pl.when(g > 0)
-    def _():
-        acc[...] += part
-
-    @pl.when(g == pl.num_programs(0) - 1)
-    def _():
-        out[...] = acc[...].astype(BF16)
+def token_grads(dz, wt, out, dbuf, wbuf, dsem, sems):
+    groups, width, depth = wbuf.shape
+    dcopy = pltpu.make_async_copy(dz, dbuf, dsem)
+    dcopy.start()
+    coming = [part_copies(wt, g * width, wbuf.at[g], sems.at[g]) for g in range(groups)]
+    for copies in coming:
+        for copy in copies:
+            copy.start()
+    dcopy.wait()
+    total = None
+    for g in range(groups):
+        for copy in coming[g]:
+            copy.wait()
+        part = jnp.dot(dbuf[g, :, 0:width], wbuf[g], preferred_element_type=F32)
+        total = part if total is None else total + part
+    out[...] = total.astype(BF16)
 
 
 def weight_term(yi, ci, arrived, *refs):
@@ -410,6 +426,7 @@
     scale = 1.0 / math.sqrt(4 * count * own)
     smem = pl.BlockSpec(memory_space=pltpu.SMEM)
     vm = pl.BlockSpec(memory_space=pltpu.VMEM)
+    free = pl.BlockSpec()
     names = ("x", "zl", "y", "core")
     feats, cot, rates, *where = lax.optimization_barrier(
         (feats, cot, rates, *[lax.axis_index(n) for n in names])
@@ -437,7 +454,8 @@
             pltpu.VMEM(rates.shape, F32),
             pltpu.VMEM(rates.shape, F32),
             pltpu.VMEM(conv_taps.shape, F32),
-            pltpu.SemaphoreType.DMA((8,)),
+            pltpu.SemaphoreType.DMA((7,)),
+            pltpu.SemaphoreType.DMA((PARTS,)),
         ],
         compiler_params=params(54),
         name="prepare",
@@ -457,7 +475,7 @@
             in_specs=[vm] * 5 + [anywhere] * more,
             out_specs=[vm] * (2 + more),
             out_shape=project_out + [jax.ShapeDtypeStruct((width, depth), BF16)] * more,
-            scratch_shapes=[pltpu.SemaphoreType.DMA] * more,
+            scratch_shapes=[pltpu.SemaphoreType.DMA((PARTS,))] * more,
             compiler_params=params((50, 50, 50)[g]),
             cost_estimate=project_cost,
             name="project",
@@ -589,8 +607,8 @@
     def summed(parts):
         return pl.pallas_call(
             add_parts,
-            in_specs=[vm] * len(parts),
-            out_specs=vm,
+            in_specs=[free] * len(parts),
+            out_specs=free,
             out_shape=jax.ShapeDtypeStruct((40, PADC), BF16),
             compiler_params=params(4),
             name="add_parts",
@@ -600,26 +618,11 @@
     sums = summed(swap(sums, "core"))
     *theirs, sums = lax.optimization_barrier((*theirs, sums))
     parts = spread(sums, "zl")
-    grad_feats = pl.pallas_call(
-        token_grads,
-        grid=(3,),
-        in_specs=[
-            pl.BlockSpec((1, own, PADC), lambda g: (g, 0, 0)),
-            pl.BlockSpec((width, depth), lambda g: (g, 0)),
-        ],
-        out_specs=pl.BlockSpec((own, depth), lambda g: (0, 0)),
-        out_shape=jax.ShapeDtypeStruct((own, depth), BF16),
-        scratch_shapes=[pltpu.VMEM((own, depth), F32)],
-        compiler_params=params(57),
-        cost_estimate=pl.CostEstimate(flops=1200000000, bytes_accessed=11000000, transcendentals=0),
-        name="token_grads",
-    )(dz, w_in.T)
-    *parts, grad_feats = lax.optimization_barrier((*parts, grad_feats))
     sums = summed(parts)
     arrived, sums = lax.optimization_barrier((arrived, sums))
     term = pl.pallas_call(
         weight_term,
-        in_specs=[smem] * 2 + [vm] * 9,
+        in_specs=[smem] * 2 + [vm] + [free] * 8,
         out_specs=vm,
         out_shape=jax.ShapeDtypeStruct((4, 2 * piece, depth // 4), BF16),
         compiler_params=params(24),
@@ -642,9 +645,26 @@
     last = lax.all_to_all(blocks, ("zl", "y", "zh"), 0, 0, tiled=True)
     sums, _ = lax.optimization_barrier((sums, blocks))
     parts = spread(sums, "x")
+    dz, _ = lax.optimization_barrier((dz, blocks))
+    grad_feats = pl.pallas_call(
+        token_grads,
+        in_specs=[anywhere] * 2,
+        out_specs=vm,
+        out_shape=jax.ShapeDtypeStruct((own, depth), BF16),
+        scratch_shapes=[
+            pltpu.VMEM((3, own, PADC), BF16),
+            pltpu.VMEM((3, width, depth), BF16),
+            pltpu.SemaphoreType.DMA,
+            pltpu.SemaphoreType.DMA((3, PARTS)),
+        ],
+        compiler_params=params(57),
+        cost_estimate=pl.CostEstimate(flops=1200000000, bytes_accessed=11000000, transcendentals=0),
+        name="token_grads",
+    )(dz, w_in.T)
+    *parts, grad_feats = lax.optimization_barrier((*parts, grad_feats))
     grad_taps, grad_residues = pl.pallas_call(
         make_close_sums(scale),
-        in_specs=[smem] * 3 + [vm] * 5,
+        in_specs=[smem] * 3 + [free] * 5,
         out_specs=[vm] * 2,
         out_shape=[
             jax.ShapeDtypeStruct((7, chans), F32),

time: 165 us -> 168 us (1.018)
  Pallas kernels: 42.7 us -> 45.3 us
    ppermute x27, waiting for transfers between devices: 18.6 us -> 21.6 us  [ring(): return lax.ppermute(a, ax, [(i, (i + d) % 4) for i in range(4)])]
    all_to_all x1, waiting for transfers between devices: 2.61 us -> 0.01 us  [local(): last = lax.all_to_all(blocks, ('zl', 'y', 'zh'), 0, 0, tiled=True)]
    pallas_call x3, Pallas kernels: 14.1 us -> 16 us  [local(): pl.pallas_call(make_project(g), in_specs=[vm] * 5 + [anywhere] * more, ou...]
  transfers between devices with their start and end apart: 41 -> 41, of which waited for: 19 -> 17; matrix products, arithmetic and copies ran while one was open for 0% -> 0% of each run, Pallas kernels for 19% -> 20%
where the time goes in v8:
time: 168 us; the launch traced here: 167 us
  starting transfers between devices  83.8 us (50%)
  Pallas kernels  45.3 us (27%)
  waiting for transfers between devices  29.2 us (17%)
  local copies, waits for them, and re-layouts  7.56 us (4%)
    ppermute x27, starting transfers between devices, ring(): return lax.ppermute(a, ax, [(i, (i + d) % 4) for i in range(4)])  50.5 us
    ppermute x27, waiting for transfers between devices, ring(): return lax.ppermute(a, ax, [(i, (i + d) % 4) for i in range(4)])  21.6 us
    pallas_call x3, Pallas kernels, local(): pl.pallas_call(make_project(g), in_specs=[vm] * 5 + [anywhere] * more, ou...  16 us
    pallas_call x1, Pallas kernels, local(): pl.pallas_call(finish, grid=(PADC // 128,), in_specs=[smem, smem, *[tiles...  9.38 us
    all_to_all x1, starting transfers between devices, local(): last = lax.all_to_all(blocks, ('zl', 'y', 'zh'), 0, 0, tiled=True)  8.58 us
    unnamed x26, local copies, waits for them, and re-layouts  7.56 us
    pallas_call x1, Pallas kernels, local(): pl.pallas_call(token_grads, in_specs=[anywhere] * 2, out_specs=vm, out_sh...  6.63 us
    ppermute x2, waiting for transfers between devices, swap(): return [a, lax.ppermute(a, ax, [(0, 1), (1, 0)])]  6.06 us
  transfers between devices with their start and end apart: 41, of which 17 were waited for; matrix products, arithmetic and copies ran while one was open for 0% of the time, Pallas kernels for 20%

profile of v8, /device:TPU:32, one launch (start us, length us, event | category | flops | bytes accessed | tf_op | source)
XLA Modules:
  0.0 166.9 jit_solution(4248189467535119650)
XLA Ops:
  0.6 4.3 %prepare.1 = (bf16[16,2560]{1,0:T(8,128)(2,1)}, bf16[16,1536]{1,0:T(8,128)(2,1)}, f32[32,15]{1,0:T(8,128)}, f32[3,8,1024]{2,1,0:T(8,128)}, f32[15,16]{1,0:T(8,12...) custom-call(bf16[128,1536]{1,0:T(8,128)(2,1)} %bitcast.12, ...), custom_call_target="tpu_custom_call" | custom-call | tf_op jit(solution)/shard_map/prepare/pallas_call | solution.py:436
  5.0 4.5 %collective-permute-start.4 = (bf16[16,2560]{1,0:T(8,128)(2,1)}, bf16[16,2560]{1,0:T(8,128)(2,1)S(1)}, u32[]{:S(2)}, u32[]{:S(2)}) collective-permute-start(bf16[16,2560]{1,0:T(8,128)(2,1)} %get-tuple-element.96), channel_id=1, source_target_pairs={{4,0},{8,4},{12,8},{16,12},{20,16},{24,20},{28,24},{32,28},{36,32}... | collective-permute-start | bytes 245768 | tf_op jit(solution)/shard_map/ppermute | solution.py:464
  9.4 1.9 %collective-permute-start.3 = (bf16[16,1536]{1,0:T(8,128)(2,1)}, bf16[16,1536]{1,0:T(8,128)(2,1)S(1)}, u32[]{:S(2)}, u32[]{:S(2)}) collective-permute-start(bf16[16,1536]{1,0:T(8,128)(2,1)} %get-tuple-element.95), channel_id=1, source_target_pairs={{0,4},{4,8},{8,12},{12,16},{16,20},{20,24},{24,28},{28,32},{32,36}... | collective-permute-start | bytes 147464 | tf_op jit(solution)/shard_map/ppermute | solution.py:463
  11.4 1.1 collective-permute-start
  12.5 5.0 %collective-permute-start.1 = (f32[32,15]{1,0:T(8,128)}, f32[32,15]{1,0:T(8,128)S(1)}, u32[]{:S(2)}, u32[]{:S(2)}) collective-permute-start(f32[32,15]{1,0:T(8,128)} %get-tuple-element.103.r0), channel_id=1, source_target_pairs={{0,8},{4,12},{8,0},{12,4},{1,9},{5,13},{9,1},{13,5},{2,10},{6,14},... | collective-permute-start | bytes 5768 | tf_op jit(solution)/shard_map/ppermute | solution.py:409
  17.8 1.0 copy-done
  19.7 6.3 %project.3 = (f32[160,1024]{1,0:T(8,128)S(1)}, f32[136,1024]{1,0:T(8,128)S(1)}, bf16[960,1536]{1,0:T(8,128)(2,1)}) custom-call(bf16[16,1536]{1,0:T(8,128)(2,1)S(1)} %collective-permute-done.3.refs_0_, bf16[16,2560]{1,0:T(8,128)(2,1)S(1)} %collective-permute-done.4.refs_1_.nexts, f32[3,8,1024]{2,1,0:T(8,128)S(1)} %copy-done.1, bf16[128,1536]{1,0:T(8,128)(2,1)S(1)} %copy-done, ...), custom_call_target="tpu_custom_call" | custom-call | flops 500000000 | bytes 4000000 | tf_op jit(solution)/shard_map/project/pallas_call | solution.py:473
  26.1 2.0 %collective-permute-start.5 = (f32[32,60]{1,0:T(8,128)S(1)}, f32[32,60]{1,0:T(8,128)S(1)}, u32[]{:S(2)}, u32[]{:S(2)}) collective-permute-start(f32[32,60]{1,0:T(8,128)S(1)} %join_params.2.r0), channel_id=1, source_target_pairs={{0,16},{16,32},{32,48},{48,0},{1,17},{17,33},{33,49},{49,1},{2,18}... | collective-permute-start | bytes 23048 | tf_op jit(solution)/shard_map/ppermute | solution.py:409
  28.1 3.9 %collective-permute-start.6 = (f32[32,60]{1,0:T(8,128)S(1)}, f32[32,60]{1,0:T(8,128)S(1)}, u32[]{:S(2)}, u32[]{:S(2)}) collective-permute-start(f32[32,60]{1,0:T(8,128)S(1)} %join_params.2.r0), channel_id=1, source_target_pairs={{0,32},{16,48},{32,0},{48,16},{1,33},{17,49},{33,1},{49,17},{2,34}... | collective-permute-start | bytes 23048 | tf_op jit(solution)/shard_map/ppermute | solution.py:409
  32.0 1.9 %collective-permute-start.7 = (f32[32,60]{1,0:T(8,128)S(1)}, f32[32,60]{1,0:T(8,128)S(1)}, u32[]{:S(2)}, u32[]{:S(2)}) collective-permute-start(f32[32,60]{1,0:T(8,128)S(1)} %join_params.2.r0), channel_id=1, source_target_pairs={{0,48},{16,0},{32,16},{48,32},{1,49},{17,1},{33,17},{49,33},{2,50}... | collective-permute-start | bytes 23048 | tf_op jit(solution)/shard_map/ppermute | solution.py:409
  33.9 6.2 %project.4 = (f32[160,1024]{1,0:T(8,128)S(1)}, f32[136,1024]{1,0:T(8,128)S(1)}, bf16[960,1536]{1,0:T(8,128)(2,1)}) custom-call(bf16[16,1536]{1,0:T(8,128)(2,1)S(1)} %collective-permute-done.3.refs_0_, bf16[16,2560]{1,0:T(8,128)(2,1)S(1)} %collective-permute-done.4.refs_1_.nexts, f32[3,8,1024]{2,1,0:T(8,128)S(1)} %copy-done.1, bf16[128,1536]{1,0:T(8,128)(2,1)S(1)} %copy-done, ...), custom_call_target="tpu_custom_call" | custom-call | flops 500000000 | bytes 4000000 | tf_op jit(solution)/shard_map/project/pallas_call | solution.py:473
  40.3 5.0 %collective-permute-start.10 = (f32[32,240]{1,0:T(8,128)S(1)}, f32[32,240]{1,0:T(8,128)S(1)}, u32[]{:S(2)}, u32[]{:S(2)}) collective-permute-start(f32[32,240]{1,0:T(8,128)S(1)} %join_params.3.r0), channel_id=1, source_target_pairs={{0,192},{64,0},{128,64},{192,128},{1,193},{65,1},{129,65},{193,129... | collective-permute-start | bytes 92168 | tf_op jit(solution)/shard_map/ppermute | solution.py:409
  45.3 2.0 %collective-permute-start.9 = (f32[32,240]{1,0:T(8,128)S(1)}, f32[32,240]{1,0:T(8,128)S(1)}, u32[]{:S(2)}, u32[]{:S(2)}) collective-permute-start(f32[32,240]{1,0:T(8,128)S(1)} %join_params.3.r0), channel_id=1, source_target_pairs={{0,128},{64,192},{128,0},{192,64},{1,129},{65,193},{129,1},{193,65... | collective-permute-start | bytes 92168 | tf_op jit(solution)/shard_map/ppermute | solution.py:409
  47.3 3.5 %project.5 = (f32[160,1024]{1,0:T(8,128)S(1)}, f32[136,1024]{1,0:T(8,128)S(1)}) custom-call(bf16[16,1536]{1,0:T(8,128)(2,1)S(1)} %collective-permute-done.3.refs_0_, bf16[16,2560]{1,0:T(8,128)(2,1)S(1)} %collective-permute-done.4.refs_1_.nexts, f32[3,8,1024]{2,1,0:T(8,128)S(1)} %copy-done.1, bf16[128,1536]{1,0:T(8,128)(2,1)S(1)} %copy-done, ...), custom_call_target="tpu_custom_call" | custom-call | flops 500000000 | bytes 4000000 | tf_op jit(solution)/shard_map/project/pallas_call | solution.py:473
  50.8 2.2 %end_states.1 = (f32[136,1024]{1,0:T(8,128)S(1)}, f32[16,1024]{1,0:T(8,128)S(1)}, f32[16,1024]{1,0:T(8,128)S(1)}, f32[2,16,8,1024]{3,2,1,0:T(8,128)S(1)}, f32[32...) custom-call(s32[1]{0:T(128)} %bitcast.6.me.index.xi, f32[32,240]{1,0:T(8,128)S(1)} %join_params.3.r0, ...), custom_call_target="tpu_custom_call" | custom-call | flops 20000000 | bytes 3000000 | tf_op jit(solution)/shard_map/end_states/pallas_call | solution.py:499
  53.2 3.1 %collective-permute-start.13 = (bf16[32,1024]{1,0:T(8,128)(2,1)S(1)}, bf16[32,1024]{1,0:T(8,128)(2,1)S(1)}, u32[]{:S(2)}, u32[]{:S(2)}) collective-permute-start(bf16[32,1024]{1,0:T(8,128)(2,1)S(1)} %get-tuple-element.130), channel_id=1, source_target_pairs={{0,12},{4,0},{8,4},{12,8},{1,13},{5,1},{9,5},{13,9},{2,14},{6,2},{... | collective-permute-start | bytes 196616 | tf_op jit(solution)/shard_map/ppermute | solution.py:409
  56.4 2.9 %collective-permute-done.11.r1 = bf16[32,1024]{1,0:T(8,128)(2,1)S(1)} collective-permute-done((bf16[32,1024]{1,0:T(8,128)(2,1)S(1)}, bf16[32,1024]{1,0:T(8,128)(2,1)S(1)}, u32[]{:S(2)}, u32[]{:S(2)}) %collective-permute-start.11) | collective-permute-done | bytes 65568 | tf_op jit(solution)/shard_map/ppermute | solution.py:409
  60.4 2.3 %collective-permute-start.14 = (bf16[32,1024]{1,0:T(8,128)(2,1)S(1)}, bf16[32,1024]{1,0:T(8,128)(2,1)S(1)}, u32[]{:S(2)}, u32[]{:S(2)}) collective-permute-start(bf16[32,1024]{1,0:T(8,128)(2,1)S(1)} %get-tuple-element.134), channel_id=1, source_target_pairs={{0,16},{16,32},{32,48},{48,0},{1,17},{17,33},{33,49},{49,1},{2,18}... | collective-permute-start | bytes 196616 | tf_op jit(solution)/shard_map/ppermute | solution.py:409
  62.6 1.8 %collective-permute-start.15 = (bf16[32,1024]{1,0:T(8,128)(2,1)S(1)}, bf16[32,1024]{1,0:T(8,128)(2,1)S(1)}, u32[]{:S(2)}, u32[]{:S(2)}) collective-permute-start(bf16[32,1024]{1,0:T(8,128)(2,1)S(1)} %get-tuple-element.134), channel_id=1, source_target_pairs={{0,32},{16,48},{32,0},{48,16},{1,33},{17,49},{33,1},{49,17},{2,34}... | collective-permute-start | bytes 196616 | tf_op jit(solution)/shard_map/ppermute | solution.py:409
  64.9 2.9 %collective-permute-done.15.r2 = bf16[32,1024]{1,0:T(8,128)(2,1)S(1)} collective-permute-done((bf16[32,1024]{1,0:T(8,128)(2,1)S(1)}, bf16[32,1024]{1,0:T(8,128)(2,1)S(1)}, u32[]{:S(2)}, u32[]{:S(2)}) %collective-permute-start.15) | collective-permute-done | bytes 65568 | tf_op jit(solution)/shard_map/ppermute | solution.py:409
  68.9 1.4 collective-permute-start.17
  70.3 1.2 collective-permute-start.18
  71.5 2.1 %collective-permute-start.19 = (bf16[32,1024]{1,0:T(8,128)(2,1)S(1)}, bf16[32,1024]{1,0:T(8,128)(2,1)S(1)}, u32[]{:S(2)}, u32[]{:S(2)}) collective-permute-start(bf16[32,1024]{1,0:T(8,128)(2,1)S(1)} %get-tuple-element.136), channel_id=1, source_target_pairs={{0,64},{64,128},{128,192},{192,0},{1,65},{65,129},{129,193},{193,1... | collective-permute-start | bytes 196616 | tf_op jit(solution)/shard_map/ppermute | solution.py:409
  73.6 2.5 %collective-permute-start.20 = (bf16[32,1024]{1,0:T(8,128)(2,1)S(1)}, bf16[32,1024]{1,0:T(8,128)(2,1)S(1)}, u32[]{:S(2)}, u32[]{:S(2)}) collective-permute-start(bf16[32,1024]{1,0:T(8,128)(2,1)S(1)} %get-tuple-element.136), channel_id=1, source_target_pairs={{0,128},{64,192},{128,0},{192,64},{1,129},{65,193},{129,1},{193,65... | collective-permute-start | bytes 196616 | tf_op jit(solution)/shard_map/ppermute | solution.py:409
  77.0 2.4 %collective-permute-done.20.r2 = bf16[32,1024]{1,0:T(8,128)(2,1)S(1)} collective-permute-done((bf16[32,1024]{1,0:T(8,128)(2,1)S(1)}, bf16[32,1024]{1,0:T(8,128)(2,1)S(1)}, u32[]{:S(2)}, u32[]{:S(2)}) %collective-permute-start.20) | collective-permute-done | bytes 65568 | tf_op jit(solution)/shard_map/ppermute | solution.py:409
  81.1 1.3 collective-permute-done.18.refs_2_
  83.3 9.4 %finish.1 = (bf16[960,128]{1,0:T(8,128)(2,1)}, bf16[3,128,1024]{2,1,0:T(8,128)(2,1)S(1)}, bf16[8,360,128]{2,1,0:T(8,128)(2,1)}, bf16[40,1024]{1,0:T(8,128)(2,1)S(1)}) custom-call(s32[1]{0:T(128)} %bitcast.2.me.index.zi, s32[1]{0:T(128)} %bitcast.3.me.index.yi, f32[160,1024]{1,0:T(8,128)S(1)} %get-tuple-element.102.zq, ...), custom_call_target="tpu_custom_call" | custom-call | flops 200000000 | bytes 10000000 | tf_op jit(solution)/shard_map/finish/pallas_call | solution.py:552
  94.2 3.6 %all-to-all-start = ((bf16[8,360,128]{2,1,0:T(8,128)(2,1)}), bf16[8,360,128]{2,1,0:T(8,128)(2,1)S(1)}, u32[]{:S(2)}, u32[]{:S(2)}) async-start(bf16[8,360,128]{2,1,0:T(8,128)(2,1)} %get-tuple-element.145), calls=%async_computation | async-start | bytes 1474560 | tf_op jit(solution)/shard_map/all_to_all | solution.py:617
  99.3 1.3 collective-permute-done.27.refs_1_
  102.6 3.0 %collective-permute-start.29 = (bf16[40,1024]{1,0:T(8,128)(2,1)S(1)}, bf16[40,1024]{1,0:T(8,128)(2,1)S(1)}, u32[]{:S(2)}, u32[]{:S(2)}) collective-permute-start(bf16[40,1024]{1,0:T(8,128)(2,1)S(1)} %add_parts.4.refs_0_), channel_id=1, source_target_pairs={{0,32},{16,48},{32,0},{48,16},{1,33},{17,49},{33,1},{49,17},{2,34}... | collective-permute-start | bytes 245768 | tf_op jit(solution)/shard_map/ppermute | solution.py:409
  105.7 2.0 %collective-permute-start.30 = (bf16[40,1024]{1,0:T(8,128)(2,1)S(1)}, bf16[40,1024]{1,0:T(8,128)(2,1)S(1)}, u32[]{:S(2)}, u32[]{:S(2)}) collective-permute-start(bf16[40,1024]{1,0:T(8,128)(2,1)S(1)} %add_parts.4.refs_0_), channel_id=1, source_target_pairs={{0,48},{16,0},{32,16},{48,32},{1,49},{17,1},{33,17},{49,33},{2,50}... | collective-permute-start | bytes 245768 | tf_op jit(solution)/shard_map/ppermute | solution.py:409
  107.7 3.8 %collective-permute-done.29.refs_2_ = bf16[40,1024]{1,0:T(8,128)(2,1)S(1)} collective-permute-done((bf16[40,1024]{1,0:T(8,128)(2,1)S(1)}, bf16[40,1024]{1,0:T(8,128)(2,1)S(1)}, u32[]{:S(2)}, u32[]{:S(2)}) %collective-permute-start.29) | collective-permute-done | bytes 81952 | tf_op jit(solution)/shard_map/ppermute | solution.py:409
  111.5 2.5 %collective-permute-done.30.refs_3_ = bf16[40,1024]{1,0:T(8,128)(2,1)S(1)} collective-permute-done((bf16[40,1024]{1,0:T(8,128)(2,1)S(1)}, bf16[40,1024]{1,0:T(8,128)(2,1)S(1)}, u32[]{:S(2)}, u32[]{:S(2)}) %collective-permute-start.30) | collective-permute-done | bytes 81952 | tf_op jit(solution)/shard_map/ppermute | solution.py:409
  114.6 1.0 copy-done.6
  115.6 2.8 %weight_term.1 = bf16[4,360,384]{2,1,0:T(8,128)(2,1)} custom-call(s32[1]{0:T(128)} %bitcast.3.me.index.yi, s32[1]{0:T(128)} %bitcast.9.ci, bf16[8,360,128]{2,1,0:T(8,128)(2,1)S(1)} %all-to-all-done.arrived, bf16[128,1536]{1,0:T(8,128)(2,1)S(1)} %bitcast.16, bf16[128,1536]{1,0:T(8,128)(2,1)S(1)} %collective-permute-done.17.refs_1_, ...), custom_call_target="tpu_custom_call" | custom-call | flops 1200000000 | bytes 6000000 | tf_op jit(solution)/shard_map/weight_term/pallas_call | solution.py:623
  118.4 5.1 %all-to-all-start.1 = ((bf16[4,360,384]{2,1,0:T(8,128)(2,1)}), bf16[4,360,384]{2,1,0:T(8,128)(2,1)S(1)}, u32[]{:S(2)}, u32[]{:S(2)}) async-start(bf16[4,360,384]{2,1,0:T(8,128)(2,1)} %weight_term.1), calls=%async_computation.1 | async-start | bytes 2211840 | tf_op jit(solution)/shard_map/all_to_all | solution.py:632
  123.5 1.7 %collective-permute-start.31 = (bf16[40,1024]{1,0:T(8,128)(2,1)}, bf16[40,1024]{1,0:T(8,128)(2,1)S(1)}, u32[]{:S(2)}, u32[]{:S(2)}) collective-permute-start(bf16[40,1024]{1,0:T(8,128)(2,1)} %copy-done.7), channel_id=1, source_target_pairs={{0,4},{4,8},{8,12},{12,0},{1,5},{5,9},{9,13},{13,1},{2,6},{6,10},{... | collective-permute-start | bytes 245768 | tf_op jit(solution)/shard_map/ppermute | solution.py:409
  125.2 2.7 %collective-permute-start.32 = (bf16[40,1024]{1,0:T(8,128)(2,1)}, bf16[40,1024]{1,0:T(8,128)(2,1)S(1)}, u32[]{:S(2)}, u32[]{:S(2)}) collective-permute-start(bf16[40,1024]{1,0:T(8,128)(2,1)} %copy-done.7), channel_id=1, source_target_pairs={{0,8},{4,12},{8,0},{12,4},{1,9},{5,13},{9,1},{13,5},{2,10},{6,14},... | collective-permute-start | bytes 245768 | tf_op jit(solution)/shard_map/ppermute | solution.py:409
  127.9 1.4 collective-permute-start.33
  129.4 2.5 %collective-permute-done.32.refs_2_ = bf16[40,1024]{1,0:T(8,128)(2,1)S(1)} collective-permute-done((bf16[40,1024]{1,0:T(8,128)(2,1)}, bf16[40,1024]{1,0:T(8,128)(2,1)S(1)}, u32[]{:S(2)}, u32[]{:S(2)}) %collective-permute-start.32) | collective-permute-done | bytes 81952 | tf_op jit(solution)/shard_map/ppermute | solution.py:409
  133.5 4.6 %collective-permute-start.34 = (bf16[40,1024]{1,0:T(8,128)(2,1)S(1)}, bf16[40,1024]{1,0:T(8,128)(2,1)S(1)}, u32[]{:S(2)}, u32[]{:S(2)}) collective-permute-start(bf16[40,1024]{1,0:T(8,128)(2,1)S(1)} %add_parts.6.refs_0_), channel_id=1, source_target_pairs={{0,2},{2,0},{1,3},{3,1},{4,6},{6,4},{5,7},{7,5},{8,10},{10,8},{9,1... | collective-permute-start | bytes 245768 | tf_op jit(solution)/shard_map/ppermute | solution.py:605
  138.1 4.7 %collective-permute-done.34.refs_1_ = bf16[40,1024]{1,0:T(8,128)(2,1)S(1)} collective-permute-done((bf16[40,1024]{1,0:T(8,128)(2,1)S(1)}, bf16[40,1024]{1,0:T(8,128)(2,1)S(1)}, u32[]{:S(2)}, u32[]{:S(2)}) %collective-permute-start.34) | collective-permute-done | bytes 81952 | tf_op jit(solution)/shard_map/ppermute | solution.py:605
  142.8 1.1 split_rows.1
  143.9 8.6 %all-to-all-start.2 = ((bf16[32,24,180]{2,1,0:T(8,128)(2,1)}), bf16[32,24,180]{2,1,0:T(8,128)(2,1)S(1)}, u32[]{:S(2)}, u32[]{:S(2)}) async-start(bf16[32,24,180]{2,1,0:T(8,128)(2,1)} %split_rows.1), calls=%async_computation.2 | async-start | bytes 786432 | tf_op jit(solution)/shard_map/all_to_all | solution.py:645
  152.5 2.1 %collective-permute-start.35 = (bf16[40,1024]{1,0:T(8,128)(2,1)S(1)}, bf16[40,1024]{1,0:T(8,128)(2,1)S(1)}, u32[]{:S(2)}, u32[]{:S(2)}) collective-permute-start(bf16[40,1024]{1,0:T(8,128)(2,1)S(1)} %add_parts.7.refs_0_), channel_id=1, source_target_pairs={{0,64},{64,128},{128,192},{192,0},{1,65},{65,129},{129,193},{193,1... | collective-permute-start | bytes 245768 | tf_op jit(solution)/shard_map/ppermute | solution.py:409
  154.6 2.7 %collective-permute-start.36 = (bf16[40,1024]{1,0:T(8,128)(2,1)S(1)}, bf16[40,1024]{1,0:T(8,128)(2,1)S(1)}, u32[]{:S(2)}, u32[]{:S(2)}) collective-permute-start(bf16[40,1024]{1,0:T(8,128)(2,1)S(1)} %add_parts.7.refs_0_), channel_id=1, source_target_pairs={{0,128},{64,192},{128,0},{192,64},{1,129},{65,193},{129,1},{193,65... | collective-permute-start | bytes 245768 | tf_op jit(solution)/shard_map/ppermute | solution.py:409
  157.2 1.5 collective-permute-start.37
  158.7 6.6 %token_grads.1 = bf16[128,1536]{1,0:T(8,128)(2,1)} custom-call(bf16[3,128,1024]{2,1,0:T(8,128)(2,1)} %copy-done.3, bf16[2880,1536]{1,0:T(8,128)(2,1)} %bitcast.20), custom_call_target="tpu_custom_call" | custom-call | flops 1200000000 | bytes 11000000 | tf_op jit(solution)/shard_map/token_grads/pallas_call | solution.py:649
  (80 shorter events, 16.5 us)
Async XLA Ops:
  5.0 12.8 %collective-permute-start.4 = (bf16[16,2560]{1,0:T(8,128)(2,1)}, bf16[16,2560]{1,0:T(8,128)(2,1)S(1)}, u32[]{:S(2)}, u32[]{:S(2)}) collective-permute-start(bf16[16,2560]{1,0:T(8,128)(2,1)} %get-tuple-element.96), channel_id=1, source_target_pairs={{4,0},{8,4},{12,8},{16,12},{20,16},{24,20},{28,24},{32,28},{36,32}... | collective-permute-start | bytes 245768 | tf_op jit(solution)/shard_map/ppermute | solution.py:464
  9.4 8.3 %collective-permute-start.3 = (bf16[16,1536]{1,0:T(8,128)(2,1)}, bf16[16,1536]{1,0:T(8,128)(2,1)S(1)}, u32[]{:S(2)}, u32[]{:S(2)}) collective-permute-start(bf16[16,1536]{1,0:T(8,128)(2,1)} %get-tuple-element.95), channel_id=1, source_target_pairs={{0,4},{4,8},{8,12},{12,16},{16,20},{20,24},{24,28},{28,32},{32,36}... | collective-permute-start | bytes 147464 | tf_op jit(solution)/shard_map/ppermute | solution.py:463
  11.4 14.6 %collective-permute-start = (f32[32,15]{1,0:T(8,128)}, f32[32,15]{1,0:T(8,128)S(1)}, u32[]{:S(2)}, u32[]{:S(2)}) collective-permute-start(f32[32,15]{1,0:T(8,128)} %get-tuple-element.103.r0), channel_id=1, source_target_pairs={{0,4},{4,8},{8,12},{12,0},{1,5},{5,9},{9,13},{13,1},{2,6},{6,10},{... | collective-permute-start | bytes 5768 | tf_op jit(solution)/shard_map/ppermute | solution.py:409
  12.5 13.5 %collective-permute-start.1 = (f32[32,15]{1,0:T(8,128)}, f32[32,15]{1,0:T(8,128)S(1)}, u32[]{:S(2)}, u32[]{:S(2)}) collective-permute-start(f32[32,15]{1,0:T(8,128)} %get-tuple-element.103.r0), channel_id=1, source_target_pairs={{0,8},{4,12},{8,0},{12,4},{1,9},{5,13},{9,1},{13,5},{2,10},{6,14},... | collective-permute-start | bytes 5768 | tf_op jit(solution)/shard_map/ppermute | solution.py:409
  17.5 8.5 %collective-permute-start.2 = (f32[32,15]{1,0:T(8,128)}, f32[32,15]{1,0:T(8,128)S(1)}, u32[]{:S(2)}, u32[]{:S(2)}) collective-permute-start(f32[32,15]{1,0:T(8,128)} %get-tuple-element.103.r0), channel_id=1, source_target_pairs={{0,12},{4,0},{8,4},{12,8},{1,13},{5,1},{9,5},{13,9},{2,14},{6,2},{... | collective-permute-start | bytes 5768 | tf_op jit(solution)/shard_map/ppermute | solution.py:409
  17.8 1.0 copy-start
  18.8 0.9 copy-start.1
  19.7 6.3 %copy-start.11 = (f32[32,15]{1,0:T(8,128)S(1)}, f32[32,15]{1,0:T(8,128)}, u32[]{:S(2)}) copy-start(f32[32,15]{1,0:T(8,128)} %get-tuple-element.103.r0) | copy-start | bytes 5764
  26.1 14.0 %collective-permute-start.5 = (f32[32,60]{1,0:T(8,128)S(1)}, f32[32,60]{1,0:T(8,128)S(1)}, u32[]{:S(2)}, u32[]{:S(2)}) collective-permute-start(f32[32,60]{1,0:T(8,128)S(1)} %join_params.2.r0), channel_id=1, source_target_pairs={{0,16},{16,32},{32,48},{48,0},{1,17},{17,33},{33,49},{49,1},{2,18}... | collective-permute-start | bytes 23048 | tf_op jit(solution)/shard_map/ppermute | solution.py:409
  28.1 12.0 %collective-permute-start.6 = (f32[32,60]{1,0:T(8,128)S(1)}, f32[32,60]{1,0:T(8,128)S(1)}, u32[]{:S(2)}, u32[]{:S(2)}) collective-permute-start(f32[32,60]{1,0:T(8,128)S(1)} %join_params.2.r0), channel_id=1, source_target_pairs={{0,32},{16,48},{32,0},{48,16},{1,33},{17,49},{33,1},{49,17},{2,34}... | collective-permute-start | bytes 23048 | tf_op jit(solution)/shard_map/ppermute | solution.py:409
  32.0 8.2 %collective-permute-start.7 = (f32[32,60]{1,0:T(8,128)S(1)}, f32[32,60]{1,0:T(8,128)S(1)}, u32[]{:S(2)}, u32[]{:S(2)}) collective-permute-start(f32[32,60]{1,0:T(8,128)S(1)} %join_params.2.r0), channel_id=1, source_target_pairs={{0,48},{16,0},{32,16},{48,32},{1,49},{17,1},{33,17},{49,33},{2,50}... | collective-permute-start | bytes 23048 | tf_op jit(solution)/shard_map/ppermute | solution.py:409
  40.1 10.7 %copy-start.4 = (f32[128,1024]{1,0:T(8,128)S(1)}, f32[128,1024]{1,0:T(8,128)}, u32[]{:S(2)}) copy-start(f32[128,1024]{1,0:T(8,128)} %get-tuple-element.127.cown) | copy-start | bytes 1572868
  40.3 10.5 %collective-permute-start.10 = (f32[32,240]{1,0:T(8,128)S(1)}, f32[32,240]{1,0:T(8,128)S(1)}, u32[]{:S(2)}, u32[]{:S(2)}) collective-permute-start(f32[32,240]{1,0:T(8,128)S(1)} %join_params.3.r0), channel_id=1, source_target_pairs={{0,192},{64,0},{128,64},{192,128},{1,193},{65,1},{129,65},{193,129... | collective-permute-start | bytes 92168 | tf_op jit(solution)/shard_map/ppermute | solution.py:409
  45.3 5.5 %collective-permute-start.8 = (f32[32,240]{1,0:T(8,128)S(1)}, f32[32,240]{1,0:T(8,128)S(1)}, u32[]{:S(2)}, u32[]{:S(2)}) collective-permute-start(f32[32,240]{1,0:T(8,128)S(1)} %join_params.3.r0), channel_id=1, source_target_pairs={{0,64},{64,128},{128,192},{192,0},{1,65},{65,129},{129,193},{193,1... | collective-permute-start | bytes 92168 | tf_op jit(solution)/shard_map/ppermute | solution.py:409
  45.3 5.5 %collective-permute-start.9 = (f32[32,240]{1,0:T(8,128)S(1)}, f32[32,240]{1,0:T(8,128)S(1)}, u32[]{:S(2)}, u32[]{:S(2)}) collective-permute-start(f32[32,240]{1,0:T(8,128)S(1)} %join_params.3.r0), channel_id=1, source_target_pairs={{0,128},{64,192},{128,0},{192,64},{1,129},{65,193},{129,1},{193,65... | collective-permute-start | bytes 92168 | tf_op jit(solution)/shard_map/ppermute | solution.py:409
  47.3 21.6 %copy-start.2 = (bf16[1,128,1536]{2,1,0:T(8,128)(2,1)S(1)}, bf16[1,128,1536]{2,1,0:T(8,128)(2,1)}, u32[]{:S(2)}) copy-start(bf16[1,128,1536]{2,1,0:T(8,128)(2,1)} %param.6) | copy-start | bytes 1179652
  53.0 6.3 %collective-permute-start.11 = (bf16[32,1024]{1,0:T(8,128)(2,1)S(1)}, bf16[32,1024]{1,0:T(8,128)(2,1)S(1)}, u32[]{:S(2)}, u32[]{:S(2)}) collective-permute-start(bf16[32,1024]{1,0:T(8,128)(2,1)S(1)} %get-tuple-element.130), channel_id=1, source_target_pairs={{0,4},{4,8},{8,12},{12,0},{1,5},{5,9},{9,13},{13,1},{2,6},{6,10},{... | collective-permute-start | bytes 196616 | tf_op jit(solution)/shard_map/ppermute | solution.py:409
  53.2 6.1 %collective-permute-start.12 = (bf16[32,1024]{1,0:T(8,128)(2,1)S(1)}, bf16[32,1024]{1,0:T(8,128)(2,1)S(1)}, u32[]{:S(2)}, u32[]{:S(2)}) collective-permute-start(bf16[32,1024]{1,0:T(8,128)(2,1)S(1)} %get-tuple-element.130), channel_id=1, source_target_pairs={{0,8},{4,12},{8,0},{12,4},{1,9},{5,13},{9,1},{13,5},{2,10},{6,14},... | collective-permute-start | bytes 196616 | tf_op jit(solution)/shard_map/ppermute | solution.py:409
  53.2 6.9 %collective-permute-start.13 = (bf16[32,1024]{1,0:T(8,128)(2,1)S(1)}, bf16[32,1024]{1,0:T(8,128)(2,1)S(1)}, u32[]{:S(2)}, u32[]{:S(2)}) collective-permute-start(bf16[32,1024]{1,0:T(8,128)(2,1)S(1)} %get-tuple-element.130), channel_id=1, source_target_pairs={{0,12},{4,0},{8,4},{12,8},{1,13},{5,1},{9,5},{13,9},{2,14},{6,2},{... | collective-permute-start | bytes 196616 | tf_op jit(solution)/shard_map/ppermute | solution.py:409
  60.4 4.5 %collective-permute-start.14 = (bf16[32,1024]{1,0:T(8,128)(2,1)S(1)}, bf16[32,1024]{1,0:T(8,128)(2,1)S(1)}, u32[]{:S(2)}, u32[]{:S(2)}) collective-permute-start(bf16[32,1024]{1,0:T(8,128)(2,1)S(1)} %get-tuple-element.134), channel_id=1, source_target_pairs={{0,16},{16,32},{32,48},{48,0},{1,17},{17,33},{33,49},{49,1},{2,18}... | collective-permute-start | bytes 196616 | tf_op jit(solution)/shard_map/ppermute | solution.py:409
  62.6 5.2 %collective-permute-start.15 = (bf16[32,1024]{1,0:T(8,128)(2,1)S(1)}, bf16[32,1024]{1,0:T(8,128)(2,1)S(1)}, u32[]{:S(2)}, u32[]{:S(2)}) collective-permute-start(bf16[32,1024]{1,0:T(8,128)(2,1)S(1)} %get-tuple-element.134), channel_id=1, source_target_pairs={{0,32},{16,48},{32,0},{48,16},{1,33},{17,49},{33,1},{49,17},{2,34}... | collective-permute-start | bytes 196616 | tf_op jit(solution)/shard_map/ppermute | solution.py:409
  64.4 4.3 %collective-permute-start.16 = (bf16[32,1024]{1,0:T(8,128)(2,1)S(1)}, bf16[32,1024]{1,0:T(8,128)(2,1)S(1)}, u32[]{:S(2)}, u32[]{:S(2)}) collective-permute-start(bf16[32,1024]{1,0:T(8,128)(2,1)S(1)} %get-tuple-element.134), channel_id=1, source_target_pairs={{0,48},{16,0},{32,16},{48,32},{1,49},{17,1},{33,17},{49,33},{2,50}... | collective-permute-start | bytes 196616 | tf_op jit(solution)/shard_map/ppermute | solution.py:409
  68.9 12.2 %collective-permute-start.17 = (bf16[128,1536]{1,0:T(8,128)(2,1)S(1)}, bf16[128,1536]{1,0:T(8,128)(2,1)S(1)}, u32[]{:S(2)}, u32[]{:S(2)}) collective-permute-start(bf16[128,1536]{1,0:T(8,128)(2,1)S(1)} %bitcast.13), channel_id=1, source_target_pairs={{0,4},{4,0},{8,12},{12,8},{1,5},{5,1},{9,13},{13,9},{2,6},{6,2},{1... | collective-permute-start | bytes 1179656 | tf_op jit(solution)/shard_map/ppermute | solution.py:540
  70.3 12.1 %collective-permute-start.18 = (bf16[128,1536]{1,0:T(8,128)(2,1)S(1)}, bf16[128,1536]{1,0:T(8,128)(2,1)S(1)}, u32[]{:S(2)}, u32[]{:S(2)}) collective-permute-start(bf16[128,1536]{1,0:T(8,128)(2,1)S(1)} %bitcast.14), channel_id=1, source_target_pairs={{0,12},{4,8},{8,4},{12,0},{1,13},{5,9},{9,5},{13,1},{2,14},{6,10},... | collective-permute-start | bytes 1179656 | tf_op jit(solution)/shard_map/ppermute | solution.py:541
  71.5 5.5 %collective-permute-start.19 = (bf16[32,1024]{1,0:T(8,128)(2,1)S(1)}, bf16[32,1024]{1,0:T(8,128)(2,1)S(1)}, u32[]{:S(2)}, u32[]{:S(2)}) collective-permute-start(bf16[32,1024]{1,0:T(8,128)(2,1)S(1)} %get-tuple-element.136), channel_id=1, source_target_pairs={{0,64},{64,128},{128,192},{192,0},{1,65},{65,129},{129,193},{193,1... | collective-permute-start | bytes 196616 | tf_op jit(solution)/shard_map/ppermute | solution.py:409
  73.6 5.8 %collective-permute-start.20 = (bf16[32,1024]{1,0:T(8,128)(2,1)S(1)}, bf16[32,1024]{1,0:T(8,128)(2,1)S(1)}, u32[]{:S(2)}, u32[]{:S(2)}) collective-permute-start(bf16[32,1024]{1,0:T(8,128)(2,1)S(1)} %get-tuple-element.136), channel_id=1, source_target_pairs={{0,128},{64,192},{128,0},{192,64},{1,129},{65,193},{129,1},{193,65... | collective-permute-start | bytes 196616 | tf_op jit(solution)/shard_map/ppermute | solution.py:409
  76.1 4.3 %collective-permute-start.21 = (bf16[32,1024]{1,0:T(8,128)(2,1)S(1)}, bf16[32,1024]{1,0:T(8,128)(2,1)S(1)}, u32[]{:S(2)}, u32[]{:S(2)}) collective-permute-start(bf16[32,1024]{1,0:T(8,128)(2,1)S(1)} %get-tuple-element.136), channel_id=1, source_target_pairs={{0,192},{64,0},{128,64},{192,128},{1,193},{65,1},{129,65},{193,129... | collective-permute-start | bytes 196616 | tf_op jit(solution)/shard_map/ppermute | solution.py:409
  82.4 16.4 %collective-permute-start.25 = (bf16[128,1536]{1,0:T(8,128)(2,1)S(1)}, bf16[128,1536]{1,0:T(8,128)(2,1)S(1)}, u32[]{:S(2)}, u32[]{:S(2)}) collective-permute-start(bf16[128,1536]{1,0:T(8,128)(2,1)S(1)} %collective-permute-done.17.refs_1_), channel_id=1, source_target_pairs={{0,12},{4,8},{8,4},{12,0},{1,13},{5,9},{9,5},{13,1},{2,14},{6,10},... | collective-permute-start | bytes 1179656 | tf_op jit(solution)/shard_map/ppermute | solution.py:543
  94.2 20.4 %all-to-all-start = ((bf16[8,360,128]{2,1,0:T(8,128)(2,1)}), bf16[8,360,128]{2,1,0:T(8,128)(2,1)S(1)}, u32[]{:S(2)}, u32[]{:S(2)}) async-start(bf16[8,360,128]{2,1,0:T(8,128)(2,1)} %get-tuple-element.145), calls=%async_computation | async-start | bytes 1474560 | tf_op jit(solution)/shard_map/all_to_all | solution.py:617
  97.8 3.8 %collective-permute-start.22 = (bf16[128,1536]{1,0:T(8,128)(2,1)S(1)}, bf16[128,1536]{1,0:T(8,128)(2,1)S(1)}, u32[]{:S(2)}, u32[]{:S(2)}) collective-permute-start(bf16[128,1536]{1,0:T(8,128)(2,1)S(1)} %bitcast.15), channel_id=1, source_target_pairs={{0,1},{1,0},{2,3},{3,2},{4,5},{5,4},{6,7},{7,6},{8,9},{9,8},{10,11... | collective-permute-start | bytes 1179656 | tf_op jit(solution)/shard_map/ppermute | solution.py:546
  98.3 3.3 %collective-permute-start.23 = (bf16[128,1536]{1,0:T(8,128)(2,1)S(1)}, bf16[128,1536]{1,0:T(8,128)(2,1)S(1)}, u32[]{:S(2)}, u32[]{:S(2)}) collective-permute-start(bf16[128,1536]{1,0:T(8,128)(2,1)S(1)} %collective-permute-done.17.refs_1_), channel_id=1, source_target_pairs={{0,1},{1,0},{2,3},{3,2},{4,5},{5,4},{6,7},{7,6},{8,9},{9,8},{10,11... | collective-permute-start | bytes 1179656 | tf_op jit(solution)/shard_map/ppermute | solution.py:546
  98.4 3.2 %collective-permute-start.24 = (bf16[128,1536]{1,0:T(8,128)(2,1)S(1)}, bf16[128,1536]{1,0:T(8,128)(2,1)S(1)}, u32[]{:S(2)}, u32[]{:S(2)}) collective-permute-start(bf16[128,1536]{1,0:T(8,128)(2,1)S(1)} %collective-permute-done.18.refs_2_), channel_id=1, source_target_pairs={{0,1},{1,0},{2,3},{3,2},{4,5},{5,4},{6,7},{7,6},{8,9},{9,8},{10,11... | collective-permute-start | bytes 1179656 | tf_op jit(solution)/shard_map/ppermute | solution.py:546
  98.8 2.8 %collective-permute-start.26 = (bf16[128,1536]{1,0:T(8,128)(2,1)S(1)}, bf16[128,1536]{1,0:T(8,128)(2,1)S(1)}, u32[]{:S(2)}, u32[]{:S(2)}) collective-permute-start(bf16[128,1536]{1,0:T(8,128)(2,1)S(1)} %collective-permute-done.25.refs_3_), channel_id=1, source_target_pairs={{0,1},{1,0},{2,3},{3,2},{4,5},{5,4},{6,7},{7,6},{8,9},{9,8},{10,11... | collective-permute-start | bytes 1179656 | tf_op jit(solution)/shard_map/ppermute | solution.py:546
  98.9 1.8 %collective-permute-start.27 = (bf16[40,1024]{1,0:T(8,128)(2,1)}, bf16[40,1024]{1,0:T(8,128)(2,1)S(1)}, u32[]{:S(2)}, u32[]{:S(2)}) collective-permute-start(bf16[40,1024]{1,0:T(8,128)(2,1)} %copy-done.9), channel_id=1, source_target_pairs={{0,1},{1,0},{2,3},{3,2},{4,5},{5,4},{6,7},{7,6},{8,9},{9,8},{10,11... | collective-permute-start | bytes 245768 | tf_op jit(solution)/shard_map/ppermute | solution.py:605
  102.4 5.3 %collective-permute-start.28 = (bf16[40,1024]{1,0:T(8,128)(2,1)S(1)}, bf16[40,1024]{1,0:T(8,128)(2,1)S(1)}, u32[]{:S(2)}, u32[]{:S(2)}) collective-permute-start(bf16[40,1024]{1,0:T(8,128)(2,1)S(1)} %add_parts.4.refs_0_), channel_id=1, source_target_pairs={{0,16},{16,32},{32,48},{48,0},{1,17},{17,33},{33,49},{49,1},{2,18}... | collective-permute-start | bytes 245768 | tf_op jit(solution)/shard_map/ppermute | solution.py:409
  102.6 8.9 %collective-permute-start.29 = (bf16[40,1024]{1,0:T(8,128)(2,1)S(1)}, bf16[40,1024]{1,0:T(8,128)(2,1)S(1)}, u32[]{:S(2)}, u32[]{:S(2)}) collective-permute-start(bf16[40,1024]{1,0:T(8,128)(2,1)S(1)} %add_parts.4.refs_0_), channel_id=1, source_target_pairs={{0,32},{16,48},{32,0},{48,16},{1,33},{17,49},{33,1},{49,17},{2,34}... | collective-permute-start | bytes 245768 | tf_op jit(solution)/shard_map/ppermute | solution.py:409
  105.7 8.3 %collective-permute-start.30 = (bf16[40,1024]{1,0:T(8,128)(2,1)S(1)}, bf16[40,1024]{1,0:T(8,128)(2,1)S(1)}, u32[]{:S(2)}, u32[]{:S(2)}) collective-permute-start(bf16[40,1024]{1,0:T(8,128)(2,1)S(1)} %add_parts.4.refs_0_), channel_id=1, source_target_pairs={{0,48},{16,0},{32,16},{48,32},{1,49},{17,1},{33,17},{49,33},{2,50}... | collective-permute-start | bytes 245768 | tf_op jit(solution)/shard_map/ppermute | solution.py:409
  114.6 1.0 copy-start.6
  118.4 24.4 %all-to-all-start.1 = ((bf16[4,360,384]{2,1,0:T(8,128)(2,1)}), bf16[4,360,384]{2,1,0:T(8,128)(2,1)S(1)}, u32[]{:S(2)}, u32[]{:S(2)}) async-start(bf16[4,360,384]{2,1,0:T(8,128)(2,1)} %weight_term.1), calls=%async_computation.1 | async-start | bytes 2211840 | tf_op jit(solution)/shard_map/all_to_all | solution.py:632
  123.5 5.9 %collective-permute-start.31 = (bf16[40,1024]{1,0:T(8,128)(2,1)}, bf16[40,1024]{1,0:T(8,128)(2,1)S(1)}, u32[]{:S(2)}, u32[]{:S(2)}) collective-permute-start(bf16[40,1024]{1,0:T(8,128)(2,1)} %copy-done.7), channel_id=1, source_target_pairs={{0,4},{4,8},{8,12},{12,0},{1,5},{5,9},{9,13},{13,1},{2,6},{6,10},{... | collective-permute-start | bytes 245768 | tf_op jit(solution)/shard_map/ppermute | solution.py:409
  125.2 6.7 %collective-permute-start.32 = (bf16[40,1024]{1,0:T(8,128)(2,1)}, bf16[40,1024]{1,0:T(8,128)(2,1)S(1)}, u32[]{:S(2)}, u32[]{:S(2)}) collective-permute-start(bf16[40,1024]{1,0:T(8,128)(2,1)} %copy-done.7), channel_id=1, source_target_pairs={{0,8},{4,12},{8,0},{12,4},{1,9},{5,13},{9,1},{13,5},{2,10},{6,14},... | collective-permute-start | bytes 245768 | tf_op jit(solution)/shard_map/ppermute | solution.py:409
  127.9 4.7 %collective-permute-start.33 = (bf16[40,1024]{1,0:T(8,128)(2,1)}, bf16[40,1024]{1,0:T(8,128)(2,1)S(1)}, u32[]{:S(2)}, u32[]{:S(2)}) collective-permute-start(bf16[40,1024]{1,0:T(8,128)(2,1)} %copy-done.7), channel_id=1, source_target_pairs={{0,12},{4,0},{8,4},{12,8},{1,13},{5,1},{9,5},{13,9},{2,14},{6,2},{... | collective-permute-start | bytes 245768 | tf_op jit(solution)/shard_map/ppermute | solution.py:409
  133.5 9.3 %collective-permute-start.34 = (bf16[40,1024]{1,0:T(8,128)(2,1)S(1)}, bf16[40,1024]{1,0:T(8,128)(2,1)S(1)}, u32[]{:S(2)}, u32[]{:S(2)}) collective-permute-start(bf16[40,1024]{1,0:T(8,128)(2,1)S(1)} %add_parts.6.refs_0_), channel_id=1, source_target_pairs={{0,2},{2,0},{1,3},{3,1},{4,6},{6,4},{5,7},{7,5},{8,10},{10,8},{9,1... | collective-permute-start | bytes 245768 | tf_op jit(solution)/shard_map/ppermute | solution.py:605
  143.9 22.3 %all-to-all-start.2 = ((bf16[32,24,180]{2,1,0:T(8,128)(2,1)}), bf16[32,24,180]{2,1,0:T(8,128)(2,1)S(1)}, u32[]{:S(2)}, u32[]{:S(2)}) async-start(bf16[32,24,180]{2,1,0:T(8,128)(2,1)} %split_rows.1), calls=%async_computation.2 | async-start | bytes 786432 | tf_op jit(solution)/shard_map/all_to_all | solution.py:645
  152.5 12.9 %collective-permute-start.35 = (bf16[40,1024]{1,0:T(8,128)(2,1)S(1)}, bf16[40,1024]{1,0:T(8,128)(2,1)S(1)}, u32[]{:S(2)}, u32[]{:S(2)}) collective-permute-start(bf16[40,1024]{1,0:T(8,128)(2,1)S(1)} %add_parts.7.refs_0_), channel_id=1, source_target_pairs={{0,64},{64,128},{128,192},{192,0},{1,65},{65,129},{129,193},{193,1... | collective-permute-start | bytes 245768 | tf_op jit(solution)/shard_map/ppermute | solution.py:409
  154.6 10.8 %collective-permute-start.36 = (bf16[40,1024]{1,0:T(8,128)(2,1)S(1)}, bf16[40,1024]{1,0:T(8,128)(2,1)S(1)}, u32[]{:S(2)}, u32[]{:S(2)}) collective-permute-start(bf16[40,1024]{1,0:T(8,128)(2,1)S(1)} %add_parts.7.refs_0_), channel_id=1, source_target_pairs={{0,128},{64,192},{128,0},{192,64},{1,129},{65,193},{129,1},{193,65... | collective-permute-start | bytes 245768 | tf_op jit(solution)/shard_map/ppermute | solution.py:409
  157.2 8.1 %collective-permute-start.37 = (bf16[40,1024]{1,0:T(8,128)(2,1)S(1)}, bf16[40,1024]{1,0:T(8,128)(2,1)S(1)}, u32[]{:S(2)}, u32[]{:S(2)}) collective-permute-start(bf16[40,1024]{1,0:T(8,128)(2,1)S(1)} %add_parts.7.refs_0_), channel_id=1, source_target_pairs={{0,192},{64,0},{128,64},{192,128},{1,193},{65,1},{129,65},{193,129... | collective-permute-start | bytes 245768 | tf_op jit(solution)/shard_map/ppermute | solution.py:409
  158.7 6.7 %copy-start.12 = (f32[15,16]{1,0:T(8,128)S(1)}, f32[15,16]{1,0:T(8,128)}, u32[]{:S(2)}) copy-start(f32[15,16]{1,0:T(8,128)} %get-tuple-element.166.amp) | copy-start | bytes 2884
  (6 other events, 4.7 us)

commit v9 on v7

--- a/solution.py
+++ b/solution.py
@@ -21,35 +21,59 @@
     return a.astype(BF16).astype(F32)
 
 
-def make_project(g):
+KBLK = 256
+
+
+def make_project(part):
     def project(*refs):
-        if g < 2:
-            *ins, wt, zf, mix, wnext, sem = refs
-            coming = pltpu.make_async_copy(wt.at[pl.ds((g + 1) * wnext.shape[0], wnext.shape[0])], wnext, sem)
-            coming.start()
+        if part == 0:
+            tp, nexts, feats, wt, acc, tk, wbuf, tsem, sems = refs
         else:
-            *ins, zf, mix = refs
-        tp, nexts, taps, tk, w = ins
-        width, depth = w.shape
-        zf[:, width:] = jnp.zeros((zf.shape[0], PADC - width), F32)
-        rows = jnp.concatenate([tp[...], tk[...], nexts[:, 0:depth]], axis=0)
-        for low, size in ((0, 512), (512, width - 512)):
-            part = lax.dot_general(rows, w[low : low + size, :], NT, preferred_element_type=F32)
-            zf[:, low : low + size] = rounded(part)
-
-        def tile(ct, carry):
-            lanes = pl.ds(pl.multiple_of(ct * 128, 128), 128)
-            total = taps[g, 0:1, lanes] * zf[pl.ds(HALO, EXT), lanes]
+            tp, nexts, before, feats, wt, zq, zk, zv, tk, wbuf, tsem, sems, acc = refs
+        steps, chans, _ = wbuf.shape
+        low = part * steps * KBLK
+        arrival = pltpu.make_async_copy(feats.at[:, pl.ds(low, steps * KBLK)], tk, tsem)
+        arrival.start()
+        copies = [
+            pltpu.make_async_copy(wt.at[:, pl.ds(low + k * KBLK, KBLK)], wbuf.at[k], sems.at[k])
+            for k in range(steps)
+        ]
+        for copy in copies:
+            copy.start()
+        arrival.wait()
+        for k in range(steps):
+            wide = slice(low + k * KBLK, low + (k + 1) * KBLK)
+            rows = jnp.concatenate(
+                [tp[:, wide], tk[:, k * KBLK : (k + 1) * KBLK], nexts[:, wide]], axis=0
+            )
+            copies[k].wait()
+            total = lax.dot_general(rows, wbuf[k], NT, preferred_element_type=F32)
+            if k > 0:
+                total = acc[...] + total
+            elif part == 1:
+                total = before[...] + total
+            if part == 0 or k < steps - 1:
+                acc[...] = total
+            else:
+                width = chans // 3
+                for g, z in enumerate((zq, zk, zv)):
+                    z[:, 0:width] = rounded(total[:, g * width : (g + 1) * width])
+                    z[:, width:] = jnp.zeros((z.shape[0], PADC - width), F32)
+
+    return project
+
+
+def mix_taps(taps, zq, zk, zv, mq, mk, mv):
+    def tile(ct, carry):
+        lanes = pl.ds(pl.multiple_of(ct * 128, 128), 128)
+        for g, (z, m) in enumerate(((zq, mq), (zk, mk), (zv, mv))):
+            total = taps[g, 0:1, lanes] * z[pl.ds(HALO, EXT), lanes]
             for j in range(1, 7):
-                total = total + taps[g, j : j + 1, lanes] * zf[pl.ds(HALO - j, EXT), lanes]
-            mix[:, lanes] = total
-            return carry
-
-        lax.fori_loop(0, PADC // 128, tile, 0)
-        if g < 2:
-            coming.wait()
-
-    return project
+                total = total + taps[g, j : j + 1, lanes] * z[pl.ds(HALO - j, EXT), lanes]
+            m[:, lanes] = total
+        return carry
+
+    lax.fori_loop(0, PADC // 128, tile, 0)
 
 
 def one_minus_exp(x):
@@ -60,7 +84,7 @@
 
 
 def prepare(
-    feats, cott, rates, residues, conv, wt, head, tail, block, taps, amp, tokens, cots, wfirst,
+    feats, cott, rates, residues, conv, head, tail, block, taps, amp, cots,
     held, turn, cbuf, rbuf, sbuf, vbuf, sems,
 ):
     count = rates.shape[0]
@@ -73,8 +97,6 @@
         pltpu.make_async_copy(conv, vbuf, sems.at[3]),
         pltpu.make_async_copy(feats.at[pl.ds(0, HALO)], head.at[:, pl.ds(0, depth)], sems.at[4]),
         pltpu.make_async_copy(feats.at[pl.ds(own - HALO, HALO)], tail, sems.at[5]),
-        pltpu.make_async_copy(feats, tokens, sems.at[6]),
-        pltpu.make_async_copy(wt.at[pl.ds(0, width)], wfirst, sems.at[7]),
     ]
     for copy in copies:
         copy.start()
@@ -410,25 +432,24 @@
     scale = 1.0 / math.sqrt(4 * count * own)
     smem = pl.BlockSpec(memory_space=pltpu.SMEM)
     vm = pl.BlockSpec(memory_space=pltpu.VMEM)
+    free = pl.BlockSpec()
     names = ("x", "zl", "y", "core")
     feats, cot, rates, *where = lax.optimization_barrier(
         (feats, cot, rates, *[lax.axis_index(n) for n in names])
     )
     xi, zi, yi, ci = [w.reshape(1) for w in where]
     anywhere = pl.BlockSpec(memory_space=pl.ANY)
-    head, tail, block, taps, amp_mine, tk, cown, wg = pl.pallas_call(
+    head, tail, block, taps, amp_mine, cown = pl.pallas_call(
         prepare,
-        in_specs=[anywhere] * 6,
-        out_specs=[vm] * 8,
+        in_specs=[anywhere] * 5,
+        out_specs=[vm] * 6,
         out_shape=[
             jax.ShapeDtypeStruct((HALO, depth + PADC), BF16),
             jax.ShapeDtypeStruct((HALO, depth), BF16),
             jax.ShapeDtypeStruct((2 * MODES, width // count), F32),
             jax.ShapeDtypeStruct((3, 8, PADC), F32),
             jax.ShapeDtypeStruct(rates.shape, F32),
-            jax.ShapeDtypeStruct((own, depth), BF16),
             jax.ShapeDtypeStruct((own, PADC), F32),
-            jax.ShapeDtypeStruct((width, depth), BF16),
         ],
         scratch_shapes=[
             pltpu.VMEM((128, 128), F32),
@@ -437,36 +458,58 @@
             pltpu.VMEM(rates.shape, F32),
             pltpu.VMEM(rates.shape, F32),
             pltpu.VMEM(conv_taps.shape, F32),
-            pltpu.SemaphoreType.DMA((8,)),
+            pltpu.SemaphoreType.DMA((6,)),
         ],
         compiler_params=params(54),
         name="prepare",
-    )(feats, cot.T, rates, residues, conv_taps, w_in.T)
+    )(feats, cot.T, rates, residues, conv_taps)
     tprev = lax.ppermute(tail, ctx, [(i, i + 1) for i in range(count - 1)])
     nexts = lax.ppermute(head, ctx, [(i, i - 1) for i in range(1, count)])
     ext_rows = own + 2 * HALO
-    project_out = [jax.ShapeDtypeStruct((ext_rows, PADC), F32), jax.ShapeDtypeStruct((EXT, PADC), F32)]
-    project_cost = pl.CostEstimate(flops=500000000, bytes_accessed=4000000, transcendentals=0)
+    steps = depth // KBLK // 2
+
+    def project(part, *before):
+        many = 3 if part else 1
+        shape = (ext_rows, PADC) if part else (ext_rows, chans)
+        return pl.pallas_call(
+            make_project(part),
+            in_specs=[vm] * (2 + part) + [anywhere] * 2,
+            out_specs=[vm] * many,
+            out_shape=[jax.ShapeDtypeStruct(shape, F32)] * many,
+            scratch_shapes=[
+                pltpu.VMEM((own, steps * KBLK), BF16),
+                pltpu.VMEM((steps, chans, KBLK), BF16),
+                pltpu.SemaphoreType.DMA,
+                pltpu.SemaphoreType.DMA((steps,)),
+                *[pltpu.VMEM((ext_rows, chans), F32)] * part,
+            ],
+            compiler_params=params((52, 51)[part]),
+            cost_estimate=pl.CostEstimate(flops=800000000, bytes_accessed=6000000, transcendentals=0),
+            name="project",
+        )(tprev, nexts, *before, feats, w_in.T)
+
+    def mixed(*zs):
+        return pl.pallas_call(
+            mix_taps,
+            in_specs=[vm] * 4,
+            out_specs=[vm] * 3,
+            out_shape=[jax.ShapeDtypeStruct((EXT, PADC), F32)] * 3,
+            compiler_params=params(8),
+            cost_estimate=pl.CostEstimate(flops=800000000, bytes_accessed=6000000, transcendentals=0),
+            name="mix_taps",
+        )(taps, *zs)
+
     held, each = block, width // count
-    projected = []
+    work = []
     for g, (me, ax) in enumerate(((yi, "y"), (zi, "zl"), (xi, "x"))):
         blocks = [held] + [ring(held, ax, d) for d in (1, 2, 3)]
-        more = g < 2
-        done = pl.pallas_call(
-            make_project(g),
-            in_specs=[vm] * 5 + [anywhere] * more,
-            out_specs=[vm] * (2 + more),
-            out_shape=project_out + [jax.ShapeDtypeStruct((width, depth), BF16)] * more,
-            scratch_shapes=[pltpu.SemaphoreType.DMA] * more,
-            compiler_params=params((50, 50, 50)[g]),
-            cost_estimate=project_cost,
-            name="project",
-        )(tprev, nexts, taps, tk, wg, *[w_in.T] * more)
-        *blocks, zg, mg = lax.optimization_barrier((*blocks, done[0], done[1]))
-        projected.append((zg, mg))
+        work = project(0) if g == 0 else project(1, *work) if g == 1 else mixed(*work)
+        *blocks, last_work = lax.optimization_barrier((*blocks, work[-1]))
+        work = [*work[:-1], last_work]
+        if g == 1:
+            zq, zk, zv = work
         if g == 2:
             break
-        wg = done[2]
         each = 4 * each
         held = pl.pallas_call(
             join_params,
@@ -477,7 +520,7 @@
             compiler_params=params(4),
             name="join_params",
         )(me, *blocks)
-    (zq, mq), (zk, mk), (zv, mv) = projected
+    mq, mk, mv = work
     cots, rate, gain, es, ends, endb = pl.pallas_call(
         end_states,
         in_specs=[smem] + [vm] * 9,
@@ -570,7 +613,7 @@
             pltpu.VMEM((3, EXT, 128), F32),
             pltpu.VMEM((3, PADC, own), F32),
         ],
-        compiler_params=params(24),
+        compiler_params=params(50),
         cost_estimate=pl.CostEstimate(flops=200000000, bytes_accessed=10000000, transcendentals=0),
         name="finish",
     )(zi, yi, zq, zk, zv, mq, mk, mv, es, *prefixes, taps, rate, gain, cots)
@@ -589,8 +632,8 @@
     def summed(parts):
         return pl.pallas_call(
             add_parts,
-            in_specs=[vm] * len(parts),
-            out_specs=vm,
+            in_specs=[free] * len(parts),
+            out_specs=free,
             out_shape=jax.ShapeDtypeStruct((40, PADC), BF16),
             compiler_params=params(4),
             name="add_parts",
@@ -619,7 +662,7 @@
     arrived, sums = lax.optimization_barrier((arrived, sums))
     term = pl.pallas_call(
         weight_term,
-        in_specs=[smem] * 2 + [vm] * 9,
+        in_specs=[smem] * 2 + [vm] + [free] * 8,
         out_specs=vm,
         out_shape=jax.ShapeDtypeStruct((4, 2 * piece, depth // 4), BF16),
         compiler_params=params(24),
@@ -644,7 +687,7 @@
     parts = spread(sums, "x")
     grad_taps, grad_residues = pl.pallas_call(
         make_close_sums(scale),
-        in_specs=[smem] * 3 + [vm] * 5,
+        in_specs=[smem] * 3 + [free] * 5,
         out_specs=[vm] * 2,
         out_shape=[
             jax.ShapeDtypeStruct((7, chans), F32),

time: 165 us -> 157 us (0.952)
  starting transfers between devices: 83.9 us -> 74.1 us
  waiting for transfers between devices: 28.8 us -> 38.4 us
  Pallas kernels: 42.7 us -> 37.9 us
  local copies, waits for them, and re-layouts: 7.58 us -> 4.93 us
    ppermute x27, waiting for transfers between devices: 18.6 us -> 25.3 us  [ring(): return lax.ppermute(a, ax, [(i, (i + d) % 4) for i in range(4)])]
    ppermute x27, starting transfers between devices: 50.5 us -> 44 us  [ring(): return lax.ppermute(a, ax, [(i, (i + d) % 4) for i in range(4)])]
    pallas_call x10, Pallas kernels: 22 us -> 16.9 us  [the longest x2 9.63 us: project(): pl.pallas_call(make_project(part), in_specs=[vm] * (2 + part) + [anywhere...]
    ppermute x1, waiting for transfers between devices: 1.26 us -> 4.19 us  [local(): opposite = lax.ppermute(mine, 'y', [(i, 3 - i) for i in range(4)])]
    unnamed x26 -> x30, local copies, waits for them, and re-layouts: 7.58 us -> 4.93 us
  transfers between devices with their start and end apart: 41 -> 41, of which waited for: 19 -> 22; matrix products, arithmetic and copies ran while one was open for 0% -> 0% of each run, Pallas kernels for 19% -> 18%
where the time goes in v9:
time: 157 us; the launch traced here: 156 us
  starting transfers between devices  74.1 us (47%)
  waiting for transfers between devices  38.4 us (24%)
  Pallas kernels  37.9 us (24%)
  local copies, waits for them, and re-layouts  4.93 us (3%)
    ppermute x27, starting transfers between devices, ring(): return lax.ppermute(a, ax, [(i, (i + d) % 4) for i in range(4)])  44 us
    ppermute x27, waiting for transfers between devices, ring(): return lax.ppermute(a, ax, [(i, (i + d) % 4) for i in range(4)])  25.3 us
    pallas_call x2, Pallas kernels, project(): pl.pallas_call(make_project(part), in_specs=[vm] * (2 + part) + [anywhere...  9.63 us
    pallas_call x1, Pallas kernels, local(): pl.pallas_call(finish, grid=(PADC // 128,), in_specs=[smem, smem, *[tiles...  9.61 us
    all_to_all x1, starting transfers between devices, local(): last = lax.all_to_all(blocks, ('zl', 'y', 'zh'), 0, 0, tiled=True)  8.33 us
    pallas_call x1, Pallas kernels, local(): pl.pallas_call(token_grads, grid=(3,), in_specs=[pl.BlockSpec((1, own, PA...  6 us
    ppermute x2, waiting for transfers between devices, swap(): return [a, lax.ppermute(a, ax, [(0, 1), (1, 0)])]  5.28 us
    ppermute x2, starting transfers between devices, swap(): return [a, lax.ppermute(a, ax, [(0, 1), (1, 0)])]  5.09 us
  transfers between devices with their start and end apart: 41, of which 22 were waited for; matrix products, arithmetic and copies ran while one was open for 0% of the time, Pallas kernels for 18%

profile of v9, /device:TPU:32, one launch (start us, length us, event | category | flops | bytes accessed | tf_op | source)
XLA Modules:
  0.0 156.3 jit_solution(9218028247816157720)
XLA Ops:
  0.6 2.2 %prepare.1 = (bf16[16,2560]{1,0:T(8,128)(2,1)}, bf16[16,1536]{1,0:T(8,128)(2,1)}, f32[32,15]{1,0:T(8,128)}, f32[3,8,1024]{2,1,0:T(8,128)}, f32[15,16]{1,0:T(8,128)}, /*index=5*/f32[128,1024]{1,0:T(8,128)}) custom-call(bf16[128,1536]{1,0:T(8,128)(2,1)} %bitcast.12, bf16[960,128]{1,0:T(8,128)(2,1)} %bitcast.23, f32[15,16]{1,0:T(8,128)} %rates, ...), custom_call_target="tpu_custom_call" | custom-call | tf_op jit(solution)/shard_map/prepare/pallas_call | solution.py:442
  2.8 4.5 %collective-permute-start.1 = (bf16[16,2560]{1,0:T(8,128)(2,1)}, bf16[16,2560]{1,0:T(8,128)(2,1)S(1)}, u32[]{:S(2)}, u32[]{:S(2)}) collective-permute-start(bf16[16,2560]{1,0:T(8,128)(2,1)} %get-tuple-element.87), channel_id=1, source_target_pairs={{4,0},{8,4},{12,8},{16,12},{20,16},{24,20},{28,24},{32,28},{36,32}... | collective-permute-start | bytes 245768 | tf_op jit(solution)/shard_map/ppermute | solution.py:467
  7.3 1.9 %collective-permute-start = (bf16[16,1536]{1,0:T(8,128)(2,1)}, bf16[16,1536]{1,0:T(8,128)(2,1)S(1)}, u32[]{:S(2)}, u32[]{:S(2)}) collective-permute-start(bf16[16,1536]{1,0:T(8,128)(2,1)} %get-tuple-element.86), channel_id=1, source_target_pairs={{0,4},{4,8},{8,12},{12,16},{16,20},{20,24},{24,28},{28,32},{32,36}... | collective-permute-start | bytes 147464 | tf_op jit(solution)/shard_map/ppermute | solution.py:466
  9.2 4.7 %collective-permute-start.4 = (f32[32,15]{1,0:T(8,128)}, f32[32,15]{1,0:T(8,128)S(1)}, u32[]{:S(2)}, u32[]{:S(2)}) collective-permute-start(f32[32,15]{1,0:T(8,128)} %get-tuple-element.92.r0), channel_id=1, source_target_pairs={{0,12},{4,0},{8,4},{12,8},{1,13},{5,1},{9,5},{13,9},{2,14},{6,2},{... | collective-permute-start | bytes 5768 | tf_op jit(solution)/shard_map/ppermute | solution.py:415
  13.9 1.0 collective-permute-start.2
  15.6 1.0 copy-done
  16.6 4.7 %project.2.refs_2_ = f32[160,2880]{1,0:T(8,128)} custom-call(bf16[16,1536]{1,0:T(8,128)(2,1)S(1)} %collective-permute-done.refs_0_, bf16[16,2560]{1,0:T(8,128)(2,1)S(1)} %collective-permute-done.1.refs_1_.nexts, bf16[128,1536]{1,0:T(8,128)(2,1)S(1)} %bitcast.13, bf16[2880,1536]{1,0:T(8,128)(2,1)} %bitcast.19), custom_call_target="tpu_custom_call" | custom-call | flops 800000000 | bytes 6000000 | tf_op jit(solution)/shard_map/project/pallas_call | solution.py:474
  21.6 5.3 %collective-permute-start.6 = (f32[32,60]{1,0:T(8,128)S(1)}, f32[32,60]{1,0:T(8,128)S(1)}, u32[]{:S(2)}, u32[]{:S(2)}) collective-permute-start(f32[32,60]{1,0:T(8,128)S(1)} %join_params.2.r0), channel_id=1, source_target_pairs={{0,32},{16,48},{32,0},{48,16},{1,33},{17,49},{33,1},{49,17},{2,34}... | collective-permute-start | bytes 23048 | tf_op jit(solution)/shard_map/ppermute | solution.py:415
  26.9 2.8 %collective-permute-start.5 = (f32[32,60]{1,0:T(8,128)S(1)}, f32[32,60]{1,0:T(8,128)S(1)}, u32[]{:S(2)}, u32[]{:S(2)}) collective-permute-start(f32[32,60]{1,0:T(8,128)S(1)} %join_params.2.r0), channel_id=1, source_target_pairs={{0,16},{16,32},{32,48},{48,0},{1,17},{17,33},{33,49},{49,1},{2,18}... | collective-permute-start | bytes 23048 | tf_op jit(solution)/shard_map/ppermute | solution.py:415
  29.7 4.9 %project.3 = (f32[160,1024]{1,0:T(8,128)S(1)}, f32[160,1024]{1,0:T(8,128)S(1)}, f32[160,1024]{1,0:T(8,128)S(1)}) custom-call(bf16[16,1536]{1,0:T(8,128)(2,1)S(1)} %collective-permute-done.refs_0_, bf16[16,2560]{1,0:T(8,128)(2,1)S(1)} %collective-permute-done.1.refs_1_.nexts, f32[160,2880]{1,0:T(8,128)} %project.2.refs_2_, bf16[128,1536]{1,0:T(8,128)(2,1)S(1)} %bitcast.14, ...), custom_call_target="tpu_custom_call" | custom-call | flops 800000000 | bytes 6000000 | tf_op jit(solution)/shard_map/project/pallas_call | solution.py:474
  34.8 3.9 %collective-permute-start.10 = (f32[32,240]{1,0:T(8,128)S(1)}, f32[32,240]{1,0:T(8,128)S(1)}, u32[]{:S(2)}, u32[]{:S(2)}) collective-permute-start(f32[32,240]{1,0:T(8,128)S(1)} %join_params.3.r0), channel_id=1, source_target_pairs={{0,192},{64,0},{128,64},{192,128},{1,193},{65,1},{129,65},{193,129... | collective-permute-start | bytes 92168 | tf_op jit(solution)/shard_map/ppermute | solution.py:415
  39.2 0.9 collective-permute-start.8
  40.1 1.4 mix_taps.1
  41.5 2.6 %collective-permute-done.9.r2 = f32[32,240]{1,0:T(8,128)S(1)} collective-permute-done((f32[32,240]{1,0:T(8,128)S(1)}, f32[32,240]{1,0:T(8,128)S(1)}, u32[]{:S(2)}, u32[]{:S(2)}) %collective-permute-start.9) | collective-permute-done | bytes 30752 | tf_op jit(solution)/shard_map/ppermute | solution.py:415
  44.4 2.2 %end_states.1 = (f32[136,1024]{1,0:T(8,128)S(1)}, f32[16,1024]{1,0:T(8,128)S(1)}, f32[16,1024]{1,0:T(8,128)S(1)}, f32[2,16,8,1024]{3,2,1,0:T(8,128)S(1)}, f32[32...) custom-call(s32[1]{0:T(128)} %bitcast.6.me.index.xi, f32[32,240]{1,0:T(8,128)S(1)} %join_params.3.r0, ...), custom_call_target="tpu_custom_call" | custom-call | flops 20000000 | bytes 3000000 | tf_op jit(solution)/shard_map/end_states/pallas_call | solution.py:524
  46.7 1.5 collective-permute-start.13
  48.1 2.3 %collective-permute-start.12 = (bf16[32,1024]{1,0:T(8,128)(2,1)S(1)}, bf16[32,1024]{1,0:T(8,128)(2,1)S(1)}, u32[]{:S(2)}, u32[]{:S(2)}) collective-permute-start(bf16[32,1024]{1,0:T(8,128)(2,1)S(1)} %get-tuple-element.115), channel_id=1, source_target_pairs={{0,8},{4,12},{8,0},{12,4},{1,9},{5,13},{9,1},{13,5},{2,10},{6,14},... | collective-permute-start | bytes 196616 | tf_op jit(solution)/shard_map/ppermute | solution.py:415
  51.0 2.9 %collective-permute-done.12.r2 = bf16[32,1024]{1,0:T(8,128)(2,1)S(1)} collective-permute-done((bf16[32,1024]{1,0:T(8,128)(2,1)S(1)}, bf16[32,1024]{1,0:T(8,128)(2,1)S(1)}, u32[]{:S(2)}, u32[]{:S(2)}) %collective-permute-start.12) | collective-permute-done | bytes 65568 | tf_op jit(solution)/shard_map/ppermute | solution.py:415
  53.9 2.0 %collective-permute-done.11.r1 = bf16[32,1024]{1,0:T(8,128)(2,1)S(1)} collective-permute-done((bf16[32,1024]{1,0:T(8,128)(2,1)S(1)}, bf16[32,1024]{1,0:T(8,128)(2,1)S(1)}, u32[]{:S(2)}, u32[]{:S(2)}) %collective-permute-start.11) | collective-permute-done | bytes 65568 | tf_op jit(solution)/shard_map/ppermute | solution.py:415
  56.2 1.5 collective-permute-start.15
  57.7 2.4 %collective-permute-start.14 = (bf16[32,1024]{1,0:T(8,128)(2,1)S(1)}, bf16[32,1024]{1,0:T(8,128)(2,1)S(1)}, u32[]{:S(2)}, u32[]{:S(2)}) collective-permute-start(bf16[32,1024]{1,0:T(8,128)(2,1)S(1)} %get-tuple-element.119), channel_id=1, source_target_pairs={{0,16},{16,32},{32,48},{48,0},{1,17},{17,33},{33,49},{49,1},{2,18}... | collective-permute-start | bytes 196616 | tf_op jit(solution)/shard_map/ppermute | solution.py:415
  60.5 1.0 collective-permute-done.15.r2
  61.5 1.2 collective-permute-done.14.r1
  62.9 1.1 collective-permute-start.18
  64.5 1.1 collective-permute-start.20
  65.6 1.4 collective-permute-start.19
  67.0 1.2 collective-permute-done.21.r3
  68.2 2.1 %collective-permute-done.20.r2 = bf16[32,1024]{1,0:T(8,128)(2,1)S(1)} collective-permute-done((bf16[32,1024]{1,0:T(8,128)(2,1)S(1)}, bf16[32,1024]{1,0:T(8,128)(2,1)S(1)}, u32[]{:S(2)}, u32[]{:S(2)}) %collective-permute-start.20) | collective-permute-done | bytes 65568 | tf_op jit(solution)/shard_map/ppermute | solution.py:415
  71.9 4.2 %collective-permute-done.18.refs_2_ = bf16[128,1536]{1,0:T(8,128)(2,1)S(1)} collective-permute-done((bf16[128,1536]{1,0:T(8,128)(2,1)S(1)}, bf16[128,1536]{1,0:T(8,128)(2,1)S(1)}, u32[]{:S(2)}, u32[]{:S(2)}) %collective-permute-start.18) | collective-permute-done | bytes 393248 | tf_op jit(solution)/shard_map/ppermute | solution.py:566
  76.3 9.6 %finish.1 = (bf16[960,128]{1,0:T(8,128)(2,1)}, bf16[3,128,1024]{2,1,0:T(8,128)(2,1)}, bf16[8,360,128]{2,1,0:T(8,128)(2,1)}, bf16[40,1024]{1,0:T(8,128)(2,1)S(1)}) custom-call(s32[1]{0:T(128)} %bitcast.2.me.index.zi, s32[1]{0:T(128)} %bitcast.3.me.index.yi, f32[160,1024]{1,0:T(8,128)S(1)} %get-tuple-element.90.zq, f32[160,1024]{1,0:T(8,128)} %copy-done.3, ...), custom_call_target="tpu_custom_call" | custom-call | flops 200000000 | bytes 10000000 | tf_op jit(solution)/shard_map/finish/pallas_call | solution.py:577
  86.6 4.3 %all-to-all-start = ((bf16[8,360,128]{2,1,0:T(8,128)(2,1)}), bf16[8,360,128]{2,1,0:T(8,128)(2,1)S(1)}, u32[]{:S(2)}, u32[]{:S(2)}) async-start(bf16[8,360,128]{2,1,0:T(8,128)(2,1)} %get-tuple-element.139), calls=%async_computation | async-start | bytes 1474560 | tf_op jit(solution)/shard_map/all_to_all | solution.py:642
  92.4 1.3 collective-permute-done.27.refs_1_
  93.7 0.9 copy-done.12
  95.4 2.6 %collective-permute-start.30 = (bf16[40,1024]{1,0:T(8,128)(2,1)S(1)}, bf16[40,1024]{1,0:T(8,128)(2,1)S(1)}, u32[]{:S(2)}, u32[]{:S(2)}) collective-permute-start(bf16[40,1024]{1,0:T(8,128)(2,1)S(1)} %add_parts.4.refs_0_), channel_id=1, source_target_pairs={{0,48},{16,0},{32,16},{48,32},{1,49},{17,1},{33,17},{49,33},{2,50}... | collective-permute-start | bytes 245768 | tf_op jit(solution)/shard_map/ppermute | solution.py:415
  98.3 1.7 %collective-permute-start.28 = (bf16[40,1024]{1,0:T(8,128)(2,1)S(1)}, bf16[40,1024]{1,0:T(8,128)(2,1)S(1)}, u32[]{:S(2)}, u32[]{:S(2)}) collective-permute-start(bf16[40,1024]{1,0:T(8,128)(2,1)S(1)} %add_parts.4.refs_0_), channel_id=1, source_target_pairs={{0,16},{16,32},{32,48},{48,0},{1,17},{17,33},{33,49},{49,1},{2,18}... | collective-permute-start | bytes 245768 | tf_op jit(solution)/shard_map/ppermute | solution.py:415
  99.9 6.0 %token_grads.1 = bf16[128,1536]{1,0:T(8,128)(2,1)} custom-call(bf16[3,128,1024]{2,1,0:T(8,128)(2,1)} %get-tuple-element.136.dz, bf16[2880,1536]{1,0:T(8,128)(2,1)} %bitcast.21), custom_call_target="tpu_custom_call" | custom-call | flops 1200000000 | bytes 11000000 | tf_op jit(solution)/shard_map/token_grads/pallas_call | solution.py:646
  106.7 1.0 copy-done.7
  107.6 2.8 %weight_term.1 = bf16[4,360,384]{2,1,0:T(8,128)(2,1)} custom-call(s32[1]{0:T(128)} %bitcast.3.me.index.yi, s32[1]{0:T(128)} %bitcast.10.ci, bf16[8,360,128]{2,1,0:T(8,128)(2,1)S(1)} %all-to-all-done.arrived, bf16[128,1536]{1,0:T(8,128)(2,1)S(1)} %bitcast.18, bf16[128,1536]{1,0:T(8,128)(2,1)S(1)} %collective-permute-done.17.refs_1_, ...), custom_call_target="tpu_custom_call" | custom-call | flops 1200000000 | bytes 6000000 | tf_op jit(solution)/shard_map/weight_term/pallas_call | solution.py:663
  110.5 3.7 %all-to-all-start.1 = ((bf16[4,360,384]{2,1,0:T(8,128)(2,1)}), bf16[4,360,384]{2,1,0:T(8,128)(2,1)S(1)}, u32[]{:S(2)}, u32[]{:S(2)}) async-start(bf16[4,360,384]{2,1,0:T(8,128)(2,1)} %weight_term.1), calls=%async_computation.1 | async-start | bytes 2211840 | tf_op jit(solution)/shard_map/all_to_all | solution.py:672
  114.1 3.2 %collective-permute-start.33 = (bf16[40,1024]{1,0:T(8,128)(2,1)S(1)}, bf16[40,1024]{1,0:T(8,128)(2,1)S(1)}, u32[]{:S(2)}, u32[]{:S(2)}) collective-permute-start(bf16[40,1024]{1,0:T(8,128)(2,1)S(1)} %copy-done.9), channel_id=1, source_target_pairs={{0,12},{4,0},{8,4},{12,8},{1,13},{5,1},{9,5},{13,9},{2,14},{6,2},{... | collective-permute-start | bytes 245768 | tf_op jit(solution)/shard_map/ppermute | solution.py:415
  119.4 3.9 %collective-permute-done.32.refs_2_ = bf16[40,1024]{1,0:T(8,128)(2,1)S(1)} collective-permute-done((bf16[40,1024]{1,0:T(8,128)(2,1)S(1)}, bf16[40,1024]{1,0:T(8,128)(2,1)S(1)}, u32[]{:S(2)}, u32[]{:S(2)}) %collective-permute-start.32) | collective-permute-done | bytes 81952 | tf_op jit(solution)/shard_map/ppermute | solution.py:415
  124.2 4.6 %collective-permute-start.34 = (bf16[40,1024]{1,0:T(8,128)(2,1)S(1)}, bf16[40,1024]{1,0:T(8,128)(2,1)S(1)}, u32[]{:S(2)}, u32[]{:S(2)}) collective-permute-start(bf16[40,1024]{1,0:T(8,128)(2,1)S(1)} %add_parts.6.refs_0_), channel_id=1, source_target_pairs={{0,2},{2,0},{1,3},{3,1},{4,6},{6,4},{5,7},{7,5},{8,10},{10,8},{9,1... | collective-permute-start | bytes 245768 | tf_op jit(solution)/shard_map/ppermute | solution.py:630
  128.8 4.0 %collective-permute-done.34.refs_1_ = bf16[40,1024]{1,0:T(8,128)(2,1)S(1)} collective-permute-done((bf16[40,1024]{1,0:T(8,128)(2,1)S(1)}, bf16[40,1024]{1,0:T(8,128)(2,1)S(1)}, u32[]{:S(2)}, u32[]{:S(2)}) %collective-permute-start.34) | collective-permute-done | bytes 81952 | tf_op jit(solution)/shard_map/ppermute | solution.py:630
  132.8 1.1 split_rows.1
  133.8 8.3 %all-to-all-start.2 = ((bf16[32,24,180]{2,1,0:T(8,128)(2,1)}), bf16[32,24,180]{2,1,0:T(8,128)(2,1)S(1)}, u32[]{:S(2)}, u32[]{:S(2)}) async-start(bf16[32,24,180]{2,1,0:T(8,128)(2,1)} %split_rows.1), calls=%async_computation.2 | async-start | bytes 786432 | tf_op jit(solution)/shard_map/all_to_all | solution.py:685
  142.2 3.0 %collective-permute-start.37 = (bf16[40,1024]{1,0:T(8,128)(2,1)S(1)}, bf16[40,1024]{1,0:T(8,128)(2,1)S(1)}, u32[]{:S(2)}, u32[]{:S(2)}) collective-permute-start(bf16[40,1024]{1,0:T(8,128)(2,1)S(1)} %add_parts.7.refs_0_), channel_id=1, source_target_pairs={{0,192},{64,0},{128,64},{192,128},{1,193},{65,1},{129,65},{193,129... | collective-permute-start | bytes 245768 | tf_op jit(solution)/shard_map/ppermute | solution.py:415
  147.2 3.9 %collective-permute-done.36.refs_2_ = bf16[40,1024]{1,0:T(8,128)(2,1)S(1)} collective-permute-done((bf16[40,1024]{1,0:T(8,128)(2,1)S(1)}, bf16[40,1024]{1,0:T(8,128)(2,1)S(1)}, u32[]{:S(2)}, u32[]{:S(2)}) %collective-permute-start.36) | collective-permute-done | bytes 81952 | tf_op jit(solution)/shard_map/ppermute | solution.py:415
  152.7 2.9 %all-to-all-done.2.last = bf16[32,24,180]{2,1,0:T(8,128)(2,1)S(1)} async-done(((bf16[32,24,180]{2,1,0:T(8,128)(2,1)}), bf16[32,24,180]{2,1,0:T(8,128)(2,1)S(1)}, u32[]{:S(2)}, u32[]{:S(2)}) %all-to-all-start.2) | async-done | bytes 276512 | tf_op jit(solution)/shard_map/all_to_all | solution.py:685
  (84 shorter events, 17.2 us)
Async XLA Ops:
  2.8 12.8 %collective-permute-start.1 = (bf16[16,2560]{1,0:T(8,128)(2,1)}, bf16[16,2560]{1,0:T(8,128)(2,1)S(1)}, u32[]{:S(2)}, u32[]{:S(2)}) collective-permute-start(bf16[16,2560]{1,0:T(8,128)(2,1)} %get-tuple-element.87), channel_id=1, source_target_pairs={{4,0},{8,4},{12,8},{16,12},{20,16},{24,20},{28,24},{32,28},{36,32}... | collective-permute-start | bytes 245768 | tf_op jit(solution)/shard_map/ppermute | solution.py:467
  7.3 8.3 %collective-permute-start = (bf16[16,1536]{1,0:T(8,128)(2,1)}, bf16[16,1536]{1,0:T(8,128)(2,1)S(1)}, u32[]{:S(2)}, u32[]{:S(2)}) collective-permute-start(bf16[16,1536]{1,0:T(8,128)(2,1)} %get-tuple-element.86), channel_id=1, source_target_pairs={{0,4},{4,8},{8,12},{12,16},{16,20},{20,24},{24,28},{28,32},{32,36}... | collective-permute-start | bytes 147464 | tf_op jit(solution)/shard_map/ppermute | solution.py:466
  9.2 12.1 %collective-permute-start.4 = (f32[32,15]{1,0:T(8,128)}, f32[32,15]{1,0:T(8,128)S(1)}, u32[]{:S(2)}, u32[]{:S(2)}) collective-permute-start(f32[32,15]{1,0:T(8,128)} %get-tuple-element.92.r0), channel_id=1, source_target_pairs={{0,12},{4,0},{8,4},{12,8},{1,13},{5,1},{9,5},{13,9},{2,14},{6,2},{... | collective-permute-start | bytes 5768 | tf_op jit(solution)/shard_map/ppermute | solution.py:415
  13.9 7.5 %collective-permute-start.3 = (f32[32,15]{1,0:T(8,128)}, f32[32,15]{1,0:T(8,128)S(1)}, u32[]{:S(2)}, u32[]{:S(2)}) collective-permute-start(f32[32,15]{1,0:T(8,128)} %get-tuple-element.92.r0), channel_id=1, source_target_pairs={{0,8},{4,12},{8,0},{12,4},{1,9},{5,13},{9,1},{13,5},{2,10},{6,14},... | collective-permute-start | bytes 5768 | tf_op jit(solution)/shard_map/ppermute | solution.py:415
  13.9 7.5 %collective-permute-start.2 = (f32[32,15]{1,0:T(8,128)}, f32[32,15]{1,0:T(8,128)S(1)}, u32[]{:S(2)}, u32[]{:S(2)}) collective-permute-start(f32[32,15]{1,0:T(8,128)} %get-tuple-element.92.r0), channel_id=1, source_target_pairs={{0,4},{4,8},{8,12},{12,0},{1,5},{5,9},{9,13},{13,1},{2,6},{6,10},{... | collective-permute-start | bytes 5768 | tf_op jit(solution)/shard_map/ppermute | solution.py:415
  16.6 13.1 %copy-start.1 = (bf16[1,128,1536]{2,1,0:T(8,128)(2,1)S(1)}, bf16[1,128,1536]{2,1,0:T(8,128)(2,1)}, u32[]{:S(2)}) copy-start(bf16[1,128,1536]{2,1,0:T(8,128)(2,1)} %param.6) | copy-start | bytes 1179652
  21.5 18.6 %copy-start.10 = (f32[3,8,1024]{2,1,0:T(8,128)S(1)}, f32[3,8,1024]{2,1,0:T(8,128)}, u32[]{:S(2)}) copy-start(f32[3,8,1024]{2,1,0:T(8,128)} %get-tuple-element.98.taps) | copy-start | bytes 294916
  21.5 13.2 %collective-permute-start.7 = (f32[32,60]{1,0:T(8,128)S(1)}, f32[32,60]{1,0:T(8,128)S(1)}, u32[]{:S(2)}, u32[]{:S(2)}) collective-permute-start(f32[32,60]{1,0:T(8,128)S(1)} %join_params.2.r0), channel_id=1, source_target_pairs={{0,48},{16,0},{32,16},{48,32},{1,49},{17,1},{33,17},{49,33},{2,50}... | collective-permute-start | bytes 23048 | tf_op jit(solution)/shard_map/ppermute | solution.py:415
  21.6 13.1 %collective-permute-start.6 = (f32[32,60]{1,0:T(8,128)S(1)}, f32[32,60]{1,0:T(8,128)S(1)}, u32[]{:S(2)}, u32[]{:S(2)}) collective-permute-start(f32[32,60]{1,0:T(8,128)S(1)} %join_params.2.r0), channel_id=1, source_target_pairs={{0,32},{16,48},{32,0},{48,16},{1,33},{17,49},{33,1},{49,17},{2,34}... | collective-permute-start | bytes 23048 | tf_op jit(solution)/shard_map/ppermute | solution.py:415
  26.9 7.8 %collective-permute-start.5 = (f32[32,60]{1,0:T(8,128)S(1)}, f32[32,60]{1,0:T(8,128)S(1)}, u32[]{:S(2)}, u32[]{:S(2)}) collective-permute-start(f32[32,60]{1,0:T(8,128)S(1)} %join_params.2.r0), channel_id=1, source_target_pairs={{0,16},{16,32},{32,48},{48,0},{1,17},{17,33},{33,49},{49,1},{2,18}... | collective-permute-start | bytes 23048 | tf_op jit(solution)/shard_map/ppermute | solution.py:415
  34.6 12.0 %copy-start.3 = (f32[160,1024]{1,0:T(8,128)}, f32[160,1024]{1,0:T(8,128)S(1)}, u32[]{:S(2)}) copy-start(f32[160,1024]{1,0:T(8,128)S(1)} %get-tuple-element.91.zk) | copy-start | bytes 1966084
  34.6 12.0 %copy-start.4 = (f32[160,1024]{1,0:T(8,128)}, f32[160,1024]{1,0:T(8,128)S(1)}, u32[]{:S(2)}) copy-start(f32[160,1024]{1,0:T(8,128)S(1)} %get-tuple-element.97.zv) | copy-start | bytes 1966084
  34.7 9.8 %copy-start.5 = (f32[128,1024]{1,0:T(8,128)S(1)}, f32[128,1024]{1,0:T(8,128)}, u32[]{:S(2)}) copy-start(f32[128,1024]{1,0:T(8,128)} %get-tuple-element.112.cown) | copy-start | bytes 1572868
  34.8 6.7 %collective-permute-start.10 = (f32[32,240]{1,0:T(8,128)S(1)}, f32[32,240]{1,0:T(8,128)S(1)}, u32[]{:S(2)}, u32[]{:S(2)}) collective-permute-start(f32[32,240]{1,0:T(8,128)S(1)} %join_params.3.r0), channel_id=1, source_target_pairs={{0,192},{64,0},{128,64},{192,128},{1,193},{65,1},{129,65},{193,129... | collective-permute-start | bytes 92168 | tf_op jit(solution)/shard_map/ppermute | solution.py:415
  38.7 5.4 %collective-permute-start.9 = (f32[32,240]{1,0:T(8,128)S(1)}, f32[32,240]{1,0:T(8,128)S(1)}, u32[]{:S(2)}, u32[]{:S(2)}) collective-permute-start(f32[32,240]{1,0:T(8,128)S(1)} %join_params.3.r0), channel_id=1, source_target_pairs={{0,128},{64,192},{128,0},{192,64},{1,129},{65,193},{129,1},{193,65... | collective-permute-start | bytes 92168 | tf_op jit(solution)/shard_map/ppermute | solution.py:415
  39.2 5.3 %collective-permute-start.8 = (f32[32,240]{1,0:T(8,128)S(1)}, f32[32,240]{1,0:T(8,128)S(1)}, u32[]{:S(2)}, u32[]{:S(2)}) collective-permute-start(f32[32,240]{1,0:T(8,128)S(1)} %join_params.3.r0), channel_id=1, source_target_pairs={{0,64},{64,128},{128,192},{192,0},{1,65},{65,129},{129,193},{193,1... | collective-permute-start | bytes 92168 | tf_op jit(solution)/shard_map/ppermute | solution.py:415
  46.6 29.4 %copy-start.2 = (f32[2,16,8,1024]{3,2,1,0:T(8,128)}, f32[2,16,8,1024]{3,2,1,0:T(8,128)S(1)}, u32[]{:S(2)}) copy-start(f32[2,16,8,1024]{3,2,1,0:T(8,128)S(1)} %get-tuple-element.113.es) | copy-start | bytes 3145732
  46.7 4.3 %collective-permute-start.13 = (bf16[32,1024]{1,0:T(8,128)(2,1)S(1)}, bf16[32,1024]{1,0:T(8,128)(2,1)S(1)}, u32[]{:S(2)}, u32[]{:S(2)}) collective-permute-start(bf16[32,1024]{1,0:T(8,128)(2,1)S(1)} %get-tuple-element.115), channel_id=1, source_target_pairs={{0,12},{4,0},{8,4},{12,8},{1,13},{5,1},{9,5},{13,9},{2,14},{6,2},{... | collective-permute-start | bytes 196616 | tf_op jit(solution)/shard_map/ppermute | solution.py:415
  48.1 5.8 %collective-permute-start.12 = (bf16[32,1024]{1,0:T(8,128)(2,1)S(1)}, bf16[32,1024]{1,0:T(8,128)(2,1)S(1)}, u32[]{:S(2)}, u32[]{:S(2)}) collective-permute-start(bf16[32,1024]{1,0:T(8,128)(2,1)S(1)} %get-tuple-element.115), channel_id=1, source_target_pairs={{0,8},{4,12},{8,0},{12,4},{1,9},{5,13},{9,1},{13,5},{2,10},{6,14},... | collective-permute-start | bytes 196616 | tf_op jit(solution)/shard_map/ppermute | solution.py:415
  50.5 5.5 %collective-permute-start.11 = (bf16[32,1024]{1,0:T(8,128)(2,1)S(1)}, bf16[32,1024]{1,0:T(8,128)(2,1)S(1)}, u32[]{:S(2)}, u32[]{:S(2)}) collective-permute-start(bf16[32,1024]{1,0:T(8,128)(2,1)S(1)} %get-tuple-element.115), channel_id=1, source_target_pairs={{0,4},{4,8},{8,12},{12,0},{1,5},{5,9},{9,13},{13,1},{2,6},{6,10},{... | collective-permute-start | bytes 196616 | tf_op jit(solution)/shard_map/ppermute | solution.py:415
  56.1 4.3 %collective-permute-start.16 = (bf16[32,1024]{1,0:T(8,128)(2,1)S(1)}, bf16[32,1024]{1,0:T(8,128)(2,1)S(1)}, u32[]{:S(2)}, u32[]{:S(2)}) collective-permute-start(bf16[32,1024]{1,0:T(8,128)(2,1)S(1)} %get-tuple-element.119), channel_id=1, source_target_pairs={{0,48},{16,0},{32,16},{48,32},{1,49},{17,1},{33,17},{49,33},{2,50}... | collective-permute-start | bytes 196616 | tf_op jit(solution)/shard_map/ppermute | solution.py:415
  56.2 5.3 %collective-permute-start.15 = (bf16[32,1024]{1,0:T(8,128)(2,1)S(1)}, bf16[32,1024]{1,0:T(8,128)(2,1)S(1)}, u32[]{:S(2)}, u32[]{:S(2)}) collective-permute-start(bf16[32,1024]{1,0:T(8,128)(2,1)S(1)} %get-tuple-element.119), channel_id=1, source_target_pairs={{0,32},{16,48},{32,0},{48,16},{1,33},{17,49},{33,1},{49,17},{2,34}... | collective-permute-start | bytes 196616 | tf_op jit(solution)/shard_map/ppermute | solution.py:415
  57.7 5.0 %collective-permute-start.14 = (bf16[32,1024]{1,0:T(8,128)(2,1)S(1)}, bf16[32,1024]{1,0:T(8,128)(2,1)S(1)}, u32[]{:S(2)}, u32[]{:S(2)}) collective-permute-start(bf16[32,1024]{1,0:T(8,128)(2,1)S(1)} %get-tuple-element.119), channel_id=1, source_target_pairs={{0,16},{16,32},{32,48},{48,0},{1,17},{17,33},{33,49},{49,1},{2,18}... | collective-permute-start | bytes 196616 | tf_op jit(solution)/shard_map/ppermute | solution.py:415
  62.9 13.2 %collective-permute-start.18 = (bf16[128,1536]{1,0:T(8,128)(2,1)S(1)}, bf16[128,1536]{1,0:T(8,128)(2,1)S(1)}, u32[]{:S(2)}, u32[]{:S(2)}) collective-permute-start(bf16[128,1536]{1,0:T(8,128)(2,1)S(1)} %bitcast.15), channel_id=1, source_target_pairs={{0,12},{4,8},{8,4},{12,0},{1,13},{5,9},{9,5},{13,1},{2,14},{6,10},... | collective-permute-start | bytes 1179656 | tf_op jit(solution)/shard_map/ppermute | solution.py:566
  63.9 12.1 %collective-permute-start.17 = (bf16[128,1536]{1,0:T(8,128)(2,1)S(1)}, bf16[128,1536]{1,0:T(8,128)(2,1)S(1)}, u32[]{:S(2)}, u32[]{:S(2)}) collective-permute-start(bf16[128,1536]{1,0:T(8,128)(2,1)S(1)} %bitcast.16), channel_id=1, source_target_pairs={{0,4},{4,0},{8,12},{12,8},{1,5},{5,1},{9,13},{13,9},{2,6},{6,2},{1... | collective-permute-start | bytes 1179656 | tf_op jit(solution)/shard_map/ppermute | solution.py:565
  63.9 4.3 %collective-permute-start.21 = (bf16[32,1024]{1,0:T(8,128)(2,1)S(1)}, bf16[32,1024]{1,0:T(8,128)(2,1)S(1)}, u32[]{:S(2)}, u32[]{:S(2)}) collective-permute-start(bf16[32,1024]{1,0:T(8,128)(2,1)S(1)} %get-tuple-element.121), channel_id=1, source_target_pairs={{0,192},{64,0},{128,64},{192,128},{1,193},{65,1},{129,65},{193,129... | collective-permute-start | bytes 196616 | tf_op jit(solution)/shard_map/ppermute | solution.py:415
  64.5 5.8 %collective-permute-start.20 = (bf16[32,1024]{1,0:T(8,128)(2,1)S(1)}, bf16[32,1024]{1,0:T(8,128)(2,1)S(1)}, u32[]{:S(2)}, u32[]{:S(2)}) collective-permute-start(bf16[32,1024]{1,0:T(8,128)(2,1)S(1)} %get-tuple-element.121), channel_id=1, source_target_pairs={{0,128},{64,192},{128,0},{192,64},{1,129},{65,193},{129,1},{193,65... | collective-permute-start | bytes 196616 | tf_op jit(solution)/shard_map/ppermute | solution.py:415
  65.6 5.5 %collective-permute-start.19 = (bf16[32,1024]{1,0:T(8,128)(2,1)S(1)}, bf16[32,1024]{1,0:T(8,128)(2,1)S(1)}, u32[]{:S(2)}, u32[]{:S(2)}) collective-permute-start(bf16[32,1024]{1,0:T(8,128)(2,1)S(1)} %get-tuple-element.121), channel_id=1, source_target_pairs={{0,64},{64,128},{128,192},{192,0},{1,65},{65,129},{129,193},{193,1... | collective-permute-start | bytes 196616 | tf_op jit(solution)/shard_map/ppermute | solution.py:415
  76.1 15.8 %collective-permute-start.25 = (bf16[128,1536]{1,0:T(8,128)(2,1)S(1)}, bf16[128,1536]{1,0:T(8,128)(2,1)S(1)}, u32[]{:S(2)}, u32[]{:S(2)}) collective-permute-start(bf16[128,1536]{1,0:T(8,128)(2,1)S(1)} %collective-permute-done.17.refs_1_), channel_id=1, source_target_pairs={{0,12},{4,8},{8,4},{12,0},{1,13},{5,9},{9,5},{13,1},{2,14},{6,10},... | collective-permute-start | bytes 1179656 | tf_op jit(solution)/shard_map/ppermute | solution.py:568
  86.6 20.1 %all-to-all-start = ((bf16[8,360,128]{2,1,0:T(8,128)(2,1)}), bf16[8,360,128]{2,1,0:T(8,128)(2,1)S(1)}, u32[]{:S(2)}, u32[]{:S(2)}) async-start(bf16[8,360,128]{2,1,0:T(8,128)(2,1)} %get-tuple-element.139), calls=%async_computation | async-start | bytes 1474560 | tf_op jit(solution)/shard_map/all_to_all | solution.py:642
  90.8 3.8 %collective-permute-start.22 = (bf16[128,1536]{1,0:T(8,128)(2,1)S(1)}, bf16[128,1536]{1,0:T(8,128)(2,1)S(1)}, u32[]{:S(2)}, u32[]{:S(2)}) collective-permute-start(bf16[128,1536]{1,0:T(8,128)(2,1)S(1)} %bitcast.17), channel_id=1, source_target_pairs={{0,1},{1,0},{2,3},{3,2},{4,5},{5,4},{6,7},{7,6},{8,9},{9,8},{10,11... | collective-permute-start | bytes 1179656 | tf_op jit(solution)/shard_map/ppermute | solution.py:571
  91.3 3.3 %collective-permute-start.23 = (bf16[128,1536]{1,0:T(8,128)(2,1)S(1)}, bf16[128,1536]{1,0:T(8,128)(2,1)S(1)}, u32[]{:S(2)}, u32[]{:S(2)}) collective-permute-start(bf16[128,1536]{1,0:T(8,128)(2,1)S(1)} %collective-permute-done.17.refs_1_), channel_id=1, source_target_pairs={{0,1},{1,0},{2,3},{3,2},{4,5},{5,4},{6,7},{7,6},{8,9},{9,8},{10,11... | collective-permute-start | bytes 1179656 | tf_op jit(solution)/shard_map/ppermute | solution.py:571
  91.3 3.3 %collective-permute-start.24 = (bf16[128,1536]{1,0:T(8,128)(2,1)S(1)}, bf16[128,1536]{1,0:T(8,128)(2,1)S(1)}, u32[]{:S(2)}, u32[]{:S(2)}) collective-permute-start(bf16[128,1536]{1,0:T(8,128)(2,1)S(1)} %collective-permute-done.18.refs_2_), channel_id=1, source_target_pairs={{0,1},{1,0},{2,3},{3,2},{4,5},{5,4},{6,7},{7,6},{8,9},{9,8},{10,11... | collective-permute-start | bytes 1179656 | tf_op jit(solution)/shard_map/ppermute | solution.py:571
  91.9 2.8 %collective-permute-start.26 = (bf16[128,1536]{1,0:T(8,128)(2,1)S(1)}, bf16[128,1536]{1,0:T(8,128)(2,1)S(1)}, u32[]{:S(2)}, u32[]{:S(2)}) collective-permute-start(bf16[128,1536]{1,0:T(8,128)(2,1)S(1)} %collective-permute-done.25.refs_3_), channel_id=1, source_target_pairs={{0,1},{1,0},{2,3},{3,2},{4,5},{5,4},{6,7},{7,6},{8,9},{9,8},{10,11... | collective-permute-start | bytes 1179656 | tf_op jit(solution)/shard_map/ppermute | solution.py:571
  91.9 1.8 %collective-permute-start.27 = (bf16[40,1024]{1,0:T(8,128)(2,1)}, bf16[40,1024]{1,0:T(8,128)(2,1)S(1)}, u32[]{:S(2)}, u32[]{:S(2)}) collective-permute-start(bf16[40,1024]{1,0:T(8,128)(2,1)} %copy-done.11), channel_id=1, source_target_pairs={{0,1},{1,0},{2,3},{3,2},{4,5},{5,4},{6,7},{7,6},{8,9},{9,8},{10,11... | collective-permute-start | bytes 245768 | tf_op jit(solution)/shard_map/ppermute | solution.py:630
  95.4 10.5 %collective-permute-start.30 = (bf16[40,1024]{1,0:T(8,128)(2,1)S(1)}, bf16[40,1024]{1,0:T(8,128)(2,1)S(1)}, u32[]{:S(2)}, u32[]{:S(2)}) collective-permute-start(bf16[40,1024]{1,0:T(8,128)(2,1)S(1)} %add_parts.4.refs_0_), channel_id=1, source_target_pairs={{0,48},{16,0},{32,16},{48,32},{1,49},{17,1},{33,17},{49,33},{2,50}... | collective-permute-start | bytes 245768 | tf_op jit(solution)/shard_map/ppermute | solution.py:415
  98.0 8.0 %collective-permute-start.29 = (bf16[40,1024]{1,0:T(8,128)(2,1)S(1)}, bf16[40,1024]{1,0:T(8,128)(2,1)S(1)}, u32[]{:S(2)}, u32[]{:S(2)}) collective-permute-start(bf16[40,1024]{1,0:T(8,128)(2,1)S(1)} %add_parts.4.refs_0_), channel_id=1, source_target_pairs={{0,32},{16,48},{32,0},{48,16},{1,33},{17,49},{33,1},{49,17},{2,34}... | collective-permute-start | bytes 245768 | tf_op jit(solution)/shard_map/ppermute | solution.py:415
  98.3 7.7 %collective-permute-start.28 = (bf16[40,1024]{1,0:T(8,128)(2,1)S(1)}, bf16[40,1024]{1,0:T(8,128)(2,1)S(1)}, u32[]{:S(2)}, u32[]{:S(2)}) collective-permute-start(bf16[40,1024]{1,0:T(8,128)(2,1)S(1)} %add_parts.4.refs_0_), channel_id=1, source_target_pairs={{0,16},{16,32},{32,48},{48,0},{1,17},{17,33},{33,49},{49,1},{2,18}... | collective-permute-start | bytes 245768 | tf_op jit(solution)/shard_map/ppermute | solution.py:415
  110.5 22.3 %all-to-all-start.1 = ((bf16[4,360,384]{2,1,0:T(8,128)(2,1)}), bf16[4,360,384]{2,1,0:T(8,128)(2,1)S(1)}, u32[]{:S(2)}, u32[]{:S(2)}) async-start(bf16[4,360,384]{2,1,0:T(8,128)(2,1)} %weight_term.1), calls=%async_computation.1 | async-start | bytes 2211840 | tf_op jit(solution)/shard_map/all_to_all | solution.py:672
  114.1 37.9 %copy-start.14 = (f32[15,16]{1,0:T(8,128)S(1)}, f32[15,16]{1,0:T(8,128)}, u32[]{:S(2)}) copy-start(f32[15,16]{1,0:T(8,128)} %get-tuple-element.152.amp) | copy-start | bytes 2884
  114.1 5.3 %collective-permute-start.33 = (bf16[40,1024]{1,0:T(8,128)(2,1)S(1)}, bf16[40,1024]{1,0:T(8,128)(2,1)S(1)}, u32[]{:S(2)}, u32[]{:S(2)}) collective-permute-start(bf16[40,1024]{1,0:T(8,128)(2,1)S(1)} %copy-done.9), channel_id=1, source_target_pairs={{0,12},{4,0},{8,4},{12,8},{1,13},{5,1},{9,5},{13,9},{2,14},{6,2},{... | collective-permute-start | bytes 245768 | tf_op jit(solution)/shard_map/ppermute | solution.py:415
  117.3 6.0 %collective-permute-start.32 = (bf16[40,1024]{1,0:T(8,128)(2,1)S(1)}, bf16[40,1024]{1,0:T(8,128)(2,1)S(1)}, u32[]{:S(2)}, u32[]{:S(2)}) collective-permute-start(bf16[40,1024]{1,0:T(8,128)(2,1)S(1)} %copy-done.9), channel_id=1, source_target_pairs={{0,8},{4,12},{8,0},{12,4},{1,9},{5,13},{9,1},{13,5},{2,10},{6,14},... | collective-permute-start | bytes 245768 | tf_op jit(solution)/shard_map/ppermute | solution.py:415
  118.2 6.0 %collective-permute-start.31 = (bf16[40,1024]{1,0:T(8,128)(2,1)S(1)}, bf16[40,1024]{1,0:T(8,128)(2,1)S(1)}, u32[]{:S(2)}, u32[]{:S(2)}) collective-permute-start(bf16[40,1024]{1,0:T(8,128)(2,1)S(1)} %copy-done.9), channel_id=1, source_target_pairs={{0,4},{4,8},{8,12},{12,0},{1,5},{5,9},{9,13},{13,1},{2,6},{6,10},{... | collective-permute-start | bytes 245768 | tf_op jit(solution)/shard_map/ppermute | solution.py:415
  124.2 8.5 %collective-permute-start.34 = (bf16[40,1024]{1,0:T(8,128)(2,1)S(1)}, bf16[40,1024]{1,0:T(8,128)(2,1)S(1)}, u32[]{:S(2)}, u32[]{:S(2)}) collective-permute-start(bf16[40,1024]{1,0:T(8,128)(2,1)S(1)} %add_parts.6.refs_0_), channel_id=1, source_target_pairs={{0,2},{2,0},{1,3},{3,1},{4,6},{6,4},{5,7},{7,5},{8,10},{10,8},{9,1... | collective-permute-start | bytes 245768 | tf_op jit(solution)/shard_map/ppermute | solution.py:630
  133.8 21.8 %all-to-all-start.2 = ((bf16[32,24,180]{2,1,0:T(8,128)(2,1)}), bf16[32,24,180]{2,1,0:T(8,128)(2,1)S(1)}, u32[]{:S(2)}, u32[]{:S(2)}) async-start(bf16[32,24,180]{2,1,0:T(8,128)(2,1)} %split_rows.1), calls=%async_computation.2 | async-start | bytes 786432 | tf_op jit(solution)/shard_map/all_to_all | solution.py:685
  142.2 5.1 %collective-permute-start.37 = (bf16[40,1024]{1,0:T(8,128)(2,1)S(1)}, bf16[40,1024]{1,0:T(8,128)(2,1)S(1)}, u32[]{:S(2)}, u32[]{:S(2)}) collective-permute-start(bf16[40,1024]{1,0:T(8,128)(2,1)S(1)} %add_parts.7.refs_0_), channel_id=1, source_target_pairs={{0,192},{64,0},{128,64},{192,128},{1,193},{65,1},{129,65},{193,129... | collective-permute-start | bytes 245768 | tf_op jit(solution)/shard_map/ppermute | solution.py:415
  145.2 6.0 %collective-permute-start.36 = (bf16[40,1024]{1,0:T(8,128)(2,1)S(1)}, bf16[40,1024]{1,0:T(8,128)(2,1)S(1)}, u32[]{:S(2)}, u32[]{:S(2)}) collective-permute-start(bf16[40,1024]{1,0:T(8,128)(2,1)S(1)} %add_parts.7.refs_0_), channel_id=1, source_target_pairs={{0,128},{64,192},{128,0},{192,64},{1,129},{65,193},{129,1},{193,65... | collective-permute-start | bytes 245768 | tf_op jit(solution)/shard_map/ppermute | solution.py:415
  146.0 6.0 %collective-permute-start.35 = (bf16[40,1024]{1,0:T(8,128)(2,1)S(1)}, bf16[40,1024]{1,0:T(8,128)(2,1)S(1)}, u32[]{:S(2)}, u32[]{:S(2)}) collective-permute-start(bf16[40,1024]{1,0:T(8,128)(2,1)S(1)} %add_parts.7.refs_0_), channel_id=1, source_target_pairs={{0,64},{64,128},{128,192},{192,0},{1,65},{65,129},{129,193},{193,1... | collective-permute-start | bytes 245768 | tf_op jit(solution)/shard_map/ppermute | solution.py:415
  (8 other events, 13.3 us)
